TPU v7x, 256 devices: a whole 4x4x8 slice. The times are simulated.
256 devices in a mesh: segment: 32 (over y_hi, z, core), tensor: 8 (over x, y_lo).
Axes of the slice: x: 4, y: 4 (y_hi: 2, y_lo: 2; y = y_hi * 2 + y_lo), z: 8, core: 2. Of those that a mesh axis runs over, the one named last changes fastest.
Arguments:
- teacher_slabs: bfloat16 [96, 128, 16384], P('segment', None, 'tensor'), may hold values from -6 to 6
- proj_weight: bfloat16 [8, 2048, 8192], P(None, 'segment', 'tensor'), may hold values from -0.046875 to 0.046875
- child_hidden: bfloat16 [96, 128, 8192], P('segment', None, 'tensor'), may hold values from -6 to 6
- norm_gain: float32 [32, 8192], P('segment', 'tensor'), may hold values from 0.5 to 1.5
- key_weight: bfloat16 [32, 8192, 1024], P('segment', 'tensor'), may hold values from -0.0625 to 0.0625
- value_weight: bfloat16 [32, 8192, 1024], P('segment', 'tensor'), may hold values from -0.0625 to 0.0625
- key_cotangent: bfloat16 [32, 128, 1024], P('segment'), may hold values from -3 to 3
- value_cotangent: bfloat16 [32, 128, 1024], P('segment'), may hold values from -3 to 3
- layer_map: int32 [32], replicated, may hold values from 0 to 47, as said below
- layer_counts: int32 [16], replicated, may hold values from 1 to 3, 32 in all
Outputs:
- hidden_grad: bfloat16 [96, 128, 8192], P('segment', None, 'tensor')
- key_weight_grad: bfloat16 [32, 8192, 1024], P('segment', 'tensor')
- value_weight_grad: bfloat16 [32, 8192, 1024], P('segment', 'tensor')
- gain_grad: float32 [32, 8192], P('segment', 'tensor')
Inputs may be any that keep to these rules, and one draw needn't show every extreme that they name: `layer_map`: strictly increasing. Teacher layer g is held by segment g // 3 in its slot g % 3. Child segment 16 + i owns layer_counts[i] consecutive child layers, in order; they sum to 32, and some segment owns 3.
All inputs are finite; a program needn't handle non-finite values.
Results may differ from a plain program's by a relative error of at most 0.023.
Values may be sent and summed in bfloat16 or wider, within the bound.
No kernel may reach another device: no remote copies, remote signals or barrier semaphores. Data moves between devices by JAX's collectives and lax.ppermute only.
A program may use at most 128 MiB of HBM per device.

v0:
```python
import jax
import jax.numpy as jnp
from jax import lax
from jax.sharding import PartitionSpec as P

EPSILON = 1e-05


def body(
    teacher_slabs,
    proj_weight,
    child_hidden,
    norm_gain,
    key_weight,
    value_weight,
    key_cotangent,
    value_cotangent,
    layer_map,
    layer_counts,
):
    segments = lax.axis_size("segment")
    tensors = lax.axis_size("tensor")
    middle = segments // 2
    segment_id = lax.axis_index("segment")
    slab_count, tokens, slab_width = teacher_slabs.shape
    piece_width = slab_width // segments
    layers = layer_map.shape[0]
    columns = proj_weight.shape[2]
    full_width = columns * tensors
    slot_count = child_hidden.shape[0]
    arranged = (
        teacher_slabs.reshape(slab_count, tokens, segments, piece_width)
        .transpose(0, 2, 1, 3)
        .reshape(slab_count, segments * tokens * piece_width)
    )
    received = lax.all_to_all(arranged, "segment", split_axis=1, concat_axis=0, tiled=True)
    row_count = received.shape[0]
    shard_piece = lax.all_gather(received, "tensor", axis=0, tiled=True)
    block_count = shard_piece.shape[0] // row_count
    grouped = shard_piece.reshape(block_count, row_count, tokens * piece_width)
    picked = jnp.take(grouped, layer_map, axis=1).reshape(block_count, layers, tokens, piece_width)
    partial_value = jnp.einsum(
        "tcks,tsd->ckd", picked, proj_weight, preferred_element_type=jnp.float32
    )
    prefix_end = jnp.cumsum(layer_counts)
    prefix_start = prefix_end - layer_counts
    projected = lax.psum(partial_value.astype(jnp.bfloat16), "segment").astype(jnp.float32)
    child_index = segment_id - middle
    child_slot = jnp.clip(child_index, 0, middle - 1)
    own_count = jnp.where(child_index >= 0, layer_counts[child_slot], 0)
    slot_ids = jnp.arange(slot_count)
    owned = slot_ids < own_count
    layer_of = jnp.clip(prefix_start[child_slot] + slot_ids, 0, layers - 1)
    target = jnp.take(projected, layer_of, axis=0)
    regression = jnp.where(owned[:, None, None], child_hidden.astype(jnp.float32) - target, 0.0)
    first_hidden = child_hidden[0].astype(jnp.float32)
    norm_scale = norm_gain[0]
    contract_last = (((1,), (1,)), ((), ()))
    delta_norm = lax.dot_general(
        key_cotangent[0], key_weight[0], contract_last, preferred_element_type=jnp.float32
    )
    delta_norm = delta_norm + lax.dot_general(
        value_cotangent[0], value_weight[0], contract_last, preferred_element_type=jnp.float32
    )
    squares, inner_sum = lax.psum(
        (
            jnp.sum(first_hidden * first_hidden, axis=1),
            jnp.sum(first_hidden * norm_scale * delta_norm, axis=1),
        ),
        "tensor",
    )
    inverse_rms = lax.rsqrt(squares / full_width + EPSILON)[:, None]
    normed = (first_hidden * inverse_rms * norm_scale).astype(jnp.bfloat16)
    contract_rows = (((0,), (0,)), ((), ()))
    key_grad = lax.dot_general(
        normed, key_cotangent[0], contract_rows, preferred_element_type=jnp.float32
    ).astype(jnp.bfloat16)
    value_grad = lax.dot_general(
        normed, value_cotangent[0], contract_rows, preferred_element_type=jnp.float32
    ).astype(jnp.bfloat16)
    gain_grad = jnp.sum(first_hidden * inverse_rms * delta_norm, axis=0)
    layer_grad = (
        inverse_rms * norm_scale * delta_norm
        - first_hidden * inverse_rms**3 * inner_sum[:, None] / full_width
    )
    is_child = segment_id >= middle
    layer_grad = jnp.where(is_child, layer_grad, 0.0)
    hidden_grad = regression.at[0].add(layer_grad).astype(jnp.bfloat16)
    key_grad = jnp.where(is_child, key_grad, jnp.zeros_like(key_grad))
    value_grad = jnp.where(is_child, value_grad, jnp.zeros_like(value_grad))
    gain_grad = jnp.where(is_child, gain_grad, 0.0)
    return (hidden_grad, key_grad[None], value_grad[None], gain_grad[None])


def solution(mesh):
    placed = (
        P("segment", None, "tensor"),
        P(None, "segment", "tensor"),
        P("segment", None, "tensor"),
        P("segment", "tensor"),
        P("segment", "tensor", None),
        P("segment", "tensor", None),
        P("segment", None, None),
        P("segment", None, None),
        P(),
        P(),
    )
    return jax.shard_map(
        body,
        mesh=mesh,
        in_specs=placed,
        out_specs=(
            P("segment", None, "tensor"),
            P("segment", "tensor", None),
            P("segment", "tensor", None),
            P("segment", "tensor"),
        ),
        check_vma=False,
    )
```

profile of v0, /device:TPU:1, one launch (start us, length us, event | category | flops | bytes accessed | tf_op | source)
XLA Modules:
  0.0 708.5 jit_solution(13283844756004594279)
XLA Ops:
  7.2 2.7 copy.29
  9.9 4.1 copy.37
  14.0 6.9 reshape.177
  20.9 63.1 %all_to_all.19 = bf16[3,32,8192]{2,0,1:T(4,128)(2,1)} all-to-all(bf16[3,32,8192]{2,0,1:T(4,128)(2,1)} %reshape.177), channel_id=1, replica_groups=mesh['segment'=32,'tensor'=8] {'segment'}, dimensions={1} | all-to-all | bytes 3145728 | tf_op jit(solution)/shard_map/all_to_all | solution.py:36
  84.0 4.3 all_to_all.17
  88.4 247.0 %all-gather.2.cloned.1.call-done = bf16[768,8192]{1,0:T(8,128)(2,1)} async-done(((bf16[96,8192]{1,0:T(8,128)(2,1)}), bf16[768,8192]{1,0:T(8,128)(2,1)}) %all-gather.2.cloned.1.call-update) | async-done | bytes 12582928 | tf_op jit(solution)/shard_map/all_gather | solution.py:38
  335.4 14.4 %copy.32 = bf16[8,96,8192]{2,0,1:T(8,128)(2,1)} copy(bf16[8,96,8192]{2,1,0:T(8,128)(2,1)} %bitcast.95) | data formatting | bytes 25165824 | tf_op jit(solution)/shard_map/reshape | solution.py:40
  349.8 7.3 %gather_fusion = bf16[32,8,8192]{2,1,0:T(8,128)(2,1)} fusion(bf16[8,96,8192]{2,0,1:T(8,128)(2,1)} %copy.32, s32[1024]{0:T(1024)S(1)} %pad_clamp_fusion.1), kind=kCustom, calls=%fused_computation | custom fusion | bytes 8388736 | tf_op jit(solution)/shard_map/jit(_take)/gather | solution.py:41
  357.1 6.5 copy.33
  363.6 12.7 %gather.11 = bf16[8,32,128,64]{3,2,1,0:T(8,128)(2,1)} reshape(bf16[8,32,8192]{2,1,0:T(8,128)(2,1)} %copy.33) | data formatting | bytes 8388608 | tf_op jit(solution)/shard_map/jit(_take)/gather | solution.py:41
  376.2 11.8 %bitcast_convert_fusion = bf16[32,128,1024]{2,1,0:T(8,128)(2,1)} fusion(bf16[8,32,128,64]{3,2,1,0:T(8,128)(2,1)} %gather.11, pred[32]{0:T(512)(128)(4,1)S(1)} %compare_and_fusion, bf16[8,64,1024]{2,1,0:T(8,128)(2,1)S(1)} %copy-done.6), kind=kOutput, calls=%fused_computation.2 | convolution fusion | flops 4301258752 | bytes 13631520 | tf_op jit(solution)/shard_map/tcks,tsd->ckd/dot_general | solution.py:42
  388.1 0.6 copy-done.5
  388.7 0.1 copy.28
  388.8 0.1 reduce.2
  388.9 0.6 dynamic_slice.6
  389.5 0.6 dynamic_slice.7
  390.7 0.1 fusion.15
  390.9 15.5 %psum.22 = f32[128]{0:T(128)S(1)} all-reduce(f32[128]{0:T(128)S(1)} %fusion.15), channel_id=1, replica_groups=mesh['segment'=32,'tensor'=8] {'tensor'}, use_global_device_ids=true, to_apply=%region_3.4 | all-reduce | flops 128 | bytes 1024 | tf_op jit(solution)/shard_map/psum | solution.py:65
  406.4 2.4 fusion.3
  408.8 1.9 fusion.26
  410.7 13.1 %psum.23 = f32[128]{0:T(128)S(1)} all-reduce(f32[128]{0:T(128)S(1)} %get-tuple-element.17), channel_id=1, replica_groups=mesh['segment'=32,'tensor'=8] {'tensor'}, use_global_device_ids=true, to_apply=%region_5.6 | all-reduce | flops 128 | bytes 1024 | tf_op jit(solution)/shard_map/psum | solution.py:65
  423.8 0.7 fusion.36
  424.5 0.7 compare_and_fusion.1
  425.2 3.1 select_bitcast_fusion.1
  428.3 2.1 select_bitcast_fusion
  430.4 0.6 broadcast_select_fusion
  431.0 248.8 %all-reduce.2.cloned.1.call-done = bf16[32,128,1024]{2,1,0:T(8,128)(2,1)} async-done(((bf16[32,128,1024]{2,1,0:T(8,128)(2,1)}), bf16[32,128,1024]{2,1,0:T(8,128)(2,1)}) %all-reduce.2.cloned.1.call-update) | async-done | bytes 8388624 | tf_op jit(solution)/shard_map/psum | solution.py:47
  679.8 11.3 %convert_element_type.37 = f32[32,128,1024]{2,1,0:T(8,128)} convert(bf16[32,128,1024]{2,1,0:T(8,128)(2,1)} %all-reduce.2.cloned.1.call-done) | non-fusion elementwise | flops 4194304 | bytes 25165824 | tf_op jit(solution)/shard_map/convert_element_type | solution.py:47
  691.1 7.6 %gather_fusion.1 = f32[3,128,1024]{2,1,0:T(8,128)} fusion(f32[32,128,1024]{2,1,0:T(8,128)} %convert_element_type.37, s32[1024]{0:T(1024)S(1)} %pad_clamp_fusion), kind=kCustom, calls=%fused_computation.1 | custom fusion | bytes 3145740 | tf_op jit(solution)/shard_map/jit(_take)/gather | solution.py:54
  698.7 1.7 subtract_select_fusion
  700.4 0.3 fusion.22
  700.7 1.0 convert_element_type.40
  (26 shorter events, 0.2 us)
Async XLA Ops:
  7.2 401.6 %copy-start = (bf16[1,1024,1024]{2,1,0:T(8,128)(2,1)S(1)}, bf16[1,1024,1024]{2,1,0:T(8,128)(2,1)}, u32[]{:S(2)}) copy-start(bf16[1,1024,1024]{2,1,0:T(8,128)(2,1)} %param.16) | copy-start | bytes 6291460
  7.2 328.2 %all-gather.2.cloned.1.call-start = ((), (), s32[]{:S(2)}) async-start(), calls=%async_computation.1 | async-start | bytes 14155776 | tf_op jit(solution)/shard_map/all_gather | solution.py:38
  84.0 4.4 copy-start.7
  88.3 591.5 %all-reduce.2.cloned.1.call-start = ((), (), s32[]{:S(2)}) async-start(), calls=%async_computation.2 | async-start | bytes 16777216 | tf_op jit(solution)/shard_map/psum | solution.py:47
  363.6 12.7 %copy-start.6 = (bf16[8,64,1024]{2,1,0:T(8,128)(2,1)S(1)}, bf16[8,64,1024]{2,1,0:T(8,128)(2,1)}, u32[]{:S(2)}) copy-start(bf16[8,64,1024]{2,1,0:T(8,128)(2,1)} %param.13) | copy-start | bytes 3145732
  388.0 0.7 copy-start.5
  388.0 2.7 copy-start.1
  388.0 18.4 %copy-start.2 = (bf16[1,128,1024]{2,1,0:T(8,128)(2,1)S(1)}, bf16[1,128,1024]{2,1,0:T(8,128)(2,1)}, u32[]{:S(2)}) copy-start(bf16[1,128,1024]{2,1,0:T(8,128)(2,1)} %param.19) | copy-start | bytes 786436
  388.0 20.8 %copy-start.4 = (f32[1,1024]{1,0:T(1,128)S(1)}, f32[1,1024]{1,0:T(1,128)}, u32[]{:S(2)}) copy-start(f32[1,1024]{1,0:T(1,128)} %param.15) | copy-start | bytes 12292
  423.8 4.5 copy-start.3
Sparse Core Ops, SparseCore 0:
  88.4 246.9 all-gather.1
  388.2 291.5 all-reduce.1
where the time goes:
time: 710 us; the launch traced here: 709 us
  waiting for transfers between devices  496 us (70%)
  blocking collectives  91.6 us (13%)
  local copies, waits for them, and re-layouts  68.3 us (10%)
  matrix products  21.3 us (3%)
  other arithmetic  16.5 us (2%)
  between operations  14.8 us (2%)
    psum x1, waiting for transfers between devices, body(): lax.psum(partial_value.astype(jnp.bfloat16), 'segment').astype(jnp.float32)  249 us
    all_gather x1, waiting for transfers between devices, body(): shard_piece = lax.all_gather(received, 'tensor', axis=0, tiled=True)  247 us
    all_to_all x1, blocking collectives, body(): lax.all_to_all(arranged, 'segment', split_axis=1, concat_axis=0, tiled=True)  63.1 us
    psum x2, blocking collectives, body(): lax.psum((jnp.sum(first_hidden * first_hidden, axis=1), jnp.sum(first_hid...  28.5 us
    gather x3, local copies, waits for them, and re-layouts, body(): jnp.take(grouped, layer_map, axis=1)  26.5 us
    all_to_all x3, local copies, waits for them, and re-layouts, body(): lax.all_to_all(arranged, 'segment', split_axis=1, concat_axis=0, tiled=True)  15.2 us
    reshape x1, local copies, waits for them, and re-layouts, body(): grouped = shard_piece.reshape(block_count, row_count, tokens * piece_width)  14.4 us
  transfers between devices with their start and end apart: 2, of which 2 were waited for; matrix products, arithmetic and copies ran while one was open for 2% of the time, Pallas kernels for 0%

commit v1 on v0

v1 whole, which is shorter than its diff:
```python
import jax
import jax.numpy as jnp
from jax import lax
from jax.experimental import pallas as pl
from jax.experimental.pallas import tpu as pltpu
from jax.sharding import Mesh, PartitionSpec as P

EPSILON = 1e-05
MIB = 1 << 20

SEGMENT = ("yh", "z", "c")
TENSOR = ("x", "yl")
YH, Z, C, X, YL = 2, 8, 2, 4, 2
QUARTERS = YH * C
LANES = 128


def pick_kernel(layer_map, received, picked):
    def step(layer, carry):
        picked[layer] = received[layer_map[layer]]
        return carry

    lax.fori_loop(0, picked.shape[0], step, 0)


def pick(layer_map, received):
    layers = layer_map.shape[0]
    return pl.pallas_call(
        pick_kernel,
        out_shape=jax.ShapeDtypeStruct((layers, *received.shape[1:]), received.dtype),
        in_specs=[
            pl.BlockSpec(memory_space=pltpu.SMEM),
            pl.BlockSpec(memory_space=pltpu.VMEM),
        ],
        out_specs=pl.BlockSpec(memory_space=pltpu.VMEM),
        cost_estimate=pl.CostEstimate(flops=0, bytes_accessed=1300000, transcendentals=0),
        name="pick_layers",
    )(layer_map, received)


def project_kernel(place, slot_layer, features, w0, w1, w2, w3, out, weight, product):
    blocks, layers, halves, tokens, lanes = features.shape
    piece = w0.shape[1]
    depth = halves * lanes
    for part, block in enumerate((w0, w1, w2, w3)):
        for t in range(blocks):
            row = pl.multiple_of(t * depth + place[part] * piece, piece)
            weight[pl.ds(row, piece), :] = block[t]
    group = 8
    rows = group * tokens

    def step(index, carry):
        first = index * group
        left = jnp.concatenate(
            [
                features[t, pl.ds(first, group), h].reshape(rows, lanes)
                for t in range(blocks)
                for h in range(halves)
            ],
            axis=1,
        )
        value = jnp.dot(left, weight[...], preferred_element_type=jnp.float32)
        product[pl.ds(first, group)] = value.astype(product.dtype).reshape(group, tokens, value.shape[1])
        return carry

    lax.fori_loop(0, layers // group, step, 0)

    def place_slot(slot, carry):
        out[slot] = product[slot_layer[slot]]
        return carry

    lax.fori_loop(0, out.shape[0], place_slot, 0)


def project(place, slot_layer, features, weights):
    blocks, layers, halves, tokens, lanes = features.shape
    columns = weights[0].shape[2]
    slots = slot_layer.shape[0]
    depth = blocks * halves * lanes
    vmem = pl.BlockSpec(memory_space=pltpu.VMEM)
    smem = pl.BlockSpec(memory_space=pltpu.SMEM)
    return pl.pallas_call(
        project_kernel,
        out_shape=jax.ShapeDtypeStruct((slots, tokens, columns), jnp.bfloat16),
        in_specs=[smem, smem] + [vmem] * 5,
        out_specs=vmem,
        scratch_shapes=[
            pltpu.VMEM((depth, columns), jnp.bfloat16),
            pltpu.VMEM((layers, tokens, columns), jnp.bfloat16),
        ],
        compiler_params=pltpu.CompilerParams(vmem_limit_bytes=40 * MIB),
        cost_estimate=pl.CostEstimate(
            flops=2 * layers * tokens * depth * columns, bytes_accessed=11 * MIB, transcendentals=0
        ),
        name="project",
    )(place, slot_layer, features, *weights)


def body(
    teacher_slabs,
    proj_weight,
    child_hidden,
    norm_gain,
    key_weight,
    value_weight,
    key_cotangent,
    value_cotangent,
    layer_map,
    layer_counts,
):
    yh, z, c = lax.axis_index("yh"), lax.axis_index("z"), lax.axis_index("c")
    slab_count, tokens, slab_width = teacher_slabs.shape
    layers = layer_map.shape[0]
    columns = proj_weight.shape[2]
    full_width = columns * X * YL
    slot_count = child_hidden.shape[0]
    quarter = tokens // QUARTERS
    segments = YH * Z * C
    middle = segments // 2

    swap = [(0, 1), (1, 0)]
    w_own = proj_weight
    w_sib = lax.ppermute(w_own, "c", swap)
    w_far = lax.ppermute(w_own, "yh", swap)
    w_far_sib = lax.ppermute(w_far, "c", swap)
    place = jnp.stack([2 * yh + c, 2 * yh + 1 - c, 2 * (1 - yh) + c, 2 * (1 - yh) + 1 - c]).astype(jnp.int32)

    arranged = (
        teacher_slabs.reshape(slab_count, YH, C, quarter, YH, Z, LANES)
        .transpose(1, 5, 2, 0, 4, 3, 6)
        .reshape(segments, slab_count * YH * quarter, LANES)
    )
    received = lax.all_to_all(arranged, SEGMENT, split_axis=0, concat_axis=0, tiled=True)
    received = received[:middle].reshape(middle * slab_count, YH * quarter, LANES)
    picked = pick(layer_map, received)
    gathered = lax.all_gather(picked, TENSOR, axis=0, tiled=False)
    features = gathered.reshape(X * YL, layers, YH, quarter, LANES)

    prefix_end = jnp.cumsum(layer_counts)
    prefix_start = prefix_end - layer_counts
    slot_ids = jnp.arange(slot_count)
    slot_layer = jnp.clip(prefix_start[:, None] + slot_ids[None, :], 0, layers - 1).reshape(-1).astype(jnp.int32)
    partial = project(place, slot_layer, features, (w_own, w_sib, w_far, w_far_sib))
    per_z = C * slot_count
    mine = lax.psum_scatter(
        partial.reshape(Z, per_z * quarter, columns), "z", scatter_dimension=0, tiled=False
    ).reshape(C, slot_count, quarter, columns)
    from_teacher = lax.ppermute(mine, "yh", [(0, 1)])
    both = jnp.stack([from_teacher, mine])
    keep = jnp.where(c == 0, both[:, 0], both[:, 1])
    give = jnp.where(c == 0, both[:, 1], both[:, 0])
    other = lax.ppermute(give, "c", swap)
    low = jnp.where(c == 0, keep, other)
    high = jnp.where(c == 0, other, keep)
    target = jnp.stack([low, high], axis=2).transpose(1, 0, 2, 3, 4).reshape(slot_count, tokens, columns)

    is_child = yh == 1
    child_slot = 2 * z + c
    own_count = jnp.where(is_child, layer_counts[child_slot], 0)
    owned = slot_ids < own_count
    regression = jnp.where(
        owned[:, None, None], child_hidden.astype(jnp.float32) - target.astype(jnp.float32), 0.0
    )

    first_hidden = child_hidden[0].astype(jnp.float32)
    norm_scale = norm_gain[0]
    contract_last = (((1,), (1,)), ((), ()))
    delta_norm = lax.dot_general(
        key_cotangent[0], key_weight[0], contract_last, preferred_element_type=jnp.float32
    )
    delta_norm = delta_norm + lax.dot_general(
        value_cotangent[0], value_weight[0], contract_last, preferred_element_type=jnp.float32
    )
    sums = lax.psum(
        jnp.stack(
            [
                jnp.sum(first_hidden * first_hidden, axis=1),
                jnp.sum(first_hidden * norm_scale * delta_norm, axis=1),
            ]
        ),
        TENSOR,
    )
    squares, inner_sum = sums[0], sums[1]
    inverse_rms = lax.rsqrt(squares / full_width + EPSILON)[:, None]
    normed = (first_hidden * inverse_rms * norm_scale).astype(jnp.bfloat16)
    contract_rows = (((0,), (0,)), ((), ()))
    key_grad = lax.dot_general(
        normed, key_cotangent[0], contract_rows, preferred_element_type=jnp.float32
    ).astype(jnp.bfloat16)
    value_grad = lax.dot_general(
        normed, value_cotangent[0], contract_rows, preferred_element_type=jnp.float32
    ).astype(jnp.bfloat16)
    gain_grad = jnp.sum(first_hidden * inverse_rms * delta_norm, axis=0)
    layer_grad = (
        inverse_rms * norm_scale * delta_norm
        - first_hidden * inverse_rms**3 * inner_sum[:, None] / full_width
    )
    layer_grad = jnp.where(is_child, layer_grad, 0.0)
    hidden_grad = regression.at[0].add(layer_grad).astype(jnp.bfloat16)
    key_grad = jnp.where(is_child, key_grad, jnp.zeros_like(key_grad))
    value_grad = jnp.where(is_child, value_grad, jnp.zeros_like(value_grad))
    gain_grad = jnp.where(is_child, gain_grad, 0.0)
    return (hidden_grad, key_grad[None], value_grad[None], gain_grad[None])


def solution(mesh):
    fine = Mesh(mesh.devices.reshape(YH, Z, C, X, YL), (*SEGMENT, *TENSOR))
    placed = (
        P(SEGMENT, None, TENSOR),
        P(None, SEGMENT, TENSOR),
        P(SEGMENT, None, TENSOR),
        P(SEGMENT, TENSOR),
        P(SEGMENT, TENSOR, None),
        P(SEGMENT, TENSOR, None),
        P(SEGMENT, None, None),
        P(SEGMENT, None, None),
        P(),
        P(),
    )
    return jax.shard_map(
        body,
        mesh=fine,
        in_specs=placed,
        out_specs=(
            P(SEGMENT, None, TENSOR),
            P(SEGMENT, TENSOR, None),
            P(SEGMENT, TENSOR, None),
            P(SEGMENT, TENSOR),
        ),
        check_vma=False,
    )
```

time: 710 us -> 249 us (0.35)
  waiting for transfers between devices: 496 us -> 108 us
  local copies, waits for them, and re-layouts: 68.3 us -> 7.93 us
  starting transfers between devices: 0.08 us -> 26.5 us
  blocking collectives: 91.6 us -> 68.5 us
  other arithmetic: 16.5 us -> 3.05 us
  matrix products: 21.3 us -> 10.5 us
  Pallas kernels: 0 us -> 9.7 us
    psum x1 -> x0, waiting for transfers between devices: 249 us -> none  [body(): lax.psum(partial_value.astype(jnp.bfloat16), 'segment').astype(jnp.float32)]
    all_gather x1, waiting for transfers between devices: 247 us -> 34.5 us  [body(): gathered = lax.all_gather(picked, TENSOR, axis=0, tiled=False)]
    ppermute x0 -> x5, waiting for transfers between devices: none -> 54.6 us  [the longest x1 49.5 us: body(): w_far = lax.ppermute(w_own, 'yh', swap)]
    gather x4 -> x0, local copies, waits for them, and re-layouts: 34 us -> none  [the longest x3 26.5 us: body(): jnp.take(grouped, layer_map, axis=1)]
    ppermute x0 -> x5, starting transfers between devices: none -> 26.4 us  [the longest x1 14.5 us: body(): w_far_sib = lax.ppermute(w_far, 'c', swap)]
    reduce_scatter x0 -> x1, waiting for transfers between devices: none -> 18.7 us  [body(): lax.psum_scatter(partial.reshape(Z, per_z * quarter, columns), 'z', scatt...]
    all_to_all x3 -> x0, local copies, waits for them, and re-layouts: 15.2 us -> none  [body(): lax.all_to_all(arranged, 'segment', split_axis=1, concat_axis=0, tiled=True)]
    reshape x1 -> x0, local copies, waits for them, and re-layouts: 14.4 us -> none  [body(): grouped = shard_piece.reshape(block_count, row_count, tokens * piece_width)]
  transfers between devices with their start and end apart: 2 -> 7, of which waited for: 2 -> 6; matrix products, arithmetic and copies ran while one was open for 2% -> 5% of each run, Pallas kernels for 0% -> 0%
where the time goes in v1:
time: 249 us
  waiting for transfers between devices  108 us (43%)
  blocking collectives  68.5 us (28%)
  starting transfers between devices  26.5 us (11%)
  between operations  14.9 us (6%)
  matrix products  10.5 us (4%)
  Pallas kernels  9.7 us (4%)
  local copies, waits for them, and re-layouts  7.93 us (3%)
  other arithmetic  3.05 us (1%)
    all_to_all x1, blocking collectives, body(): lax.all_to_all(arranged, SEGMENT, split_axis=0, concat_axis=0, tiled=True)  53 us
    ppermute x1, waiting for transfers between devices, body(): w_far = lax.ppermute(w_own, 'yh', swap)  49.5 us
    all_gather x1, waiting for transfers between devices, body(): gathered = lax.all_gather(picked, TENSOR, axis=0, tiled=False)  34.5 us
    reduce_scatter x1, waiting for transfers between devices, body(): lax.psum_scatter(partial.reshape(Z, per_z * quarter, columns), 'z', scatt...  18.7 us
    psum x1, blocking collectives, body(): lax.psum(jnp.stack([jnp.sum(first_hidden * first_hidden, axis=1), jnp.sum...  15.5 us
    ppermute x1, starting transfers between devices, body(): w_far_sib = lax.ppermute(w_far, 'c', swap)  14.5 us
    pallas_call x1, Pallas kernels, project(): pl.pallas_call(project_kernel, out_shape=jax.ShapeDtypeStruct((slots, tok...  7.57 us
    unnamed x19, local copies, waits for them, and re-layouts  5.82 us
  transfers between devices with their start and end apart: 7, of which 6 were waited for; matrix products, arithmetic and copies ran while one was open for 5% of the time, Pallas kernels for 0%

profile of v1, /device:TPU:1, one launch (start us, length us, event | category | flops | bytes accessed | tf_op | source)
XLA Modules:
  0.0 248.8 jit_solution(14977887657889461361)
XLA Ops:
  7.2 2.0 copy.26
  9.2 0.4 copy.23
  9.6 53.0 %all_to_all.5 = bf16[32,192,128]{2,1,0:T(8,128)(2,1)S(1)} all-to-all(bf16[32,192,128]{2,1,0:T(8,128)(2,1)S(1)} %bitcast.123), channel_id=1, replica_groups=mesh['yh'=2,'z'=8,'c'=2,'x'=4,'yl'=2] {'yh','z','c'}, dimensions={0} | all-to-all | bytes 3145728 | tf_op jit(solution)/shard_map/all_to_all | solution.py:133
  62.6 0.9 slice.49
  63.5 2.1 pick_layers.1
  65.8 0.4 collective-permute-start.1
  66.2 2.5 %collective-permute-start = (bf16[8,64,1024]{2,1,0:T(8,128)(2,1)S(1)}, bf16[8,64,1024]{2,1,0:T(8,128)(2,1)}, u32[]{:S(2)}, u32[]{:S(2)}) collective-permute-start(bf16[8,64,1024]{2,1,0:T(8,128)(2,1)S(1)} %copy-done.3), channel_id=1, source_target_pairs={{0,8},{8,0},{1,9},{9,1},{2,10},{10,2},{3,11},{11,3},{4,12},{12,4},... | collective-permute-start | bytes 3145736 | tf_op jit(solution)/shard_map/ppermute | solution.py:123
  68.7 49.5 %collective-permute-done.1.w2 = bf16[8,64,1024]{2,1,0:T(8,128)(2,1)} collective-permute-done((bf16[8,64,1024]{2,1,0:T(8,128)(2,1)S(1)}, bf16[8,64,1024]{2,1,0:T(8,128)(2,1)}, u32[]{:S(2)}, u32[]{:S(2)}) %collective-permute-start.1) | collective-permute-done | bytes 1048608 | tf_op jit(solution)/shard_map/ppermute | solution.py:124
  118.2 14.5 %collective-permute-start.2 = (bf16[8,64,1024]{2,1,0:T(8,128)(2,1)}, bf16[8,64,1024]{2,1,0:T(8,128)(2,1)}, u32[]{:S(2)}, u32[]{:S(2)}) collective-permute-start(bf16[8,64,1024]{2,1,0:T(8,128)(2,1)} %collective-permute-done.1.w2), channel_id=1, source_target_pairs={{0,8},{8,0},{1,9},{9,1},{2,10},{10,2},{3,11},{11,3},{4,12},{12,4},... | collective-permute-start | bytes 3145736 | tf_op jit(solution)/shard_map/ppermute | solution.py:125
  132.8 0.1 reduce.2
  133.2 2.1 collective-permute-done.2.w3
  135.3 34.5 %all-gather.3.cloned.1.call-done = bf16[256,64,128]{2,1,0:T(8,128)(2,1)} async-done(((bf16[32,64,128]{2,1,0:T(8,128)(2,1)}), bf16[256,64,128]{2,1,0:T(8,128)(2,1)}) %all-gather.3.cloned.1.call-update) | async-done | bytes 4194320 | tf_op jit(solution)/shard_map/all_gather | solution.py:136
  169.8 2.2 copy-done.2
  172.0 7.6 %project.1 = bf16[48,32,1024]{2,1,0:T(8,128)(2,1)S(1)} custom-call(s32[4]{0:T(128)S(1)} %pad_add_fusion.place, s32[48]{0:T(128)S(1)} %min.12.slot_layer, bf16[8,32,2,32,128]{4,3,2,1,0:T(8,128)(2,1)S(1)} %bitcast.122, bf16[8,64,1024]{2,1,0:T(8,128)(2,1)S(1)} %copy-done.3, bf16[8,64,1024]{2,1,0:T(8,128)(2,1)} %collective-permute-done.w1, ...), custom_call_target="tpu_custom_call" | custom-call | flops 4294967296 | bytes 11534336 | tf_op jit(solution)/shard_map/project/pallas_call | solution.py:82
  179.6 1.6 copy-done.1
  181.3 0.6 dynamic_slice.3
  182.5 2.4 fusion
  185.0 1.9 fusion.12
  186.9 15.5 %psum.7 = f32[2,128]{1,0:T(2,128)S(1)} all-reduce(f32[2,128]{1,0:T(2,128)S(1)} %pad_maximum_fusion.1), channel_id=1, replica_groups=mesh['yh'=2,'z'=8,'c'=2,'x'=4,'yl'=2] {'x','yl'}, use_global_device_ids=true, to_apply=%region_4.5 | all-reduce | flops 256 | bytes 2048 | tf_op jit(solution)/shard_map/psum | solution.py:174
  202.4 3.1 %select_bitcast_fusion = bf16[1,1024,1024]{2,1,0:T(8,128)(2,1)} fusion(pred[]{:T(512)S(6)} %eq.4, bf16[1,128,1024]{2,1,0:T(8,128)(2,1)} %param.19, f32[1024]{0:T(1024)S(1)} %bitcast.133, f32[128]{0:T(128)S(1)} %get-tuple-element.19, bf16[3,128,1024]{2,1,0:T(8,128)(2,1)S(1)} %copy-done.4), kind=kOutput, calls=%fused_computation.4 | convolution fusion | flops 271056896 | bytes 2626049 | tf_op jit(solution)/shard_map/dot_general | solution.py:190
  205.5 18.7 %reduce-scatter.2.cloned.1.call-done = bf16[1,192,1024]{2,1,0:T(8,128)(2,1)} async-done(((bf16[8,192,1024]{2,1,0:T(8,128)(2,1)}), bf16[1,192,1024]{2,1,0:T(8,128)(2,1)}) %reduce-scatter.2.cloned.1.call-update) | async-done | bytes 393232 | tf_op jit(solution)/shard_map/reduce_scatter | solution.py:145
  224.2 4.7 %collective-permute-start.3 = (bf16[2,3,32,1024]{3,2,1,0:T(8,128)(2,1)}, bf16[2,3,32,1024]{3,2,1,0:T(8,128)(2,1)S(1)}, u32[]{:S(2)}, u32[]{:S(2)}) collective-permute-start(bf16[2,3,32,1024]{3,2,1,0:T(8,128)(2,1)} %bitcast.127), channel_id=1, source_target_pairs={{0,128},{1,129},{2,130},{3,131},{4,132},{5,133},{6,134},{7,135},{8... | collective-permute-start | bytes 1179656 | tf_op jit(solution)/shard_map/ppermute | solution.py:148
  228.9 3.1 %select_bitcast_fusion.1 = bf16[1,1024,1024]{2,1,0:T(8,128)(2,1)} fusion(pred[]{:T(512)S(6)} %eq.4, bf16[1,128,1024]{2,1,0:T(8,128)(2,1)} %param.18, f32[1024]{0:T(1024)S(1)} %bitcast.134, f32[128]{0:T(128)S(1)} %get-tuple-element.19, bf16[3,128,1024]{2,1,0:T(8,128)(2,1)S(1)} %copy-done.4), kind=kOutput, calls=%fused_computation.5 | convolution fusion | flops 271056896 | bytes 2626049 | tf_op jit(solution)/shard_map/dot_general | solution.py:187
  232.0 2.3 collective-permute-done.3
  234.4 4.3 %collective-permute-start.4 = (bf16[2,3,32,1024]{3,2,0,1:T(8,128)(2,1)S(1)}, bf16[2,3,32,1024]{3,2,0,1:T(8,128)(2,1)S(1)}, u32[]{:S(2)}, u32[]{:S(2)}) collective-permute-start(bf16[2,3,32,1024]{3,2,0,1:T(8,128)(2,1)S(1)} %select_bitcast_fusion.2), channel_id=1, source_target_pairs={{0,8},{8,0},{1,9},{9,1},{2,10},{10,2},{3,11},{11,3},{4,12},{12,4},... | collective-permute-start | bytes 1179656 | tf_op jit(solution)/shard_map/ppermute | solution.py:152
  238.7 0.1 fusion.23
  238.8 0.6 broadcast_select_fusion.1
  239.4 0.6 collective-permute-done.4
  240.0 0.1 fusion.27
  240.3 0.4 fusion.4
  240.6 0.3 fusion.21
  240.9 1.0 convert_element_type.44
  (33 shorter events, 0.7 us)
Async XLA Ops:
  7.2 177.8 %copy-start = (bf16[1,1024,1024]{2,1,0:T(8,128)(2,1)S(1)}, bf16[1,1024,1024]{2,1,0:T(8,128)(2,1)}, u32[]{:S(2)}) copy-start(bf16[1,1024,1024]{2,1,0:T(8,128)(2,1)} %param.16) | copy-start | bytes 6291460
  7.2 162.6 %all-gather.3.cloned.1.call-start = ((), (), s32[]{:S(2)}) async-start(), calls=%async_computation.3 | async-start | bytes 4718592 | tf_op jit(solution)/shard_map/all_gather | solution.py:136
  62.6 3.1 %copy-start.3 = (bf16[8,64,1024]{2,1,0:T(8,128)(2,1)S(1)}, bf16[8,64,1024]{2,1,0:T(8,128)(2,1)}, u32[]{:S(2)}) copy-start(bf16[8,64,1024]{2,1,0:T(8,128)(2,1)} %w0.1) | copy-start | bytes 3145732
  62.6 70.1 %copy-start.8 = (s32[16]{0:T(128)S(1)}, s32[16]{0:T(128)}, u32[]{:S(2)}) copy-start(s32[16]{0:T(128)} %param.21) | copy-start | bytes 196
  65.7 158.5 %reduce-scatter.2.cloned.1.call-start = ((), (), s32[]{:S(2)}) async-start(), calls=%async_computation.2 | async-start | bytes 3538944 | tf_op jit(solution)/shard_map/reduce_scatter | solution.py:145
  65.8 52.5 %collective-permute-start.1 = (bf16[8,64,1024]{2,1,0:T(8,128)(2,1)S(1)}, bf16[8,64,1024]{2,1,0:T(8,128)(2,1)}, u32[]{:S(2)}, u32[]{:S(2)}) collective-permute-start(bf16[8,64,1024]{2,1,0:T(8,128)(2,1)S(1)} %copy-done.3), channel_id=1, source_target_pairs={{0,128},{128,0},{1,129},{129,1},{2,130},{130,2},{3,131},{131,3},{4... | collective-permute-start | bytes 3145736 | tf_op jit(solution)/shard_map/ppermute | solution.py:124
  66.2 67.0 %collective-permute-start = (bf16[8,64,1024]{2,1,0:T(8,128)(2,1)S(1)}, bf16[8,64,1024]{2,1,0:T(8,128)(2,1)}, u32[]{:S(2)}, u32[]{:S(2)}) collective-permute-start(bf16[8,64,1024]{2,1,0:T(8,128)(2,1)S(1)} %copy-done.3), channel_id=1, source_target_pairs={{0,8},{8,0},{1,9},{9,1},{2,10},{10,2},{3,11},{11,3},{4,12},{12,4},... | collective-permute-start | bytes 3145736 | tf_op jit(solution)/shard_map/ppermute | solution.py:123
  118.2 17.1 %collective-permute-start.2 = (bf16[8,64,1024]{2,1,0:T(8,128)(2,1)}, bf16[8,64,1024]{2,1,0:T(8,128)(2,1)}, u32[]{:S(2)}, u32[]{:S(2)}) collective-permute-start(bf16[8,64,1024]{2,1,0:T(8,128)(2,1)} %collective-permute-done.1.w2), channel_id=1, source_target_pairs={{0,8},{8,0},{1,9},{9,1},{2,10},{10,2},{3,11},{11,3},{4,12},{12,4},... | collective-permute-start | bytes 3145736 | tf_op jit(solution)/shard_map/ppermute | solution.py:125
  169.8 2.2 copy-start.2
  179.6 1.7 copy-start.1
  181.2 1.3 copy-start.6
  181.2 3.7 %copy-start.4 = (bf16[3,128,1024]{2,1,0:T(8,128)(2,1)S(1)}, bf16[3,128,1024]{2,1,0:T(8,128)(2,1)}, u32[]{:S(2)}) copy-start(bf16[3,128,1024]{2,1,0:T(8,128)(2,1)} %param.14) | copy-start | bytes 2359300
  181.3 3.7 %copy-start.7 = (f32[1,1024]{1,0:T(1,128)S(1)}, f32[1,1024]{1,0:T(1,128)}, u32[]{:S(2)}) copy-start(f32[1,1024]{1,0:T(1,128)} %param.15) | copy-start | bytes 12292
  224.2 10.1 %copy-start.5 = (bf16[1,192,1024]{2,1,0:T(8,128)(2,1)S(1)}, bf16[1,192,1024]{2,1,0:T(8,128)(2,1)}, u32[]{:S(2)}) copy-start(bf16[1,192,1024]{2,1,0:T(8,128)(2,1)} %reduce-scatter.2.cloned.1.call-done) | copy-start | bytes 1179652
  224.2 10.1 %collective-permute-start.3 = (bf16[2,3,32,1024]{3,2,1,0:T(8,128)(2,1)}, bf16[2,3,32,1024]{3,2,1,0:T(8,128)(2,1)S(1)}, u32[]{:S(2)}, u32[]{:S(2)}) collective-permute-start(bf16[2,3,32,1024]{3,2,1,0:T(8,128)(2,1)} %bitcast.127), channel_id=1, source_target_pairs={{0,128},{1,129},{2,130},{3,131},{4,132},{5,133},{6,134},{7,135},{8... | collective-permute-start | bytes 1179656 | tf_op jit(solution)/shard_map/ppermute | solution.py:148
  234.4 5.6 %collective-permute-start.4 = (bf16[2,3,32,1024]{3,2,0,1:T(8,128)(2,1)S(1)}, bf16[2,3,32,1024]{3,2,0,1:T(8,128)(2,1)S(1)}, u32[]{:S(2)}, u32[]{:S(2)}) collective-permute-start(bf16[2,3,32,1024]{3,2,0,1:T(8,128)(2,1)S(1)} %select_bitcast_fusion.2), channel_id=1, source_target_pairs={{0,8},{8,0},{1,9},{9,1},{2,10},{10,2},{3,11},{11,3},{4,12},{12,4},... | collective-permute-start | bytes 1179656 | tf_op jit(solution)/shard_map/ppermute | solution.py:152
Sparse Core Ops, SparseCore 0:
  65.8 103.9 all-gather.2
  181.4 42.7 reduce-scatter.1

commit v2 on v1

--- a/solution.py
+++ b/solution.py
@@ -38,32 +38,42 @@
     )(layer_map, received)
 
 
-def project_kernel(place, slot_layer, features, w0, w1, w2, w3, out, weight, product):
-    blocks, layers, halves, tokens, lanes = features.shape
-    piece = w0.shape[1]
+def project_kernel(
+    place, block_row, slot_layer, f0, f1, f2a, f2b, f3, g0, g1, g2a, g2b, g3,
+    w_own, w_sib, w_far_a, w_far_b, w_fs_a, w_fs_b, out, weight, product,
+):
+    layers, halves, tokens, lanes = f0.shape
+    piece = w_own.shape[1]
     depth = halves * lanes
-    for part, block in enumerate((w0, w1, w2, w3)):
-        for t in range(blocks):
-            row = pl.multiple_of(t * depth + place[part] * piece, piece)
-            weight[pl.ds(row, piece), :] = block[t]
-    group = 8
-    rows = group * tokens
-
-    def step(index, carry):
-        first = index * group
-        left = jnp.concatenate(
-            [
-                features[t, pl.ds(first, group), h].reshape(rows, lanes)
-                for t in range(blocks)
-                for h in range(halves)
-            ],
-            axis=1,
-        )
-        value = jnp.dot(left, weight[...], preferred_element_type=jnp.float32)
-        product[pl.ds(first, group)] = value.astype(product.dtype).reshape(group, tokens, value.shape[1])
-        return carry
-
-    lax.fori_loop(0, layers // group, step, 0)
+    blocks = block_row.shape[0]
+    far = w_far_a.shape[0]
+    for t in range(blocks):
+        first, second = (w_far_a, w_fs_a) if t < far else (w_far_b, w_fs_b)
+        for part, block in enumerate((w_own[t], w_sib[t], first[t % far], second[t % far])):
+            row = pl.multiple_of(block_row[t] * depth + place[part] * piece, piece)
+            weight[pl.ds(row, piece), :] = block
+    rows = 256
+    group = rows // tokens
+    half = layers // 2
+    for side in range(2):
+        f2, g2 = ((f2a, g2a), (f2b, g2b))[side]
+
+        def step(index, carry):
+            near = pl.ds(side * half + index * group, group)
+            far_off = pl.ds(index * group, group)
+            left = jnp.concatenate(
+                [
+                    ref[far_off if place_of % 4 == 2 else near, h].reshape(rows, lanes)
+                    for place_of, ref in enumerate((f0, f1, f2, f3, g0, g1, g2, g3))
+                    for h in range(halves)
+                ],
+                axis=1,
+            )
+            value = jnp.dot(left, weight[...], preferred_element_type=jnp.float32)
+            product[near] = value.astype(product.dtype).reshape(group, tokens, value.shape[1])
+            return carry
+
+        lax.fori_loop(0, half // group, step, 0)
 
     def place_slot(slot, carry):
         out[slot] = product[slot_layer[slot]]
@@ -72,17 +82,17 @@
     lax.fori_loop(0, out.shape[0], place_slot, 0)
 
 
-def project(place, slot_layer, features, weights):
-    blocks, layers, halves, tokens, lanes = features.shape
+def project(place, block_row, slot_layer, features, weights):
+    layers, halves, tokens, lanes = features[0].shape
     columns = weights[0].shape[2]
     slots = slot_layer.shape[0]
-    depth = blocks * halves * lanes
+    depth = block_row.shape[0] * halves * lanes
     vmem = pl.BlockSpec(memory_space=pltpu.VMEM)
     smem = pl.BlockSpec(memory_space=pltpu.SMEM)
     return pl.pallas_call(
         project_kernel,
         out_shape=jax.ShapeDtypeStruct((slots, tokens, columns), jnp.bfloat16),
-        in_specs=[smem, smem] + [vmem] * 5,
+        in_specs=[smem] * 3 + [vmem] * (len(features) + len(weights)),
         out_specs=vmem,
         scratch_shapes=[
             pltpu.VMEM((depth, columns), jnp.bfloat16),
@@ -93,7 +103,24 @@
             flops=2 * layers * tokens * depth * columns, bytes_accessed=11 * MIB, transcendentals=0
         ),
         name="project",
-    )(place, slot_layer, features, *weights)
+    )(place, block_row, slot_layer, *features, *weights)
+
+
+def gather_tensor(own):
+    up = [(i, (i + 1) % X) for i in range(X)]
+    down = [(i, (i - 1) % X) for i in range(X)]
+    swap = [(0, 1), (1, 0)]
+    half = own.shape[0] // 2
+    f3 = lax.ppermute(own, "x", up)
+    f1 = lax.ppermute(own, "x", down)
+    g0 = lax.ppermute(own, "yl", swap)
+    f2a = lax.ppermute(f3[:half], "x", up)
+    f2b = lax.ppermute(f1[half:], "x", down)
+    g3 = lax.ppermute(g0, "x", up)
+    g1 = lax.ppermute(g0, "x", down)
+    g2a = lax.ppermute(f2a, "yl", swap)
+    g2b = lax.ppermute(f2b, "yl", swap)
+    return (own, f1, f2a, f2b, f3, g0, g1, g2a, g2b, g3)
 
 
 def body(
@@ -109,38 +136,50 @@
     layer_counts,
 ):
     yh, z, c = lax.axis_index("yh"), lax.axis_index("z"), lax.axis_index("c")
+    x, yl = lax.axis_index("x"), lax.axis_index("yl")
     slab_count, tokens, slab_width = teacher_slabs.shape
     layers = layer_map.shape[0]
     columns = proj_weight.shape[2]
     full_width = columns * X * YL
     slot_count = child_hidden.shape[0]
     quarter = tokens // QUARTERS
-    segments = YH * Z * C
-    middle = segments // 2
 
     swap = [(0, 1), (1, 0)]
-    w_own = proj_weight
-    w_sib = lax.ppermute(w_own, "c", swap)
-    w_far = lax.ppermute(w_own, "yh", swap)
-    w_far_sib = lax.ppermute(w_far, "c", swap)
+    ring = YH * YL
+    up = [(i, (i + 1) % ring) for i in range(ring)]
+    down = [(i, (i - 1) % ring) for i in range(ring)]
+    side = ("yh", "yl")
+    half_blocks = proj_weight.shape[0] // 2
+    w_far_a = lax.ppermute(lax.ppermute(proj_weight[:half_blocks], side, up), side, up)
+    w_far_b = lax.ppermute(lax.ppermute(proj_weight[half_blocks:], side, down), side, down)
+    w_sib = lax.ppermute(proj_weight, "c", swap)
+    w_fs_a = lax.ppermute(w_far_a, "c", swap)
+    w_fs_b = lax.ppermute(w_far_b, "c", swap)
+    weights = (proj_weight, w_sib, w_far_a, w_far_b, w_fs_a, w_fs_b)
     place = jnp.stack([2 * yh + c, 2 * yh + 1 - c, 2 * (1 - yh) + c, 2 * (1 - yh) + 1 - c]).astype(jnp.int32)
 
-    arranged = (
-        teacher_slabs.reshape(slab_count, YH, C, quarter, YH, Z, LANES)
-        .transpose(1, 5, 2, 0, 4, 3, 6)
-        .reshape(segments, slab_count * YH * quarter, LANES)
-    )
-    received = lax.all_to_all(arranged, SEGMENT, split_axis=0, concat_axis=0, tiled=True)
-    received = received[:middle].reshape(middle * slab_count, YH * quarter, LANES)
-    picked = pick(layer_map, received)
-    gathered = lax.all_gather(picked, TENSOR, axis=0, tiled=False)
-    features = gathered.reshape(X * YL, layers, YH, quarter, LANES)
+    def arrange(section):
+        width = tokens // YH
+        return (
+            teacher_slabs[:, section * width : (section + 1) * width]
+            .reshape(slab_count, C, quarter, YH, Z, LANES)
+            .transpose(4, 1, 0, 3, 2, 5)
+            .reshape(Z * C, slab_count * YH * quarter, LANES)
+        )
+
+    sent = lax.ppermute(arrange(1), side, [(0, 3), (1, 2)])
+    arranged = jnp.where(yh == 0, arrange(0), sent)
+    received = lax.all_to_all(arranged, ("z", "c"), split_axis=0, concat_axis=0, tiled=True)
+    received = received.reshape(Z * C * slab_count, YH, quarter, LANES)
+    features = gather_tensor(pick(layer_map, received))
+    block = jnp.arange(X * YL)
+    block_row = ((block // YL - x) % X + X * (block % YL != (yl + yh) % 2)).astype(jnp.int32)
 
     prefix_end = jnp.cumsum(layer_counts)
     prefix_start = prefix_end - layer_counts
     slot_ids = jnp.arange(slot_count)
     slot_layer = jnp.clip(prefix_start[:, None] + slot_ids[None, :], 0, layers - 1).reshape(-1).astype(jnp.int32)
-    partial = project(place, slot_layer, features, (w_own, w_sib, w_far, w_far_sib))
+    partial = project(place, block_row, slot_layer, features, weights)
     per_z = C * slot_count
     mine = lax.psum_scatter(
         partial.reshape(Z, per_z * quarter, columns), "z", scatter_dimension=0, tiled=False

time: 249 us -> 193 us (0.78)
  blocking collectives: 68.5 us -> 13.9 us
  waiting for transfers between devices: 108 us -> 83 us
  starting transfers between devices: 26.5 us -> 41 us
  local copies, waits for them, and re-layouts: 7.93 us -> 13.9 us
    all_to_all x1 -> x0, blocking collectives: 53 us -> none  [body(): lax.all_to_all(arranged, SEGMENT, split_axis=0, concat_axis=0, tiled=True)]
    all_gather x1 -> x0, waiting for transfers between devices: 34.5 us -> none  [body(): gathered = lax.all_gather(picked, TENSOR, axis=0, tiled=False)]
    all_to_all x0 -> x1, starting transfers between devices: none -> 10 us  [body(): lax.all_to_all(arranged, ('z', 'c'), split_axis=0, concat_axis=0, tiled=T...]
    all_to_all x0 -> x1, waiting for transfers between devices: none -> 6.14 us  [body(): lax.all_to_all(arranged, ('z', 'c'), split_axis=0, concat_axis=0, tiled=T...]
    ppermute x3 -> x17, starting transfers between devices: 17.4 us -> 22 us  [the longest x1 6.35 us: body(): sent = lax.ppermute(arrange(1), side, [(0, 3), (1, 2)])]
    ppermute x3 -> x17, waiting for transfers between devices: 51.6 us -> 55.9 us  [the longest x1 14.4 us: body(): sent = lax.ppermute(arrange(1), side, [(0, 3), (1, 2)])]
    slice x1 -> x4, local copies, waits for them, and re-layouts: 0.93 us -> 4.04 us  [the longest x1 1.66 us: arrange(): teacher_slabs[:, section * width:(section + 1) * width]]
    unnamed x19 -> x32, local copies, waits for them, and re-layouts: 5.82 us -> 6.95 us
  transfers between devices with their start and end apart: 7 -> 21, of which waited for: 6 -> 12; matrix products, arithmetic and copies ran while one was open for 5% -> 8% of each run, Pallas kernels for 0% -> 1%
where the time goes in v2:
time: 193 us
  waiting for transfers between devices  83 us (43%)
  starting transfers between devices  41 us (21%)
  between operations  14.9 us (8%)
  local copies, waits for them, and re-layouts  13.9 us (7%)
  blocking collectives  13.9 us (7%)
  matrix products  10.5 us (5%)
  Pallas kernels  10.3 us (5%)
  other arithmetic  5.15 us (3%)
    reduce_scatter x1, waiting for transfers between devices, body(): lax.psum_scatter(partial.reshape(Z, per_z * quarter, columns), 'z', scatt...  18 us
    ppermute x1, waiting for transfers between devices, body(): sent = lax.ppermute(arrange(1), side, [(0, 3), (1, 2)])  14.4 us
    psum x1, blocking collectives, body(): lax.psum(jnp.stack([jnp.sum(first_hidden * first_hidden, axis=1), jnp.sum...  13.9 us
    ppermute x1, waiting for transfers between devices, body(): lax.ppermute(proj_weight[:half_blocks], side, up)  11.8 us
    all_to_all x1, starting transfers between devices, body(): lax.all_to_all(arranged, ('z', 'c'), split_axis=0, concat_axis=0, tiled=T...  10 us
    ppermute x1, waiting for transfers between devices, gather_tensor(): g0 = lax.ppermute(own, 'yl', swap)  8.16 us
    pallas_call x1, Pallas kernels, project(): pl.pallas_call(project_kernel, out_shape=jax.ShapeDtypeStruct((slots, tok...  8.15 us
    ppermute x1, waiting for transfers between devices, gather_tensor(): f3 = lax.ppermute(own, 'x', up)  7.56 us
  transfers between devices with their start and end apart: 21, of which 12 were waited for; matrix products, arithmetic and copies ran while one was open for 8% of the time, Pallas kernels for 1%

profile of v2, /device:TPU:1, one launch (start us, length us, event | category | flops | bytes accessed | tf_op | source)
XLA Modules:
  0.0 192.7 jit_solution(7465181523161567249)
XLA Ops:
  7.2 1.7 fusion.39
  10.1 6.4 %collective-permute-start = (bf16[16,192,128]{2,1,0:T(8,128)(2,1)}, bf16[16,192,128]{2,1,0:T(8,128)(2,1)}, u32[]{:S(2)}, u32[]{:S(2)}) collective-permute-start(bf16[16,192,128]{2,1,0:T(8,128)(2,1)} %bitcast.9), channel_id=1, source_target_pairs={{0,129},{1,128},{2,131},{3,130},{4,133},{5,132},{6,135},{7,134},{8... | collective-permute-start | bytes 2359304 | tf_op jit(solution)/shard_map/ppermute | solution.py:170
  17.7 14.4 %collective-permute-done = bf16[16,192,128]{2,1,0:T(8,128)(2,1)} collective-permute-done((bf16[16,192,128]{2,1,0:T(8,128)(2,1)}, bf16[16,192,128]{2,1,0:T(8,128)(2,1)}, u32[]{:S(2)}, u32[]{:S(2)}) %collective-permute-start) | collective-permute-done | bytes 786464 | tf_op jit(solution)/shard_map/ppermute | solution.py:170
  32.1 2.1 %broadcast_select_fusion = bf16[16,192,128]{2,1,0:T(8,128)(2,1)} fusion(bf16[16,192,128]{2,1,0:T(8,128)(2,1)} %bitcast.128, bf16[16,192,128]{2,1,0:T(8,128)(2,1)} %collective-permute-done, pred[]{:T(512)S(6)} %eq.19), kind=kLoop, calls=%fused_computation.12 | loop fusion | flops 393216 | bytes 2359297 | tf_op jit(solution)/shard_map/jit(_where)/select_n | solution.py:171
  34.2 10.0 %all-to-all-start = ((bf16[16,192,128]{2,1,0:T(8,128)(2,1)}), bf16[16,192,128]{2,1,0:T(8,128)(2,1)}, u32[]{:S(2)}, u32[]{:S(2)}) async-start(bf16[16,192,128]{2,1,0:T(8,128)(2,1)} %broadcast_select_fusion), calls=%async_computation | async-start | bytes 1572864 | tf_op jit(solution)/shard_map/all_to_all | solution.py:172
  45.2 3.4 %collective-permute-start.13 = (bf16[4,64,1024]{2,1,0:T(8,128)(2,1)}, bf16[4,64,1024]{2,1,0:T(8,128)(2,1)}, u32[]{:S(2)}, u32[]{:S(2)}) collective-permute-start(bf16[4,64,1024]{2,1,0:T(8,128)(2,1)} %get-tuple-element.24), channel_id=1, source_target_pairs={{0,129},{1,0},{128,1},{129,128},{2,131},{3,2},{130,3},{131,130},{4... | collective-permute-start | bytes 1572872 | tf_op jit(solution)/shard_map/ppermute | solution.py:154
  49.0 11.8 %collective-permute-done.11 = bf16[4,64,1024]{2,1,0:T(8,128)(2,1)} collective-permute-done((bf16[4,64,1024]{2,1,0:T(8,128)(2,1)S(1)}, bf16[4,64,1024]{2,1,0:T(8,128)(2,1)}, u32[]{:S(2)}, u32[]{:S(2)}) %collective-permute-start.11) | collective-permute-done | bytes 524320 | tf_op jit(solution)/shard_map/ppermute | solution.py:153
  60.8 6.1 %all-to-all-done = bf16[16,192,128]{2,1,0:T(8,128)(2,1)} async-done(((bf16[16,192,128]{2,1,0:T(8,128)(2,1)}), bf16[16,192,128]{2,1,0:T(8,128)(2,1)}, u32[]{:S(2)}, u32[]{:S(2)}) %all-to-all-start) | async-done | bytes 786464 | tf_op jit(solution)/shard_map/all_to_all | solution.py:172
  67.0 2.1 %pick_layers.1.f0 = bf16[32,2,32,128]{3,2,1,0:T(8,128)(2,1)} custom-call(s32[32]{0:T(128)} %layer_map.1, bf16[48,2,32,128]{3,2,1,0:T(8,128)(2,1)} %bitcast.10.received), custom_call_target="tpu_custom_call" | custom-call | bytes 1300000 | tf_op jit(solution)/shard_map/pick_layers/pallas_call | solution.py:28
  69.1 1.2 collective-permute-start.2
  70.3 1.5 collective-permute-start.1
  71.8 3.4 %collective-permute-start.14 = (bf16[4,64,1024]{2,1,0:T(8,128)(2,1)}, bf16[4,64,1024]{2,1,0:T(8,128)(2,1)}, u32[]{:S(2)}, u32[]{:S(2)}) collective-permute-start(bf16[4,64,1024]{2,1,0:T(8,128)(2,1)} %collective-permute-done.13), channel_id=1, source_target_pairs={{0,129},{1,0},{128,1},{129,128},{2,131},{3,2},{130,3},{131,130},{4... | collective-permute-start | bytes 1572872 | tf_op jit(solution)/shard_map/ppermute | solution.py:154
  75.2 7.6 %collective-permute-done.2.f3 = bf16[32,2,32,128]{3,2,1,0:T(8,128)(2,1)S(1)} collective-permute-done((bf16[32,2,32,128]{3,2,1,0:T(8,128)(2,1)}, bf16[32,2,32,128]{3,2,1,0:T(8,128)(2,1)S(1)}, u32[]{:S(2)}, u32[]{:S(2)}) %collective-permute-start.2) | collective-permute-done | bytes 524320 | tf_op jit(solution)/shard_map/ppermute | solution.py:114
  83.5 1.1 collective-permute-start.3
  86.4 1.3 collective-permute-start.4
  88.0 8.2 %collective-permute-done.5.g0 = bf16[32,2,32,128]{3,2,1,0:T(8,128)(2,1)} collective-permute-done((bf16[32,2,32,128]{3,2,1,0:T(8,128)(2,1)}, bf16[32,2,32,128]{3,2,1,0:T(8,128)(2,1)}, u32[]{:S(2)}, u32[]{:S(2)}) %collective-permute-start.5) | collective-permute-done | bytes 524320 | tf_op jit(solution)/shard_map/ppermute | solution.py:116
  96.1 1.4 collective-permute-start.6
  98.8 1.4 collective-permute-start.8
  100.5 5.8 %collective-permute-done.7.g2a = bf16[16,2,32,128]{3,2,1,0:T(8,128)(2,1)} collective-permute-done((bf16[16,2,32,128]{3,2,1,0:T(8,128)(2,1)S(1)}, bf16[16,2,32,128]{3,2,1,0:T(8,128)(2,1)}, u32[]{:S(2)}, u32[]{:S(2)}) %collective-permute-start.7) | collective-permute-done | bytes 262176 | tf_op jit(solution)/shard_map/ppermute | solution.py:121
  106.3 5.6 %collective-permute-done.8.g2b = bf16[16,2,32,128]{3,2,1,0:T(8,128)(2,1)} collective-permute-done((bf16[16,2,32,128]{3,2,1,0:T(8,128)(2,1)}, bf16[16,2,32,128]{3,2,1,0:T(8,128)(2,1)}, u32[]{:S(2)}, u32[]{:S(2)}) %collective-permute-start.8) | collective-permute-done | bytes 262176 | tf_op jit(solution)/shard_map/ppermute | solution.py:122
  111.9 1.5 collective-permute-done.9.g3
  117.6 8.1 %project.1 = bf16[48,32,1024]{2,1,0:T(8,128)(2,1)S(1)} custom-call(s32[4]{0:T(128)S(1)} %pad_add_fusion.place, s32[8]{0:T(128)S(1)} %fusion.36.block_row, s32[48]{0:T(128)S(1)} %min.12.slot_layer, bf16[32,2,32,128]{3,2,1,0:T(8,128)(2,1)S(1)} %copy-done.3, bf16[32,2,32,128]{3,2,1,0:T(8,128)(2,1)S(1)} %copy-done.7, ...), custom_call_target="tpu_custom_call" | custom-call | flops 4294967296 | bytes 11534336 | tf_op jit(solution)/shard_map/project/pallas_call | solution.py:92
  125.7 1.6 copy-done.1
  128.7 2.4 %fusion = f32[128,1024]{1,0:T(8,128)S(1)} fusion(bf16[1,1024,1024]{2,1,0:T(8,128)(2,1)} %param.17, bf16[1,128,1024]{2,1,0:T(8,128)(2,1)S(1)} %copy-done.12), kind=kOutput, calls=%fused_computation | convolution fusion | flops 268435456 | bytes 2883584 | tf_op jit(solution)/shard_map/dot_general | solution.py:210
  131.1 1.9 fusion.12
  133.0 13.9 %psum.7 = f32[2,128]{1,0:T(2,128)S(1)} all-reduce(f32[2,128]{1,0:T(2,128)S(1)} %pad_maximum_fusion.1), channel_id=1, replica_groups=mesh['yh'=2,'z'=8,'c'=2,'x'=4,'yl'=2] {'x','yl'}, use_global_device_ids=true, to_apply=%region_4.5 | all-reduce | flops 256 | bytes 2048 | tf_op jit(solution)/shard_map/psum | solution.py:213
  146.9 3.1 %select_bitcast_fusion = bf16[1,1024,1024]{2,1,0:T(8,128)(2,1)} fusion(pred[]{:T(512)S(6)} %eq.17, bf16[1,128,1024]{2,1,0:T(8,128)(2,1)} %param.19, f32[1024]{0:T(1024)S(1)} %bitcast.139, f32[128]{0:T(128)S(1)} %get-tuple-element.19, bf16[3,128,1024]{2,1,0:T(8,128)(2,1)S(1)} %copy-done.10), kind=kOutput, calls=%fused_computation.4 | convolution fusion | flops 271056896 | bytes 2626049 | tf_op jit(solution)/shard_map/dot_general | solution.py:229
  150.0 18.0 %reduce-scatter.2.cloned.1.call-done = bf16[1,192,1024]{2,1,0:T(8,128)(2,1)} async-done(((bf16[8,192,1024]{2,1,0:T(8,128)(2,1)}), bf16[1,192,1024]{2,1,0:T(8,128)(2,1)}) %reduce-scatter.2.cloned.1.call-update) | async-done | bytes 393232 | tf_op jit(solution)/shard_map/reduce_scatter | solution.py:184
  168.0 4.7 %collective-permute-start.17 = (bf16[2,3,32,1024]{3,2,1,0:T(8,128)(2,1)}, bf16[2,3,32,1024]{3,2,1,0:T(8,128)(2,1)S(1)}, u32[]{:S(2)}, u32[]{:S(2)}) collective-permute-start(bf16[2,3,32,1024]{3,2,1,0:T(8,128)(2,1)} %bitcast.133), channel_id=1, source_target_pairs={{0,128},{1,129},{2,130},{3,131},{4,132},{5,133},{6,134},{7,135},{8... | collective-permute-start | bytes 1179656 | tf_op jit(solution)/shard_map/ppermute | solution.py:187
  172.8 3.1 %select_bitcast_fusion.1 = bf16[1,1024,1024]{2,1,0:T(8,128)(2,1)} fusion(pred[]{:T(512)S(6)} %eq.17, bf16[1,128,1024]{2,1,0:T(8,128)(2,1)} %param.18, f32[1024]{0:T(1024)S(1)} %bitcast.140, f32[128]{0:T(128)S(1)} %get-tuple-element.19, bf16[3,128,1024]{2,1,0:T(8,128)(2,1)S(1)} %copy-done.10), kind=kOutput, calls=%fused_computation.5 | convolution fusion | flops 271056896 | bytes 2626049 | tf_op jit(solution)/shard_map/dot_general | solution.py:226
  175.9 2.4 %collective-permute-done.17 = bf16[2,3,32,1024]{3,2,1,0:T(8,128)(2,1)S(1)} collective-permute-done((bf16[2,3,32,1024]{3,2,1,0:T(8,128)(2,1)}, bf16[2,3,32,1024]{3,2,1,0:T(8,128)(2,1)S(1)}, u32[]{:S(2)}, u32[]{:S(2)}) %collective-permute-start.17) | collective-permute-done | bytes 393248 | tf_op jit(solution)/shard_map/ppermute | solution.py:187
  178.3 4.3 %collective-permute-start.18 = (bf16[2,3,32,1024]{3,2,0,1:T(8,128)(2,1)S(1)}, bf16[2,3,32,1024]{3,2,0,1:T(8,128)(2,1)S(1)}, u32[]{:S(2)}, u32[]{:S(2)}) collective-permute-start(bf16[2,3,32,1024]{3,2,0,1:T(8,128)(2,1)S(1)} %select_bitcast_fusion.2), channel_id=1, source_target_pairs={{0,8},{8,0},{1,9},{9,1},{2,10},{10,2},{3,11},{11,3},{4,12},{12,4},... | collective-permute-start | bytes 1179656 | tf_op jit(solution)/shard_map/ppermute | solution.py:191
  (78 shorter events, 16.3 us)
Async XLA Ops:
  7.2 123.9 %copy-start = (bf16[1,1024,1024]{2,1,0:T(8,128)(2,1)S(1)}, bf16[1,1024,1024]{2,1,0:T(8,128)(2,1)}, u32[]{:S(2)}) copy-start(bf16[1,1024,1024]{2,1,0:T(8,128)(2,1)} %param.16) | copy-start | bytes 6291460
  10.1 22.0 %collective-permute-start = (bf16[16,192,128]{2,1,0:T(8,128)(2,1)}, bf16[16,192,128]{2,1,0:T(8,128)(2,1)}, u32[]{:S(2)}, u32[]{:S(2)}) collective-permute-start(bf16[16,192,128]{2,1,0:T(8,128)(2,1)} %bitcast.9), channel_id=1, source_target_pairs={{0,129},{1,128},{2,131},{3,130},{4,133},{5,132},{6,135},{7,134},{8... | collective-permute-start | bytes 2359304 | tf_op jit(solution)/shard_map/ppermute | solution.py:170
  17.7 26.6 %copy-start.2 = (bf16[8,64,1024]{2,1,0:T(8,128)(2,1)S(1)}, bf16[8,64,1024]{2,1,0:T(8,128)(2,1)}, u32[]{:S(2)}) copy-start(bf16[8,64,1024]{2,1,0:T(8,128)(2,1)} %w_own.1) | copy-start | bytes 3145732
  34.2 32.8 %all-to-all-start = ((bf16[16,192,128]{2,1,0:T(8,128)(2,1)}), bf16[16,192,128]{2,1,0:T(8,128)(2,1)}, u32[]{:S(2)}, u32[]{:S(2)}) async-start(bf16[16,192,128]{2,1,0:T(8,128)(2,1)} %broadcast_select_fusion), calls=%async_computation | async-start | bytes 1572864 | tf_op jit(solution)/shard_map/all_to_all | solution.py:172
  44.2 54.2 %copy-start.14 = (s32[16]{0:T(128)S(1)}, s32[16]{0:T(128)}, u32[]{:S(2)}) copy-start(s32[16]{0:T(128)} %param.21) | copy-start | bytes 196
  44.2 123.8 %reduce-scatter.2.cloned.1.call-start = ((), (), s32[]{:S(2)}) async-start(), calls=%async_computation.2 | async-start | bytes 3538944 | tf_op jit(solution)/shard_map/reduce_scatter | solution.py:184
  45.1 15.7 %collective-permute-start.11 = (bf16[4,64,1024]{2,1,0:T(8,128)(2,1)S(1)}, bf16[4,64,1024]{2,1,0:T(8,128)(2,1)}, u32[]{:S(2)}, u32[]{:S(2)}) collective-permute-start(bf16[4,64,1024]{2,1,0:T(8,128)(2,1)S(1)} %get-tuple-element.25), channel_id=1, source_target_pairs={{0,1},{1,128},{128,129},{129,0},{2,3},{3,130},{130,131},{131,2},{4... | collective-permute-start | bytes 1572872 | tf_op jit(solution)/shard_map/ppermute | solution.py:153
  45.2 26.6 %collective-permute-start.13 = (bf16[4,64,1024]{2,1,0:T(8,128)(2,1)}, bf16[4,64,1024]{2,1,0:T(8,128)(2,1)}, u32[]{:S(2)}, u32[]{:S(2)}) collective-permute-start(bf16[4,64,1024]{2,1,0:T(8,128)(2,1)} %get-tuple-element.24), channel_id=1, source_target_pairs={{0,129},{1,0},{128,1},{129,128},{2,131},{3,2},{130,3},{131,130},{4... | collective-permute-start | bytes 1572872 | tf_op jit(solution)/shard_map/ppermute | solution.py:154
  48.6 39.1 %collective-permute-start.10 = (bf16[8,64,1024]{2,1,0:T(8,128)(2,1)S(1)}, bf16[8,64,1024]{2,1,0:T(8,128)(2,1)}, u32[]{:S(2)}, u32[]{:S(2)}) collective-permute-start(bf16[8,64,1024]{2,1,0:T(8,128)(2,1)S(1)} %copy-done.2), channel_id=1, source_target_pairs={{0,8},{8,0},{1,9},{9,1},{2,10},{10,2},{3,11},{11,3},{4,12},{12,4},... | collective-permute-start | bytes 3145736 | tf_op jit(solution)/shard_map/ppermute | solution.py:155
  60.8 14.4 %collective-permute-start.12 = (bf16[4,64,1024]{2,1,0:T(8,128)(2,1)}, bf16[4,64,1024]{2,1,0:T(8,128)(2,1)}, u32[]{:S(2)}, u32[]{:S(2)}) collective-permute-start(bf16[4,64,1024]{2,1,0:T(8,128)(2,1)} %collective-permute-done.11), channel_id=1, source_target_pairs={{0,1},{1,128},{128,129},{129,0},{2,3},{3,130},{130,131},{131,2},{4... | collective-permute-start | bytes 1572872 | tf_op jit(solution)/shard_map/ppermute | solution.py:153
  69.1 13.7 %collective-permute-start.2 = (bf16[32,2,32,128]{3,2,1,0:T(8,128)(2,1)}, bf16[32,2,32,128]{3,2,1,0:T(8,128)(2,1)S(1)}, u32[]{:S(2)}, u32[]{:S(2)}) collective-permute-start(bf16[32,2,32,128]{3,2,1,0:T(8,128)(2,1)} %pick_layers.1.f0), channel_id=1, source_target_pairs={{0,2},{2,4},{4,6},{6,0},{1,3},{3,5},{5,7},{7,1},{8,10},{10,12},{12... | collective-permute-start | bytes 1572872 | tf_op jit(solution)/shard_map/ppermute | solution.py:114
  70.3 13.2 %collective-permute-start.1 = (bf16[32,2,32,128]{3,2,1,0:T(8,128)(2,1)}, bf16[32,2,32,128]{3,2,1,0:T(8,128)(2,1)S(1)}, u32[]{:S(2)}, u32[]{:S(2)}) collective-permute-start(bf16[32,2,32,128]{3,2,1,0:T(8,128)(2,1)} %pick_layers.1.f0), channel_id=1, source_target_pairs={{0,6},{2,0},{4,2},{6,4},{1,7},{3,1},{5,3},{7,5},{8,14},{10,8},{12,... | collective-permute-start | bytes 1572872 | tf_op jit(solution)/shard_map/ppermute | solution.py:115
  71.8 14.6 %collective-permute-start.14 = (bf16[4,64,1024]{2,1,0:T(8,128)(2,1)}, bf16[4,64,1024]{2,1,0:T(8,128)(2,1)}, u32[]{:S(2)}, u32[]{:S(2)}) collective-permute-start(bf16[4,64,1024]{2,1,0:T(8,128)(2,1)} %collective-permute-done.13), channel_id=1, source_target_pairs={{0,129},{1,0},{128,1},{129,128},{2,131},{3,2},{130,3},{131,130},{4... | collective-permute-start | bytes 1572872 | tf_op jit(solution)/shard_map/ppermute | solution.py:154
  75.2 20.9 %collective-permute-start.5 = (bf16[32,2,32,128]{3,2,1,0:T(8,128)(2,1)}, bf16[32,2,32,128]{3,2,1,0:T(8,128)(2,1)}, u32[]{:S(2)}, u32[]{:S(2)}) collective-permute-start(bf16[32,2,32,128]{3,2,1,0:T(8,128)(2,1)} %pick_layers.1.f0), channel_id=1, source_target_pairs={{0,1},{1,0},{2,3},{3,2},{4,5},{5,4},{6,7},{7,6},{8,9},{9,8},{10,11... | collective-permute-start | bytes 1572872 | tf_op jit(solution)/shard_map/ppermute | solution.py:116
  82.8 4.9 %copy-start.4 = (bf16[32,2,32,128]{3,2,1,0:T(8,128)(2,1)}, bf16[32,2,32,128]{3,2,1,0:T(8,128)(2,1)S(1)}, u32[]{:S(2)}) copy-start(bf16[32,2,32,128]{3,2,1,0:T(8,128)(2,1)S(1)} %collective-permute-done.2.f3) | copy-start | bytes 1572868
  82.8 14.8 %collective-permute-start.15 = (bf16[4,64,1024]{2,1,0:T(8,128)(2,1)}, bf16[4,64,1024]{2,1,0:T(8,128)(2,1)S(1)}, u32[]{:S(2)}, u32[]{:S(2)}) collective-permute-start(bf16[4,64,1024]{2,1,0:T(8,128)(2,1)} %collective-permute-done.12.w_far_a), channel_id=1, source_target_pairs={{0,8},{8,0},{1,9},{9,1},{2,10},{10,2},{3,11},{11,3},{4,12},{12,4},... | collective-permute-start | bytes 1572872 | tf_op jit(solution)/shard_map/ppermute | solution.py:156
  83.5 4.4 %copy-start.6 = (bf16[32,2,32,128]{3,2,1,0:T(8,128)(2,1)}, bf16[32,2,32,128]{3,2,1,0:T(8,128)(2,1)S(1)}, u32[]{:S(2)}) copy-start(bf16[32,2,32,128]{3,2,1,0:T(8,128)(2,1)S(1)} %collective-permute-done.1.f1) | copy-start | bytes 1572868
  83.5 15.1 %collective-permute-start.3 = (bf16[16,2,32,128]{3,2,1,0:T(8,128)(2,1)}, bf16[16,2,32,128]{3,2,1,0:T(8,128)(2,1)S(1)}, u32[]{:S(2)}, u32[]{:S(2)}) collective-permute-start(bf16[16,2,32,128]{3,2,1,0:T(8,128)(2,1)} %slice.69), channel_id=1, source_target_pairs={{0,2},{2,4},{4,6},{6,0},{1,3},{3,5},{5,7},{7,1},{8,10},{10,12},{12... | collective-permute-start | bytes 786440 | tf_op jit(solution)/shard_map/ppermute | solution.py:117
  86.4 12.4 %collective-permute-start.4 = (bf16[16,2,32,128]{3,2,1,0:T(8,128)(2,1)}, bf16[16,2,32,128]{3,2,1,0:T(8,128)(2,1)}, u32[]{:S(2)}, u32[]{:S(2)}) collective-permute-start(bf16[16,2,32,128]{3,2,1,0:T(8,128)(2,1)} %slice.70), channel_id=1, source_target_pairs={{0,6},{2,0},{4,2},{6,4},{1,7},{3,1},{5,3},{7,5},{8,14},{10,8},{12,... | collective-permute-start | bytes 786440 | tf_op jit(solution)/shard_map/ppermute | solution.py:118
  87.7 12.8 %collective-permute-start.16 = (bf16[4,64,1024]{2,1,0:T(8,128)(2,1)}, bf16[4,64,1024]{2,1,0:T(8,128)(2,1)}, u32[]{:S(2)}, u32[]{:S(2)}) collective-permute-start(bf16[4,64,1024]{2,1,0:T(8,128)(2,1)} %collective-permute-done.14.w_far_b), channel_id=1, source_target_pairs={{0,8},{8,0},{1,9},{9,1},{2,10},{10,2},{3,11},{11,3},{4,12},{12,4},... | collective-permute-start | bytes 1572872 | tf_op jit(solution)/shard_map/ppermute | solution.py:157
  96.1 15.8 %collective-permute-start.6 = (bf16[32,2,32,128]{3,2,1,0:T(8,128)(2,1)}, bf16[32,2,32,128]{3,2,1,0:T(8,128)(2,1)}, u32[]{:S(2)}, u32[]{:S(2)}) collective-permute-start(bf16[32,2,32,128]{3,2,1,0:T(8,128)(2,1)} %collective-permute-done.5.g0), channel_id=1, source_target_pairs={{0,6},{2,0},{4,2},{6,4},{1,7},{3,1},{5,3},{7,5},{8,14},{10,8},{12,... | collective-permute-start | bytes 1572872 | tf_op jit(solution)/shard_map/ppermute | solution.py:120
  98.3 15.1 %collective-permute-start.9 = (bf16[32,2,32,128]{3,2,1,0:T(8,128)(2,1)}, bf16[32,2,32,128]{3,2,1,0:T(8,128)(2,1)}, u32[]{:S(2)}, u32[]{:S(2)}) collective-permute-start(bf16[32,2,32,128]{3,2,1,0:T(8,128)(2,1)} %collective-permute-done.5.g0), channel_id=1, source_target_pairs={{0,2},{2,4},{4,6},{6,0},{1,3},{3,5},{5,7},{7,1},{8,10},{10,12},{12... | collective-permute-start | bytes 1572872 | tf_op jit(solution)/shard_map/ppermute | solution.py:119
  98.6 7.6 %collective-permute-start.7 = (bf16[16,2,32,128]{3,2,1,0:T(8,128)(2,1)S(1)}, bf16[16,2,32,128]{3,2,1,0:T(8,128)(2,1)}, u32[]{:S(2)}, u32[]{:S(2)}) collective-permute-start(bf16[16,2,32,128]{3,2,1,0:T(8,128)(2,1)S(1)} %collective-permute-done.3.f2a), channel_id=1, source_target_pairs={{0,1},{1,0},{2,3},{3,2},{4,5},{5,4},{6,7},{7,6},{8,9},{9,8},{10,11... | collective-permute-start | bytes 786440 | tf_op jit(solution)/shard_map/ppermute | solution.py:121
  98.8 13.1 %collective-permute-start.8 = (bf16[16,2,32,128]{3,2,1,0:T(8,128)(2,1)}, bf16[16,2,32,128]{3,2,1,0:T(8,128)(2,1)}, u32[]{:S(2)}, u32[]{:S(2)}) collective-permute-start(bf16[16,2,32,128]{3,2,1,0:T(8,128)(2,1)} %collective-permute-done.4.f2b), channel_id=1, source_target_pairs={{0,1},{1,0},{2,3},{3,2},{4,5},{5,4},{6,7},{7,6},{8,9},{9,8},{10,11... | collective-permute-start | bytes 786440 | tf_op jit(solution)/shard_map/ppermute | solution.py:122
  113.4 1.0 copy-start.3
  125.7 1.6 copy-start.1
  127.4 1.3 copy-start.12
  127.4 3.7 %copy-start.10 = (bf16[3,128,1024]{2,1,0:T(8,128)(2,1)S(1)}, bf16[3,128,1024]{2,1,0:T(8,128)(2,1)}, u32[]{:S(2)}) copy-start(bf16[3,128,1024]{2,1,0:T(8,128)(2,1)} %param.14) | copy-start | bytes 2359300
  127.4 3.7 %copy-start.13 = (f32[1,1024]{1,0:T(1,128)S(1)}, f32[1,1024]{1,0:T(1,128)}, u32[]{:S(2)}) copy-start(f32[1,1024]{1,0:T(1,128)} %param.15) | copy-start | bytes 12292
  168.0 10.2 %copy-start.11 = (bf16[1,192,1024]{2,1,0:T(8,128)(2,1)S(1)}, bf16[1,192,1024]{2,1,0:T(8,128)(2,1)}, u32[]{:S(2)}) copy-start(bf16[1,192,1024]{2,1,0:T(8,128)(2,1)} %reduce-scatter.2.cloned.1.call-done) | copy-start | bytes 1179652
  168.0 10.2 %collective-permute-start.17 = (bf16[2,3,32,1024]{3,2,1,0:T(8,128)(2,1)}, bf16[2,3,32,1024]{3,2,1,0:T(8,128)(2,1)S(1)}, u32[]{:S(2)}, u32[]{:S(2)}) collective-permute-start(bf16[2,3,32,1024]{3,2,1,0:T(8,128)(2,1)} %bitcast.133), channel_id=1, source_target_pairs={{0,128},{1,129},{2,130},{3,131},{4,132},{5,133},{6,134},{7,135},{8... | collective-permute-start | bytes 1179656 | tf_op jit(solution)/shard_map/ppermute | solution.py:187
  178.3 5.6 %collective-permute-start.18 = (bf16[2,3,32,1024]{3,2,0,1:T(8,128)(2,1)S(1)}, bf16[2,3,32,1024]{3,2,0,1:T(8,128)(2,1)S(1)}, u32[]{:S(2)}, u32[]{:S(2)}) collective-permute-start(bf16[2,3,32,1024]{3,2,0,1:T(8,128)(2,1)S(1)} %select_bitcast_fusion.2), channel_id=1, source_target_pairs={{0,8},{8,0},{1,9},{9,1},{2,10},{10,2},{3,11},{11,3},{4,12},{12,4},... | collective-permute-start | bytes 1179656 | tf_op jit(solution)/shard_map/ppermute | solution.py:191
  (4 other events, 3.9 us)
Sparse Core Ops, SparseCore 0:
  127.5 40.4 reduce-scatter.1

commit v3 on v2

--- a/solution.py
+++ b/solution.py
@@ -13,6 +13,38 @@
 YH, Z, C, X, YL = 2, 8, 2, 4, 2
 QUARTERS = YH * C
 LANES = 128
+PARTS = 2
+
+
+def arrange_kernel(slabs, *out):
+    slab_count, width, _ = slabs.shape
+    tokens = width // (C * PARTS)
+    for part in range(PARTS):
+        for c in range(C):
+            first = (c * PARTS + part) * tokens
+            for z in range(Z):
+                for slab in range(slab_count):
+                    for h in range(YH):
+                        lane = (h * Z + z) * LANES
+                        row = (slab * YH + h) * tokens
+                        out[part][z * C + c, row : row + tokens, :] = slabs[
+                            slab, first : first + tokens, lane : lane + LANES
+                        ]
+
+
+def arrange(teacher_slabs, section):
+    slab_count, tokens, width = teacher_slabs.shape
+    rows = slab_count * YH * (tokens // (QUARTERS * PARTS))
+    shape = jax.ShapeDtypeStruct((Z * C, rows, LANES), teacher_slabs.dtype)
+    return pl.pallas_call(
+        arrange_kernel,
+        grid=(1,),
+        out_shape=[shape] * PARTS,
+        in_specs=[pl.BlockSpec((slab_count, tokens // YH, width), lambda i: (0, section, 0))],
+        out_specs=[pl.BlockSpec(shape.shape, lambda i: (0, 0, 0))] * PARTS,
+        cost_estimate=pl.CostEstimate(flops=0, bytes_accessed=1600000, transcendentals=0),
+        name="arrange",
+    )(teacher_slabs)
 
 
 def pick_kernel(layer_map, received, picked):
@@ -38,20 +70,28 @@
     )(layer_map, received)
 
 
-def project_kernel(
-    place, block_row, slot_layer, f0, f1, f2a, f2b, f3, g0, g1, g2a, g2b, g3,
-    w_own, w_sib, w_far_a, w_far_b, w_fs_a, w_fs_b, out, weight, product,
-):
-    layers, halves, tokens, lanes = f0.shape
+def project_kernel(place, block_row, slot_layer, *refs):
+    features, weights = refs[:10], refs[10:16]
+    out, weight, product, *held, spare, feature_sem, weight_sem = refs[17:]
+    layers, halves, tokens, lanes = features[0].shape
+    w_own, w_sib, w_far_a, w_far_b, w_fs_a, w_fs_b = weights
     piece = w_own.shape[1]
     depth = halves * lanes
     blocks = block_row.shape[0]
     far = w_far_a.shape[0]
+    copies = []
     for t in range(blocks):
         first, second = (w_far_a, w_fs_a) if t < far else (w_far_b, w_fs_b)
-        for part, block in enumerate((w_own[t], w_sib[t], first[t % far], second[t % far])):
+        for part, block in enumerate((w_own.at[t], w_sib.at[t], first.at[t % far], second.at[t % far])):
             row = pl.multiple_of(block_row[t] * depth + place[part] * piece, piece)
-            weight[pl.ds(row, piece), :] = block
+            copies.append(pltpu.make_async_copy(block, weight.at[pl.ds(row, piece)], weight_sem.at[t, part]))
+    for index, (block, slot) in enumerate(zip((*features, refs[16].at[0]), (*held, spare))):
+        copies.append(pltpu.make_async_copy(block, slot, feature_sem.at[index]))
+    for copy in copies:
+        copy.start()
+    for copy in copies:
+        copy.wait()
+    f0, f1, f2a, f2b, f3, g0, g1, g2a, g2b, g3 = held
     rows = 256
     group = rows // tokens
     half = layers // 2
@@ -82,28 +122,32 @@
     lax.fori_loop(0, out.shape[0], place_slot, 0)
 
 
-def project(place, block_row, slot_layer, features, weights):
+def project(place, block_row, slot_layer, features, weights, after):
     layers, halves, tokens, lanes = features[0].shape
     columns = weights[0].shape[2]
     slots = slot_layer.shape[0]
-    depth = block_row.shape[0] * halves * lanes
-    vmem = pl.BlockSpec(memory_space=pltpu.VMEM)
+    blocks = block_row.shape[0]
+    depth = blocks * halves * lanes
     smem = pl.BlockSpec(memory_space=pltpu.SMEM)
     return pl.pallas_call(
         project_kernel,
         out_shape=jax.ShapeDtypeStruct((slots, tokens, columns), jnp.bfloat16),
-        in_specs=[smem] * 3 + [vmem] * (len(features) + len(weights)),
-        out_specs=vmem,
+        in_specs=[smem] * 3 + [pl.BlockSpec(memory_space=pl.ANY)] * (len(features) + len(weights) + 1),
+        out_specs=pl.BlockSpec(memory_space=pltpu.VMEM),
         scratch_shapes=[
             pltpu.VMEM((depth, columns), jnp.bfloat16),
             pltpu.VMEM((layers, tokens, columns), jnp.bfloat16),
+            *[pltpu.VMEM(feature.shape, feature.dtype) for feature in features],
+            pltpu.VMEM(after.shape[1:], after.dtype),
+            pltpu.SemaphoreType.DMA((len(features) + 1,)),
+            pltpu.SemaphoreType.DMA((blocks, QUARTERS)),
         ],
         compiler_params=pltpu.CompilerParams(vmem_limit_bytes=40 * MIB),
         cost_estimate=pl.CostEstimate(
-            flops=2 * layers * tokens * depth * columns, bytes_accessed=11 * MIB, transcendentals=0
+            flops=2 * layers * tokens * depth * columns, bytes_accessed=8 * MIB, transcendentals=0
         ),
         name="project",
-    )(place, block_row, slot_layer, *features, *weights)
+    )(place, block_row, slot_layer, *features, *weights, after)
 
 
 def gather_tensor(own):
@@ -158,40 +202,41 @@
     weights = (proj_weight, w_sib, w_far_a, w_far_b, w_fs_a, w_fs_b)
     place = jnp.stack([2 * yh + c, 2 * yh + 1 - c, 2 * (1 - yh) + c, 2 * (1 - yh) + 1 - c]).astype(jnp.int32)
 
-    def arrange(section):
-        width = tokens // YH
-        return (
-            teacher_slabs[:, section * width : (section + 1) * width]
-            .reshape(slab_count, C, quarter, YH, Z, LANES)
-            .transpose(4, 1, 0, 3, 2, 5)
-            .reshape(Z * C, slab_count * YH * quarter, LANES)
-        )
-
-    sent = lax.ppermute(arrange(1), side, [(0, 3), (1, 2)])
-    arranged = jnp.where(yh == 0, arrange(0), sent)
-    received = lax.all_to_all(arranged, ("z", "c"), split_axis=0, concat_axis=0, tiled=True)
-    received = received.reshape(Z * C * slab_count, YH, quarter, LANES)
-    features = gather_tensor(pick(layer_map, received))
     block = jnp.arange(X * YL)
     block_row = ((block // YL - x) % X + X * (block % YL != (yl + yh) % 2)).astype(jnp.int32)
-
     prefix_end = jnp.cumsum(layer_counts)
     prefix_start = prefix_end - layer_counts
     slot_ids = jnp.arange(slot_count)
     slot_layer = jnp.clip(prefix_start[:, None] + slot_ids[None, :], 0, layers - 1).reshape(-1).astype(jnp.int32)
-    partial = project(place, block_row, slot_layer, features, weights)
-    per_z = C * slot_count
-    mine = lax.psum_scatter(
-        partial.reshape(Z, per_z * quarter, columns), "z", scatter_dimension=0, tiled=False
-    ).reshape(C, slot_count, quarter, columns)
-    from_teacher = lax.ppermute(mine, "yh", [(0, 1)])
-    both = jnp.stack([from_teacher, mine])
-    keep = jnp.where(c == 0, both[:, 0], both[:, 1])
-    give = jnp.where(c == 0, both[:, 1], both[:, 0])
-    other = lax.ppermute(give, "c", swap)
-    low = jnp.where(c == 0, keep, other)
-    high = jnp.where(c == 0, other, keep)
-    target = jnp.stack([low, high], axis=2).transpose(1, 0, 2, 3, 4).reshape(slot_count, tokens, columns)
+
+    part_tokens = quarter // PARTS
+    sent = [lax.ppermute(part, side, [(0, 3), (1, 2)]) for part in arrange(teacher_slabs, 1)]
+    kept = arrange(teacher_slabs, 0)
+
+    received = []
+    for part in range(PARTS):
+        arranged = jnp.where(yh == 0, kept[part], sent[part])
+        blocks = lax.all_to_all(arranged, ("z", "c"), split_axis=0, concat_axis=0, tiled=True)
+        received.append(blocks.reshape(Z * C * slab_count, YH, part_tokens, LANES))
+
+    def part_target(part):
+        features = gather_tensor(pick(layer_map, received[part]))
+        after = received[(part + 1) % PARTS]
+        partial = project(place, block_row, slot_layer, features, weights, after)
+        mine = lax.psum_scatter(
+            partial.reshape(Z, C * slot_count * part_tokens, columns), "z", scatter_dimension=0, tiled=False
+        ).reshape(C, slot_count, part_tokens, columns)
+        from_teacher = lax.ppermute(mine, "yh", [(0, 1)])
+        both = jnp.stack([from_teacher, mine])
+        keep = jnp.where(c == 0, both[:, 0], both[:, 1])
+        give = jnp.where(c == 0, both[:, 1], both[:, 0])
+        other = lax.ppermute(give, "c", swap)
+        low = jnp.where(c == 0, keep, other)
+        high = jnp.where(c == 0, other, keep)
+        return jnp.stack([low, high], axis=2)
+
+    target = jnp.stack([part_target(part) for part in range(PARTS)], axis=3)
+    target = target.transpose(1, 0, 2, 3, 4, 5).reshape(slot_count, tokens, columns)
 
     is_child = yh == 1
     child_slot = 2 * z + c

time: 193 us -> 207 us (1.073)
  waiting for transfers between devices: 83 us -> 46.1 us
  starting transfers between devices: 41 us -> 76.4 us
  Pallas kernels: 10.3 us -> 21.1 us
  other arithmetic: 5.15 us -> 11.1 us
  local copies, waits for them, and re-layouts: 13.9 us -> 11.5 us
    ppermute x3 -> x6, starting transfers between devices: 15.3 us -> 29.4 us  [the longest x2 11.1 us: body(): lax.ppermute(part, side, [(0, 3), (1, 2)])]
    ppermute x3 -> x6, waiting for transfers between devices: 17.3 us -> 4.82 us  [the longest x2 4.81 us: body(): lax.ppermute(part, side, [(0, 3), (1, 2)])]
    ppermute x1, waiting for transfers between devices: 11.8 us -> 0.01 us  [body(): lax.ppermute(proj_weight[:half_blocks], side, up)]
    all_to_all x1 -> x2, starting transfers between devices: 10 us -> 19.1 us  [body(): lax.all_to_all(arranged, ('z', 'c'), split_axis=0, concat_axis=0, tiled=T...]
    ppermute x1 -> x2, waiting for transfers between devices: 8.16 us -> 0.94 us  [gather_tensor(): g0 = lax.ppermute(own, 'yl', swap)]
    ppermute x1, waiting for transfers between devices: 0.01 us -> 5.4 us  [body(): lax.ppermute(proj_weight[half_blocks:], side, down)]
    all_to_all x1 -> x2, waiting for transfers between devices: 6.14 us -> 1.37 us  [body(): lax.all_to_all(arranged, ('z', 'c'), split_axis=0, concat_axis=0, tiled=T...]
    pallas_call x1 -> x2, Pallas kernels: 8.15 us -> 12.8 us  [project(): pl.pallas_call(project_kernel, out_shape=jax.ShapeDtypeStruct((slots, tok...]
  transfers between devices with their start and end apart: 21 -> 35, of which waited for: 12 -> 13; matrix products, arithmetic and copies ran while one was open for 8% -> 12% of each run, Pallas kernels for 1% -> 6%
where the time goes in v3:
time: 207 us; the launch traced here: 206 us
  starting transfers between devices  76.4 us (37%)
  waiting for transfers between devices  46.1 us (22%)
  Pallas kernels  21.1 us (10%)
  between operations  15 us (7%)
  blocking collectives  13.9 us (7%)
  local copies, waits for them, and re-layouts  11.5 us (6%)
  other arithmetic  11.1 us (5%)
  matrix products  10.6 us (5%)
    reduce_scatter x2, waiting for transfers between devices, part_target(): lax.psum_scatter(partial.reshape(Z, C * slot_count * part_tokens, columns...  20.4 us
    all_to_all x2, starting transfers between devices, body(): lax.all_to_all(arranged, ('z', 'c'), split_axis=0, concat_axis=0, tiled=T...  19.1 us
    psum x1, blocking collectives, body(): lax.psum(jnp.stack([jnp.sum(first_hidden * first_hidden, axis=1), jnp.sum...  13.9 us
    pallas_call x2, Pallas kernels, project(): pl.pallas_call(project_kernel, out_shape=jax.ShapeDtypeStruct((slots, tok...  12.8 us
    ppermute x2, starting transfers between devices, body(): lax.ppermute(part, side, [(0, 3), (1, 2)])  11.1 us
    ppermute x2, starting transfers between devices, part_target(): from_teacher = lax.ppermute(mine, 'yh', [(0, 1)])  11 us
    ppermute x2, starting transfers between devices, part_target(): other = lax.ppermute(give, 'c', swap)  7.29 us
    unnamed x28, local copies, waits for them, and re-layouts  5.76 us
  transfers between devices with their start and end apart: 35, of which 13 were waited for; matrix products, arithmetic and copies ran while one was open for 12% of the time, Pallas kernels for 6%

profile of v3, /device:TPU:1, one launch (start us, length us, event | category | flops | bytes accessed | tf_op | source)
XLA Modules:
  0.0 205.7 jit_solution(8043170456245671722)
XLA Ops:
  7.2 2.3 %arrange.3 = (bf16[16,96,128]{2,1,0:T(8,128)(2,1)}, bf16[16,96,128]{2,1,0:T(8,128)(2,1)}) custom-call(bf16[3,128,2048]{2,1,0:T(8,128)(2,1)} %slabs.3), custom_call_target="tpu_custom_call" | custom-call | bytes 1600000 | tf_op jit(solution)/shard_map/arrange/pallas_call | solution.py:39
  9.5 5.5 %collective-permute-start.17 = (bf16[16,96,128]{2,1,0:T(8,128)(2,1)}, bf16[16,96,128]{2,1,0:T(8,128)(2,1)S(1)}, u32[]{:S(2)}, u32[]{:S(2)}) collective-permute-start(bf16[16,96,128]{2,1,0:T(8,128)(2,1)} %get-tuple-element.23), channel_id=1, source_target_pairs={{0,129},{1,128},{2,131},{3,130},{4,133},{5,132},{6,135},{7,134},{8... | collective-permute-start | bytes 1179656 | tf_op jit(solution)/shard_map/ppermute | solution.py:213
  16.1 2.2 %arrange.2 = (bf16[16,96,128]{2,1,0:T(8,128)(2,1)}, bf16[16,96,128]{2,1,0:T(8,128)(2,1)}) custom-call(bf16[3,128,2048]{2,1,0:T(8,128)(2,1)} %slabs.3), custom_call_target="tpu_custom_call" | custom-call | bytes 1600000 | tf_op jit(solution)/shard_map/arrange/pallas_call | solution.py:39
  18.2 4.8 %collective-permute-done.17 = bf16[16,96,128]{2,1,0:T(8,128)(2,1)S(1)} collective-permute-done((bf16[16,96,128]{2,1,0:T(8,128)(2,1)}, bf16[16,96,128]{2,1,0:T(8,128)(2,1)S(1)}, u32[]{:S(2)}, u32[]{:S(2)}) %collective-permute-start.17) | collective-permute-done | bytes 393248 | tf_op jit(solution)/shard_map/ppermute | solution.py:213
  23.1 1.8 broadcast_select_fusion
  24.8 10.2 %all-to-all-start.1 = ((bf16[16,96,128]{2,1,0:T(8,128)(2,1)}), bf16[16,96,128]{2,1,0:T(8,128)(2,1)S(1)}, u32[]{:S(2)}, u32[]{:S(2)}) async-start(bf16[16,96,128]{2,1,0:T(8,128)(2,1)} %broadcast_select_fusion), calls=%async_computation.1 | async-start | bytes 786432 | tf_op jit(solution)/shard_map/all_to_all | solution.py:219
  35.0 2.3 %collective-permute-start.13 = (bf16[4,64,1024]{2,1,0:T(8,128)(2,1)}, bf16[4,64,1024]{2,1,0:T(8,128)(2,1)}, u32[]{:S(2)}, u32[]{:S(2)}) collective-permute-start(bf16[4,64,1024]{2,1,0:T(8,128)(2,1)} %get-tuple-element.28), channel_id=1, source_target_pairs={{0,129},{1,0},{128,1},{129,128},{2,131},{3,2},{130,3},{131,130},{4... | collective-permute-start | bytes 1572872 | tf_op jit(solution)/shard_map/ppermute | solution.py:198
  37.8 5.6 %collective-permute-start = (bf16[16,96,128]{2,1,0:T(8,128)(2,1)}, bf16[16,96,128]{2,1,0:T(8,128)(2,1)}, u32[]{:S(2)}, u32[]{:S(2)}) collective-permute-start(bf16[16,96,128]{2,1,0:T(8,128)(2,1)} %get-tuple-element.21), channel_id=1, source_target_pairs={{0,129},{1,128},{2,131},{3,130},{4,133},{5,132},{6,135},{7,134},{8... | collective-permute-start | bytes 1179656 | tf_op jit(solution)/shard_map/ppermute | solution.py:213
  43.4 5.4 %collective-permute-done.13 = bf16[4,64,1024]{2,1,0:T(8,128)(2,1)} collective-permute-done((bf16[4,64,1024]{2,1,0:T(8,128)(2,1)}, bf16[4,64,1024]{2,1,0:T(8,128)(2,1)}, u32[]{:S(2)}, u32[]{:S(2)}) %collective-permute-start.13) | collective-permute-done | bytes 524320 | tf_op jit(solution)/shard_map/ppermute | solution.py:198
  48.8 3.4 %collective-permute-start.14 = (bf16[4,64,1024]{2,1,0:T(8,128)(2,1)}, bf16[4,64,1024]{2,1,0:T(8,128)(2,1)}, u32[]{:S(2)}, u32[]{:S(2)}) collective-permute-start(bf16[4,64,1024]{2,1,0:T(8,128)(2,1)} %collective-permute-done.13), channel_id=1, source_target_pairs={{0,129},{1,0},{128,1},{129,128},{2,131},{3,2},{130,3},{131,130},{4... | collective-permute-start | bytes 1572872 | tf_op jit(solution)/shard_map/ppermute | solution.py:198
  52.2 1.8 collective-permute-start.15
  54.8 1.9 pick_layers.3.refs_0_
  61.5 8.9 %all-to-all-start = ((bf16[16,96,128]{2,1,0:T(8,128)(2,1)}), bf16[16,96,128]{2,1,0:T(8,128)(2,1)S(1)}, u32[]{:S(2)}, u32[]{:S(2)}) async-start(bf16[16,96,128]{2,1,0:T(8,128)(2,1)} %broadcast_select_fusion.1), calls=%async_computation | async-start | bytes 786432 | tf_op jit(solution)/shard_map/all_to_all | solution.py:219
  74.9 2.9 %collective-permute-start.23 = (bf16[16,2,16,128]{3,2,1,0:T(8,128)(2,1)}, bf16[16,2,16,128]{3,2,1,0:T(8,128)(2,1)}, u32[]{:S(2)}, u32[]{:S(2)}) collective-permute-start(bf16[16,2,16,128]{3,2,1,0:T(8,128)(2,1)} %slice.84), channel_id=1, source_target_pairs={{0,6},{2,0},{4,2},{6,4},{1,7},{3,1},{5,3},{7,5},{8,14},{10,8},{12,... | collective-permute-start | bytes 393224 | tf_op jit(solution)/shard_map/ppermute | solution.py:162
  85.6 2.8 %collective-permute-done.27.refs_8_ = bf16[16,2,16,128]{3,2,1,0:T(8,128)(2,1)} collective-permute-done((bf16[16,2,16,128]{3,2,1,0:T(8,128)(2,1)}, bf16[16,2,16,128]{3,2,1,0:T(8,128)(2,1)}, u32[]{:S(2)}, u32[]{:S(2)}) %collective-permute-start.27) | collective-permute-done | bytes 131104 | tf_op jit(solution)/shard_map/ppermute | solution.py:166
  89.3 6.7 %project.3 = bf16[48,16,1024]{2,1,0:T(8,128)(2,1)S(1)} custom-call(s32[4]{0:T(128)S(1)} %pad_add_fusion.place, s32[8]{0:T(128)S(1)} %fusion.39.block_row, s32[48]{0:T(128)S(1)} %min.12.slot_layer, bf16[32,2,16,128]{3,2,1,0:T(8,128)(2,1)S(1)} %copy-done.7, bf16[32,2,16,128]{3,2,1,0:T(8,128)(2,1)} %collective-permute-done.20.refs_1_, ...), custom_call_target="tpu_custom_call" | custom-call | flops 2147483648 | bytes 8388608 | tf_op jit(solution)/shard_map/project/pallas_call | solution.py:132
  98.0 1.9 pick_layers.2.refs_0_
  99.9 3.5 %collective-permute-start.1 = (bf16[32,2,16,128]{3,2,1,0:T(8,128)(2,1)}, bf16[32,2,16,128]{3,2,1,0:T(8,128)(2,1)S(1)}, u32[]{:S(2)}, u32[]{:S(2)}) collective-permute-start(bf16[32,2,16,128]{3,2,1,0:T(8,128)(2,1)} %pick_layers.2.refs_0_), channel_id=1, source_target_pairs={{0,6},{2,0},{4,2},{6,4},{1,7},{3,1},{5,3},{7,5},{8,14},{10,8},{12,... | collective-permute-start | bytes 786440 | tf_op jit(solution)/shard_map/ppermute | solution.py:159
  104.6 3.9 %collective-permute-done.2.refs_4_ = bf16[32,2,16,128]{3,2,1,0:T(8,128)(2,1)S(1)} collective-permute-done((bf16[32,2,16,128]{3,2,1,0:T(8,128)(2,1)}, bf16[32,2,16,128]{3,2,1,0:T(8,128)(2,1)S(1)}, u32[]{:S(2)}, u32[]{:S(2)}) %collective-permute-start.2) | collective-permute-done | bytes 262176 | tf_op jit(solution)/shard_map/ppermute | solution.py:158
  108.6 2.7 %collective-permute-start.4 = (bf16[16,2,16,128]{3,2,1,0:T(8,128)(2,1)S(1)}, bf16[16,2,16,128]{3,2,1,0:T(8,128)(2,1)S(1)}, u32[]{:S(2)}, u32[]{:S(2)}) collective-permute-start(bf16[16,2,16,128]{3,2,1,0:T(8,128)(2,1)S(1)} %slice.80), channel_id=1, source_target_pairs={{0,6},{2,0},{4,2},{6,4},{1,7},{3,1},{5,3},{7,5},{8,14},{10,8},{12,... | collective-permute-start | bytes 393224 | tf_op jit(solution)/shard_map/ppermute | solution.py:162
  115.1 2.7 %collective-permute-done.7.refs_7_ = bf16[16,2,16,128]{3,2,1,0:T(8,128)(2,1)S(1)} collective-permute-done((bf16[16,2,16,128]{3,2,1,0:T(8,128)(2,1)S(1)}, bf16[16,2,16,128]{3,2,1,0:T(8,128)(2,1)S(1)}, u32[]{:S(2)}, u32[]{:S(2)}) %collective-permute-start.7) | collective-permute-done | bytes 131104 | tf_op jit(solution)/shard_map/ppermute | solution.py:165
  120.8 6.1 %project.2 = bf16[48,16,1024]{2,1,0:T(8,128)(2,1)S(1)} custom-call(s32[4]{0:T(128)S(1)} %pad_add_fusion.place, s32[8]{0:T(128)S(1)} %fusion.39.block_row, s32[48]{0:T(128)S(1)} %min.12.slot_layer, bf16[32,2,16,128]{3,2,1,0:T(8,128)(2,1)S(1)} %copy-done.8, bf16[32,2,16,128]{3,2,1,0:T(8,128)(2,1)S(1)} %collective-permute-done.1.refs_1_, ...), custom_call_target="tpu_custom_call" | custom-call | flops 2147483648 | bytes 8388608 | tf_op jit(solution)/shard_map/project/pallas_call | solution.py:132
  129.5 2.5 %fusion = f32[128,1024]{1,0:T(8,128)S(1)} fusion(bf16[1,1024,1024]{2,1,0:T(8,128)(2,1)} %param.17, bf16[1,128,1024]{2,1,0:T(8,128)(2,1)} %param.19), kind=kOutput, calls=%fused_computation | convolution fusion | flops 268435456 | bytes 2883584 | tf_op jit(solution)/shard_map/dot_general | solution.py:255
  132.1 1.9 fusion.12
  134.0 13.9 %psum.7 = f32[2,128]{1,0:T(2,128)S(1)} all-reduce(f32[2,128]{1,0:T(2,128)S(1)} %pad_maximum_fusion.2), channel_id=1, replica_groups=mesh['yh'=2,'z'=8,'c'=2,'x'=4,'yl'=2] {'x','yl'}, use_global_device_ids=true, to_apply=%region_5.6 | all-reduce | flops 256 | bytes 2048 | tf_op jit(solution)/shard_map/psum | solution.py:258
  148.1 3.1 %select_bitcast_fusion = bf16[1,1024,1024]{2,1,0:T(8,128)(2,1)} fusion(pred[]{:T(512)S(6)} %eq.11, bf16[1,128,1024]{2,1,0:T(8,128)(2,1)} %param.19, f32[1024]{0:T(1024)S(1)} %bitcast.154, f32[128]{0:T(128)S(1)} %get-tuple-element.27, bf16[3,128,1024]{2,1,0:T(8,128)(2,1)S(1)} %copy-done.9), kind=kOutput, calls=%fused_computation.4 | convolution fusion | flops 271056896 | bytes 2626049 | tf_op jit(solution)/shard_map/dot_general | solution.py:274
  151.8 6.2 %collective-permute-start.29 = (bf16[2,3,16,1024]{3,2,1,0:T(8,128)(2,1)}, bf16[2,3,16,1024]{3,2,1,0:T(8,128)(2,1)}, u32[]{:S(2)}, u32[]{:S(2)}) collective-permute-start(bf16[2,3,16,1024]{3,2,1,0:T(8,128)(2,1)} %bitcast.145), channel_id=1, source_target_pairs={{0,128},{1,129},{2,130},{3,131},{4,132},{5,133},{6,134},{7,135},{8... | collective-permute-start | bytes 589832 | tf_op jit(solution)/shard_map/ppermute | solution.py:229
  158.0 3.1 %select_bitcast_fusion.1 = bf16[1,1024,1024]{2,1,0:T(8,128)(2,1)} fusion(pred[]{:T(512)S(6)} %eq.11, bf16[1,128,1024]{2,1,0:T(8,128)(2,1)} %param.18, f32[1024]{0:T(1024)S(1)} %bitcast.155, f32[128]{0:T(128)S(1)} %get-tuple-element.27, bf16[3,128,1024]{2,1,0:T(8,128)(2,1)S(1)} %copy-done.9), kind=kOutput, calls=%fused_computation.5 | convolution fusion | flops 271056896 | bytes 2626049 | tf_op jit(solution)/shard_map/dot_general | solution.py:271
  161.0 20.4 %reduce-scatter.3.cloned.1.call-done = bf16[1,96,1024]{2,1,0:T(8,128)(2,1)} async-done(((bf16[8,96,1024]{2,1,0:T(8,128)(2,1)}), bf16[1,96,1024]{2,1,0:T(8,128)(2,1)}) %reduce-scatter.3.cloned.1.call-update) | async-done | bytes 196624 | tf_op jit(solution)/shard_map/reduce_scatter | solution.py:226
  181.4 4.8 %collective-permute-start.18 = (bf16[2,3,16,1024]{3,2,1,0:T(8,128)(2,1)}, bf16[2,3,16,1024]{3,2,1,0:T(8,128)(2,1)S(1)}, u32[]{:S(2)}, u32[]{:S(2)}) collective-permute-start(bf16[2,3,16,1024]{3,2,1,0:T(8,128)(2,1)} %bitcast.148), channel_id=1, source_target_pairs={{0,128},{1,129},{2,130},{3,131},{4,132},{5,133},{6,134},{7,135},{8... | collective-permute-start | bytes 589832 | tf_op jit(solution)/shard_map/ppermute | solution.py:229
  187.4 4.9 %collective-permute-start.30 = (bf16[2,3,16,1024]{3,2,0,1:T(8,128)(2,1)S(1)}, bf16[2,3,16,1024]{3,2,0,1:T(8,128)(2,1)S(1)}, u32[]{:S(2)}, u32[]{:S(2)}) collective-permute-start(bf16[2,3,16,1024]{3,2,0,1:T(8,128)(2,1)S(1)} %select_bitcast_fusion.2), channel_id=1, source_target_pairs={{0,8},{8,0},{1,9},{9,1},{2,10},{10,2},{3,11},{11,3},{4,12},{12,4},... | collective-permute-start | bytes 589832 | tf_op jit(solution)/shard_map/ppermute | solution.py:233
  193.3 2.4 %collective-permute-start.19 = (bf16[2,3,16,1024]{3,2,0,1:T(8,128)(2,1)S(1)}, bf16[2,3,16,1024]{3,2,0,1:T(8,128)(2,1)S(1)}, u32[]{:S(2)}, u32[]{:S(2)}) collective-permute-start(bf16[2,3,16,1024]{3,2,0,1:T(8,128)(2,1)S(1)} %select_bitcast_fusion.3), channel_id=1, source_target_pairs={{0,8},{8,0},{1,9},{9,1},{2,10},{10,2},{3,11},{11,3},{4,12},{12,4},... | collective-permute-start | bytes 589832 | tf_op jit(solution)/shard_map/ppermute | solution.py:233
  (110 shorter events, 38.1 us)
Async XLA Ops:
  9.5 13.5 %collective-permute-start.17 = (bf16[16,96,128]{2,1,0:T(8,128)(2,1)}, bf16[16,96,128]{2,1,0:T(8,128)(2,1)S(1)}, u32[]{:S(2)}, u32[]{:S(2)}) collective-permute-start(bf16[16,96,128]{2,1,0:T(8,128)(2,1)} %get-tuple-element.23), channel_id=1, source_target_pairs={{0,129},{1,128},{2,131},{3,130},{4,133},{5,132},{6,135},{7,134},{8... | collective-permute-start | bytes 1179656 | tf_op jit(solution)/shard_map/ppermute | solution.py:213
  16.1 21.2 %collective-permute-start.11 = (bf16[4,64,1024]{2,1,0:T(8,128)(2,1)}, bf16[4,64,1024]{2,1,0:T(8,128)(2,1)}, u32[]{:S(2)}, u32[]{:S(2)}) collective-permute-start(bf16[4,64,1024]{2,1,0:T(8,128)(2,1)} %get-tuple-element.29), channel_id=1, source_target_pairs={{0,1},{1,128},{128,129},{129,0},{2,3},{3,130},{130,131},{131,2},{4... | collective-permute-start | bytes 1572872 | tf_op jit(solution)/shard_map/ppermute | solution.py:197
  24.8 29.2 %all-to-all-start.1 = ((bf16[16,96,128]{2,1,0:T(8,128)(2,1)}), bf16[16,96,128]{2,1,0:T(8,128)(2,1)S(1)}, u32[]{:S(2)}, u32[]{:S(2)}) async-start(bf16[16,96,128]{2,1,0:T(8,128)(2,1)} %broadcast_select_fusion), calls=%async_computation.1 | async-start | bytes 786432 | tf_op jit(solution)/shard_map/all_to_all | solution.py:219
  35.0 13.8 %collective-permute-start.13 = (bf16[4,64,1024]{2,1,0:T(8,128)(2,1)}, bf16[4,64,1024]{2,1,0:T(8,128)(2,1)}, u32[]{:S(2)}, u32[]{:S(2)}) collective-permute-start(bf16[4,64,1024]{2,1,0:T(8,128)(2,1)} %get-tuple-element.28), channel_id=1, source_target_pairs={{0,129},{1,0},{128,1},{129,128},{2,131},{3,2},{130,3},{131,130},{4... | collective-permute-start | bytes 1572872 | tf_op jit(solution)/shard_map/ppermute | solution.py:198
  37.3 14.9 %collective-permute-start.12 = (bf16[4,64,1024]{2,1,0:T(8,128)(2,1)}, bf16[4,64,1024]{2,1,0:T(8,128)(2,1)}, u32[]{:S(2)}, u32[]{:S(2)}) collective-permute-start(bf16[4,64,1024]{2,1,0:T(8,128)(2,1)} %collective-permute-done.11), channel_id=1, source_target_pairs={{0,1},{1,128},{128,129},{129,0},{2,3},{3,130},{130,131},{131,2},{4... | collective-permute-start | bytes 1572872 | tf_op jit(solution)/shard_map/ppermute | solution.py:197
  37.3 37.6 %collective-permute-start.10 = (bf16[8,64,1024]{2,1,0:T(8,128)(2,1)S(1)}, bf16[8,64,1024]{2,1,0:T(8,128)(2,1)}, u32[]{:S(2)}, u32[]{:S(2)}) collective-permute-start(bf16[8,64,1024]{2,1,0:T(8,128)(2,1)S(1)} %copy-done.1), channel_id=1, source_target_pairs={{0,8},{8,0},{1,9},{9,1},{2,10},{10,2},{3,11},{11,3},{4,12},{12,4},... | collective-permute-start | bytes 3145736 | tf_op jit(solution)/shard_map/ppermute | solution.py:199
  37.8 20.1 %collective-permute-start = (bf16[16,96,128]{2,1,0:T(8,128)(2,1)}, bf16[16,96,128]{2,1,0:T(8,128)(2,1)}, u32[]{:S(2)}, u32[]{:S(2)}) collective-permute-start(bf16[16,96,128]{2,1,0:T(8,128)(2,1)} %get-tuple-element.21), channel_id=1, source_target_pairs={{0,129},{1,128},{2,131},{3,130},{4,133},{5,132},{6,135},{7,134},{8... | collective-permute-start | bytes 1179656 | tf_op jit(solution)/shard_map/ppermute | solution.py:213
  48.8 23.3 %collective-permute-start.14 = (bf16[4,64,1024]{2,1,0:T(8,128)(2,1)}, bf16[4,64,1024]{2,1,0:T(8,128)(2,1)}, u32[]{:S(2)}, u32[]{:S(2)}) collective-permute-start(bf16[4,64,1024]{2,1,0:T(8,128)(2,1)} %collective-permute-done.13), channel_id=1, source_target_pairs={{0,129},{1,0},{128,1},{129,128},{2,131},{3,2},{130,3},{131,130},{4... | collective-permute-start | bytes 1572872 | tf_op jit(solution)/shard_map/ppermute | solution.py:198
  52.2 30.4 %collective-permute-start.15 = (bf16[4,64,1024]{2,1,0:T(8,128)(2,1)}, bf16[4,64,1024]{2,1,0:T(8,128)(2,1)}, u32[]{:S(2)}, u32[]{:S(2)}) collective-permute-start(bf16[4,64,1024]{2,1,0:T(8,128)(2,1)} %collective-permute-done.12.refs_12_), channel_id=1, source_target_pairs={{0,8},{8,0},{1,9},{9,1},{2,10},{10,2},{3,11},{11,3},{4,12},{12,4},... | collective-permute-start | bytes 1572872 | tf_op jit(solution)/shard_map/ppermute | solution.py:200
  56.7 13.7 %collective-permute-start.21 = (bf16[32,2,16,128]{3,2,1,0:T(8,128)(2,1)}, bf16[32,2,16,128]{3,2,1,0:T(8,128)(2,1)}, u32[]{:S(2)}, u32[]{:S(2)}) collective-permute-start(bf16[32,2,16,128]{3,2,1,0:T(8,128)(2,1)} %pick_layers.3.refs_0_), channel_id=1, source_target_pairs={{0,2},{2,4},{4,6},{6,0},{1,3},{3,5},{5,7},{7,1},{8,10},{10,12},{12... | collective-permute-start | bytes 786440 | tf_op jit(solution)/shard_map/ppermute | solution.py:158
  57.9 14.2 %collective-permute-start.20 = (bf16[32,2,16,128]{3,2,1,0:T(8,128)(2,1)}, bf16[32,2,16,128]{3,2,1,0:T(8,128)(2,1)}, u32[]{:S(2)}, u32[]{:S(2)}) collective-permute-start(bf16[32,2,16,128]{3,2,1,0:T(8,128)(2,1)} %pick_layers.3.refs_0_), channel_id=1, source_target_pairs={{0,6},{2,0},{4,2},{6,4},{1,7},{3,1},{5,3},{7,5},{8,14},{10,8},{12,... | collective-permute-start | bytes 786440 | tf_op jit(solution)/shard_map/ppermute | solution.py:159
  61.5 23.5 %all-to-all-start = ((bf16[16,96,128]{2,1,0:T(8,128)(2,1)}), bf16[16,96,128]{2,1,0:T(8,128)(2,1)S(1)}, u32[]{:S(2)}, u32[]{:S(2)}) async-start(bf16[16,96,128]{2,1,0:T(8,128)(2,1)} %broadcast_select_fusion.1), calls=%async_computation | async-start | bytes 786432 | tf_op jit(solution)/shard_map/all_to_all | solution.py:219
  70.4 81.4 %reduce-scatter.5.cloned.1.call-start = ((), (), s32[]{:S(2)}) async-start(), calls=%async_computation.5 | async-start | bytes 1769472 | tf_op jit(solution)/shard_map/reduce_scatter | solution.py:226
  70.4 8.3 %collective-permute-start.24 = (bf16[32,2,16,128]{3,2,1,0:T(8,128)(2,1)}, bf16[32,2,16,128]{3,2,1,0:T(8,128)(2,1)}, u32[]{:S(2)}, u32[]{:S(2)}) collective-permute-start(bf16[32,2,16,128]{3,2,1,0:T(8,128)(2,1)} %pick_layers.3.refs_0_), channel_id=1, source_target_pairs={{0,1},{1,0},{2,3},{3,2},{4,5},{5,4},{6,7},{7,6},{8,9},{9,8},{10,11... | collective-permute-start | bytes 786440 | tf_op jit(solution)/shard_map/ppermute | solution.py:160
  72.1 7.1 %collective-permute-start.22 = (bf16[16,2,16,128]{3,2,1,0:T(8,128)(2,1)}, bf16[16,2,16,128]{3,2,1,0:T(8,128)(2,1)}, u32[]{:S(2)}, u32[]{:S(2)}) collective-permute-start(bf16[16,2,16,128]{3,2,1,0:T(8,128)(2,1)} %slice.83), channel_id=1, source_target_pairs={{0,2},{2,4},{4,6},{6,0},{1,3},{3,5},{5,7},{7,1},{8,10},{10,12},{12... | collective-permute-start | bytes 393224 | tf_op jit(solution)/shard_map/ppermute | solution.py:161
  72.1 12.8 %collective-permute-start.16 = (bf16[4,64,1024]{2,1,0:T(8,128)(2,1)}, bf16[4,64,1024]{2,1,0:T(8,128)(2,1)}, u32[]{:S(2)}, u32[]{:S(2)}) collective-permute-start(bf16[4,64,1024]{2,1,0:T(8,128)(2,1)} %collective-permute-done.14.refs_13_), channel_id=1, source_target_pairs={{0,8},{8,0},{1,9},{9,1},{2,10},{10,2},{3,11},{11,3},{4,12},{12,4},... | collective-permute-start | bytes 1572872 | tf_op jit(solution)/shard_map/ppermute | solution.py:201
  74.9 6.1 %collective-permute-start.23 = (bf16[16,2,16,128]{3,2,1,0:T(8,128)(2,1)}, bf16[16,2,16,128]{3,2,1,0:T(8,128)(2,1)}, u32[]{:S(2)}, u32[]{:S(2)}) collective-permute-start(bf16[16,2,16,128]{3,2,1,0:T(8,128)(2,1)} %slice.84), channel_id=1, source_target_pairs={{0,6},{2,0},{4,2},{6,4},{1,7},{3,1},{5,3},{7,5},{8,14},{10,8},{12,... | collective-permute-start | bytes 393224 | tf_op jit(solution)/shard_map/ppermute | solution.py:162
  78.7 9.7 %collective-permute-start.25 = (bf16[32,2,16,128]{3,2,1,0:T(8,128)(2,1)}, bf16[32,2,16,128]{3,2,1,0:T(8,128)(2,1)}, u32[]{:S(2)}, u32[]{:S(2)}) collective-permute-start(bf16[32,2,16,128]{3,2,1,0:T(8,128)(2,1)} %collective-permute-done.24.refs_5_), channel_id=1, source_target_pairs={{0,6},{2,0},{4,2},{6,4},{1,7},{3,1},{5,3},{7,5},{8,14},{10,8},{12,... | collective-permute-start | bytes 786440 | tf_op jit(solution)/shard_map/ppermute | solution.py:164
  79.3 9.1 %collective-permute-start.28 = (bf16[32,2,16,128]{3,2,1,0:T(8,128)(2,1)}, bf16[32,2,16,128]{3,2,1,0:T(8,128)(2,1)}, u32[]{:S(2)}, u32[]{:S(2)}) collective-permute-start(bf16[32,2,16,128]{3,2,1,0:T(8,128)(2,1)} %collective-permute-done.24.refs_5_), channel_id=1, source_target_pairs={{0,2},{2,4},{4,6},{6,0},{1,3},{3,5},{5,7},{7,1},{8,10},{10,12},{12... | collective-permute-start | bytes 786440 | tf_op jit(solution)/shard_map/ppermute | solution.py:163
  82.7 5.7 %collective-permute-start.27 = (bf16[16,2,16,128]{3,2,1,0:T(8,128)(2,1)}, bf16[16,2,16,128]{3,2,1,0:T(8,128)(2,1)}, u32[]{:S(2)}, u32[]{:S(2)}) collective-permute-start(bf16[16,2,16,128]{3,2,1,0:T(8,128)(2,1)} %collective-permute-done.23.refs_3_), channel_id=1, source_target_pairs={{0,1},{1,0},{2,3},{3,2},{4,5},{5,4},{6,7},{7,6},{8,9},{9,8},{10,11... | collective-permute-start | bytes 393224 | tf_op jit(solution)/shard_map/ppermute | solution.py:166
  97.9 83.5 %reduce-scatter.3.cloned.1.call-start = ((), (), s32[]{:S(2)}) async-start(), calls=%async_computation.4 | async-start | bytes 1769472 | tf_op jit(solution)/shard_map/reduce_scatter | solution.py:226
  99.9 8.5 %collective-permute-start.2 = (bf16[32,2,16,128]{3,2,1,0:T(8,128)(2,1)}, bf16[32,2,16,128]{3,2,1,0:T(8,128)(2,1)S(1)}, u32[]{:S(2)}, u32[]{:S(2)}) collective-permute-start(bf16[32,2,16,128]{3,2,1,0:T(8,128)(2,1)} %pick_layers.2.refs_0_), channel_id=1, source_target_pairs={{0,2},{2,4},{4,6},{6,0},{1,3},{3,5},{5,7},{7,1},{8,10},{10,12},{12... | collective-permute-start | bytes 786440 | tf_op jit(solution)/shard_map/ppermute | solution.py:158
  99.9 8.6 %collective-permute-start.1 = (bf16[32,2,16,128]{3,2,1,0:T(8,128)(2,1)}, bf16[32,2,16,128]{3,2,1,0:T(8,128)(2,1)S(1)}, u32[]{:S(2)}, u32[]{:S(2)}) collective-permute-start(bf16[32,2,16,128]{3,2,1,0:T(8,128)(2,1)} %pick_layers.2.refs_0_), channel_id=1, source_target_pairs={{0,6},{2,0},{4,2},{6,4},{1,7},{3,1},{5,3},{7,5},{8,14},{10,8},{12,... | collective-permute-start | bytes 786440 | tf_op jit(solution)/shard_map/ppermute | solution.py:159
  103.4 7.9 %collective-permute-start.5 = (bf16[32,2,16,128]{3,2,1,0:T(8,128)(2,1)}, bf16[32,2,16,128]{3,2,1,0:T(8,128)(2,1)S(1)}, u32[]{:S(2)}, u32[]{:S(2)}) collective-permute-start(bf16[32,2,16,128]{3,2,1,0:T(8,128)(2,1)} %pick_layers.2.refs_0_), channel_id=1, source_target_pairs={{0,1},{1,0},{2,3},{3,2},{4,5},{5,4},{6,7},{7,6},{8,9},{9,8},{10,11... | collective-permute-start | bytes 786440 | tf_op jit(solution)/shard_map/ppermute | solution.py:160
  108.5 5.1 %collective-permute-start.3 = (bf16[16,2,16,128]{3,2,1,0:T(8,128)(2,1)S(1)}, bf16[16,2,16,128]{3,2,1,0:T(8,128)(2,1)S(1)}, u32[]{:S(2)}, u32[]{:S(2)}) collective-permute-start(bf16[16,2,16,128]{3,2,1,0:T(8,128)(2,1)S(1)} %slice.79), channel_id=1, source_target_pairs={{0,2},{2,4},{4,6},{6,0},{1,3},{3,5},{5,7},{7,1},{8,10},{10,12},{12... | collective-permute-start | bytes 393224 | tf_op jit(solution)/shard_map/ppermute | solution.py:161
  108.6 5.8 %collective-permute-start.4 = (bf16[16,2,16,128]{3,2,1,0:T(8,128)(2,1)S(1)}, bf16[16,2,16,128]{3,2,1,0:T(8,128)(2,1)S(1)}, u32[]{:S(2)}, u32[]{:S(2)}) collective-permute-start(bf16[16,2,16,128]{3,2,1,0:T(8,128)(2,1)S(1)} %slice.80), channel_id=1, source_target_pairs={{0,6},{2,0},{4,2},{6,4},{1,7},{3,1},{5,3},{7,5},{8,14},{10,8},{12,... | collective-permute-start | bytes 393224 | tf_op jit(solution)/shard_map/ppermute | solution.py:162
  111.3 7.9 %collective-permute-start.6 = (bf16[32,2,16,128]{3,2,1,0:T(8,128)(2,1)S(1)}, bf16[32,2,16,128]{3,2,1,0:T(8,128)(2,1)S(1)}, u32[]{:S(2)}, u32[]{:S(2)}) collective-permute-start(bf16[32,2,16,128]{3,2,1,0:T(8,128)(2,1)S(1)} %collective-permute-done.5.refs_5_), channel_id=1, source_target_pairs={{0,6},{2,0},{4,2},{6,4},{1,7},{3,1},{5,3},{7,5},{8,14},{10,8},{12,... | collective-permute-start | bytes 786440 | tf_op jit(solution)/shard_map/ppermute | solution.py:164
  111.4 8.5 %collective-permute-start.9 = (bf16[32,2,16,128]{3,2,1,0:T(8,128)(2,1)S(1)}, bf16[32,2,16,128]{3,2,1,0:T(8,128)(2,1)S(1)}, u32[]{:S(2)}, u32[]{:S(2)}) collective-permute-start(bf16[32,2,16,128]{3,2,1,0:T(8,128)(2,1)S(1)} %collective-permute-done.5.refs_5_), channel_id=1, source_target_pairs={{0,2},{2,4},{4,6},{6,0},{1,3},{3,5},{5,7},{7,1},{8,10},{10,12},{12... | collective-permute-start | bytes 786440 | tf_op jit(solution)/shard_map/ppermute | solution.py:163
  114.4 4.8 %collective-permute-start.8 = (bf16[16,2,16,128]{3,2,1,0:T(8,128)(2,1)S(1)}, bf16[16,2,16,128]{3,2,1,0:T(8,128)(2,1)S(1)}, u32[]{:S(2)}, u32[]{:S(2)}) collective-permute-start(bf16[16,2,16,128]{3,2,1,0:T(8,128)(2,1)S(1)} %collective-permute-done.4.refs_3_), channel_id=1, source_target_pairs={{0,1},{1,0},{2,3},{3,2},{4,5},{5,4},{6,7},{7,6},{8,9},{9,8},{10,11... | collective-permute-start | bytes 393224 | tf_op jit(solution)/shard_map/ppermute | solution.py:166
  151.8 34.5 %collective-permute-start.29 = (bf16[2,3,16,1024]{3,2,1,0:T(8,128)(2,1)}, bf16[2,3,16,1024]{3,2,1,0:T(8,128)(2,1)}, u32[]{:S(2)}, u32[]{:S(2)}) collective-permute-start(bf16[2,3,16,1024]{3,2,1,0:T(8,128)(2,1)} %bitcast.145), channel_id=1, source_target_pairs={{0,128},{1,129},{2,130},{3,131},{4,132},{5,133},{6,134},{7,135},{8... | collective-permute-start | bytes 589832 | tf_op jit(solution)/shard_map/ppermute | solution.py:229
  181.4 10.8 %collective-permute-start.18 = (bf16[2,3,16,1024]{3,2,1,0:T(8,128)(2,1)}, bf16[2,3,16,1024]{3,2,1,0:T(8,128)(2,1)S(1)}, u32[]{:S(2)}, u32[]{:S(2)}) collective-permute-start(bf16[2,3,16,1024]{3,2,1,0:T(8,128)(2,1)} %bitcast.148), channel_id=1, source_target_pairs={{0,128},{1,129},{2,130},{3,131},{4,132},{5,133},{6,134},{7,135},{8... | collective-permute-start | bytes 589832 | tf_op jit(solution)/shard_map/ppermute | solution.py:229
  187.4 8.3 %collective-permute-start.30 = (bf16[2,3,16,1024]{3,2,0,1:T(8,128)(2,1)S(1)}, bf16[2,3,16,1024]{3,2,0,1:T(8,128)(2,1)S(1)}, u32[]{:S(2)}, u32[]{:S(2)}) collective-permute-start(bf16[2,3,16,1024]{3,2,0,1:T(8,128)(2,1)S(1)} %select_bitcast_fusion.2), channel_id=1, source_target_pairs={{0,8},{8,0},{1,9},{9,1},{2,10},{10,2},{3,11},{11,3},{4,12},{12,4},... | collective-permute-start | bytes 589832 | tf_op jit(solution)/shard_map/ppermute | solution.py:233
  (17 other events, 263.3 us)
Sparse Core Ops, SparseCore 0:
  98.1 41.4 reduce-scatter.4
  142.1 39.2 reduce-scatter.2

commit v4 on v2

v4 whole, which is shorter than its diff:
```python
import jax
import jax.numpy as jnp
from jax import lax
from jax.experimental import pallas as pl
from jax.experimental.pallas import tpu as pltpu
from jax.sharding import Mesh, PartitionSpec as P

EPSILON = 1e-05
MIB = 1 << 20

SEGMENT = ("yh", "z", "c")
TENSOR = ("x", "yl")
YH, Z, C, X, YL = 2, 8, 2, 4, 2
QUARTERS = YH * C
LANES = 128


def arrange_kernel(slabs, *refs):
    if len(refs) > 1:
        after, out, spare, sem = refs
        copy = pltpu.make_async_copy(after, spare, sem)
        copy.start()
        copy.wait()
    else:
        (out,) = refs
    slab_count, width, _ = slabs.shape
    tokens = width // C
    for c in range(C):
        for z in range(Z):
            for slab in range(slab_count):
                for h in range(YH):
                    lane = (h * Z + z) * LANES
                    row = (slab * YH + h) * tokens
                    out[z * C + c, row : row + tokens, :] = slabs[
                        slab, c * tokens : (c + 1) * tokens, lane : lane + LANES
                    ]


def arrange(teacher_slabs, section, after=()):
    slab_count, tokens, width = teacher_slabs.shape
    rows = slab_count * YH * (tokens // QUARTERS)
    shape = jax.ShapeDtypeStruct((Z * C, rows, LANES), teacher_slabs.dtype)
    return pl.pallas_call(
        arrange_kernel,
        grid=(1,),
        out_shape=shape,
        in_specs=[pl.BlockSpec((slab_count, tokens // YH, width), lambda i: (0, section, 0))]
        + [pl.BlockSpec(memory_space=pl.ANY)] * len(after),
        out_specs=pl.BlockSpec(shape.shape, lambda i: (0, 0, 0)),
        scratch_shapes=[pltpu.VMEM(array.shape, array.dtype) for array in after]
        + [pltpu.SemaphoreType.DMA] * len(after),
        cost_estimate=pl.CostEstimate(flops=0, bytes_accessed=1600000, transcendentals=0),
        name="arrange",
    )(teacher_slabs, *after)


def pick_kernel(layer_map, received, picked):
    def step(layer, carry):
        picked[layer] = received[layer_map[layer]]
        return carry

    lax.fori_loop(0, picked.shape[0], step, 0)


def pick(layer_map, received):
    layers = layer_map.shape[0]
    return pl.pallas_call(
        pick_kernel,
        out_shape=jax.ShapeDtypeStruct((layers, *received.shape[1:]), received.dtype),
        in_specs=[
            pl.BlockSpec(memory_space=pltpu.SMEM),
            pl.BlockSpec(memory_space=pltpu.VMEM),
        ],
        out_specs=pl.BlockSpec(memory_space=pltpu.VMEM),
        cost_estimate=pl.CostEstimate(flops=0, bytes_accessed=1300000, transcendentals=0),
        name="pick_layers",
    )(layer_map, received)


DISTANCES = (4, 3, -3, 2, -2, 1, -1, 0)
FIRST = ((0, 0), (1, 0), (3, 0), (0, 1))
REST = ((2, 0), (1, 1), (2, 1), (3, 1))
GROUPS = 4
WEIGHTS = 6


def load_weight(place, blocks, weights, weight, sem):
    piece = weights[0].shape[1]
    half = piece // 2
    copies = []
    for index in range(sem.shape[0]):
        for source, ref in enumerate(weights):
            part = source if source < 2 else 2 + (source - 2) // 2
            shift = half if source in (3, 5) else 0
            row = pl.multiple_of(index * QUARTERS * piece + place[part] * piece + shift, half)
            target = weight.at[pl.ds(row, ref.shape[1])]
            copies.append(pltpu.make_async_copy(ref.at[blocks[index]], target, sem.at[index, source]))
    for copy in copies:
        copy.start()
    return copies


def load_features(features, held, sem):
    copies = [
        pltpu.make_async_copy(ref, slot, sem.at[index]) for index, (ref, slot) in enumerate(zip(features, held))
    ]
    for copy in copies:
        copy.start()
    return copies


def left_rows(refs, firsts, group):
    _, halves, tokens, lanes = refs[0].shape
    return jnp.concatenate(
        [
            ref[pl.ds(first, group), h].reshape(group * tokens, lanes)
            for ref, first in zip(refs, firsts)
            for h in range(halves)
        ],
        axis=1,
    )


def project_first_kernel(place, blocks, *refs):
    features, refs = refs[: len(FIRST)], refs[len(FIRST) :]
    weights, (out, weight, *held, feature_sem, weight_sem) = refs[:WEIGHTS], refs[WEIGHTS:]
    copies = load_weight(place, blocks, weights, weight, weight_sem) + load_features(features, held, feature_sem)
    for copy in copies:
        copy.wait()
    group = features[0].shape[0] // GROUPS
    for number in range(GROUPS):
        left = left_rows(held, [number * group] * len(held), group)
        out[number] = jnp.dot(left, weight[...], preferred_element_type=jnp.float32)


def project_rest_kernel(place, blocks, slot_layer, partial, *refs):
    count = len(REST) + 2
    features, refs = refs[:count], refs[count:]
    weights, refs = refs[:WEIGHTS], refs[WEIGHTS:]
    outs, refs = refs[: len(DISTANCES) + 1], refs[len(DISTANCES) + 1 :]
    weight, before, product, *held, feature_sem, weight_sem, before_sem = refs
    copies = load_weight(place, blocks, weights, weight, weight_sem) + load_features(features, held, feature_sem)
    befores = [
        pltpu.make_async_copy(partial.at[number], before.at[number], before_sem.at[number]) for number in range(GROUPS)
    ]
    for copy in befores:
        copy.start()
    for copy in copies:
        copy.wait()
    layers, halves, tokens, lanes = features[2].shape
    group = layers // GROUPS
    near_a, near_b, row_1, row_2a, row_2b, row_3 = held
    for number in range(GROUPS):
        first = number * group
        side = number // (GROUPS // 2)
        offset = (number - side * (GROUPS // 2)) * group
        refs = ((near_a, near_b)[side], row_1, (row_2a, row_2b)[side], row_3)
        left = left_rows(refs, (offset, first, offset, first), group)
        value = jnp.dot(left, weight[...], preferred_element_type=jnp.float32)
        befores[number].wait()
        value = (value + before[number]).astype(product.dtype)
        product[pl.ds(first, group)] = value.reshape(group, tokens, value.shape[1])
    slots = outs[-1].shape[1]
    for index, out in enumerate(outs):
        chunk = max(index - 1, 0)
        for c in range(C):
            for slot in range(slots):
                value = product[slot_layer[(chunk * C + c) * slots + slot]]
                if index > 1:
                    out[c, slot] = value
                elif index == c:
                    out[slot] = value


def project_first(place, blocks, features, weights):
    layers, halves, tokens, lanes = features[0].shape
    columns = weights[0].shape[2]
    depth = len(FIRST) * halves * lanes
    shape = (GROUPS, layers * tokens // GROUPS, columns)
    smem, anywhere = pl.BlockSpec(memory_space=pltpu.SMEM), pl.BlockSpec(memory_space=pl.ANY)
    return pl.pallas_call(
        project_first_kernel,
        out_shape=jax.ShapeDtypeStruct(shape, jnp.float32),
        in_specs=[smem] * 2 + [anywhere] * (len(features) + len(weights)),
        out_specs=pl.BlockSpec(memory_space=pltpu.VMEM),
        scratch_shapes=[
            pltpu.VMEM((depth, columns), jnp.bfloat16),
            *[pltpu.VMEM(feature.shape, feature.dtype) for feature in features],
            pltpu.SemaphoreType.DMA((len(features),)),
            pltpu.SemaphoreType.DMA((len(FIRST), WEIGHTS)),
        ],
        compiler_params=pltpu.CompilerParams(vmem_limit_bytes=40 * MIB),
        cost_estimate=pl.CostEstimate(
            flops=2 * layers * tokens * depth * columns, bytes_accessed=8 * MIB, transcendentals=0
        ),
        name="project_first",
    )(place, blocks, *features, *weights)


def project_rest(place, blocks, slot_layer, partial, features, weights):
    layers, halves, tokens, lanes = features[2].shape
    columns = weights[0].shape[2]
    depth = len(REST) * halves * lanes
    slots = slot_layer.shape[0] // (len(DISTANCES) * C)
    smem, vmem = pl.BlockSpec(memory_space=pltpu.SMEM), pl.BlockSpec(memory_space=pltpu.VMEM)
    shapes = [(slots, tokens, columns)] * C + [(C, slots, tokens, columns)] * (len(DISTANCES) - 1)
    return pl.pallas_call(
        project_rest_kernel,
        out_shape=[jax.ShapeDtypeStruct(shape, jnp.bfloat16) for shape in shapes],
        in_specs=[smem] * 3 + [pl.BlockSpec(memory_space=pl.ANY)] * (1 + len(features) + len(weights)),
        out_specs=[vmem] * len(shapes),
        scratch_shapes=[
            pltpu.VMEM((depth, columns), jnp.bfloat16),
            pltpu.VMEM(partial.shape, partial.dtype),
            pltpu.VMEM((layers, tokens, columns), jnp.bfloat16),
            *[pltpu.VMEM(feature.shape, feature.dtype) for feature in features],
            pltpu.SemaphoreType.DMA((len(features),)),
            pltpu.SemaphoreType.DMA((len(REST), WEIGHTS)),
            pltpu.SemaphoreType.DMA((GROUPS,)),
        ],
        compiler_params=pltpu.CompilerParams(vmem_limit_bytes=62 * MIB),
        cost_estimate=pl.CostEstimate(
            flops=2 * layers * tokens * depth * columns, bytes_accessed=11 * MIB, transcendentals=0
        ),
        name="project_rest",
    )(place, blocks, slot_layer, partial, *features, *weights)


def reduce_z(chunks):
    up = [(i, (i + 1) % Z) for i in range(Z)]
    down = [(i, (i - 1) % Z) for i in range(Z)]
    low, high, up3, down3, up2, down2, up1, down1, own = chunks

    def add(left, right):
        return (left.astype(jnp.float32) + right.astype(jnp.float32)).astype(left.dtype)

    rest = [(0, 0)] * low.ndim
    from_below = jnp.pad(lax.ppermute(high, "z", up)[None], [(1, 0), *rest])
    from_above = jnp.pad(lax.ppermute(low, "z", down)[None], [(0, 1), *rest])
    for to_up, to_down in ((up3, down3), (up2, down2), (up1, down1)):
        from_below = lax.ppermute(add(to_up, from_below), "z", up)
        from_above = lax.ppermute(add(to_down, from_above), "z", down)
    return own, from_below, from_above


def combine_kernel(core, own, below, above, kept, given):
    for out, c in ((kept, core[0]), (given, 1 - core[0])):
        total = own[c].astype(jnp.float32) + below[c].astype(jnp.float32) + above[c].astype(jnp.float32)
        out[...] = total.astype(out.dtype)


def combine(c, own, below, above):
    vmem = pl.BlockSpec(memory_space=pltpu.VMEM)
    shape = jax.ShapeDtypeStruct(own.shape[1:], own.dtype)
    return pl.pallas_call(
        combine_kernel,
        out_shape=[shape] * 2,
        in_specs=[pl.BlockSpec(memory_space=pltpu.SMEM)] + [vmem] * 3,
        out_specs=[vmem] * 2,
        cost_estimate=pl.CostEstimate(flops=3 * own.size, bytes_accessed=8 * own.size, transcendentals=0),
        name="combine",
    )(c.reshape(1).astype(jnp.int32), own, below, above)


def finish_kernel(state, hidden, layer_grad, near, across, teacher, teacher_across, out):
    core, count = state[0], state[1]
    slots, quarter, _ = near.shape
    quarters = ((C + core, near), (C + 1 - core, across), (core, teacher), (1 - core, teacher_across))
    for index, ref in quarters:
        rows = pl.ds(pl.multiple_of(index * quarter, quarter), quarter)
        for slot in range(slots):
            value = hidden[slot, rows, :].astype(jnp.float32) - ref[slot].astype(jnp.float32)
            value = jnp.where(slot < count, value, 0.0)
            if slot == 0:
                value = value + layer_grad[rows, :]
            out[slot, rows, :] = value.astype(out.dtype)


def finish(c, own_count, hidden, layer_grad, pieces):
    vmem = pl.BlockSpec(memory_space=pltpu.VMEM)
    return pl.pallas_call(
        finish_kernel,
        out_shape=jax.ShapeDtypeStruct(hidden.shape, hidden.dtype),
        in_specs=[pl.BlockSpec(memory_space=pltpu.SMEM)] + [vmem] * 6,
        out_specs=vmem,
        cost_estimate=pl.CostEstimate(flops=2 * hidden.size, bytes_accessed=8 * hidden.size, transcendentals=0),
        name="finish",
    )(jnp.stack([c, own_count]).astype(jnp.int32), hidden, layer_grad, *pieces)


def gather_tensor(own):
    up = [(i, (i + 1) % X) for i in range(X)]
    down = [(i, (i - 1) % X) for i in range(X)]
    swap = [(0, 1), (1, 0)]
    half = own.shape[0] // 2
    f3 = lax.ppermute(own, "x", up)
    f1 = lax.ppermute(own, "x", down)
    g0 = lax.ppermute(own, "yl", swap)
    f2a = lax.ppermute(f3[:half], "x", up)
    f2b = lax.ppermute(f1[half:], "x", down)
    g3 = lax.ppermute(g0, "x", up)
    g1 = lax.ppermute(g0, "x", down)
    g2a = lax.ppermute(f2a, "yl", swap)
    g2b = lax.ppermute(f2b, "yl", swap)
    return (own, f1, f2a, f2b, f3, g0, g1, g2a, g2b, g3)


def body(
    teacher_slabs,
    proj_weight,
    child_hidden,
    norm_gain,
    key_weight,
    value_weight,
    key_cotangent,
    value_cotangent,
    layer_map,
    layer_counts,
):
    yh, z, c = lax.axis_index("yh"), lax.axis_index("z"), lax.axis_index("c")
    x, yl = lax.axis_index("x"), lax.axis_index("yl")
    slab_count, tokens, slab_width = teacher_slabs.shape
    layers = layer_map.shape[0]
    columns = proj_weight.shape[2]
    full_width = columns * X * YL
    slot_count = child_hidden.shape[0]
    quarter = tokens // QUARTERS

    swap = [(0, 1), (1, 0)]
    ring = YH * YL
    up = [(i, (i + 1) % ring) for i in range(ring)]
    down = [(i, (i - 1) % ring) for i in range(ring)]
    side = ("yh", "yl")
    half_rows = proj_weight.shape[1] // 2
    w_far_a = lax.ppermute(lax.ppermute(proj_weight[:, :half_rows], side, up), side, up)
    w_far_b = lax.ppermute(lax.ppermute(proj_weight[:, half_rows:], side, down), side, down)
    w_sib = lax.ppermute(proj_weight, "c", swap)
    w_fs_a = lax.ppermute(w_far_a, "c", swap)
    w_fs_b = lax.ppermute(w_far_b, "c", swap)
    weights = (proj_weight, w_sib, w_far_a, w_far_b, w_fs_a, w_fs_b)
    place = jnp.stack([2 * yh + c, 2 * yh + 1 - c, 2 * (1 - yh) + c, 2 * (1 - yh) + 1 - c]).astype(jnp.int32)

    is_child = yh == 1
    first_hidden = child_hidden[0].astype(jnp.float32)
    norm_scale = norm_gain[0]
    contract_last = (((1,), (1,)), ((), ()))
    delta_norm = lax.dot_general(
        key_cotangent[0], key_weight[0], contract_last, preferred_element_type=jnp.float32
    )
    delta_norm = delta_norm + lax.dot_general(
        value_cotangent[0], value_weight[0], contract_last, preferred_element_type=jnp.float32
    )
    sums = lax.psum(
        jnp.stack(
            [
                jnp.sum(first_hidden * first_hidden, axis=1),
                jnp.sum(first_hidden * norm_scale * delta_norm, axis=1),
            ]
        ),
        TENSOR,
    )
    squares, inner_sum = sums[0], sums[1]
    inverse_rms = lax.rsqrt(squares / full_width + EPSILON)[:, None]
    normed = (first_hidden * inverse_rms * norm_scale).astype(jnp.bfloat16)
    contract_rows = (((0,), (0,)), ((), ()))
    key_grad = lax.dot_general(
        normed, key_cotangent[0], contract_rows, preferred_element_type=jnp.float32
    ).astype(jnp.bfloat16)
    value_grad = lax.dot_general(
        normed, value_cotangent[0], contract_rows, preferred_element_type=jnp.float32
    ).astype(jnp.bfloat16)
    gain_grad = jnp.sum(first_hidden * inverse_rms * delta_norm, axis=0)
    layer_grad = (
        inverse_rms * norm_scale * delta_norm
        - first_hidden * inverse_rms**3 * inner_sum[:, None] / full_width
    )
    layer_grad = jnp.where(is_child, layer_grad, 0.0)
    sent = lax.ppermute(arrange(teacher_slabs, 1), side, [(0, 3), (1, 2)])
    arranged = jnp.where(yh == 0, arrange(teacher_slabs, 0, (sums,)), sent)
    received = lax.all_to_all(arranged, ("z", "c"), split_axis=0, concat_axis=0, tiled=True)
    received = received.reshape(Z * C * slab_count, YH, quarter, LANES)

    f0, f1, f2a, f2b, f3, g0, g1, g2a, g2b, g3 = gather_tensor(pick(layer_map, received))
    first_blocks, rest_blocks = (
        jnp.stack([(x + step) % X * YL + (yl + yh + other) % YL for step, other in places]).astype(jnp.int32)
        for places in (FIRST, REST)
    )
    prefix_end = jnp.cumsum(layer_counts)
    prefix_start = prefix_end - layer_counts
    slot_layer = jnp.clip(prefix_start[:, None] + jnp.arange(slot_count)[None, :], 0, layers - 1)
    slot_layer = slot_layer.reshape(Z, C * slot_count)[(z + jnp.array(DISTANCES)) % Z].reshape(-1).astype(jnp.int32)
    partial = project_first(place, first_blocks, (f0, f1, f3, g0), weights)
    chunks = project_rest(place, rest_blocks, slot_layer, partial, (f2a, f2b, g1, g2a, g2b, g3), weights)
    kept, given = combine(c, *reduce_z(chunks))
    across = lax.ppermute(given, "c", swap)
    teacher = lax.ppermute(kept, "yh", [(0, 1)])
    teacher_across = lax.ppermute(given, ("yh", "c"), [(0, 3), (1, 2)])
    own_count = jnp.where(is_child, layer_counts[2 * z + c], 0)
    hidden_grad = finish(c, own_count, child_hidden, layer_grad, (kept, across, teacher, teacher_across))
    key_grad = jnp.where(is_child, key_grad, jnp.zeros_like(key_grad))
    value_grad = jnp.where(is_child, value_grad, jnp.zeros_like(value_grad))
    gain_grad = jnp.where(is_child, gain_grad, 0.0)
    return (hidden_grad, key_grad[None], value_grad[None], gain_grad[None])


def solution(mesh):
    fine = Mesh(mesh.devices.reshape(YH, Z, C, X, YL), (*SEGMENT, *TENSOR))
    placed = (
        P(SEGMENT, None, TENSOR),
        P(None, SEGMENT, TENSOR),
        P(SEGMENT, None, TENSOR),
        P(SEGMENT, TENSOR),
        P(SEGMENT, TENSOR, None),
        P(SEGMENT, TENSOR, None),
        P(SEGMENT, None, None),
        P(SEGMENT, None, None),
        P(),
        P(),
    )
    return jax.shard_map(
        body,
        mesh=fine,
        in_specs=placed,
        out_specs=(
            P(SEGMENT, None, TENSOR),
            P(SEGMENT, TENSOR, None),
            P(SEGMENT, TENSOR, None),
            P(SEGMENT, TENSOR),
        ),
        check_vma=False,
    )
```

time: 193 us -> 180 us (0.933)
  waiting for transfers between devices: 83 us -> 48.7 us
  Pallas kernels: 10.3 us -> 27.8 us
  between operations: 14.9 us -> 1.75 us
  starting transfers between devices: 41 us -> 52.7 us
  other arithmetic: 5.15 us -> 9.93 us
  local copies, waits for them, and re-layouts: 13.9 us -> 11.7 us
    reduce_scatter x1 -> x0, waiting for transfers between devices: 18 us -> none  [body(): lax.psum_scatter(partial.reshape(Z, per_z * quarter, columns), 'z', scatt...]
    pallas_call x1 -> x6, Pallas kernels: 8.15 us -> 25.6 us  [the longest x1 9.52 us: project_rest(): pl.pallas_call(project_rest_kernel, out_shape=[jax.ShapeDtypeStruct(shape...]
    ppermute x1, waiting for transfers between devices: 8.16 us -> 0.01 us  [gather_tensor(): g0 = lax.ppermute(own, 'yl', swap)]
    ppermute x7 -> x16, starting transfers between devices: 22.2 us -> 29.2 us  [the longest x3 9.6 us: reduce_z(): from_above = lax.ppermute(add(to_down, from_above), 'z', down)]
    ppermute x1, waiting for transfers between devices: 5.8 us -> 0.01 us  [gather_tensor(): g2a = lax.ppermute(f2a, 'yl', swap)]
    ppermute x1, waiting for transfers between devices: 5.62 us -> 0.01 us  [gather_tensor(): g2b = lax.ppermute(f2b, 'yl', swap)]
    convert_element_type x2 -> x6, other arithmetic: 1.1 us -> 4.48 us  [add(): (left.astype(jnp.float32) + right.astype(jnp.float32)).astype(left.dtype)]
    all_to_all x1, starting transfers between devices: 10 us -> 13.2 us  [body(): lax.all_to_all(arranged, ('z', 'c'), split_axis=0, concat_axis=0, tiled=T...]
  transfers between devices with their start and end apart: 21 -> 29, of which waited for: 12 -> 13; matrix products, arithmetic and copies ran while one was open for 8% -> 13% of each run, Pallas kernels for 1% -> 6%
where the time goes in v4:
time: 180 us; the launch traced here: 178 us
  starting transfers between devices  52.7 us (29%)
  waiting for transfers between devices  48.7 us (27%)
  Pallas kernels  27.8 us (15%)
  blocking collectives  15.1 us (8%)
  local copies, waits for them, and re-layouts  11.7 us (6%)
  matrix products  10.4 us (6%)
  other arithmetic  9.93 us (6%)
    psum x1, blocking collectives, body(): lax.psum(jnp.stack([jnp.sum(first_hidden * first_hidden, axis=1), jnp.sum...  15.1 us
    all_to_all x1, starting transfers between devices, body(): lax.all_to_all(arranged, ('z', 'c'), split_axis=0, concat_axis=0, tiled=T...  13.2 us
    ppermute x1, waiting for transfers between devices, body(): lax.ppermute(proj_weight[:, half_rows:], side, down)  11.3 us
    ppermute x3, starting transfers between devices, reduce_z(): from_above = lax.ppermute(add(to_down, from_above), 'z', down)  9.6 us
    pallas_call x1, Pallas kernels, project_rest(): pl.pallas_call(project_rest_kernel, out_shape=[jax.ShapeDtypeStruct(shape...  9.52 us
    all_to_all x1, waiting for transfers between devices, body(): lax.all_to_all(arranged, ('z', 'c'), split_axis=0, concat_axis=0, tiled=T...  7.61 us
    ppermute x1, waiting for transfers between devices, gather_tensor(): f3 = lax.ppermute(own, 'x', up)  7.04 us
    ppermute x1, starting transfers between devices, body(): across = lax.ppermute(given, 'c', swap)  6.74 us
  transfers between devices with their start and end apart: 29, of which 13 were waited for; matrix products, arithmetic and copies ran while one was open for 13% of the time, Pallas kernels for 6%

profile of v4, /device:TPU:1, one launch (start us, length us, event | category | flops | bytes accessed | tf_op | source)
XLA Modules:
  0.0 178.1 jit_solution(2492369922553718104)
XLA Ops:
  0.7 2.2 %arrange.3 = bf16[16,192,128]{2,1,0:T(8,128)(2,1)} custom-call(bf16[3,128,2048]{2,1,0:T(8,128)(2,1)} %slabs.3), custom_call_target="tpu_custom_call" | custom-call | bytes 1600000 | tf_op jit(solution)/shard_map/arrange/pallas_call | solution.py:43
  2.9 5.5 %collective-permute-start = (bf16[16,192,128]{2,1,0:T(8,128)(2,1)}, bf16[16,192,128]{2,1,0:T(8,128)(2,1)S(1)}, u32[]{:S(2)}, u32[]{:S(2)}) collective-permute-start(bf16[16,192,128]{2,1,0:T(8,128)(2,1)} %arrange.3), channel_id=1, source_target_pairs={{0,129},{1,128},{2,131},{3,130},{4,133},{5,132},{6,135},{7,134},{8... | collective-permute-start | bytes 2359304 | tf_op jit(solution)/shard_map/ppermute | solution.py:378
  8.4 2.6 %fusion = f32[128,1024]{1,0:T(8,128)S(1)} fusion(bf16[1,1024,1024]{2,1,0:T(8,128)(2,1)} %param.16, bf16[1,128,1024]{2,1,0:T(8,128)(2,1)S(1)} %copy-done.19), kind=kOutput, calls=%fused_computation.1 | convolution fusion | flops 268435456 | bytes 2883584 | tf_op jit(solution)/shard_map/dot_general | solution.py:350
  11.0 2.6 %fusion.11 = (f32[128]{0:T(128)S(1)}, f32[128]{0:T(128)S(1)}, f32[128,1024]{1,0:T(8,128)}) fusion(bf16[3,128,1024]{2,1,0:T(8,128)(2,1)} %hidden.1, f32[1024]{0:T(1024)S(1)} %bitcast.90, f32[128,1024]{1,0:T(8,128)S(1)} %fusion, bf16[1,1024,1024]{2,1,0:T(8,128)(2,1)S(1)} %copy-done.9, bf16[1,128,1024]{2,1,0:T(8,128)(2,1)S(1)} %copy-done), kind=kOutput, calls=%fused_computation.21 | convolution fusion | flops 269352704 | bytes 3675136 | tf_op jit(solution)/shard_map/dot_general | solution.py:347
  13.7 15.1 %psum.7.refs_0_ = f32[2,128]{1,0:T(2,128)} all-reduce(f32[2,128]{1,0:T(2,128)S(1)} %pad_maximum_fusion), channel_id=1, replica_groups=mesh['yh'=2,'z'=8,'c'=2,'x'=4,'yl'=2] {'x','yl'}, use_global_device_ids=true, to_apply=%region_2.0 | all-reduce | flops 256 | bytes 2048 | tf_op jit(solution)/shard_map/psum | solution.py:353
  28.7 2.8 %arrange.2 = bf16[16,192,128]{2,1,0:T(8,128)(2,1)} custom-call(bf16[3,128,2048]{2,1,0:T(8,128)(2,1)} %slabs.3, f32[2,128]{1,0:T(2,128)} %psum.7.refs_0_), custom_call_target="tpu_custom_call" | custom-call | bytes 1600000 | tf_op jit(solution)/shard_map/arrange/pallas_call | solution.py:43
  31.6 2.2 %broadcast_select_fusion = bf16[16,192,128]{2,1,0:T(8,128)(2,1)} fusion(bf16[16,192,128]{2,1,0:T(8,128)(2,1)} %arrange.2, bf16[16,192,128]{2,1,0:T(8,128)(2,1)S(1)} %collective-permute-done, pred[]{:T(512)S(6)} %eq.26), kind=kLoop, calls=%fused_computation.14 | loop fusion | flops 393216 | bytes 2359297 | tf_op jit(solution)/shard_map/jit(_where)/select_n | solution.py:379
  33.8 13.2 %all-to-all-start = ((bf16[16,192,128]{2,1,0:T(8,128)(2,1)}), bf16[16,192,128]{2,1,0:T(8,128)(2,1)}, u32[]{:S(2)}, u32[]{:S(2)}) async-start(bf16[16,192,128]{2,1,0:T(8,128)(2,1)} %broadcast_select_fusion), calls=%async_computation | async-start | bytes 1572864 | tf_op jit(solution)/shard_map/all_to_all | solution.py:380
  49.4 11.3 %collective-permute-done.7 = bf16[8,32,1024]{2,1,0:T(8,128)(2,1)} collective-permute-done((bf16[8,32,1024]{2,1,0:T(8,128)(2,1)S(1)}, bf16[8,32,1024]{2,1,0:T(8,128)(2,1)}, u32[]{:S(2)}, u32[]{:S(2)}) %collective-permute-start.7) | collective-permute-done | bytes 524320 | tf_op jit(solution)/shard_map/ppermute | solution.py:336
  62.2 7.6 %all-to-all-done = bf16[16,192,128]{2,1,0:T(8,128)(2,1)} async-done(((bf16[16,192,128]{2,1,0:T(8,128)(2,1)}), bf16[16,192,128]{2,1,0:T(8,128)(2,1)}, u32[]{:S(2)}, u32[]{:S(2)}) %all-to-all-start) | async-done | bytes 786464 | tf_op jit(solution)/shard_map/all_to_all | solution.py:380
  69.8 2.1 %pick_layers.1.refs_0_ = bf16[32,2,32,128]{3,2,1,0:T(8,128)(2,1)} custom-call(s32[32]{0:T(128)} %layer_map.1, bf16[48,2,32,128]{3,2,1,0:T(8,128)(2,1)} %bitcast.26.received), custom_call_target="tpu_custom_call" | custom-call | bytes 1300000 | tf_op jit(solution)/shard_map/pick_layers/pallas_call | solution.py:67
  71.9 2.7 %collective-permute-start.1 = (bf16[32,2,32,128]{3,2,1,0:T(8,128)(2,1)}, bf16[32,2,32,128]{3,2,1,0:T(8,128)(2,1)}, u32[]{:S(2)}, u32[]{:S(2)}) collective-permute-start(bf16[32,2,32,128]{3,2,1,0:T(8,128)(2,1)} %pick_layers.1.refs_0_), channel_id=1, source_target_pairs={{0,6},{2,0},{4,2},{6,4},{1,7},{3,1},{5,3},{7,5},{8,14},{10,8},{12,... | collective-permute-start | bytes 1572872 | tf_op jit(solution)/shard_map/ppermute | solution.py:297
  76.1 1.9 %collective-permute-start.10 = (bf16[8,32,1024]{2,1,0:T(8,128)(2,1)S(1)}, bf16[8,32,1024]{2,1,0:T(8,128)(2,1)}, u32[]{:S(2)}, u32[]{:S(2)}) collective-permute-start(bf16[8,32,1024]{2,1,0:T(8,128)(2,1)S(1)} %collective-permute-done.8.refs_7_.refs_9_), channel_id=1, source_target_pairs={{0,8},{8,0},{1,9},{9,1},{2,10},{10,2},{3,11},{11,3},{4,12},{12,4},... | collective-permute-start | bytes 1572872 | tf_op jit(solution)/shard_map/ppermute | solution.py:339
  78.6 7.0 %collective-permute-done.2.refs_2_ = bf16[32,2,32,128]{3,2,1,0:T(8,128)(2,1)} collective-permute-done((bf16[32,2,32,128]{3,2,1,0:T(8,128)(2,1)}, bf16[32,2,32,128]{3,2,1,0:T(8,128)(2,1)}, u32[]{:S(2)}, u32[]{:S(2)}) %collective-permute-start.2) | collective-permute-done | bytes 524320 | tf_op jit(solution)/shard_map/ppermute | solution.py:296
  85.7 1.7 slice.30
  87.4 1.7 slice.31
  89.1 2.7 %collective-permute-start.12 = (bf16[16,2,32,128]{3,2,1,0:T(8,128)(2,1)}, bf16[16,2,32,128]{3,2,1,0:T(8,128)(2,1)}, u32[]{:S(2)}, u32[]{:S(2)}) collective-permute-start(bf16[16,2,32,128]{3,2,1,0:T(8,128)(2,1)} %slice.31), channel_id=1, source_target_pairs={{0,6},{2,0},{4,2},{6,4},{1,7},{3,1},{5,3},{7,5},{8,14},{10,8},{12,... | collective-permute-start | bytes 786440 | tf_op jit(solution)/shard_map/ppermute | solution.py:300
  99.4 6.3 %project_first.1.partial = f32[4,256,1024]{2,1,0:T(8,128)S(1)} custom-call(s32[4]{0:T(128)S(1)} %get-tuple-element.35.place, s32[4]{0:T(128)S(1)} %get-tuple-element.36.blocks, bf16[32,2,32,128]{3,2,1,0:T(8,128)(2,1)S(1)} %copy-done.5, bf16[32,2,32,128]{3,2,1,0:T(8,128)(2,1)} %collective-permute-done.1.refs_1_, ...), custom_call_target="tpu_custom_call" | custom-call | flops 2147483648 | bytes 8388608 | tf_op jit(solution)/shard_map/project_first/pallas_call | solution.py:181
  105.7 1.9 %copy-done.1 = f32[4,256,1024]{2,1,0:T(8,128)} copy-done((f32[4,256,1024]{2,1,0:T(8,128)}, f32[4,256,1024]{2,1,0:T(8,128)S(1)}, u32[]{:S(2)}) %copy-start.1) | copy-done | bytes 4194328
  109.1 9.5 %project_rest.1 = (bf16[3,32,1024]{2,1,0:T(8,128)(2,1)}, bf16[3,32,1024]{2,1,0:T(8,128)(2,1)}, bf16[2,3,32,1024]{3,2,1,0:T(8,128)(2,1)}, bf16[2,3,32,1024]{3,2,1...) custom-call(s32[4]{0:T(128)} %copy-done.6, ...), custom_call_target="tpu_custom_call" | custom-call | flops 2147483648 | bytes 11534336 | tf_op jit(solution)/shard_map/project_rest/pallas_call | solution.py:207
  120.3 3.2 %collective-permute-done.21 = bf16[3,32,1024]{2,1,0:T(8,128)(2,1)S(1)} collective-permute-done((bf16[3,32,1024]{2,1,0:T(8,128)(2,1)}, bf16[3,32,1024]{2,1,0:T(8,128)(2,1)S(1)}, u32[]{:S(2)}, u32[]{:S(2)}) %collective-permute-start.21) | collective-permute-done | bytes 196640 | tf_op jit(solution)/shard_map/ppermute | solution.py:239
  124.6 2.7 %collective-permute-start.22 = (bf16[2,3,32,1024]{3,2,1,0:T(8,128)(2,1)S(1)}, bf16[2,3,32,1024]{3,2,1,0:T(8,128)(2,1)S(1)}, u32[]{:S(2)}, u32[]{:S(2)}) collective-permute-start(bf16[2,3,32,1024]{3,2,1,0:T(8,128)(2,1)S(1)} %add_convert_fusion.2), channel_id=1, source_target_pairs={{0,112},{16,0},{32,16},{48,32},{64,48},{80,64},{96,80},{112,96},{1... | collective-permute-start | bytes 1179656 | tf_op jit(solution)/shard_map/ppermute | solution.py:242
  128.5 4.0 %collective-permute-done.22 = bf16[2,3,32,1024]{3,2,1,0:T(8,128)(2,1)S(1)} collective-permute-done((bf16[2,3,32,1024]{3,2,1,0:T(8,128)(2,1)S(1)}, bf16[2,3,32,1024]{3,2,1,0:T(8,128)(2,1)S(1)}, u32[]{:S(2)}, u32[]{:S(2)}) %collective-permute-start.22) | collective-permute-done | bytes 393248 | tf_op jit(solution)/shard_map/ppermute | solution.py:242
  132.7 3.5 %collective-permute-start.23 = (bf16[2,3,32,1024]{3,2,1,0:T(8,128)(2,1)S(1)}, bf16[2,3,32,1024]{3,2,1,0:T(8,128)(2,1)S(1)}, u32[]{:S(2)}, u32[]{:S(2)}) collective-permute-start(bf16[2,3,32,1024]{3,2,1,0:T(8,128)(2,1)S(1)} %add_convert_fusion.1), channel_id=1, source_target_pairs={{0,112},{16,0},{32,16},{48,32},{64,48},{80,64},{96,80},{112,96},{1... | collective-permute-start | bytes 1179656 | tf_op jit(solution)/shard_map/ppermute | solution.py:242
  141.0 3.4 %collective-permute-start.24 = (bf16[2,3,32,1024]{3,2,1,0:T(8,128)(2,1)S(1)}, bf16[2,3,32,1024]{3,2,1,0:T(8,128)(2,1)S(1)}, u32[]{:S(2)}, u32[]{:S(2)}) collective-permute-start(bf16[2,3,32,1024]{3,2,1,0:T(8,128)(2,1)S(1)} %add_convert_fusion), channel_id=1, source_target_pairs={{0,112},{16,0},{32,16},{48,32},{64,48},{80,64},{96,80},{112,96},{1... | collective-permute-start | bytes 1179656 | tf_op jit(solution)/shard_map/ppermute | solution.py:242
  147.1 3.1 %select_bitcast_fusion = bf16[1,1024,1024]{2,1,0:T(8,128)(2,1)} fusion(pred[]{:T(512)S(6)} %eq.25, bf16[1,128,1024]{2,1,0:T(8,128)(2,1)} %param.18, f32[1024]{0:T(1024)S(1)} %bitcast.92, f32[128]{0:T(128)S(1)} %get-tuple-element.29, bf16[3,128,1024]{2,1,0:T(8,128)(2,1)S(1)} %copy-done.7), kind=kOutput, calls=%fused_computation.5 | convolution fusion | flops 271056896 | bytes 2626049 | tf_op jit(solution)/shard_map/dot_general | solution.py:369
  150.7 4.1 %collective-permute-done.20.below = bf16[2,3,32,1024]{3,2,1,0:T(8,128)(2,1)S(1)} collective-permute-done((bf16[2,3,32,1024]{3,2,1,0:T(8,128)(2,1)S(1)}, bf16[2,3,32,1024]{3,2,1,0:T(8,128)(2,1)S(1)}, u32[]{:S(2)}, u32[]{:S(2)}) %collective-permute-start.20) | collective-permute-done | bytes 393248 | tf_op jit(solution)/shard_map/ppermute | solution.py:241
  155.6 2.1 %combine.1 = (bf16[3,32,1024]{2,1,0:T(8,128)(2,1)}, bf16[3,32,1024]{2,1,0:T(8,128)(2,1)}) custom-call(s32[1]{0:T(128)} %bitcast.core, bf16[2,3,32,1024]{3,2,1,0:T(8,128)(2,1)} %get-tuple-element.15.own, bf16[2,3,32,1024]{3,2,1,0:T(8,128)(2,1)} %copy-done.15, bf16[2,3,32,1024]{3,2,1,0:T(8,128)(2,1)} %copy-done.14), custom_call_target="tpu_custom_call" | custom-call | flops 589824 | bytes 1572864 | tf_op jit(solution)/shard_map/combine/pallas_call | solution.py:255
  157.7 6.7 %collective-permute-start.25 = (bf16[3,32,1024]{2,1,0:T(8,128)(2,1)}, bf16[3,32,1024]{2,1,0:T(8,128)(2,1)S(1)}, u32[]{:S(2)}, u32[]{:S(2)}) collective-permute-start(bf16[3,32,1024]{2,1,0:T(8,128)(2,1)} %get-tuple-element.25), channel_id=1, source_target_pairs={{0,8},{8,0},{1,9},{9,1},{2,10},{10,2},{3,11},{11,3},{4,12},{12,4},... | collective-permute-start | bytes 589832 | tf_op jit(solution)/shard_map/ppermute | solution.py:395
  167.1 2.1 %select_bitcast_fusion.1 = bf16[1,1024,1024]{2,1,0:T(8,128)(2,1)} fusion(pred[]{:T(512)S(6)} %eq.25, bf16[1,128,1024]{2,1,0:T(8,128)(2,1)S(1)} %copy-done, f32[1024]{0:T(1024)S(1)} %bitcast.93, f32[128]{0:T(128)S(1)} %get-tuple-element.29, bf16[3,128,1024]{2,1,0:T(8,128)(2,1)S(1)} %copy-done.7), kind=kOutput, calls=%fused_computation.6 | convolution fusion | flops 271056896 | bytes 2626049 | tf_op jit(solution)/shard_map/dot_general | solution.py:366
  169.2 5.4 %collective-permute-done.26.teacher = bf16[3,32,1024]{2,1,0:T(8,128)(2,1)S(1)} collective-permute-done((bf16[3,32,1024]{2,1,0:T(8,128)(2,1)}, bf16[3,32,1024]{2,1,0:T(8,128)(2,1)S(1)}, u32[]{:S(2)}, u32[]{:S(2)}) %collective-permute-start.26) | collective-permute-done | bytes 196640 | tf_op jit(solution)/shard_map/ppermute | solution.py:396
  175.4 2.6 %finish.1 = bf16[3,128,1024]{2,1,0:T(8,128)(2,1)} custom-call(s32[2]{0:T(128)} %pad_add_fusion.state, bf16[3,128,1024]{2,1,0:T(8,128)(2,1)} %hidden.1, f32[128,1024]{1,0:T(8,128)} %get-tuple-element.31.layer_grad, bf16[3,32,1024]{2,1,0:T(8,128)(2,1)} %get-tuple-element.24.near, bf16[3,32,1024]{2,1,0:T(8,128)(2,1)} %copy-done.20, ...), custom_call_target="tpu_custom_call" | custom-call | flops 786432 | bytes 3145728 | tf_op jit(solution)/shard_map/finish/pallas_call | solution.py:281
  (127 shorter events, 30.5 us)
Async XLA Ops:
  2.9 28.7 %collective-permute-start = (bf16[16,192,128]{2,1,0:T(8,128)(2,1)}, bf16[16,192,128]{2,1,0:T(8,128)(2,1)S(1)}, u32[]{:S(2)}, u32[]{:S(2)}) collective-permute-start(bf16[16,192,128]{2,1,0:T(8,128)(2,1)} %arrange.3), channel_id=1, source_target_pairs={{0,129},{1,128},{2,131},{3,130},{4,133},{5,132},{6,135},{7,134},{8... | collective-permute-start | bytes 2359304 | tf_op jit(solution)/shard_map/ppermute | solution.py:378
  33.8 36.0 %all-to-all-start = ((bf16[16,192,128]{2,1,0:T(8,128)(2,1)}), bf16[16,192,128]{2,1,0:T(8,128)(2,1)}, u32[]{:S(2)}, u32[]{:S(2)}) async-start(bf16[16,192,128]{2,1,0:T(8,128)(2,1)} %broadcast_select_fusion), calls=%async_computation | async-start | bytes 1572864 | tf_op jit(solution)/shard_map/all_to_all | solution.py:380
  47.0 31.0 %copy-start.25 = (s32[16]{0:T(128)S(1)}, s32[16]{0:T(128)}, u32[]{:S(2)}) copy-start(s32[16]{0:T(128)} %param.20) | copy-start | bytes 196
  47.0 44.7 %copy-start.26 = (s32[8]{0:T(128)S(1)}, s32[8]{0:T(128)}, u32[]{:S(2)}) copy-start(s32[8]{0:T(128)} %constant.118.clone) | copy-start | bytes 100
  47.1 13.6 %collective-permute-start.7 = (bf16[8,32,1024]{2,1,0:T(8,128)(2,1)S(1)}, bf16[8,32,1024]{2,1,0:T(8,128)(2,1)}, u32[]{:S(2)}, u32[]{:S(2)}) collective-permute-start(bf16[8,32,1024]{2,1,0:T(8,128)(2,1)S(1)} %get-tuple-element.32), channel_id=1, source_target_pairs={{0,129},{1,0},{128,1},{129,128},{2,131},{3,2},{130,3},{131,130},{4... | collective-permute-start | bytes 1572872 | tf_op jit(solution)/shard_map/ppermute | solution.py:336
  47.2 14.9 %collective-permute-start.5 = (bf16[8,32,1024]{2,1,0:T(8,128)(2,1)S(1)}, bf16[8,32,1024]{2,1,0:T(8,128)(2,1)}, u32[]{:S(2)}, u32[]{:S(2)}) collective-permute-start(bf16[8,32,1024]{2,1,0:T(8,128)(2,1)S(1)} %get-tuple-element.33), channel_id=1, source_target_pairs={{0,1},{1,128},{128,129},{129,0},{2,3},{3,130},{130,131},{131,2},{4... | collective-permute-start | bytes 1572872 | tf_op jit(solution)/shard_map/ppermute | solution.py:335
  48.7 40.4 %collective-permute-start.4 = (bf16[8,64,1024]{2,1,0:T(8,128)(2,1)S(1)}, bf16[8,64,1024]{2,1,0:T(8,128)(2,1)S(1)}, u32[]{:S(2)}, u32[]{:S(2)}) collective-permute-start(bf16[8,64,1024]{2,1,0:T(8,128)(2,1)S(1)} %copy-done.2), channel_id=1, source_target_pairs={{0,8},{8,0},{1,9},{9,1},{2,10},{10,2},{3,11},{11,3},{4,12},{12,4},... | collective-permute-start | bytes 3145736 | tf_op jit(solution)/shard_map/ppermute | solution.py:337
  60.7 13.9 %collective-permute-start.8 = (bf16[8,32,1024]{2,1,0:T(8,128)(2,1)}, bf16[8,32,1024]{2,1,0:T(8,128)(2,1)S(1)}, u32[]{:S(2)}, u32[]{:S(2)}) collective-permute-start(bf16[8,32,1024]{2,1,0:T(8,128)(2,1)} %collective-permute-done.7), channel_id=1, source_target_pairs={{0,129},{1,0},{128,1},{129,128},{2,131},{3,2},{130,3},{131,130},{4... | collective-permute-start | bytes 1572872 | tf_op jit(solution)/shard_map/ppermute | solution.py:336
  62.1 13.9 %collective-permute-start.6 = (bf16[8,32,1024]{2,1,0:T(8,128)(2,1)}, bf16[8,32,1024]{2,1,0:T(8,128)(2,1)}, u32[]{:S(2)}, u32[]{:S(2)}) collective-permute-start(bf16[8,32,1024]{2,1,0:T(8,128)(2,1)} %collective-permute-done.5), channel_id=1, source_target_pairs={{0,1},{1,128},{128,129},{129,0},{2,3},{3,130},{130,131},{131,2},{4... | collective-permute-start | bytes 1572872 | tf_op jit(solution)/shard_map/ppermute | solution.py:335
  71.9 13.8 %collective-permute-start.2 = (bf16[32,2,32,128]{3,2,1,0:T(8,128)(2,1)}, bf16[32,2,32,128]{3,2,1,0:T(8,128)(2,1)}, u32[]{:S(2)}, u32[]{:S(2)}) collective-permute-start(bf16[32,2,32,128]{3,2,1,0:T(8,128)(2,1)} %pick_layers.1.refs_0_), channel_id=1, source_target_pairs={{0,2},{2,4},{4,6},{6,0},{1,3},{3,5},{5,7},{7,1},{8,10},{10,12},{12... | collective-permute-start | bytes 1572872 | tf_op jit(solution)/shard_map/ppermute | solution.py:296
  71.9 15.5 %collective-permute-start.1 = (bf16[32,2,32,128]{3,2,1,0:T(8,128)(2,1)}, bf16[32,2,32,128]{3,2,1,0:T(8,128)(2,1)}, u32[]{:S(2)}, u32[]{:S(2)}) collective-permute-start(bf16[32,2,32,128]{3,2,1,0:T(8,128)(2,1)} %pick_layers.1.refs_0_), channel_id=1, source_target_pairs={{0,6},{2,0},{4,2},{6,4},{1,7},{3,1},{5,3},{7,5},{8,14},{10,8},{12,... | collective-permute-start | bytes 1572872 | tf_op jit(solution)/shard_map/ppermute | solution.py:297
  74.6 31.1 %copy-start.4 = (bf16[8,32,1024]{2,1,0:T(8,128)(2,1)}, bf16[8,32,1024]{2,1,0:T(8,128)(2,1)S(1)}, u32[]{:S(2)}) copy-start(bf16[8,32,1024]{2,1,0:T(8,128)(2,1)S(1)} %collective-permute-done.8.refs_7_.refs_9_) | copy-start | bytes 1572868
  74.6 17.2 %collective-permute-start.3 = (bf16[32,2,32,128]{3,2,1,0:T(8,128)(2,1)}, bf16[32,2,32,128]{3,2,1,0:T(8,128)(2,1)}, u32[]{:S(2)}, u32[]{:S(2)}) collective-permute-start(bf16[32,2,32,128]{3,2,1,0:T(8,128)(2,1)} %pick_layers.1.refs_0_), channel_id=1, source_target_pairs={{0,1},{1,0},{2,3},{3,2},{4,5},{5,4},{6,7},{7,6},{8,9},{9,8},{10,11... | collective-permute-start | bytes 1572872 | tf_op jit(solution)/shard_map/ppermute | solution.py:298
  76.1 15.9 %collective-permute-start.10 = (bf16[8,32,1024]{2,1,0:T(8,128)(2,1)S(1)}, bf16[8,32,1024]{2,1,0:T(8,128)(2,1)}, u32[]{:S(2)}, u32[]{:S(2)}) collective-permute-start(bf16[8,32,1024]{2,1,0:T(8,128)(2,1)S(1)} %collective-permute-done.8.refs_7_.refs_9_), channel_id=1, source_target_pairs={{0,8},{8,0},{1,9},{9,1},{2,10},{10,2},{3,11},{11,3},{4,12},{12,4},... | collective-permute-start | bytes 1572872 | tf_op jit(solution)/shard_map/ppermute | solution.py:339
  85.7 12.6 %collective-permute-start.9 = (bf16[8,32,1024]{2,1,0:T(8,128)(2,1)}, bf16[8,32,1024]{2,1,0:T(8,128)(2,1)}, u32[]{:S(2)}, u32[]{:S(2)}) collective-permute-start(bf16[8,32,1024]{2,1,0:T(8,128)(2,1)} %collective-permute-done.6.refs_6_.refs_8_), channel_id=1, source_target_pairs={{0,8},{8,0},{1,9},{9,1},{2,10},{10,2},{3,11},{11,3},{4,12},{12,4},... | collective-permute-start | bytes 1572872 | tf_op jit(solution)/shard_map/ppermute | solution.py:338
  87.4 8.8 %collective-permute-start.11 = (bf16[16,2,32,128]{3,2,1,0:T(8,128)(2,1)}, bf16[16,2,32,128]{3,2,1,0:T(8,128)(2,1)S(1)}, u32[]{:S(2)}, u32[]{:S(2)}) collective-permute-start(bf16[16,2,32,128]{3,2,1,0:T(8,128)(2,1)} %slice.30), channel_id=1, source_target_pairs={{0,2},{2,4},{4,6},{6,0},{1,3},{3,5},{5,7},{7,1},{8,10},{10,12},{12... | collective-permute-start | bytes 786440 | tf_op jit(solution)/shard_map/ppermute | solution.py:299
  89.1 7.8 %collective-permute-start.12 = (bf16[16,2,32,128]{3,2,1,0:T(8,128)(2,1)}, bf16[16,2,32,128]{3,2,1,0:T(8,128)(2,1)}, u32[]{:S(2)}, u32[]{:S(2)}) collective-permute-start(bf16[16,2,32,128]{3,2,1,0:T(8,128)(2,1)} %slice.31), channel_id=1, source_target_pairs={{0,6},{2,0},{4,2},{6,4},{1,7},{3,1},{5,3},{7,5},{8,14},{10,8},{12,... | collective-permute-start | bytes 786440 | tf_op jit(solution)/shard_map/ppermute | solution.py:300
  91.8 17.3 %collective-permute-start.13 = (bf16[32,2,32,128]{3,2,1,0:T(8,128)(2,1)}, bf16[32,2,32,128]{3,2,1,0:T(8,128)(2,1)}, u32[]{:S(2)}, u32[]{:S(2)}) collective-permute-start(bf16[32,2,32,128]{3,2,1,0:T(8,128)(2,1)} %collective-permute-done.3.refs_3_), channel_id=1, source_target_pairs={{0,6},{2,0},{4,2},{6,4},{1,7},{3,1},{5,3},{7,5},{8,14},{10,8},{12,... | collective-permute-start | bytes 1572872 | tf_op jit(solution)/shard_map/ppermute | solution.py:302
  92.0 17.1 %collective-permute-start.16 = (bf16[32,2,32,128]{3,2,1,0:T(8,128)(2,1)}, bf16[32,2,32,128]{3,2,1,0:T(8,128)(2,1)}, u32[]{:S(2)}, u32[]{:S(2)}) collective-permute-start(bf16[32,2,32,128]{3,2,1,0:T(8,128)(2,1)} %collective-permute-done.3.refs_3_), channel_id=1, source_target_pairs={{0,2},{2,4},{4,6},{6,0},{1,3},{3,5},{5,7},{7,1},{8,10},{10,12},{12... | collective-permute-start | bytes 1572872 | tf_op jit(solution)/shard_map/ppermute | solution.py:301
  96.2 11.5 %collective-permute-start.14 = (bf16[16,2,32,128]{3,2,1,0:T(8,128)(2,1)S(1)}, bf16[16,2,32,128]{3,2,1,0:T(8,128)(2,1)S(1)}, u32[]{:S(2)}, u32[]{:S(2)}) collective-permute-start(bf16[16,2,32,128]{3,2,1,0:T(8,128)(2,1)S(1)} %collective-permute-done.11.refs_0_), channel_id=1, source_target_pairs={{0,1},{1,0},{2,3},{3,2},{4,5},{5,4},{6,7},{7,6},{8,9},{9,8},{10,11... | collective-permute-start | bytes 786440 | tf_op jit(solution)/shard_map/ppermute | solution.py:303
  96.9 11.5 %collective-permute-start.15 = (bf16[16,2,32,128]{3,2,1,0:T(8,128)(2,1)}, bf16[16,2,32,128]{3,2,1,0:T(8,128)(2,1)S(1)}, u32[]{:S(2)}, u32[]{:S(2)}) collective-permute-start(bf16[16,2,32,128]{3,2,1,0:T(8,128)(2,1)} %collective-permute-done.12.refs_1_), channel_id=1, source_target_pairs={{0,1},{1,0},{2,3},{3,2},{4,5},{5,4},{6,7},{7,6},{8,9},{9,8},{10,11... | collective-permute-start | bytes 786440 | tf_op jit(solution)/shard_map/ppermute | solution.py:304
  118.7 4.8 %collective-permute-start.21 = (bf16[3,32,1024]{2,1,0:T(8,128)(2,1)}, bf16[3,32,1024]{2,1,0:T(8,128)(2,1)S(1)}, u32[]{:S(2)}, u32[]{:S(2)}) collective-permute-start(bf16[3,32,1024]{2,1,0:T(8,128)(2,1)} %get-tuple-element.23), channel_id=1, source_target_pairs={{0,112},{16,0},{32,16},{48,32},{64,48},{80,64},{96,80},{112,96},{1... | collective-permute-start | bytes 589832 | tf_op jit(solution)/shard_map/ppermute | solution.py:239
  120.2 7.2 %collective-permute-start.17 = (bf16[3,32,1024]{2,1,0:T(8,128)(2,1)}, bf16[3,32,1024]{2,1,0:T(8,128)(2,1)S(1)}, u32[]{:S(2)}, u32[]{:S(2)}) collective-permute-start(bf16[3,32,1024]{2,1,0:T(8,128)(2,1)} %get-tuple-element.19), channel_id=1, source_target_pairs={{0,16},{16,32},{32,48},{48,64},{64,80},{80,96},{96,112},{112,0},{1... | collective-permute-start | bytes 589832 | tf_op jit(solution)/shard_map/ppermute | solution.py:238
  124.6 7.9 %collective-permute-start.22 = (bf16[2,3,32,1024]{3,2,1,0:T(8,128)(2,1)S(1)}, bf16[2,3,32,1024]{3,2,1,0:T(8,128)(2,1)S(1)}, u32[]{:S(2)}, u32[]{:S(2)}) collective-permute-start(bf16[2,3,32,1024]{3,2,1,0:T(8,128)(2,1)S(1)} %add_convert_fusion.2), channel_id=1, source_target_pairs={{0,112},{16,0},{32,16},{48,32},{64,48},{80,64},{96,80},{112,96},{1... | collective-permute-start | bytes 1179656 | tf_op jit(solution)/shard_map/ppermute | solution.py:242
  128.4 8.4 %collective-permute-start.18 = (bf16[2,3,32,1024]{3,2,1,0:T(8,128)(2,1)S(1)}, bf16[2,3,32,1024]{3,2,1,0:T(8,128)(2,1)S(1)}, u32[]{:S(2)}, u32[]{:S(2)}) collective-permute-start(bf16[2,3,32,1024]{3,2,1,0:T(8,128)(2,1)S(1)} %add_convert_fusion.5), channel_id=1, source_target_pairs={{0,16},{16,32},{32,48},{48,64},{64,80},{80,96},{96,112},{112,0},{1... | collective-permute-start | bytes 1179656 | tf_op jit(solution)/shard_map/ppermute | solution.py:241
  132.7 8.2 %collective-permute-start.23 = (bf16[2,3,32,1024]{3,2,1,0:T(8,128)(2,1)S(1)}, bf16[2,3,32,1024]{3,2,1,0:T(8,128)(2,1)S(1)}, u32[]{:S(2)}, u32[]{:S(2)}) collective-permute-start(bf16[2,3,32,1024]{3,2,1,0:T(8,128)(2,1)S(1)} %add_convert_fusion.1), channel_id=1, source_target_pairs={{0,112},{16,0},{32,16},{48,32},{64,48},{80,64},{96,80},{112,96},{1... | collective-permute-start | bytes 1179656 | tf_op jit(solution)/shard_map/ppermute | solution.py:242
  137.7 8.2 %collective-permute-start.19 = (bf16[2,3,32,1024]{3,2,1,0:T(8,128)(2,1)}, bf16[2,3,32,1024]{3,2,1,0:T(8,128)(2,1)}, u32[]{:S(2)}, u32[]{:S(2)}) collective-permute-start(bf16[2,3,32,1024]{3,2,1,0:T(8,128)(2,1)} %add_convert_fusion.4), channel_id=1, source_target_pairs={{0,16},{16,32},{32,48},{48,64},{64,80},{80,96},{96,112},{112,0},{1... | collective-permute-start | bytes 1179656 | tf_op jit(solution)/shard_map/ppermute | solution.py:241
  141.0 9.7 %collective-permute-start.24 = (bf16[2,3,32,1024]{3,2,1,0:T(8,128)(2,1)S(1)}, bf16[2,3,32,1024]{3,2,1,0:T(8,128)(2,1)S(1)}, u32[]{:S(2)}, u32[]{:S(2)}) collective-permute-start(bf16[2,3,32,1024]{3,2,1,0:T(8,128)(2,1)S(1)} %add_convert_fusion), channel_id=1, source_target_pairs={{0,112},{16,0},{32,16},{48,32},{64,48},{80,64},{96,80},{112,96},{1... | collective-permute-start | bytes 1179656 | tf_op jit(solution)/shard_map/ppermute | solution.py:242
  147.0 7.9 %collective-permute-start.20 = (bf16[2,3,32,1024]{3,2,1,0:T(8,128)(2,1)S(1)}, bf16[2,3,32,1024]{3,2,1,0:T(8,128)(2,1)S(1)}, u32[]{:S(2)}, u32[]{:S(2)}) collective-permute-start(bf16[2,3,32,1024]{3,2,1,0:T(8,128)(2,1)S(1)} %add_convert_fusion.3), channel_id=1, source_target_pairs={{0,16},{16,32},{32,48},{48,64},{64,80},{80,96},{96,112},{112,0},{1... | collective-permute-start | bytes 1179656 | tf_op jit(solution)/shard_map/ppermute | solution.py:241
  157.7 11.5 %collective-permute-start.25 = (bf16[3,32,1024]{2,1,0:T(8,128)(2,1)}, bf16[3,32,1024]{2,1,0:T(8,128)(2,1)S(1)}, u32[]{:S(2)}, u32[]{:S(2)}) collective-permute-start(bf16[3,32,1024]{2,1,0:T(8,128)(2,1)} %get-tuple-element.25), channel_id=1, source_target_pairs={{0,8},{8,0},{1,9},{9,1},{2,10},{10,2},{3,11},{11,3},{4,12},{12,4},... | collective-permute-start | bytes 589832 | tf_op jit(solution)/shard_map/ppermute | solution.py:395
  164.5 10.2 %collective-permute-start.27 = (bf16[3,32,1024]{2,1,0:T(8,128)(2,1)}, bf16[3,32,1024]{2,1,0:T(8,128)(2,1)S(1)}, u32[]{:S(2)}, u32[]{:S(2)}) collective-permute-start(bf16[3,32,1024]{2,1,0:T(8,128)(2,1)} %get-tuple-element.25), channel_id=1, source_target_pairs={{0,136},{8,128},{1,137},{9,129},{2,138},{10,130},{3,139},{11,131},... | collective-permute-start | bytes 589832 | tf_op jit(solution)/shard_map/ppermute | solution.py:397
  165.8 8.9 %collective-permute-start.26 = (bf16[3,32,1024]{2,1,0:T(8,128)(2,1)}, bf16[3,32,1024]{2,1,0:T(8,128)(2,1)S(1)}, u32[]{:S(2)}, u32[]{:S(2)}) collective-permute-start(bf16[3,32,1024]{2,1,0:T(8,128)(2,1)} %get-tuple-element.24.near), channel_id=1, source_target_pairs={{0,128},{1,129},{2,130},{3,131},{4,132},{5,133},{6,134},{7,135},{8... | collective-permute-start | bytes 589832 | tf_op jit(solution)/shard_map/ppermute | solution.py:396
  (24 other events, 198.5 us)

commit v5 on v4

--- a/solution.py
+++ b/solution.py
@@ -1,3 +1,5 @@
+import functools
+
 import jax
 import jax.numpy as jnp
 from jax import lax
@@ -15,14 +17,7 @@
 LANES = 128
 
 
-def arrange_kernel(slabs, *refs):
-    if len(refs) > 1:
-        after, out, spare, sem = refs
-        copy = pltpu.make_async_copy(after, spare, sem)
-        copy.start()
-        copy.wait()
-    else:
-        (out,) = refs
+def arrange_kernel(slabs, out):
     slab_count, width, _ = slabs.shape
     tokens = width // C
     for c in range(C):
@@ -36,7 +31,7 @@
                     ]
 
 
-def arrange(teacher_slabs, section, after=()):
+def arrange(teacher_slabs, section):
     slab_count, tokens, width = teacher_slabs.shape
     rows = slab_count * YH * (tokens // QUARTERS)
     shape = jax.ShapeDtypeStruct((Z * C, rows, LANES), teacher_slabs.dtype)
@@ -44,34 +39,78 @@
         arrange_kernel,
         grid=(1,),
         out_shape=shape,
-        in_specs=[pl.BlockSpec((slab_count, tokens // YH, width), lambda i: (0, section, 0))]
-        + [pl.BlockSpec(memory_space=pl.ANY)] * len(after),
+        in_specs=[pl.BlockSpec((slab_count, tokens // YH, width), lambda i: (0, section, 0))],
         out_specs=pl.BlockSpec(shape.shape, lambda i: (0, 0, 0)),
-        scratch_shapes=[pltpu.VMEM(array.shape, array.dtype) for array in after]
-        + [pltpu.SemaphoreType.DMA] * len(after),
         cost_estimate=pl.CostEstimate(flops=0, bytes_accessed=1600000, transcendentals=0),
         name="arrange",
-    )(teacher_slabs, *after)
-
-
-def pick_kernel(layer_map, received, picked):
+    )(teacher_slabs)
+
+
+def choose_kernel(count, section, first, second, *refs):
+    afters, out, sem, spares = refs[:count], refs[count], refs[count + 1], refs[count + 2 :]
+    copies = [
+        pltpu.make_async_copy(ref, spare, sem.at[1 + index])
+        for index, (ref, spare) in enumerate(zip(afters, spares))
+    ]
+    for copy in copies:
+        copy.start()
+
+    @pl.when(section[0] == 0)
+    def _():
+        copy = pltpu.make_async_copy(first, out, sem.at[0])
+        copy.start()
+        copy.wait()
+
+    @pl.when(section[0] != 0)
+    def _():
+        copy = pltpu.make_async_copy(second, out, sem.at[0])
+        copy.start()
+        copy.wait()
+
+    for copy in copies:
+        copy.wait()
+
+
+def choose(yh, first, second, after=()):
+    after = [array[:1] for array in after]
+    return pl.pallas_call(
+        functools.partial(choose_kernel, len(after)),
+        out_shape=jax.ShapeDtypeStruct(first.shape, first.dtype),
+        in_specs=[pl.BlockSpec(memory_space=pltpu.SMEM)] + [pl.BlockSpec(memory_space=pl.ANY)] * (2 + len(after)),
+        out_specs=pl.BlockSpec(memory_space=pltpu.VMEM),
+        scratch_shapes=[pltpu.SemaphoreType.DMA((1 + len(after),))]
+        + [pltpu.VMEM(array.shape, array.dtype) for array in after],
+        cost_estimate=pl.CostEstimate(flops=0, bytes_accessed=4 * first.size, transcendentals=0),
+        name="choose",
+    )(yh.reshape(1).astype(jnp.int32), first, second, *after)
+
+
+def pick_kernel(layer_map, received, picked, low, high):
+    half = low.shape[0]
+
     def step(layer, carry):
-        picked[layer] = received[layer_map[layer]]
+        value = received[layer_map[layer]]
+        picked[layer] = value
+        low[layer] = value
+        value = received[layer_map[half + layer]]
+        picked[half + layer] = value
+        high[layer] = value
         return carry
 
-    lax.fori_loop(0, picked.shape[0], step, 0)
+    lax.fori_loop(0, half, step, 0)
 
 
 def pick(layer_map, received):
     layers = layer_map.shape[0]
+    shapes = [(count, *received.shape[1:]) for count in (layers, layers // 2, layers // 2)]
     return pl.pallas_call(
         pick_kernel,
-        out_shape=jax.ShapeDtypeStruct((layers, *received.shape[1:]), received.dtype),
+        out_shape=[jax.ShapeDtypeStruct(shape, received.dtype) for shape in shapes],
         in_specs=[
             pl.BlockSpec(memory_space=pltpu.SMEM),
             pl.BlockSpec(memory_space=pltpu.VMEM),
         ],
-        out_specs=pl.BlockSpec(memory_space=pltpu.VMEM),
+        out_specs=[pl.BlockSpec(memory_space=pltpu.VMEM)] * len(shapes),
         cost_estimate=pl.CostEstimate(flops=0, bytes_accessed=1300000, transcendentals=0),
         name="pick_layers",
     )(layer_map, received)
@@ -81,19 +120,15 @@
 FIRST = ((0, 0), (1, 0), (3, 0), (0, 1))
 REST = ((2, 0), (1, 1), (2, 1), (3, 1))
 GROUPS = 4
-WEIGHTS = 6
 
 
 def load_weight(place, blocks, weights, weight, sem):
     piece = weights[0].shape[1]
-    half = piece // 2
     copies = []
     for index in range(sem.shape[0]):
         for source, ref in enumerate(weights):
-            part = source if source < 2 else 2 + (source - 2) // 2
-            shift = half if source in (3, 5) else 0
-            row = pl.multiple_of(index * QUARTERS * piece + place[part] * piece + shift, half)
-            target = weight.at[pl.ds(row, ref.shape[1])]
+            row = pl.multiple_of(index * QUARTERS * piece + place[source] * piece, piece)
+            target = weight.at[pl.ds(row, piece)]
             copies.append(pltpu.make_async_copy(ref.at[blocks[index]], target, sem.at[index, source]))
     for copy in copies:
         copy.start()
@@ -122,21 +157,27 @@
 
 
 def project_first_kernel(place, blocks, *refs):
-    features, refs = refs[: len(FIRST)], refs[len(FIRST) :]
-    weights, (out, weight, *held, feature_sem, weight_sem) = refs[:WEIGHTS], refs[WEIGHTS:]
+    count = len(FIRST) + 2
+    features, refs = refs[:count], refs[count:]
+    weights, (out, weight, *held, feature_sem, weight_sem) = refs[:QUARTERS], refs[QUARTERS:]
     copies = load_weight(place, blocks, weights, weight, weight_sem) + load_features(features, held, feature_sem)
     for copy in copies:
         copy.wait()
-    group = features[0].shape[0] // GROUPS
+    own, up_a, up_b, down_a, down_b, row = held
+    group = own.shape[0] // GROUPS
     for number in range(GROUPS):
-        left = left_rows(held, [number * group] * len(held), group)
-        out[number] = jnp.dot(left, weight[...], preferred_element_type=jnp.float32)
+        first = number * group
+        side = number // (GROUPS // 2)
+        offset = (number - side * (GROUPS // 2)) * group
+        refs = (own, (up_a, up_b)[side], (down_a, down_b)[side], row)
+        left = left_rows(refs, (first, offset, offset, first), group)
+        out[number] = jnp.dot(left, weight[...], preferred_element_type=jnp.float32).astype(out.dtype)
 
 
 def project_rest_kernel(place, blocks, slot_layer, partial, *refs):
     count = len(REST) + 2
     features, refs = refs[:count], refs[count:]
-    weights, refs = refs[:WEIGHTS], refs[WEIGHTS:]
+    weights, refs = refs[:QUARTERS], refs[QUARTERS:]
     outs, refs = refs[: len(DISTANCES) + 1], refs[len(DISTANCES) + 1 :]
     weight, before, product, *held, feature_sem, weight_sem, before_sem = refs
     copies = load_weight(place, blocks, weights, weight, weight_sem) + load_features(features, held, feature_sem)
@@ -158,7 +199,7 @@
         left = left_rows(refs, (offset, first, offset, first), group)
         value = jnp.dot(left, weight[...], preferred_element_type=jnp.float32)
         befores[number].wait()
-        value = (value + before[number]).astype(product.dtype)
+        value = (value + before[number].astype(jnp.float32)).astype(product.dtype)
         product[pl.ds(first, group)] = value.reshape(group, tokens, value.shape[1])
     slots = outs[-1].shape[1]
     for index, out in enumerate(outs):
@@ -177,17 +218,17 @@
     columns = weights[0].shape[2]
     depth = len(FIRST) * halves * lanes
     shape = (GROUPS, layers * tokens // GROUPS, columns)
-    smem, anywhere = pl.BlockSpec(memory_space=pltpu.SMEM), pl.BlockSpec(memory_space=pl.ANY)
+    smem, anywhere = pl.BlockSpec(memory_space=pltpu.SMEM), pl.BlockSpec(memory_space=pltpu.HBM)
     return pl.pallas_call(
         project_first_kernel,
-        out_shape=jax.ShapeDtypeStruct(shape, jnp.float32),
+        out_shape=jax.ShapeDtypeStruct(shape, jnp.bfloat16),
         in_specs=[smem] * 2 + [anywhere] * (len(features) + len(weights)),
         out_specs=pl.BlockSpec(memory_space=pltpu.VMEM),
         scratch_shapes=[
             pltpu.VMEM((depth, columns), jnp.bfloat16),
             *[pltpu.VMEM(feature.shape, feature.dtype) for feature in features],
             pltpu.SemaphoreType.DMA((len(features),)),
-            pltpu.SemaphoreType.DMA((len(FIRST), WEIGHTS)),
+            pltpu.SemaphoreType.DMA((len(FIRST), QUARTERS)),
         ],
         compiler_params=pltpu.CompilerParams(vmem_limit_bytes=40 * MIB),
         cost_estimate=pl.CostEstimate(
@@ -207,7 +248,7 @@
     return pl.pallas_call(
         project_rest_kernel,
         out_shape=[jax.ShapeDtypeStruct(shape, jnp.bfloat16) for shape in shapes],
-        in_specs=[smem] * 3 + [pl.BlockSpec(memory_space=pl.ANY)] * (1 + len(features) + len(weights)),
+        in_specs=[smem] * 3 + [pl.BlockSpec(memory_space=pltpu.HBM)] * (1 + len(features) + len(weights)),
         out_specs=[vmem] * len(shapes),
         scratch_shapes=[
             pltpu.VMEM((depth, columns), jnp.bfloat16),
@@ -215,7 +256,7 @@
             pltpu.VMEM((layers, tokens, columns), jnp.bfloat16),
             *[pltpu.VMEM(feature.shape, feature.dtype) for feature in features],
             pltpu.SemaphoreType.DMA((len(features),)),
-            pltpu.SemaphoreType.DMA((len(REST), WEIGHTS)),
+            pltpu.SemaphoreType.DMA((len(REST), QUARTERS)),
             pltpu.SemaphoreType.DMA((GROUPS,)),
         ],
         compiler_params=pltpu.CompilerParams(vmem_limit_bytes=62 * MIB),
@@ -288,21 +329,22 @@
     )(jnp.stack([c, own_count]).astype(jnp.int32), hidden, layer_grad, *pieces)
 
 
-def gather_tensor(own):
+def gather_tensor(own, low, high):
     up = [(i, (i + 1) % X) for i in range(X)]
     down = [(i, (i - 1) % X) for i in range(X)]
     swap = [(0, 1), (1, 0)]
-    half = own.shape[0] // 2
-    f3 = lax.ppermute(own, "x", up)
-    f1 = lax.ppermute(own, "x", down)
+    f3a = lax.ppermute(low, "x", up)
+    f1b = lax.ppermute(high, "x", down)
     g0 = lax.ppermute(own, "yl", swap)
-    f2a = lax.ppermute(f3[:half], "x", up)
-    f2b = lax.ppermute(f1[half:], "x", down)
+    f3b = lax.ppermute(high, "x", up)
+    f1a = lax.ppermute(low, "x", down)
+    f2a = lax.ppermute(f3a, "x", up)
+    f2b = lax.ppermute(f1b, "x", down)
     g3 = lax.ppermute(g0, "x", up)
     g1 = lax.ppermute(g0, "x", down)
     g2a = lax.ppermute(f2a, "yl", swap)
     g2b = lax.ppermute(f2b, "yl", swap)
-    return (own, f1, f2a, f2b, f3, g0, g1, g2a, g2b, g3)
+    return (own, f1a, f1b, f3a, f3b, g0), (f2a, f2b, g1, g2a, g2b, g3)
 
 
 def body(
@@ -327,17 +369,12 @@
     quarter = tokens // QUARTERS
 
     swap = [(0, 1), (1, 0)]
-    ring = YH * YL
-    up = [(i, (i + 1) % ring) for i in range(ring)]
-    down = [(i, (i - 1) % ring) for i in range(ring)]
     side = ("yh", "yl")
-    half_rows = proj_weight.shape[1] // 2
-    w_far_a = lax.ppermute(lax.ppermute(proj_weight[:, :half_rows], side, up), side, up)
-    w_far_b = lax.ppermute(lax.ppermute(proj_weight[:, half_rows:], side, down), side, down)
-    w_sib = lax.ppermute(proj_weight, "c", swap)
-    w_fs_a = lax.ppermute(w_far_a, "c", swap)
-    w_fs_b = lax.ppermute(w_far_b, "c", swap)
-    weights = (proj_weight, w_sib, w_far_a, w_far_b, w_fs_a, w_fs_b)
+    across_y = [(0, 3), (1, 2)]
+    w_row = lax.ppermute(proj_weight, side, [(0, 1), (1, 0)])
+    w_child = lax.ppermute(proj_weight, side, [(3, 0), (2, 1)])
+    w_teacher = lax.ppermute(w_row, side, across_y)
+    w_near = choose(yh, w_row, proj_weight)
     place = jnp.stack([2 * yh + c, 2 * yh + 1 - c, 2 * (1 - yh) + c, 2 * (1 - yh) + 1 - c]).astype(jnp.int32)
 
     is_child = yh == 1
@@ -375,12 +412,15 @@
         - first_hidden * inverse_rms**3 * inner_sum[:, None] / full_width
     )
     layer_grad = jnp.where(is_child, layer_grad, 0.0)
-    sent = lax.ppermute(arrange(teacher_slabs, 1), side, [(0, 3), (1, 2)])
-    arranged = jnp.where(yh == 0, arrange(teacher_slabs, 0, (sums,)), sent)
+    sent = lax.ppermute(arrange(teacher_slabs, 1), side, across_y)
+    arranged = choose(yh, arrange(teacher_slabs, 0), sent, (sums, w_row))
     received = lax.all_to_all(arranged, ("z", "c"), split_axis=0, concat_axis=0, tiled=True)
     received = received.reshape(Z * C * slab_count, YH, quarter, LANES)
 
-    f0, f1, f2a, f2b, f3, g0, g1, g2a, g2b, g3 = gather_tensor(pick(layer_map, received))
+    picked, low, high = pick(layer_map, received)
+    w_far = choose(yh, w_child, w_teacher, (low,))
+    weights = (w_near, lax.ppermute(w_near, "c", swap), w_far, lax.ppermute(w_far, "c", swap))
+    first_features, rest_features = gather_tensor(picked, low, high)
     first_blocks, rest_blocks = (
         jnp.stack([(x + step) % X * YL + (yl + yh + other) % YL for step, other in places]).astype(jnp.int32)
         for places in (FIRST, REST)
@@ -389,12 +429,12 @@
     prefix_start = prefix_end - layer_counts
     slot_layer = jnp.clip(prefix_start[:, None] + jnp.arange(slot_count)[None, :], 0, layers - 1)
     slot_layer = slot_layer.reshape(Z, C * slot_count)[(z + jnp.array(DISTANCES)) % Z].reshape(-1).astype(jnp.int32)
-    partial = project_first(place, first_blocks, (f0, f1, f3, g0), weights)
-    chunks = project_rest(place, rest_blocks, slot_layer, partial, (f2a, f2b, g1, g2a, g2b, g3), weights)
+    partial = project_first(place, first_blocks, first_features, weights)
+    chunks = project_rest(place, rest_blocks, slot_layer, partial, rest_features, weights)
     kept, given = combine(c, *reduce_z(chunks))
     across = lax.ppermute(given, "c", swap)
-    teacher = lax.ppermute(kept, "yh", [(0, 1)])
-    teacher_across = lax.ppermute(given, ("yh", "c"), [(0, 3), (1, 2)])
+    teacher = lax.ppermute(kept, side, across_y)
+    teacher_across = lax.ppermute(given, ("yh", "c", "yl"), [(0, 7), (1, 6), (2, 5), (3, 4)])
     own_count = jnp.where(is_child, layer_counts[2 * z + c], 0)
     hidden_grad = finish(c, own_count, child_hidden, layer_grad, (kept, across, teacher, teacher_across))
     key_grad = jnp.where(is_child, key_grad, jnp.zeros_like(key_grad))

time: 180 us -> 203 us (1.13)
  starting transfers between devices: 52.7 us -> 66.4 us
  Pallas kernels: 27.8 us -> 34.1 us
  blocking collectives: 15.1 us -> 19.9 us
  other arithmetic: 9.93 us -> 6.77 us
    ppermute x14, starting transfers between devices: 19.1 us -> 28.5 us  [the longest x1 7.2 us: body(): w_teacher = lax.ppermute(w_row, side, across_y)]
    ppermute x14, waiting for transfers between devices: 27.5 us -> 20.4 us  [the longest x1 5.84 us: gather_tensor(): f1a = lax.ppermute(low, 'x', down)]
    pallas_call x1 -> x4, Pallas kernels: 2.14 us -> 9.02 us  [the longest x3 6.58 us: choose(): pl.pallas_call(functools.partial(choose_kernel, len(after)), out_shape=ja...]
    psum x1, blocking collectives: 15.1 us -> 19.9 us  [body(): lax.psum(jnp.stack([jnp.sum(first_hidden * first_hidden, axis=1), jnp.sum...]
    ppermute x3, waiting for transfers between devices: 4.22 us -> 8.56 us  [reduce_z(): from_above = lax.ppermute(add(to_down, from_above), 'z', down)]
    all_to_all x1, waiting for transfers between devices: 7.61 us -> 11.2 us  [body(): lax.all_to_all(arranged, ('z', 'c'), split_axis=0, concat_axis=0, tiled=T...]
    select_n x1 -> x0, other arithmetic: 2.19 us -> none  [body(): arranged = jnp.where(yh == 0, arrange(teacher_slabs, 0, (sums,)), sent)]
    ppermute x1, starting transfers between devices: 6.74 us -> 8.89 us  [body(): across = lax.ppermute(given, 'c', swap)]
  transfers between devices with their start and end apart: 29 -> 29, of which waited for: 13 -> 14; matrix products, arithmetic and copies ran while one was open for 13% -> 11% of each run, Pallas kernels for 6% -> 9%
where the time goes in v5:
time: 203 us; the launch traced here: 202 us
  starting transfers between devices  66.4 us (33%)
  waiting for transfers between devices  50.1 us (25%)
  Pallas kernels  34.1 us (17%)
  blocking collectives  19.9 us (10%)
  local copies, waits for them, and re-layouts  13.6 us (7%)
  matrix products  9.29 us (5%)
  other arithmetic  6.77 us (3%)
    psum x1, blocking collectives, body(): lax.psum(jnp.stack([jnp.sum(first_hidden * first_hidden, axis=1), jnp.sum...  19.9 us
    all_to_all x1, starting transfers between devices, body(): lax.all_to_all(arranged, ('z', 'c'), split_axis=0, concat_axis=0, tiled=T...  12.6 us
    all_to_all x1, waiting for transfers between devices, body(): lax.all_to_all(arranged, ('z', 'c'), split_axis=0, concat_axis=0, tiled=T...  11.2 us
    ppermute x3, starting transfers between devices, reduce_z(): from_above = lax.ppermute(add(to_down, from_above), 'z', down)  9.47 us
    ppermute x1, starting transfers between devices, body(): across = lax.ppermute(given, 'c', swap)  8.89 us
    pallas_call x1, Pallas kernels, project_rest(): pl.pallas_call(project_rest_kernel, out_shape=[jax.ShapeDtypeStruct(shape...  8.84 us
    ppermute x3, waiting for transfers between devices, reduce_z(): from_above = lax.ppermute(add(to_down, from_above), 'z', down)  8.56 us
    unnamed x56, local copies, waits for them, and re-layouts  7.84 us
  transfers between devices with their start and end apart: 29, of which 14 were waited for; matrix products, arithmetic and copies ran while one was open for 11% of the time, Pallas kernels for 9%

profile of v5, /device:TPU:1, one launch (start us, length us, event | category | flops | bytes accessed | tf_op | source)
XLA Modules:
  0.0 201.8 jit_solution(13309835580893360351)
XLA Ops:
  0.7 4.2 %collective-permute-start.1 = (bf16[8,64,1024]{2,1,0:T(8,128)(2,1)}, bf16[8,64,1024]{2,1,0:T(8,128)(2,1)}, u32[]{:S(2)}, u32[]{:S(2)}) collective-permute-start(bf16[8,64,1024]{2,1,0:T(8,128)(2,1)} %second.1), channel_id=1, source_target_pairs={{0,1},{1,0},{2,3},{3,2},{4,5},{5,4},{6,7},{7,6},{8,9},{9,8},{10,11... | collective-permute-start | bytes 3145736 | tf_op jit(solution)/shard_map/ppermute | solution.py:374
  4.8 2.2 %arrange.3 = bf16[16,192,128]{2,1,0:T(8,128)(2,1)} custom-call(bf16[3,128,2048]{2,1,0:T(8,128)(2,1)} %slabs.3), custom_call_target="tpu_custom_call" | custom-call | bytes 1600000 | tf_op jit(solution)/shard_map/arrange/pallas_call | solution.py:38
  7.0 4.1 %collective-permute-start = (bf16[16,192,128]{2,1,0:T(8,128)(2,1)}, bf16[16,192,128]{2,1,0:T(8,128)(2,1)}, u32[]{:S(2)}, u32[]{:S(2)}) collective-permute-start(bf16[16,192,128]{2,1,0:T(8,128)(2,1)} %arrange.3), channel_id=1, source_target_pairs={{0,129},{1,128},{2,131},{3,130},{4,133},{5,132},{6,135},{7,134},{8... | collective-permute-start | bytes 2359304 | tf_op jit(solution)/shard_map/ppermute | solution.py:415
  11.1 2.4 %fusion = f32[128,1024]{1,0:T(8,128)S(1)} fusion(bf16[1,1024,1024]{2,1,0:T(8,128)(2,1)} %param.16, bf16[1,128,1024]{2,1,0:T(8,128)(2,1)S(1)} %copy-done.20), kind=kOutput, calls=%fused_computation.1 | convolution fusion | flops 268435456 | bytes 2883584 | tf_op jit(solution)/shard_map/dot_general | solution.py:387
  13.5 2.2 %arrange.2.first = bf16[16,192,128]{2,1,0:T(8,128)(2,1)} custom-call(bf16[3,128,2048]{2,1,0:T(8,128)(2,1)} %slabs.3), custom_call_target="tpu_custom_call" | custom-call | bytes 1600000 | tf_op jit(solution)/shard_map/arrange/pallas_call | solution.py:38
  15.7 2.6 %fusion.11 = (f32[128]{0:T(128)S(1)}, f32[128]{0:T(128)S(1)}, f32[128,1024]{1,0:T(8,128)}) fusion(bf16[3,128,1024]{2,1,0:T(8,128)(2,1)} %hidden.1, f32[1024]{0:T(1024)S(1)} %bitcast.92, f32[128,1024]{1,0:T(8,128)S(1)} %fusion, bf16[1,1024,1024]{2,1,0:T(8,128)(2,1)S(1)} %copy-done.11, bf16[1,128,1024]{2,1,0:T(8,128)(2,1)S(1)} %copy-done), kind=kOutput, calls=%fused_computation.20 | convolution fusion | flops 269352704 | bytes 3675136 | tf_op jit(solution)/shard_map/dot_general | solution.py:384
  18.3 19.9 %psum.7 = f32[2,128]{1,0:T(2,128)S(1)} all-reduce(f32[2,128]{1,0:T(2,128)S(1)} %pad_maximum_fusion), channel_id=1, replica_groups=mesh['yh'=2,'z'=8,'c'=2,'x'=4,'yl'=2] {'x','yl'}, use_global_device_ids=true, to_apply=%region_2.0 | all-reduce | flops 256 | bytes 2048 | tf_op jit(solution)/shard_map/psum | solution.py:390
  40.3 2.1 %choose.3 = bf16[16,192,128]{2,1,0:T(8,128)(2,1)} custom-call(s32[1]{0:T(128)} %bitcast.26.section, bf16[16,192,128]{2,1,0:T(8,128)(2,1)} %arrange.2.first, bf16[16,192,128]{2,1,0:T(8,128)(2,1)} %collective-permute-done.second, f32[1,128]{1,0:T(1,128)} %get-tuple-element.38.refs_0_, bf16[1,64,1024]{2,1,0:T(8,128)(2,1)} %slice.23.refs_1_), custom_call_target="tpu_custom_call" | custom-call | bytes 1572864 | tf_op jit(solution)/shard_map/choose/pallas_call | solution.py:76
  42.5 12.6 %all-to-all-start = ((bf16[16,192,128]{2,1,0:T(8,128)(2,1)}), bf16[16,192,128]{2,1,0:T(8,128)(2,1)S(1)}, u32[]{:S(2)}, u32[]{:S(2)}) async-start(bf16[16,192,128]{2,1,0:T(8,128)(2,1)} %choose.3), calls=%async_computation | async-start | bytes 1572864 | tf_op jit(solution)/shard_map/all_to_all | solution.py:417
  56.3 7.2 %collective-permute-start.9 = (bf16[8,64,1024]{2,1,0:T(8,128)(2,1)}, bf16[8,64,1024]{2,1,0:T(8,128)(2,1)}, u32[]{:S(2)}, u32[]{:S(2)}) collective-permute-start(bf16[8,64,1024]{2,1,0:T(8,128)(2,1)} %collective-permute-done.1.first), channel_id=1, source_target_pairs={{0,129},{1,128},{2,131},{3,130},{4,133},{5,132},{6,135},{7,134},{8... | collective-permute-start | bytes 3145736 | tf_op jit(solution)/shard_map/ppermute | solution.py:376
  63.5 2.2 %choose.4.refs_6_ = bf16[8,64,1024]{2,1,0:T(8,128)(2,1)} custom-call(s32[1]{0:T(128)} %bitcast.26.section, bf16[8,64,1024]{2,1,0:T(8,128)(2,1)} %collective-permute-done.1.first, bf16[8,64,1024]{2,1,0:T(8,128)(2,1)} %second.1), custom_call_target="tpu_custom_call" | custom-call | bytes 2097152 | tf_op jit(solution)/shard_map/choose/pallas_call | solution.py:76
  66.5 11.2 %all-to-all-done = bf16[16,192,128]{2,1,0:T(8,128)(2,1)S(1)} async-done(((bf16[16,192,128]{2,1,0:T(8,128)(2,1)}), bf16[16,192,128]{2,1,0:T(8,128)(2,1)S(1)}, u32[]{:S(2)}, u32[]{:S(2)}) %all-to-all-start) | async-done | bytes 786464 | tf_op jit(solution)/shard_map/all_to_all | solution.py:417
  78.6 2.4 %pick_layers.1 = (bf16[32,2,32,128]{3,2,1,0:T(8,128)(2,1)}, bf16[16,2,32,128]{3,2,1,0:T(8,128)(2,1)}, bf16[16,2,32,128]{3,2,1,0:T(8,128)(2,1)}) custom-call(s32[32]{0:T(128)} %layer_map.1, bf16[48,2,32,128]{3,2,1,0:T(8,128)(2,1)} %bitcast.89), custom_call_target="tpu_custom_call" | custom-call | bytes 1300000 | tf_op jit(solution)/shard_map/pick_layers/pallas_call | solution.py:106
  85.0 2.3 %choose.5.refs_8_ = bf16[8,64,1024]{2,1,0:T(8,128)(2,1)} custom-call(s32[1]{0:T(128)} %bitcast.26.section, bf16[8,64,1024]{2,1,0:T(8,128)(2,1)} %collective-permute-done.8.first, bf16[8,64,1024]{2,1,0:T(8,128)(2,1)} %collective-permute-done.9.second, bf16[1,2,32,128]{3,2,1,0:T(8,128)(2,1)} %slice.20.refs_0_), custom_call_target="tpu_custom_call" | custom-call | bytes 2097152 | tf_op jit(solution)/shard_map/choose/pallas_call | solution.py:76
  90.8 5.8 %collective-permute-done.2.refs_1_ = bf16[16,2,32,128]{3,2,1,0:T(8,128)(2,1)} collective-permute-done((bf16[16,2,32,128]{3,2,1,0:T(8,128)(2,1)}, bf16[16,2,32,128]{3,2,1,0:T(8,128)(2,1)}, u32[]{:S(2)}, u32[]{:S(2)}) %collective-permute-start.2) | collective-permute-done | bytes 262176 | tf_op jit(solution)/shard_map/ppermute | solution.py:340
  96.6 5.6 %collective-permute-done.3.refs_2_ = bf16[16,2,32,128]{3,2,1,0:T(8,128)(2,1)} collective-permute-done((bf16[16,2,32,128]{3,2,1,0:T(8,128)(2,1)}, bf16[16,2,32,128]{3,2,1,0:T(8,128)(2,1)}, u32[]{:S(2)}, u32[]{:S(2)}) %collective-permute-start.3) | collective-permute-done | bytes 262176 | tf_op jit(solution)/shard_map/ppermute | solution.py:337
  113.7 7.2 %project_first.1.partial = bf16[4,256,1024]{2,1,0:T(8,128)(2,1)S(1)} custom-call(s32[4]{0:T(128)S(1)} %get-tuple-element.41.place, s32[4]{0:T(128)S(1)} %get-tuple-element.42.blocks, bf16[32,2,32,128]{3,2,1,0:T(8,128)(2,1)S(1)} %copy-done.6, bf16[16,2,32,128]{3,2,1,0:T(8,128)(2,1)} %collective-permute-done.2.refs_1_, ...), custom_call_target="tpu_custom_call" | custom-call | flops 2147483648 | bytes 8388608 | tf_op jit(solution)/shard_map/project_first/pallas_call | solution.py:222
  123.7 8.8 %project_rest.1 = (bf16[3,32,1024]{2,1,0:T(8,128)(2,1)}, bf16[3,32,1024]{2,1,0:T(8,128)(2,1)}, bf16[2,3,32,1024]{3,2,1,0:T(8,128)(2,1)}, bf16[2,3,32,1024]{3,2,1...) custom-call(s32[4]{0:T(128)} %copy-done.7, ...), custom_call_target="tpu_custom_call" | custom-call | flops 2147483648 | bytes 11534336 | tf_op jit(solution)/shard_map/project_rest/pallas_call | solution.py:248
  132.6 2.6 %collective-permute-start.21 = (bf16[3,32,1024]{2,1,0:T(8,128)(2,1)}, bf16[3,32,1024]{2,1,0:T(8,128)(2,1)S(1)}, u32[]{:S(2)}, u32[]{:S(2)}) collective-permute-start(bf16[3,32,1024]{2,1,0:T(8,128)(2,1)} %get-tuple-element.29), channel_id=1, source_target_pairs={{0,112},{16,0},{32,16},{48,32},{64,48},{80,64},{96,80},{112,96},{1... | collective-permute-start | bytes 589832 | tf_op jit(solution)/shard_map/ppermute | solution.py:280
  135.2 2.9 %collective-permute-done.21 = bf16[3,32,1024]{2,1,0:T(8,128)(2,1)S(1)} collective-permute-done((bf16[3,32,1024]{2,1,0:T(8,128)(2,1)}, bf16[3,32,1024]{2,1,0:T(8,128)(2,1)S(1)}, u32[]{:S(2)}, u32[]{:S(2)}) %collective-permute-start.21) | collective-permute-done | bytes 196640 | tf_op jit(solution)/shard_map/ppermute | solution.py:280
  139.3 3.1 %collective-permute-start.22 = (bf16[2,3,32,1024]{3,2,1,0:T(8,128)(2,1)S(1)}, bf16[2,3,32,1024]{3,2,1,0:T(8,128)(2,1)S(1)}, u32[]{:S(2)}, u32[]{:S(2)}) collective-permute-start(bf16[2,3,32,1024]{3,2,1,0:T(8,128)(2,1)S(1)} %add_convert_fusion.2), channel_id=1, source_target_pairs={{0,112},{16,0},{32,16},{48,32},{64,48},{80,64},{96,80},{112,96},{1... | collective-permute-start | bytes 1179656 | tf_op jit(solution)/shard_map/ppermute | solution.py:283
  143.6 3.5 %collective-permute-done.22 = bf16[2,3,32,1024]{3,2,1,0:T(8,128)(2,1)S(1)} collective-permute-done((bf16[2,3,32,1024]{3,2,1,0:T(8,128)(2,1)S(1)}, bf16[2,3,32,1024]{3,2,1,0:T(8,128)(2,1)S(1)}, u32[]{:S(2)}, u32[]{:S(2)}) %collective-permute-start.22) | collective-permute-done | bytes 393248 | tf_op jit(solution)/shard_map/ppermute | solution.py:283
  147.3 3.2 %collective-permute-start.23 = (bf16[2,3,32,1024]{3,2,1,0:T(8,128)(2,1)S(1)}, bf16[2,3,32,1024]{3,2,1,0:T(8,128)(2,1)S(1)}, u32[]{:S(2)}, u32[]{:S(2)}) collective-permute-start(bf16[2,3,32,1024]{3,2,1,0:T(8,128)(2,1)S(1)} %add_convert_fusion.1), channel_id=1, source_target_pairs={{0,112},{16,0},{32,16},{48,32},{64,48},{80,64},{96,80},{112,96},{1... | collective-permute-start | bytes 1179656 | tf_op jit(solution)/shard_map/ppermute | solution.py:283
  157.2 3.2 %collective-permute-start.24 = (bf16[2,3,32,1024]{3,2,1,0:T(8,128)(2,1)S(1)}, bf16[2,3,32,1024]{3,2,1,0:T(8,128)(2,1)S(1)}, u32[]{:S(2)}, u32[]{:S(2)}) collective-permute-start(bf16[2,3,32,1024]{3,2,1,0:T(8,128)(2,1)S(1)} %add_convert_fusion), channel_id=1, source_target_pairs={{0,112},{16,0},{32,16},{48,32},{64,48},{80,64},{96,80},{112,96},{1... | collective-permute-start | bytes 1179656 | tf_op jit(solution)/shard_map/ppermute | solution.py:283
  162.1 2.1 %select_bitcast_fusion = bf16[1,1024,1024]{2,1,0:T(8,128)(2,1)} fusion(pred[]{:T(512)S(6)} %eq.22, bf16[1,128,1024]{2,1,0:T(8,128)(2,1)S(1)} %copy-done.21, f32[1024]{0:T(1024)S(1)} %bitcast.94, f32[128]{0:T(128)S(1)} %get-tuple-element.35, bf16[3,128,1024]{2,1,0:T(8,128)(2,1)S(1)} %copy-done.9), kind=kOutput, calls=%fused_computation.5 | convolution fusion | flops 271056896 | bytes 2626049 | tf_op jit(solution)/shard_map/dot_general | solution.py:406
  164.8 3.3 %collective-permute-done.24.above = bf16[2,3,32,1024]{3,2,1,0:T(8,128)(2,1)S(1)} collective-permute-done((bf16[2,3,32,1024]{3,2,1,0:T(8,128)(2,1)S(1)}, bf16[2,3,32,1024]{3,2,1,0:T(8,128)(2,1)S(1)}, u32[]{:S(2)}, u32[]{:S(2)}) %collective-permute-start.24) | collective-permute-done | bytes 393248 | tf_op jit(solution)/shard_map/ppermute | solution.py:283
  168.1 4.8 %collective-permute-done.20.below = bf16[2,3,32,1024]{3,2,1,0:T(8,128)(2,1)S(1)} collective-permute-done((bf16[2,3,32,1024]{3,2,1,0:T(8,128)(2,1)S(1)}, bf16[2,3,32,1024]{3,2,1,0:T(8,128)(2,1)S(1)}, u32[]{:S(2)}, u32[]{:S(2)}) %collective-permute-start.20) | collective-permute-done | bytes 393248 | tf_op jit(solution)/shard_map/ppermute | solution.py:282
  175.8 8.9 %collective-permute-start.25 = (bf16[3,32,1024]{2,1,0:T(8,128)(2,1)}, bf16[3,32,1024]{2,1,0:T(8,128)(2,1)S(1)}, u32[]{:S(2)}, u32[]{:S(2)}) collective-permute-start(bf16[3,32,1024]{2,1,0:T(8,128)(2,1)} %get-tuple-element.31), channel_id=1, source_target_pairs={{0,8},{8,0},{1,9},{9,1},{2,10},{10,2},{3,11},{11,3},{4,12},{12,4},... | collective-permute-start | bytes 589832 | tf_op jit(solution)/shard_map/ppermute | solution.py:435
  184.6 5.2 %collective-permute-start.27 = (bf16[3,32,1024]{2,1,0:T(8,128)(2,1)}, bf16[3,32,1024]{2,1,0:T(8,128)(2,1)S(1)}, u32[]{:S(2)}, u32[]{:S(2)}) collective-permute-start(bf16[3,32,1024]{2,1,0:T(8,128)(2,1)} %get-tuple-element.31), channel_id=1, source_target_pairs={{0,137},{1,136},{8,129},{9,128},{2,139},{3,138},{10,131},{11,130},... | collective-permute-start | bytes 589832 | tf_op jit(solution)/shard_map/ppermute | solution.py:437
  191.3 2.1 %select_bitcast_fusion.1 = bf16[1,1024,1024]{2,1,0:T(8,128)(2,1)} fusion(pred[]{:T(512)S(6)} %eq.22, bf16[1,128,1024]{2,1,0:T(8,128)(2,1)S(1)} %copy-done, f32[1024]{0:T(1024)S(1)} %bitcast.95, f32[128]{0:T(128)S(1)} %get-tuple-element.35, bf16[3,128,1024]{2,1,0:T(8,128)(2,1)S(1)} %copy-done.9), kind=kOutput, calls=%fused_computation.6 | convolution fusion | flops 271056896 | bytes 2626049 | tf_op jit(solution)/shard_map/dot_general | solution.py:403
  193.4 5.0 %collective-permute-done.26.teacher = bf16[3,32,1024]{2,1,0:T(8,128)(2,1)S(1)} collective-permute-done((bf16[3,32,1024]{2,1,0:T(8,128)(2,1)}, bf16[3,32,1024]{2,1,0:T(8,128)(2,1)S(1)}, u32[]{:S(2)}, u32[]{:S(2)}) %collective-permute-start.26) | collective-permute-done | bytes 196640 | tf_op jit(solution)/shard_map/ppermute | solution.py:436
  199.2 2.6 %finish.1 = bf16[3,128,1024]{2,1,0:T(8,128)(2,1)} custom-call(s32[2]{0:T(128)} %pad_add_fusion.state, bf16[3,128,1024]{2,1,0:T(8,128)(2,1)} %hidden.1, f32[128,1024]{1,0:T(8,128)} %get-tuple-element.37.layer_grad, bf16[3,32,1024]{2,1,0:T(8,128)(2,1)} %get-tuple-element.30.near, bf16[3,32,1024]{2,1,0:T(8,128)(2,1)} %copy-done.22, ...), custom_call_target="tpu_custom_call" | custom-call | flops 786432 | bytes 3145728 | tf_op jit(solution)/shard_map/finish/pallas_call | solution.py:322
  (130 shorter events, 42.5 us)
Async XLA Ops:
  0.7 38.1 %collective-permute-start.1 = (bf16[8,64,1024]{2,1,0:T(8,128)(2,1)}, bf16[8,64,1024]{2,1,0:T(8,128)(2,1)}, u32[]{:S(2)}, u32[]{:S(2)}) collective-permute-start(bf16[8,64,1024]{2,1,0:T(8,128)(2,1)} %second.1), channel_id=1, source_target_pairs={{0,1},{1,0},{2,3},{3,2},{4,5},{5,4},{6,7},{7,6},{8,9},{9,8},{10,11... | collective-permute-start | bytes 3145736 | tf_op jit(solution)/shard_map/ppermute | solution.py:374
  7.0 33.3 %collective-permute-start = (bf16[16,192,128]{2,1,0:T(8,128)(2,1)}, bf16[16,192,128]{2,1,0:T(8,128)(2,1)}, u32[]{:S(2)}, u32[]{:S(2)}) collective-permute-start(bf16[16,192,128]{2,1,0:T(8,128)(2,1)} %arrange.3), channel_id=1, source_target_pairs={{0,129},{1,128},{2,131},{3,130},{4,133},{5,132},{6,135},{7,134},{8... | collective-permute-start | bytes 2359304 | tf_op jit(solution)/shard_map/ppermute | solution.py:415
  42.5 35.2 %all-to-all-start = ((bf16[16,192,128]{2,1,0:T(8,128)(2,1)}), bf16[16,192,128]{2,1,0:T(8,128)(2,1)S(1)}, u32[]{:S(2)}, u32[]{:S(2)}) async-start(bf16[16,192,128]{2,1,0:T(8,128)(2,1)} %choose.3), calls=%async_computation | async-start | bytes 1572864 | tf_op jit(solution)/shard_map/all_to_all | solution.py:417
  55.0 28.1 %collective-permute-start.8 = (bf16[8,64,1024]{2,1,0:T(8,128)(2,1)}, bf16[8,64,1024]{2,1,0:T(8,128)(2,1)}, u32[]{:S(2)}, u32[]{:S(2)}) collective-permute-start(bf16[8,64,1024]{2,1,0:T(8,128)(2,1)} %second.1), channel_id=1, source_target_pairs={{129,0},{128,1},{131,2},{130,3},{133,4},{132,5},{135,6},{134,7},{1... | collective-permute-start | bytes 3145736 | tf_op jit(solution)/shard_map/ppermute | solution.py:375
  56.3 28.7 %collective-permute-start.9 = (bf16[8,64,1024]{2,1,0:T(8,128)(2,1)}, bf16[8,64,1024]{2,1,0:T(8,128)(2,1)}, u32[]{:S(2)}, u32[]{:S(2)}) collective-permute-start(bf16[8,64,1024]{2,1,0:T(8,128)(2,1)} %collective-permute-done.1.first), channel_id=1, source_target_pairs={{0,129},{1,128},{2,131},{3,130},{4,133},{5,132},{6,135},{7,134},{8... | collective-permute-start | bytes 3145736 | tf_op jit(solution)/shard_map/ppermute | solution.py:376
  65.7 38.0 %copy-start.27 = (s32[8]{0:T(128)S(1)}, s32[8]{0:T(128)}, u32[]{:S(2)}) copy-start(s32[8]{0:T(128)} %constant.118.clone) | copy-start | bytes 100
  65.7 22.8 %collective-permute-start.7 = (bf16[8,64,1024]{2,1,0:T(8,128)(2,1)}, bf16[8,64,1024]{2,1,0:T(8,128)(2,1)S(1)}, u32[]{:S(2)}, u32[]{:S(2)}) collective-permute-start(bf16[8,64,1024]{2,1,0:T(8,128)(2,1)} %choose.4.refs_6_), channel_id=1, source_target_pairs={{0,8},{8,0},{1,9},{9,1},{2,10},{10,2},{3,11},{11,3},{4,12},{12,4},... | collective-permute-start | bytes 3145736 | tf_op jit(solution)/shard_map/ppermute | solution.py:422
  78.6 32.5 %copy-start.1 = (bf16[8,64,1024]{2,1,0:T(8,128)(2,1)S(1)}, bf16[8,64,1024]{2,1,0:T(8,128)(2,1)}, u32[]{:S(2)}) copy-start(bf16[8,64,1024]{2,1,0:T(8,128)(2,1)} %choose.4.refs_6_) | copy-start | bytes 3145732
  81.0 8.3 %collective-permute-start.4 = (bf16[16,2,32,128]{3,2,1,0:T(8,128)(2,1)}, bf16[16,2,32,128]{3,2,1,0:T(8,128)(2,1)}, u32[]{:S(2)}, u32[]{:S(2)}) collective-permute-start(bf16[16,2,32,128]{3,2,1,0:T(8,128)(2,1)} %get-tuple-element.19), channel_id=1, source_target_pairs={{0,2},{2,4},{4,6},{6,0},{1,3},{3,5},{5,7},{7,1},{8,10},{10,12},{12... | collective-permute-start | bytes 786440 | tf_op jit(solution)/shard_map/ppermute | solution.py:336
  87.3 23.8 %collective-permute-start.10 = (bf16[8,64,1024]{2,1,0:T(8,128)(2,1)}, bf16[8,64,1024]{2,1,0:T(8,128)(2,1)S(1)}, u32[]{:S(2)}, u32[]{:S(2)}) collective-permute-start(bf16[8,64,1024]{2,1,0:T(8,128)(2,1)} %choose.5.refs_8_), channel_id=1, source_target_pairs={{0,8},{8,0},{1,9},{9,1},{2,10},{10,2},{3,11},{11,3},{4,12},{12,4},... | collective-permute-start | bytes 3145736 | tf_op jit(solution)/shard_map/ppermute | solution.py:422
  88.6 15.3 %collective-permute-start.6 = (bf16[32,2,32,128]{3,2,1,0:T(8,128)(2,1)}, bf16[32,2,32,128]{3,2,1,0:T(8,128)(2,1)}, u32[]{:S(2)}, u32[]{:S(2)}) collective-permute-start(bf16[32,2,32,128]{3,2,1,0:T(8,128)(2,1)} %get-tuple-element.18.refs_0_), channel_id=1, source_target_pairs={{0,1},{1,0},{2,3},{3,2},{4,5},{5,4},{6,7},{7,6},{8,9},{9,8},{10,11... | collective-permute-start | bytes 1572872 | tf_op jit(solution)/shard_map/ppermute | solution.py:338
  88.6 8.0 %collective-permute-start.2 = (bf16[16,2,32,128]{3,2,1,0:T(8,128)(2,1)}, bf16[16,2,32,128]{3,2,1,0:T(8,128)(2,1)}, u32[]{:S(2)}, u32[]{:S(2)}) collective-permute-start(bf16[16,2,32,128]{3,2,1,0:T(8,128)(2,1)} %get-tuple-element.19), channel_id=1, source_target_pairs={{0,6},{2,0},{4,2},{6,4},{1,7},{3,1},{5,3},{7,5},{8,14},{10,8},{12,... | collective-permute-start | bytes 786440 | tf_op jit(solution)/shard_map/ppermute | solution.py:340
  88.6 32.4 %copy-start.4 = (bf16[8,64,1024]{2,1,0:T(8,128)(2,1)}, bf16[8,64,1024]{2,1,0:T(8,128)(2,1)S(1)}, u32[]{:S(2)}) copy-start(bf16[8,64,1024]{2,1,0:T(8,128)(2,1)S(1)} %collective-permute-done.7.refs_7_) | copy-start | bytes 3145732
  88.6 13.6 %collective-permute-start.3 = (bf16[16,2,32,128]{3,2,1,0:T(8,128)(2,1)}, bf16[16,2,32,128]{3,2,1,0:T(8,128)(2,1)}, u32[]{:S(2)}, u32[]{:S(2)}) collective-permute-start(bf16[16,2,32,128]{3,2,1,0:T(8,128)(2,1)} %get-tuple-element.20), channel_id=1, source_target_pairs={{0,6},{2,0},{4,2},{6,4},{1,7},{3,1},{5,3},{7,5},{8,14},{10,8},{12,... | collective-permute-start | bytes 786440 | tf_op jit(solution)/shard_map/ppermute | solution.py:337
  89.3 14.7 %collective-permute-start.5 = (bf16[16,2,32,128]{3,2,1,0:T(8,128)(2,1)}, bf16[16,2,32,128]{3,2,1,0:T(8,128)(2,1)}, u32[]{:S(2)}, u32[]{:S(2)}) collective-permute-start(bf16[16,2,32,128]{3,2,1,0:T(8,128)(2,1)} %get-tuple-element.20), channel_id=1, source_target_pairs={{0,2},{2,4},{4,6},{6,0},{1,3},{3,5},{5,7},{7,1},{8,10},{10,12},{12... | collective-permute-start | bytes 786440 | tf_op jit(solution)/shard_map/ppermute | solution.py:339
  96.6 10.1 %collective-permute-start.11 = (bf16[16,2,32,128]{3,2,1,0:T(8,128)(2,1)}, bf16[16,2,32,128]{3,2,1,0:T(8,128)(2,1)}, u32[]{:S(2)}, u32[]{:S(2)}) collective-permute-start(bf16[16,2,32,128]{3,2,1,0:T(8,128)(2,1)} %collective-permute-done.4.refs_3_), channel_id=1, source_target_pairs={{0,2},{2,4},{4,6},{6,0},{1,3},{3,5},{5,7},{7,1},{8,10},{10,12},{12... | collective-permute-start | bytes 786440 | tf_op jit(solution)/shard_map/ppermute | solution.py:341
  102.2 7.1 %collective-permute-start.12 = (bf16[16,2,32,128]{3,2,1,0:T(8,128)(2,1)}, bf16[16,2,32,128]{3,2,1,0:T(8,128)(2,1)}, u32[]{:S(2)}, u32[]{:S(2)}) collective-permute-start(bf16[16,2,32,128]{3,2,1,0:T(8,128)(2,1)} %collective-permute-done.3.refs_2_), channel_id=1, source_target_pairs={{0,6},{2,0},{4,2},{6,4},{1,7},{3,1},{5,3},{7,5},{8,14},{10,8},{12,... | collective-permute-start | bytes 786440 | tf_op jit(solution)/shard_map/ppermute | solution.py:342
  103.8 19.9 %collective-permute-start.13 = (bf16[32,2,32,128]{3,2,1,0:T(8,128)(2,1)}, bf16[32,2,32,128]{3,2,1,0:T(8,128)(2,1)}, u32[]{:S(2)}, u32[]{:S(2)}) collective-permute-start(bf16[32,2,32,128]{3,2,1,0:T(8,128)(2,1)} %collective-permute-done.6.refs_5_), channel_id=1, source_target_pairs={{0,6},{2,0},{4,2},{6,4},{1,7},{3,1},{5,3},{7,5},{8,14},{10,8},{12,... | collective-permute-start | bytes 1572872 | tf_op jit(solution)/shard_map/ppermute | solution.py:344
  104.0 19.8 %collective-permute-start.16 = (bf16[32,2,32,128]{3,2,1,0:T(8,128)(2,1)}, bf16[32,2,32,128]{3,2,1,0:T(8,128)(2,1)}, u32[]{:S(2)}, u32[]{:S(2)}) collective-permute-start(bf16[32,2,32,128]{3,2,1,0:T(8,128)(2,1)} %collective-permute-done.6.refs_5_), channel_id=1, source_target_pairs={{0,2},{2,4},{4,6},{6,0},{1,3},{3,5},{5,7},{7,1},{8,10},{10,12},{12... | collective-permute-start | bytes 1572872 | tf_op jit(solution)/shard_map/ppermute | solution.py:343
  106.7 15.6 %collective-permute-start.14 = (bf16[16,2,32,128]{3,2,1,0:T(8,128)(2,1)}, bf16[16,2,32,128]{3,2,1,0:T(8,128)(2,1)S(1)}, u32[]{:S(2)}, u32[]{:S(2)}) collective-permute-start(bf16[16,2,32,128]{3,2,1,0:T(8,128)(2,1)} %collective-permute-done.11.refs_0_), channel_id=1, source_target_pairs={{0,1},{1,0},{2,3},{3,2},{4,5},{5,4},{6,7},{7,6},{8,9},{9,8},{10,11... | collective-permute-start | bytes 786440 | tf_op jit(solution)/shard_map/ppermute | solution.py:345
  109.3 13.7 %collective-permute-start.15 = (bf16[16,2,32,128]{3,2,1,0:T(8,128)(2,1)}, bf16[16,2,32,128]{3,2,1,0:T(8,128)(2,1)S(1)}, u32[]{:S(2)}, u32[]{:S(2)}) collective-permute-start(bf16[16,2,32,128]{3,2,1,0:T(8,128)(2,1)} %collective-permute-done.12.refs_1_), channel_id=1, source_target_pairs={{0,1},{1,0},{2,3},{3,2},{4,5},{5,4},{6,7},{7,6},{8,9},{9,8},{10,11... | collective-permute-start | bytes 786440 | tf_op jit(solution)/shard_map/ppermute | solution.py:346
  132.6 5.6 %collective-permute-start.21 = (bf16[3,32,1024]{2,1,0:T(8,128)(2,1)}, bf16[3,32,1024]{2,1,0:T(8,128)(2,1)S(1)}, u32[]{:S(2)}, u32[]{:S(2)}) collective-permute-start(bf16[3,32,1024]{2,1,0:T(8,128)(2,1)} %get-tuple-element.29), channel_id=1, source_target_pairs={{0,112},{16,0},{32,16},{48,32},{64,48},{80,64},{96,80},{112,96},{1... | collective-permute-start | bytes 589832 | tf_op jit(solution)/shard_map/ppermute | solution.py:280
  135.2 7.2 %collective-permute-start.17 = (bf16[3,32,1024]{2,1,0:T(8,128)(2,1)}, bf16[3,32,1024]{2,1,0:T(8,128)(2,1)S(1)}, u32[]{:S(2)}, u32[]{:S(2)}) collective-permute-start(bf16[3,32,1024]{2,1,0:T(8,128)(2,1)} %get-tuple-element.25), channel_id=1, source_target_pairs={{0,16},{16,32},{32,48},{48,64},{64,80},{80,96},{96,112},{112,0},{1... | collective-permute-start | bytes 589832 | tf_op jit(solution)/shard_map/ppermute | solution.py:279
  139.3 7.8 %collective-permute-start.22 = (bf16[2,3,32,1024]{3,2,1,0:T(8,128)(2,1)S(1)}, bf16[2,3,32,1024]{3,2,1,0:T(8,128)(2,1)S(1)}, u32[]{:S(2)}, u32[]{:S(2)}) collective-permute-start(bf16[2,3,32,1024]{3,2,1,0:T(8,128)(2,1)S(1)} %add_convert_fusion.2), channel_id=1, source_target_pairs={{0,112},{16,0},{32,16},{48,32},{64,48},{80,64},{96,80},{112,96},{1... | collective-permute-start | bytes 1179656 | tf_op jit(solution)/shard_map/ppermute | solution.py:283
  143.5 7.9 %collective-permute-start.18 = (bf16[2,3,32,1024]{3,2,1,0:T(8,128)(2,1)S(1)}, bf16[2,3,32,1024]{3,2,1,0:T(8,128)(2,1)S(1)}, u32[]{:S(2)}, u32[]{:S(2)}) collective-permute-start(bf16[2,3,32,1024]{3,2,1,0:T(8,128)(2,1)S(1)} %add_convert_fusion.5), channel_id=1, source_target_pairs={{0,16},{16,32},{32,48},{48,64},{64,80},{80,96},{96,112},{112,0},{1... | collective-permute-start | bytes 1179656 | tf_op jit(solution)/shard_map/ppermute | solution.py:282
  147.3 9.8 %collective-permute-start.23 = (bf16[2,3,32,1024]{3,2,1,0:T(8,128)(2,1)S(1)}, bf16[2,3,32,1024]{3,2,1,0:T(8,128)(2,1)S(1)}, u32[]{:S(2)}, u32[]{:S(2)}) collective-permute-start(bf16[2,3,32,1024]{3,2,1,0:T(8,128)(2,1)S(1)} %add_convert_fusion.1), channel_id=1, source_target_pairs={{0,112},{16,0},{32,16},{48,32},{64,48},{80,64},{96,80},{112,96},{1... | collective-permute-start | bytes 1179656 | tf_op jit(solution)/shard_map/ppermute | solution.py:283
  152.3 9.3 %collective-permute-start.19 = (bf16[2,3,32,1024]{3,2,1,0:T(8,128)(2,1)}, bf16[2,3,32,1024]{3,2,1,0:T(8,128)(2,1)S(1)}, u32[]{:S(2)}, u32[]{:S(2)}) collective-permute-start(bf16[2,3,32,1024]{3,2,1,0:T(8,128)(2,1)} %add_convert_fusion.4), channel_id=1, source_target_pairs={{0,16},{16,32},{32,48},{48,64},{64,80},{80,96},{96,112},{112,0},{1... | collective-permute-start | bytes 1179656 | tf_op jit(solution)/shard_map/ppermute | solution.py:282
  157.2 10.9 %collective-permute-start.24 = (bf16[2,3,32,1024]{3,2,1,0:T(8,128)(2,1)S(1)}, bf16[2,3,32,1024]{3,2,1,0:T(8,128)(2,1)S(1)}, u32[]{:S(2)}, u32[]{:S(2)}) collective-permute-start(bf16[2,3,32,1024]{3,2,1,0:T(8,128)(2,1)S(1)} %add_convert_fusion), channel_id=1, source_target_pairs={{0,112},{16,0},{32,16},{48,32},{64,48},{80,64},{96,80},{112,96},{1... | collective-permute-start | bytes 1179656 | tf_op jit(solution)/shard_map/ppermute | solution.py:283
  161.8 11.1 %collective-permute-start.20 = (bf16[2,3,32,1024]{3,2,1,0:T(8,128)(2,1)S(1)}, bf16[2,3,32,1024]{3,2,1,0:T(8,128)(2,1)S(1)}, u32[]{:S(2)}, u32[]{:S(2)}) collective-permute-start(bf16[2,3,32,1024]{3,2,1,0:T(8,128)(2,1)S(1)} %add_convert_fusion.3), channel_id=1, source_target_pairs={{0,16},{16,32},{32,48},{48,64},{64,80},{80,96},{96,112},{112,0},{1... | collective-permute-start | bytes 1179656 | tf_op jit(solution)/shard_map/ppermute | solution.py:282
  175.8 17.6 %collective-permute-start.25 = (bf16[3,32,1024]{2,1,0:T(8,128)(2,1)}, bf16[3,32,1024]{2,1,0:T(8,128)(2,1)S(1)}, u32[]{:S(2)}, u32[]{:S(2)}) collective-permute-start(bf16[3,32,1024]{2,1,0:T(8,128)(2,1)} %get-tuple-element.31), channel_id=1, source_target_pairs={{0,8},{8,0},{1,9},{9,1},{2,10},{10,2},{3,11},{11,3},{4,12},{12,4},... | collective-permute-start | bytes 589832 | tf_op jit(solution)/shard_map/ppermute | solution.py:435
  184.6 13.8 %collective-permute-start.27 = (bf16[3,32,1024]{2,1,0:T(8,128)(2,1)}, bf16[3,32,1024]{2,1,0:T(8,128)(2,1)S(1)}, u32[]{:S(2)}, u32[]{:S(2)}) collective-permute-start(bf16[3,32,1024]{2,1,0:T(8,128)(2,1)} %get-tuple-element.31), channel_id=1, source_target_pairs={{0,137},{1,136},{8,129},{9,128},{2,139},{3,138},{10,131},{11,130},... | collective-permute-start | bytes 589832 | tf_op jit(solution)/shard_map/ppermute | solution.py:437
  189.8 8.6 %collective-permute-start.26 = (bf16[3,32,1024]{2,1,0:T(8,128)(2,1)}, bf16[3,32,1024]{2,1,0:T(8,128)(2,1)S(1)}, u32[]{:S(2)}, u32[]{:S(2)}) collective-permute-start(bf16[3,32,1024]{2,1,0:T(8,128)(2,1)} %get-tuple-element.30.near), channel_id=1, source_target_pairs={{0,129},{1,128},{2,131},{3,130},{4,133},{5,132},{6,135},{7,134},{8... | collective-permute-start | bytes 589832 | tf_op jit(solution)/shard_map/ppermute | solution.py:436
  (25 other events, 207.8 us)

commit v6 on v5

--- a/solution.py
+++ b/solution.py
@@ -1,5 +1,3 @@
-import functools
-
 import jax
 import jax.numpy as jnp
 from jax import lax
@@ -44,45 +42,6 @@
         cost_estimate=pl.CostEstimate(flops=0, bytes_accessed=1600000, transcendentals=0),
         name="arrange",
     )(teacher_slabs)
-
-
-def choose_kernel(count, section, first, second, *refs):
-    afters, out, sem, spares = refs[:count], refs[count], refs[count + 1], refs[count + 2 :]
-    copies = [
-        pltpu.make_async_copy(ref, spare, sem.at[1 + index])
-        for index, (ref, spare) in enumerate(zip(afters, spares))
-    ]
-    for copy in copies:
-        copy.start()
-
-    @pl.when(section[0] == 0)
-    def _():
-        copy = pltpu.make_async_copy(first, out, sem.at[0])
-        copy.start()
-        copy.wait()
-
-    @pl.when(section[0] != 0)
-    def _():
-        copy = pltpu.make_async_copy(second, out, sem.at[0])
-        copy.start()
-        copy.wait()
-
-    for copy in copies:
-        copy.wait()
-
-
-def choose(yh, first, second, after=()):
-    after = [array[:1] for array in after]
-    return pl.pallas_call(
-        functools.partial(choose_kernel, len(after)),
-        out_shape=jax.ShapeDtypeStruct(first.shape, first.dtype),
-        in_specs=[pl.BlockSpec(memory_space=pltpu.SMEM)] + [pl.BlockSpec(memory_space=pl.ANY)] * (2 + len(after)),
-        out_specs=pl.BlockSpec(memory_space=pltpu.VMEM),
-        scratch_shapes=[pltpu.SemaphoreType.DMA((1 + len(after),))]
-        + [pltpu.VMEM(array.shape, array.dtype) for array in after],
-        cost_estimate=pl.CostEstimate(flops=0, bytes_accessed=4 * first.size, transcendentals=0),
-        name="choose",
-    )(yh.reshape(1).astype(jnp.int32), first, second, *after)
 
 
 def pick_kernel(layer_map, received, picked, low, high):
@@ -329,7 +288,7 @@
     )(jnp.stack([c, own_count]).astype(jnp.int32), hidden, layer_grad, *pieces)
 
 
-def gather_tensor(own, low, high):
+def gather_tensor(own, low, high, before):
     up = [(i, (i + 1) % X) for i in range(X)]
     down = [(i, (i - 1) % X) for i in range(X)]
     swap = [(0, 1), (1, 0)]
@@ -338,6 +297,7 @@
     g0 = lax.ppermute(own, "yl", swap)
     f3b = lax.ppermute(high, "x", up)
     f1a = lax.ppermute(low, "x", down)
+    f3a, _ = lax.optimization_barrier((f3a, before))
     f2a = lax.ppermute(f3a, "x", up)
     f2b = lax.ppermute(f1b, "x", down)
     g3 = lax.ppermute(g0, "x", up)
@@ -370,11 +330,8 @@
 
     swap = [(0, 1), (1, 0)]
     side = ("yh", "yl")
-    across_y = [(0, 3), (1, 2)]
-    w_row = lax.ppermute(proj_weight, side, [(0, 1), (1, 0)])
-    w_child = lax.ppermute(proj_weight, side, [(3, 0), (2, 1)])
-    w_teacher = lax.ppermute(w_row, side, across_y)
-    w_near = choose(yh, w_row, proj_weight)
+    w_sib = lax.ppermute(proj_weight, "c", swap)
+    w_row = lax.ppermute(proj_weight, "yl", swap)
     place = jnp.stack([2 * yh + c, 2 * yh + 1 - c, 2 * (1 - yh) + c, 2 * (1 - yh) + 1 - c]).astype(jnp.int32)
 
     is_child = yh == 1
@@ -387,15 +344,27 @@
     delta_norm = delta_norm + lax.dot_general(
         value_cotangent[0], value_weight[0], contract_last, preferred_element_type=jnp.float32
     )
-    sums = lax.psum(
-        jnp.stack(
-            [
-                jnp.sum(first_hidden * first_hidden, axis=1),
-                jnp.sum(first_hidden * norm_scale * delta_norm, axis=1),
-            ]
-        ),
-        TENSOR,
-    )
+    sums = jnp.stack(
+        [
+            jnp.sum(first_hidden * first_hidden, axis=1),
+            jnp.sum(first_hidden * norm_scale * delta_norm, axis=1),
+        ]
+    )
+    sums = sums + lax.ppermute(sums, "x", [(i, i ^ 1) for i in range(X)])
+    sums = sums + lax.ppermute(sums, "x", [(i, i ^ 2) for i in range(X)])
+    sums = sums + lax.ppermute(sums, "yl", swap)
+    sent = lax.ppermute(arrange(teacher_slabs, 1), side, [(0, 3), (1, 2)])
+    w_row, _ = lax.optimization_barrier((w_row, sent))
+    w_far = lax.ppermute(w_row, side, [(0, 3), (3, 0), (1, 2), (2, 1)])
+    arranged = jnp.where(yh == 0, arrange(teacher_slabs, 0), sent)
+    arranged, w_sib, sums = lax.optimization_barrier((arranged, w_sib, sums))
+    received = lax.all_to_all(arranged, ("z", "c"), split_axis=0, concat_axis=0, tiled=True)
+    received = received.reshape(Z * C * slab_count, YH, quarter, LANES)
+
+    received, w_far = lax.optimization_barrier((received, w_far))
+    w_far_sib = lax.ppermute(w_far, "c", swap)
+    weights = (proj_weight, w_sib, w_far, w_far_sib)
+    first_features, rest_features = gather_tensor(*pick(layer_map, received), w_far_sib)
     squares, inner_sum = sums[0], sums[1]
     inverse_rms = lax.rsqrt(squares / full_width + EPSILON)[:, None]
     normed = (first_hidden * inverse_rms * norm_scale).astype(jnp.bfloat16)
@@ -412,15 +381,6 @@
         - first_hidden * inverse_rms**3 * inner_sum[:, None] / full_width
     )
     layer_grad = jnp.where(is_child, layer_grad, 0.0)
-    sent = lax.ppermute(arrange(teacher_slabs, 1), side, across_y)
-    arranged = choose(yh, arrange(teacher_slabs, 0), sent, (sums, w_row))
-    received = lax.all_to_all(arranged, ("z", "c"), split_axis=0, concat_axis=0, tiled=True)
-    received = received.reshape(Z * C * slab_count, YH, quarter, LANES)
-
-    picked, low, high = pick(layer_map, received)
-    w_far = choose(yh, w_child, w_teacher, (low,))
-    weights = (w_near, lax.ppermute(w_near, "c", swap), w_far, lax.ppermute(w_far, "c", swap))
-    first_features, rest_features = gather_tensor(picked, low, high)
     first_blocks, rest_blocks = (
         jnp.stack([(x + step) % X * YL + (yl + yh + other) % YL for step, other in places]).astype(jnp.int32)
         for places in (FIRST, REST)
@@ -433,8 +393,8 @@
     chunks = project_rest(place, rest_blocks, slot_layer, partial, rest_features, weights)
     kept, given = combine(c, *reduce_z(chunks))
     across = lax.ppermute(given, "c", swap)
-    teacher = lax.ppermute(kept, side, across_y)
-    teacher_across = lax.ppermute(given, ("yh", "c", "yl"), [(0, 7), (1, 6), (2, 5), (3, 4)])
+    teacher = lax.ppermute(kept, "yh", [(0, 1)])
+    teacher_across = lax.ppermute(given, ("yh", "c"), [(0, 3), (1, 2)])
     own_count = jnp.where(is_child, layer_counts[2 * z + c], 0)
     hidden_grad = finish(c, own_count, child_hidden, layer_grad, (kept, across, teacher, teacher_across))
     key_grad = jnp.where(is_child, key_grad, jnp.zeros_like(key_grad))

time: 203 us -> 188 us (0.926)
  waiting for transfers between devices: 50.1 us -> 77.4 us
  blocking collectives: 19.9 us -> 0 us
  starting transfers between devices: 66.4 us -> 57.4 us
  Pallas kernels: 34.1 us -> 26 us
  local copies, waits for them, and re-layouts: 13.6 us -> 6.12 us
    ppermute x8 -> x10, waiting for transfers between devices: 7.69 us -> 50.4 us  [the longest x1 26.1 us: body(): w_far = lax.ppermute(w_row, side, [(0, 3), (3, 0), (1, 2), (2, 1)])]
    psum x1 -> x0, blocking collectives: 19.9 us -> none  [body(): lax.psum(jnp.stack([jnp.sum(first_hidden * first_hidden, axis=1), jnp.sum...]
    all_to_all x1, waiting for transfers between devices: 11.2 us -> 0.01 us  [body(): lax.all_to_all(arranged, ('z', 'c'), split_axis=0, concat_axis=0, tiled=T...]
    ppermute x8 -> x10, starting transfers between devices: 25.4 us -> 17.1 us  [the longest x1 6.5 us: body(): sent = lax.ppermute(arrange(teacher_slabs, 1), side, [(0, 3), (1, 2)])]
    pallas_call x3 -> x0, Pallas kernels: 6.58 us -> none  [choose(): pl.pallas_call(functools.partial(choose_kernel, len(after)), out_shape=ja...]
    ppermute x1, waiting for transfers between devices: 5.84 us -> 0.96 us  [gather_tensor(): f1a = lax.ppermute(low, 'x', down)]
    unnamed x56 -> x48, local copies, waits for them, and re-layouts: 7.84 us -> 3.92 us
    slice x3 -> x0, local copies, waits for them, and re-layouts: 3.51 us -> none  [the longest x2 2.92 us: choose(): after = [array[:1] for array in after]]
  transfers between devices with their start and end apart: 29 -> 31, of which waited for: 14 -> 15; matrix products, arithmetic and copies ran while one was open for 11% -> 11% of each run, Pallas kernels for 9% -> 5%
where the time goes in v6:
time: 188 us; the launch traced here: 186 us
  waiting for transfers between devices  77.4 us (41%)
  starting transfers between devices  57.4 us (31%)
  Pallas kernels  26 us (14%)
  matrix products  9.32 us (5%)
  other arithmetic  8.14 us (4%)
  local copies, waits for them, and re-layouts  6.12 us (3%)
    ppermute x1, waiting for transfers between devices, body(): w_far = lax.ppermute(w_row, side, [(0, 3), (3, 0), (1, 2), (2, 1)])  26.1 us
    ppermute x1, waiting for transfers between devices, body(): sums = sums + lax.ppermute(sums, 'yl', swap)  16.8 us
    ppermute x3, starting transfers between devices, reduce_z(): from_above = lax.ppermute(add(to_down, from_above), 'z', down)  9.99 us
    all_to_all x1, starting transfers between devices, body(): lax.all_to_all(arranged, ('z', 'c'), split_axis=0, concat_axis=0, tiled=T...  9.6 us
    pallas_call x1, Pallas kernels, project_rest(): pl.pallas_call(project_rest_kernel, out_shape=[jax.ShapeDtypeStruct(shape...  8.84 us
    ppermute x3, waiting for transfers between devices, reduce_z(): from_above = lax.ppermute(add(to_down, from_above), 'z', down)  8.45 us
    ppermute x1, starting transfers between devices, body(): across = lax.ppermute(given, 'c', swap)  6.53 us
    ppermute x1, starting transfers between devices, body(): sent = lax.ppermute(arrange(teacher_slabs, 1), side, [(0, 3), (1, 2)])  6.5 us
  transfers between devices with their start and end apart: 31, of which 15 were waited for; matrix products, arithmetic and copies ran while one was open for 11% of the time, Pallas kernels for 5%

profile of v6, /device:TPU:1, one launch (start us, length us, event | category | flops | bytes accessed | tf_op | source)
XLA Modules:
  0.0 186.1 jit_solution(14964140724577824680)
XLA Ops:
  0.7 2.3 %arrange.3 = bf16[16,192,128]{2,1,0:T(8,128)(2,1)} custom-call(bf16[3,128,2048]{2,1,0:T(8,128)(2,1)} %slabs.3), custom_call_target="tpu_custom_call" | custom-call | bytes 1600000 | tf_op jit(solution)/shard_map/arrange/pallas_call | solution.py:36
  3.0 6.5 %collective-permute-start = (bf16[16,192,128]{2,1,0:T(8,128)(2,1)}, bf16[16,192,128]{2,1,0:T(8,128)(2,1)}, u32[]{:S(2)}, u32[]{:S(2)}) collective-permute-start(bf16[16,192,128]{2,1,0:T(8,128)(2,1)} %arrange.3), channel_id=1, source_target_pairs={{0,129},{1,128},{2,131},{3,130},{4,133},{5,132},{6,135},{7,134},{8... | collective-permute-start | bytes 2359304 | tf_op jit(solution)/shard_map/ppermute | solution.py:356
  10.4 2.4 %fusion = f32[128,1024]{1,0:T(8,128)S(1)} fusion(bf16[1,1024,1024]{2,1,0:T(8,128)(2,1)} %param.16, bf16[1,128,1024]{2,1,0:T(8,128)(2,1)S(1)} %copy-done.16), kind=kOutput, calls=%fused_computation.1 | convolution fusion | flops 268435456 | bytes 2883584 | tf_op jit(solution)/shard_map/dot_general | solution.py:344
  12.9 2.6 %fusion.11 = (f32[128]{0:T(128)S(1)}, f32[128]{0:T(128)S(1)}, f32[128,1024]{1,0:T(8,128)}) fusion(bf16[3,128,1024]{2,1,0:T(8,128)(2,1)} %hidden.1, f32[1024]{0:T(1024)S(1)} %bitcast.90, f32[128,1024]{1,0:T(8,128)S(1)} %fusion, bf16[1,1024,1024]{2,1,0:T(8,128)(2,1)S(1)} %copy-done.8, bf16[1,128,1024]{2,1,0:T(8,128)(2,1)S(1)} %copy-done), kind=kOutput, calls=%fused_computation.21 | convolution fusion | flops 269352704 | bytes 3675136 | tf_op jit(solution)/shard_map/dot_general | solution.py:341
  18.0 2.8 %collective-permute-start.3 = (f32[2,128]{1,0:T(2,128)S(1)}, f32[2,128]{1,0:T(2,128)S(1)}, u32[]{:S(2)}, u32[]{:S(2)}) collective-permute-start(f32[2,128]{1,0:T(2,128)S(1)} %fusion.30), channel_id=1, source_target_pairs={{0,4},{2,6},{4,0},{6,2},{1,5},{3,7},{5,1},{7,3},{8,12},{10,14},{12... | collective-permute-start | bytes 3080 | tf_op jit(solution)/shard_map/ppermute | solution.py:354
  22.4 2.1 %arrange.2 = bf16[16,192,128]{2,1,0:T(8,128)(2,1)} custom-call(bf16[3,128,2048]{2,1,0:T(8,128)(2,1)} %slabs.3), custom_call_target="tpu_custom_call" | custom-call | bytes 1600000 | tf_op jit(solution)/shard_map/arrange/pallas_call | solution.py:36
  24.5 16.8 %collective-permute-done.4 = f32[2,128]{1,0:T(2,128)S(1)} collective-permute-done((f32[2,128]{1,0:T(2,128)S(1)}, f32[2,128]{1,0:T(2,128)S(1)}, u32[]{:S(2)}, u32[]{:S(2)}) %collective-permute-start.4) | collective-permute-done | bytes 1056 | tf_op jit(solution)/shard_map/ppermute | solution.py:355
  41.4 2.1 %broadcast_select_fusion = bf16[16,192,128]{2,1,0:T(8,128)(2,1)} fusion(bf16[16,192,128]{2,1,0:T(8,128)(2,1)} %arrange.2, bf16[16,192,128]{2,1,0:T(8,128)(2,1)} %collective-permute-done, pred[]{:T(512)S(6)} %eq.26), kind=kLoop, calls=%fused_computation.14 | loop fusion | flops 393216 | bytes 2359297 | tf_op jit(solution)/shard_map/jit(_where)/select_n | solution.py:359
  43.5 9.6 %all-to-all-start = ((bf16[16,192,128]{2,1,0:T(8,128)(2,1)}), bf16[16,192,128]{2,1,0:T(8,128)(2,1)}, u32[]{:S(2)}, u32[]{:S(2)}) async-start(bf16[16,192,128]{2,1,0:T(8,128)(2,1)} %broadcast_select_fusion), calls=%async_computation | async-start | bytes 1572864 | tf_op jit(solution)/shard_map/all_to_all | solution.py:361
  53.2 26.1 %collective-permute-done.6.refs_8_ = bf16[8,64,1024]{2,1,0:T(8,128)(2,1)} collective-permute-done((bf16[8,64,1024]{2,1,0:T(8,128)(2,1)}, bf16[8,64,1024]{2,1,0:T(8,128)(2,1)}, u32[]{:S(2)}, u32[]{:S(2)}) %collective-permute-start.6) | collective-permute-done | bytes 1048608 | tf_op jit(solution)/shard_map/ppermute | solution.py:358
  80.9 2.3 %pick_layers.1 = (bf16[32,2,32,128]{3,2,1,0:T(8,128)(2,1)}, bf16[16,2,32,128]{3,2,1,0:T(8,128)(2,1)}, bf16[16,2,32,128]{3,2,1,0:T(8,128)(2,1)}) custom-call(s32[32]{0:T(128)} %layer_map.1, bf16[48,2,32,128]{3,2,1,0:T(8,128)(2,1)} %bitcast.26.received), custom_call_target="tpu_custom_call" | custom-call | bytes 1300000 | tf_op jit(solution)/shard_map/pick_layers/pallas_call | solution.py:65
  83.5 2.4 %collective-permute-start.8 = (bf16[16,2,32,128]{3,2,1,0:T(8,128)(2,1)}, bf16[16,2,32,128]{3,2,1,0:T(8,128)(2,1)}, u32[]{:S(2)}, u32[]{:S(2)}) collective-permute-start(bf16[16,2,32,128]{3,2,1,0:T(8,128)(2,1)} %get-tuple-element.31), channel_id=1, source_target_pairs={{0,6},{2,0},{4,2},{6,4},{1,7},{3,1},{5,3},{7,5},{8,14},{10,8},{12,... | collective-permute-start | bytes 786440 | tf_op jit(solution)/shard_map/ppermute | solution.py:296
  86.0 6.2 %collective-permute-done.8.refs_2_ = bf16[16,2,32,128]{3,2,1,0:T(8,128)(2,1)} collective-permute-done((bf16[16,2,32,128]{3,2,1,0:T(8,128)(2,1)}, bf16[16,2,32,128]{3,2,1,0:T(8,128)(2,1)}, u32[]{:S(2)}, u32[]{:S(2)}) %collective-permute-start.8) | collective-permute-done | bytes 262176 | tf_op jit(solution)/shard_map/ppermute | solution.py:296
  92.1 2.9 %collective-permute-start.14 = (bf16[16,2,32,128]{3,2,1,0:T(8,128)(2,1)}, bf16[16,2,32,128]{3,2,1,0:T(8,128)(2,1)}, u32[]{:S(2)}, u32[]{:S(2)}) collective-permute-start(bf16[16,2,32,128]{3,2,1,0:T(8,128)(2,1)} %collective-permute-done.8.refs_2_), channel_id=1, source_target_pairs={{0,6},{2,0},{4,2},{6,4},{1,7},{3,1},{5,3},{7,5},{8,14},{10,8},{12,... | collective-permute-start | bytes 786440 | tf_op jit(solution)/shard_map/ppermute | solution.py:302
  96.3 2.7 %collective-permute-start.7 = (bf16[16,2,32,128]{3,2,1,0:T(8,128)(2,1)}, bf16[16,2,32,128]{3,2,1,0:T(8,128)(2,1)}, u32[]{:S(2)}, u32[]{:S(2)}) collective-permute-start(bf16[16,2,32,128]{3,2,1,0:T(8,128)(2,1)} %get-tuple-element.30), channel_id=1, source_target_pairs={{0,6},{2,0},{4,2},{6,4},{1,7},{3,1},{5,3},{7,5},{8,14},{10,8},{12,... | collective-permute-start | bytes 786440 | tf_op jit(solution)/shard_map/ppermute | solution.py:299
  106.6 5.7 %project_first.1.partial = bf16[4,256,1024]{2,1,0:T(8,128)(2,1)S(1)} custom-call(s32[4]{0:T(128)S(1)} %get-tuple-element.53.place, s32[4]{0:T(128)S(1)} %get-tuple-element.54.blocks, bf16[32,2,32,128]{3,2,1,0:T(8,128)(2,1)S(1)} %copy-done.4, bf16[16,2,32,128]{3,2,1,0:T(8,128)(2,1)} %collective-permute-done.7.refs_1_, ...), custom_call_target="tpu_custom_call" | custom-call | flops 2147483648 | bytes 8388608 | tf_op jit(solution)/shard_map/project_first/pallas_call | solution.py:181
  113.7 3.0 %collective-permute-done.15.refs_2_ = bf16[32,2,32,128]{3,2,1,0:T(8,128)(2,1)} collective-permute-done((bf16[32,2,32,128]{3,2,1,0:T(8,128)(2,1)S(1)}, bf16[32,2,32,128]{3,2,1,0:T(8,128)(2,1)}, u32[]{:S(2)}, u32[]{:S(2)}) %collective-permute-start.15) | collective-permute-done | bytes 524320 | tf_op jit(solution)/shard_map/ppermute | solution.py:304
  116.7 8.8 %project_rest.1 = (bf16[3,32,1024]{2,1,0:T(8,128)(2,1)}, bf16[3,32,1024]{2,1,0:T(8,128)(2,1)}, bf16[2,3,32,1024]{3,2,1,0:T(8,128)(2,1)}, bf16[2,3,32,1024]{3,2,1...) custom-call(s32[4]{0:T(128)} %copy-done.5, ...), custom_call_target="tpu_custom_call" | custom-call | flops 2147483648 | bytes 11534336 | tf_op jit(solution)/shard_map/project_rest/pallas_call | solution.py:207
  125.6 2.7 %collective-permute-start.23 = (bf16[3,32,1024]{2,1,0:T(8,128)(2,1)}, bf16[3,32,1024]{2,1,0:T(8,128)(2,1)S(1)}, u32[]{:S(2)}, u32[]{:S(2)}) collective-permute-start(bf16[3,32,1024]{2,1,0:T(8,128)(2,1)} %get-tuple-element.43), channel_id=1, source_target_pairs={{0,112},{16,0},{32,16},{48,32},{64,48},{80,64},{96,80},{112,96},{1... | collective-permute-start | bytes 589832 | tf_op jit(solution)/shard_map/ppermute | solution.py:239
  128.3 2.9 %collective-permute-done.23 = bf16[3,32,1024]{2,1,0:T(8,128)(2,1)S(1)} collective-permute-done((bf16[3,32,1024]{2,1,0:T(8,128)(2,1)}, bf16[3,32,1024]{2,1,0:T(8,128)(2,1)S(1)}, u32[]{:S(2)}, u32[]{:S(2)}) %collective-permute-start.23) | collective-permute-done | bytes 196640 | tf_op jit(solution)/shard_map/ppermute | solution.py:239
  132.4 3.1 %collective-permute-start.24 = (bf16[2,3,32,1024]{3,2,1,0:T(8,128)(2,1)S(1)}, bf16[2,3,32,1024]{3,2,1,0:T(8,128)(2,1)S(1)}, u32[]{:S(2)}, u32[]{:S(2)}) collective-permute-start(bf16[2,3,32,1024]{3,2,1,0:T(8,128)(2,1)S(1)} %add_convert_fusion.2), channel_id=1, source_target_pairs={{0,112},{16,0},{32,16},{48,32},{64,48},{80,64},{96,80},{112,96},{1... | collective-permute-start | bytes 1179656 | tf_op jit(solution)/shard_map/ppermute | solution.py:242
  136.7 4.1 %collective-permute-done.24 = bf16[2,3,32,1024]{3,2,1,0:T(8,128)(2,1)S(1)} collective-permute-done((bf16[2,3,32,1024]{3,2,1,0:T(8,128)(2,1)S(1)}, bf16[2,3,32,1024]{3,2,1,0:T(8,128)(2,1)S(1)}, u32[]{:S(2)}, u32[]{:S(2)}) %collective-permute-start.24) | collective-permute-done | bytes 393248 | tf_op jit(solution)/shard_map/ppermute | solution.py:242
  140.9 3.5 %collective-permute-start.25 = (bf16[2,3,32,1024]{3,2,1,0:T(8,128)(2,1)S(1)}, bf16[2,3,32,1024]{3,2,1,0:T(8,128)(2,1)S(1)}, u32[]{:S(2)}, u32[]{:S(2)}) collective-permute-start(bf16[2,3,32,1024]{3,2,1,0:T(8,128)(2,1)S(1)} %add_convert_fusion.1), channel_id=1, source_target_pairs={{0,112},{16,0},{32,16},{48,32},{64,48},{80,64},{96,80},{112,96},{1... | collective-permute-start | bytes 1179656 | tf_op jit(solution)/shard_map/ppermute | solution.py:242
  146.4 2.7 %collective-permute-done.25 = bf16[2,3,32,1024]{3,2,1,0:T(8,128)(2,1)S(1)} collective-permute-done((bf16[2,3,32,1024]{3,2,1,0:T(8,128)(2,1)S(1)}, bf16[2,3,32,1024]{3,2,1,0:T(8,128)(2,1)S(1)}, u32[]{:S(2)}, u32[]{:S(2)}) %collective-permute-start.25) | collective-permute-done | bytes 393248 | tf_op jit(solution)/shard_map/ppermute | solution.py:242
  149.3 3.4 %collective-permute-start.26 = (bf16[2,3,32,1024]{3,2,1,0:T(8,128)(2,1)S(1)}, bf16[2,3,32,1024]{3,2,1,0:T(8,128)(2,1)S(1)}, u32[]{:S(2)}, u32[]{:S(2)}) collective-permute-start(bf16[2,3,32,1024]{3,2,1,0:T(8,128)(2,1)S(1)} %add_convert_fusion), channel_id=1, source_target_pairs={{0,112},{16,0},{32,16},{48,32},{64,48},{80,64},{96,80},{112,96},{1... | collective-permute-start | bytes 1179656 | tf_op jit(solution)/shard_map/ppermute | solution.py:242
  153.4 2.1 %select_bitcast_fusion = bf16[1,1024,1024]{2,1,0:T(8,128)(2,1)} fusion(pred[]{:T(512)S(6)} %eq.25, bf16[1,128,1024]{2,1,0:T(8,128)(2,1)S(1)} %copy-done.17, f32[1024]{0:T(1024)S(1)} %bitcast.92, f32[128]{0:T(128)S(1)} %get-tuple-element.49, bf16[3,128,1024]{2,1,0:T(8,128)(2,1)S(1)} %copy-done.6), kind=kOutput, calls=%fused_computation.5 | convolution fusion | flops 271056896 | bytes 2626049 | tf_op jit(solution)/shard_map/dot_general | solution.py:375
  157.8 4.3 %collective-permute-done.22.below = bf16[2,3,32,1024]{3,2,1,0:T(8,128)(2,1)S(1)} collective-permute-done((bf16[2,3,32,1024]{3,2,1,0:T(8,128)(2,1)S(1)}, bf16[2,3,32,1024]{3,2,1,0:T(8,128)(2,1)S(1)}, u32[]{:S(2)}, u32[]{:S(2)}) %collective-permute-start.22) | collective-permute-done | bytes 393248 | tf_op jit(solution)/shard_map/ppermute | solution.py:241
  165.0 6.5 %collective-permute-start.27 = (bf16[3,32,1024]{2,1,0:T(8,128)(2,1)}, bf16[3,32,1024]{2,1,0:T(8,128)(2,1)S(1)}, u32[]{:S(2)}, u32[]{:S(2)}) collective-permute-start(bf16[3,32,1024]{2,1,0:T(8,128)(2,1)} %get-tuple-element.45), channel_id=1, source_target_pairs={{0,8},{8,0},{1,9},{9,1},{2,10},{10,2},{3,11},{11,3},{4,12},{12,4},... | collective-permute-start | bytes 589832 | tf_op jit(solution)/shard_map/ppermute | solution.py:395
  171.5 2.7 %collective-permute-start.29 = (bf16[3,32,1024]{2,1,0:T(8,128)(2,1)}, bf16[3,32,1024]{2,1,0:T(8,128)(2,1)S(1)}, u32[]{:S(2)}, u32[]{:S(2)}) collective-permute-start(bf16[3,32,1024]{2,1,0:T(8,128)(2,1)} %get-tuple-element.45), channel_id=1, source_target_pairs={{0,136},{8,128},{1,137},{9,129},{2,138},{10,130},{3,139},{11,131},... | collective-permute-start | bytes 589832 | tf_op jit(solution)/shard_map/ppermute | solution.py:397
  175.6 2.1 %select_bitcast_fusion.1 = bf16[1,1024,1024]{2,1,0:T(8,128)(2,1)} fusion(pred[]{:T(512)S(6)} %eq.25, bf16[1,128,1024]{2,1,0:T(8,128)(2,1)S(1)} %copy-done, f32[1024]{0:T(1024)S(1)} %bitcast.93, f32[128]{0:T(128)S(1)} %get-tuple-element.49, bf16[3,128,1024]{2,1,0:T(8,128)(2,1)S(1)} %copy-done.6), kind=kOutput, calls=%fused_computation.6 | convolution fusion | flops 271056896 | bytes 2626049 | tf_op jit(solution)/shard_map/dot_general | solution.py:372
  177.7 5.0 %collective-permute-done.28.teacher = bf16[3,32,1024]{2,1,0:T(8,128)(2,1)S(1)} collective-permute-done((bf16[3,32,1024]{2,1,0:T(8,128)(2,1)}, bf16[3,32,1024]{2,1,0:T(8,128)(2,1)S(1)}, u32[]{:S(2)}, u32[]{:S(2)}) %collective-permute-start.28) | collective-permute-done | bytes 196640 | tf_op jit(solution)/shard_map/ppermute | solution.py:396
  183.5 2.6 %finish.1 = bf16[3,128,1024]{2,1,0:T(8,128)(2,1)} custom-call(s32[2]{0:T(128)} %pad_add_fusion.state, bf16[3,128,1024]{2,1,0:T(8,128)(2,1)} %hidden.1, f32[128,1024]{1,0:T(8,128)} %get-tuple-element.51.layer_grad, bf16[3,32,1024]{2,1,0:T(8,128)(2,1)} %get-tuple-element.44.near, bf16[3,32,1024]{2,1,0:T(8,128)(2,1)} %copy-done.18, ...), custom_call_target="tpu_custom_call" | custom-call | flops 786432 | bytes 3145728 | tf_op jit(solution)/shard_map/finish/pallas_call | solution.py:281
  (124 shorter events, 29.1 us)
Async XLA Ops:
  3.0 38.4 %collective-permute-start = (bf16[16,192,128]{2,1,0:T(8,128)(2,1)}, bf16[16,192,128]{2,1,0:T(8,128)(2,1)}, u32[]{:S(2)}, u32[]{:S(2)}) collective-permute-start(bf16[16,192,128]{2,1,0:T(8,128)(2,1)} %arrange.3), channel_id=1, source_target_pairs={{0,129},{1,128},{2,131},{3,130},{4,133},{5,132},{6,135},{7,134},{8... | collective-permute-start | bytes 2359304 | tf_op jit(solution)/shard_map/ppermute | solution.py:356
  9.5 34.1 %collective-permute-start.1 = (bf16[8,64,1024]{2,1,0:T(8,128)(2,1)S(1)}, bf16[8,64,1024]{2,1,0:T(8,128)(2,1)S(1)}, u32[]{:S(2)}, u32[]{:S(2)}) collective-permute-start(bf16[8,64,1024]{2,1,0:T(8,128)(2,1)S(1)} %copy-done.2), channel_id=1, source_target_pairs={{0,8},{8,0},{1,9},{9,1},{2,10},{10,2},{3,11},{11,3},{4,12},{12,4},... | collective-permute-start | bytes 3145736 | tf_op jit(solution)/shard_map/ppermute | solution.py:333
  15.5 2.5 %collective-permute-start.2 = (f32[2,128]{1,0:T(2,128)S(1)}, f32[2,128]{1,0:T(2,128)S(1)}, u32[]{:S(2)}, u32[]{:S(2)}) collective-permute-start(f32[2,128]{1,0:T(2,128)S(1)} %pad_maximum_fusion), channel_id=1, source_target_pairs={{0,2},{2,0},{4,6},{6,4},{1,3},{3,1},{5,7},{7,5},{8,10},{10,8},{12,... | collective-permute-start | bytes 3080 | tf_op jit(solution)/shard_map/ppermute | solution.py:353
  16.8 36.3 %collective-permute-start.5 = (bf16[8,64,1024]{2,1,0:T(8,128)(2,1)S(1)}, bf16[8,64,1024]{2,1,0:T(8,128)(2,1)}, u32[]{:S(2)}, u32[]{:S(2)}) collective-permute-start(bf16[8,64,1024]{2,1,0:T(8,128)(2,1)S(1)} %copy-done.2), channel_id=1, source_target_pairs={{0,1},{1,0},{2,3},{3,2},{4,5},{5,4},{6,7},{7,6},{8,9},{9,8},{10,11... | collective-permute-start | bytes 3145736 | tf_op jit(solution)/shard_map/ppermute | solution.py:334
  18.0 4.0 %collective-permute-start.3 = (f32[2,128]{1,0:T(2,128)S(1)}, f32[2,128]{1,0:T(2,128)S(1)}, u32[]{:S(2)}, u32[]{:S(2)}) collective-permute-start(f32[2,128]{1,0:T(2,128)S(1)} %fusion.30), channel_id=1, source_target_pairs={{0,4},{2,6},{4,0},{6,2},{1,5},{3,7},{5,1},{7,3},{8,12},{10,14},{12... | collective-permute-start | bytes 3080 | tf_op jit(solution)/shard_map/ppermute | solution.py:354
  22.0 19.3 %collective-permute-start.4 = (f32[2,128]{1,0:T(2,128)S(1)}, f32[2,128]{1,0:T(2,128)S(1)}, u32[]{:S(2)}, u32[]{:S(2)}) collective-permute-start(f32[2,128]{1,0:T(2,128)S(1)} %fusion.31), channel_id=1, source_target_pairs={{0,1},{1,0},{2,3},{3,2},{4,5},{5,4},{6,7},{7,6},{8,9},{9,8},{10,11... | collective-permute-start | bytes 3080 | tf_op jit(solution)/shard_map/ppermute | solution.py:355
  43.5 68.8 %copy-start.3 = (bf16[8,64,1024]{2,1,0:T(8,128)(2,1)}, bf16[8,64,1024]{2,1,0:T(8,128)(2,1)S(1)}, u32[]{:S(2)}) copy-start(bf16[8,64,1024]{2,1,0:T(8,128)(2,1)S(1)} %collective-permute-done.1.refs_7_) | copy-start | bytes 3145732
  43.5 35.8 %all-to-all-start = ((bf16[16,192,128]{2,1,0:T(8,128)(2,1)}), bf16[16,192,128]{2,1,0:T(8,128)(2,1)}, u32[]{:S(2)}, u32[]{:S(2)}) async-start(bf16[16,192,128]{2,1,0:T(8,128)(2,1)} %broadcast_select_fusion), calls=%async_computation | async-start | bytes 1572864 | tf_op jit(solution)/shard_map/all_to_all | solution.py:361
  53.1 26.2 %collective-permute-start.6 = (bf16[8,64,1024]{2,1,0:T(8,128)(2,1)}, bf16[8,64,1024]{2,1,0:T(8,128)(2,1)}, u32[]{:S(2)}, u32[]{:S(2)}) collective-permute-start(bf16[8,64,1024]{2,1,0:T(8,128)(2,1)} %collective-permute-done.5), channel_id=1, source_target_pairs={{0,129},{129,0},{1,128},{128,1},{2,131},{131,2},{3,130},{130,3},{4... | collective-permute-start | bytes 3145736 | tf_op jit(solution)/shard_map/ppermute | solution.py:358
  79.3 15.7 %collective-permute-start.10 = (bf16[8,64,1024]{2,1,0:T(8,128)(2,1)}, bf16[8,64,1024]{2,1,0:T(8,128)(2,1)}, u32[]{:S(2)}, u32[]{:S(2)}) collective-permute-start(bf16[8,64,1024]{2,1,0:T(8,128)(2,1)} %collective-permute-done.6.refs_8_), channel_id=1, source_target_pairs={{0,8},{8,0},{1,9},{9,1},{2,10},{10,2},{3,11},{11,3},{4,12},{12,4},... | collective-permute-start | bytes 3145736 | tf_op jit(solution)/shard_map/ppermute | solution.py:365
  83.2 11.8 %collective-permute-start.9 = (bf16[16,2,32,128]{3,2,1,0:T(8,128)(2,1)}, bf16[16,2,32,128]{3,2,1,0:T(8,128)(2,1)S(1)}, u32[]{:S(2)}, u32[]{:S(2)}) collective-permute-start(bf16[16,2,32,128]{3,2,1,0:T(8,128)(2,1)} %get-tuple-element.30), channel_id=1, source_target_pairs={{0,2},{2,4},{4,6},{6,0},{1,3},{3,5},{5,7},{7,1},{8,10},{10,12},{12... | collective-permute-start | bytes 786440 | tf_op jit(solution)/shard_map/ppermute | solution.py:295
  83.5 15.6 %collective-permute-start.12 = (bf16[32,2,32,128]{3,2,1,0:T(8,128)(2,1)}, bf16[32,2,32,128]{3,2,1,0:T(8,128)(2,1)S(1)}, u32[]{:S(2)}, u32[]{:S(2)}) collective-permute-start(bf16[32,2,32,128]{3,2,1,0:T(8,128)(2,1)} %get-tuple-element.29.refs_0_), channel_id=1, source_target_pairs={{0,1},{1,0},{2,3},{3,2},{4,5},{5,4},{6,7},{7,6},{8,9},{9,8},{10,11... | collective-permute-start | bytes 1572872 | tf_op jit(solution)/shard_map/ppermute | solution.py:297
  83.5 8.7 %collective-permute-start.8 = (bf16[16,2,32,128]{3,2,1,0:T(8,128)(2,1)}, bf16[16,2,32,128]{3,2,1,0:T(8,128)(2,1)}, u32[]{:S(2)}, u32[]{:S(2)}) collective-permute-start(bf16[16,2,32,128]{3,2,1,0:T(8,128)(2,1)} %get-tuple-element.31), channel_id=1, source_target_pairs={{0,6},{2,0},{4,2},{6,4},{1,7},{3,1},{5,3},{7,5},{8,14},{10,8},{12,... | collective-permute-start | bytes 786440 | tf_op jit(solution)/shard_map/ppermute | solution.py:296
  85.9 13.5 %collective-permute-start.11 = (bf16[16,2,32,128]{3,2,1,0:T(8,128)(2,1)}, bf16[16,2,32,128]{3,2,1,0:T(8,128)(2,1)}, u32[]{:S(2)}, u32[]{:S(2)}) collective-permute-start(bf16[16,2,32,128]{3,2,1,0:T(8,128)(2,1)} %get-tuple-element.31), channel_id=1, source_target_pairs={{0,2},{2,4},{4,6},{6,0},{1,3},{3,5},{5,7},{7,1},{8,10},{10,12},{12... | collective-permute-start | bytes 786440 | tf_op jit(solution)/shard_map/ppermute | solution.py:298
  92.1 10.3 %collective-permute-start.14 = (bf16[16,2,32,128]{3,2,1,0:T(8,128)(2,1)}, bf16[16,2,32,128]{3,2,1,0:T(8,128)(2,1)}, u32[]{:S(2)}, u32[]{:S(2)}) collective-permute-start(bf16[16,2,32,128]{3,2,1,0:T(8,128)(2,1)} %collective-permute-done.8.refs_2_), channel_id=1, source_target_pairs={{0,6},{2,0},{4,2},{6,4},{1,7},{3,1},{5,3},{7,5},{8,14},{10,8},{12,... | collective-permute-start | bytes 786440 | tf_op jit(solution)/shard_map/ppermute | solution.py:302
  95.1 8.6 %collective-permute-start.13 = (bf16[16,2,32,128]{3,2,1,0:T(8,128)(2,1)S(1)}, bf16[16,2,32,128]{3,2,1,0:T(8,128)(2,1)}, u32[]{:S(2)}, u32[]{:S(2)}) collective-permute-start(bf16[16,2,32,128]{3,2,1,0:T(8,128)(2,1)S(1)} %collective-permute-done.9.refs_3_), channel_id=1, source_target_pairs={{0,2},{2,4},{4,6},{6,0},{1,3},{3,5},{5,7},{7,1},{8,10},{10,12},{12... | collective-permute-start | bytes 786440 | tf_op jit(solution)/shard_map/ppermute | solution.py:301
  96.3 9.2 %collective-permute-start.7 = (bf16[16,2,32,128]{3,2,1,0:T(8,128)(2,1)}, bf16[16,2,32,128]{3,2,1,0:T(8,128)(2,1)}, u32[]{:S(2)}, u32[]{:S(2)}) collective-permute-start(bf16[16,2,32,128]{3,2,1,0:T(8,128)(2,1)} %get-tuple-element.30), channel_id=1, source_target_pairs={{0,6},{2,0},{4,2},{6,4},{1,7},{3,1},{5,3},{7,5},{8,14},{10,8},{12,... | collective-permute-start | bytes 786440 | tf_op jit(solution)/shard_map/ppermute | solution.py:299
  99.1 17.6 %collective-permute-start.15 = (bf16[32,2,32,128]{3,2,1,0:T(8,128)(2,1)S(1)}, bf16[32,2,32,128]{3,2,1,0:T(8,128)(2,1)}, u32[]{:S(2)}, u32[]{:S(2)}) collective-permute-start(bf16[32,2,32,128]{3,2,1,0:T(8,128)(2,1)S(1)} %collective-permute-done.12.refs_5_), channel_id=1, source_target_pairs={{0,6},{2,0},{4,2},{6,4},{1,7},{3,1},{5,3},{7,5},{8,14},{10,8},{12,... | collective-permute-start | bytes 1572872 | tf_op jit(solution)/shard_map/ppermute | solution.py:304
  99.5 17.2 %collective-permute-start.18 = (bf16[32,2,32,128]{3,2,1,0:T(8,128)(2,1)S(1)}, bf16[32,2,32,128]{3,2,1,0:T(8,128)(2,1)}, u32[]{:S(2)}, u32[]{:S(2)}) collective-permute-start(bf16[32,2,32,128]{3,2,1,0:T(8,128)(2,1)S(1)} %collective-permute-done.12.refs_5_), channel_id=1, source_target_pairs={{0,2},{2,4},{4,6},{6,0},{1,3},{3,5},{5,7},{7,1},{8,10},{10,12},{12... | collective-permute-start | bytes 1572872 | tf_op jit(solution)/shard_map/ppermute | solution.py:303
  102.5 11.2 %collective-permute-start.17 = (bf16[16,2,32,128]{3,2,1,0:T(8,128)(2,1)}, bf16[16,2,32,128]{3,2,1,0:T(8,128)(2,1)S(1)}, u32[]{:S(2)}, u32[]{:S(2)}) collective-permute-start(bf16[16,2,32,128]{3,2,1,0:T(8,128)(2,1)} %collective-permute-done.14.refs_1_), channel_id=1, source_target_pairs={{0,1},{1,0},{2,3},{3,2},{4,5},{5,4},{6,7},{7,6},{8,9},{9,8},{10,11... | collective-permute-start | bytes 786440 | tf_op jit(solution)/shard_map/ppermute | solution.py:306
  103.7 13.0 %collective-permute-start.16 = (bf16[16,2,32,128]{3,2,1,0:T(8,128)(2,1)}, bf16[16,2,32,128]{3,2,1,0:T(8,128)(2,1)}, u32[]{:S(2)}, u32[]{:S(2)}) collective-permute-start(bf16[16,2,32,128]{3,2,1,0:T(8,128)(2,1)} %collective-permute-done.13.refs_0_), channel_id=1, source_target_pairs={{0,1},{1,0},{2,3},{3,2},{4,5},{5,4},{6,7},{7,6},{8,9},{9,8},{10,11... | collective-permute-start | bytes 786440 | tf_op jit(solution)/shard_map/ppermute | solution.py:305
  125.6 5.6 %collective-permute-start.23 = (bf16[3,32,1024]{2,1,0:T(8,128)(2,1)}, bf16[3,32,1024]{2,1,0:T(8,128)(2,1)S(1)}, u32[]{:S(2)}, u32[]{:S(2)}) collective-permute-start(bf16[3,32,1024]{2,1,0:T(8,128)(2,1)} %get-tuple-element.43), channel_id=1, source_target_pairs={{0,112},{16,0},{32,16},{48,32},{64,48},{80,64},{96,80},{112,96},{1... | collective-permute-start | bytes 589832 | tf_op jit(solution)/shard_map/ppermute | solution.py:239
  128.3 7.2 %collective-permute-start.19 = (bf16[3,32,1024]{2,1,0:T(8,128)(2,1)}, bf16[3,32,1024]{2,1,0:T(8,128)(2,1)S(1)}, u32[]{:S(2)}, u32[]{:S(2)}) collective-permute-start(bf16[3,32,1024]{2,1,0:T(8,128)(2,1)} %get-tuple-element.39), channel_id=1, source_target_pairs={{0,16},{16,32},{32,48},{48,64},{64,80},{80,96},{96,112},{112,0},{1... | collective-permute-start | bytes 589832 | tf_op jit(solution)/shard_map/ppermute | solution.py:238
  132.4 8.4 %collective-permute-start.24 = (bf16[2,3,32,1024]{3,2,1,0:T(8,128)(2,1)S(1)}, bf16[2,3,32,1024]{3,2,1,0:T(8,128)(2,1)S(1)}, u32[]{:S(2)}, u32[]{:S(2)}) collective-permute-start(bf16[2,3,32,1024]{3,2,1,0:T(8,128)(2,1)S(1)} %add_convert_fusion.2), channel_id=1, source_target_pairs={{0,112},{16,0},{32,16},{48,32},{64,48},{80,64},{96,80},{112,96},{1... | collective-permute-start | bytes 1179656 | tf_op jit(solution)/shard_map/ppermute | solution.py:242
  136.6 8.5 %collective-permute-start.20 = (bf16[2,3,32,1024]{3,2,1,0:T(8,128)(2,1)S(1)}, bf16[2,3,32,1024]{3,2,1,0:T(8,128)(2,1)S(1)}, u32[]{:S(2)}, u32[]{:S(2)}) collective-permute-start(bf16[2,3,32,1024]{3,2,1,0:T(8,128)(2,1)S(1)} %add_convert_fusion.5), channel_id=1, source_target_pairs={{0,16},{16,32},{32,48},{48,64},{64,80},{80,96},{96,112},{112,0},{1... | collective-permute-start | bytes 1179656 | tf_op jit(solution)/shard_map/ppermute | solution.py:241
  140.9 8.2 %collective-permute-start.25 = (bf16[2,3,32,1024]{3,2,1,0:T(8,128)(2,1)S(1)}, bf16[2,3,32,1024]{3,2,1,0:T(8,128)(2,1)S(1)}, u32[]{:S(2)}, u32[]{:S(2)}) collective-permute-start(bf16[2,3,32,1024]{3,2,1,0:T(8,128)(2,1)S(1)} %add_convert_fusion.1), channel_id=1, source_target_pairs={{0,112},{16,0},{32,16},{48,32},{64,48},{80,64},{96,80},{112,96},{1... | collective-permute-start | bytes 1179656 | tf_op jit(solution)/shard_map/ppermute | solution.py:242
  145.2 7.9 %collective-permute-start.21 = (bf16[2,3,32,1024]{3,2,1,0:T(8,128)(2,1)S(1)}, bf16[2,3,32,1024]{3,2,1,0:T(8,128)(2,1)S(1)}, u32[]{:S(2)}, u32[]{:S(2)}) collective-permute-start(bf16[2,3,32,1024]{3,2,1,0:T(8,128)(2,1)S(1)} %add_convert_fusion.4), channel_id=1, source_target_pairs={{0,16},{16,32},{32,48},{48,64},{64,80},{80,96},{96,112},{112,0},{1... | collective-permute-start | bytes 1179656 | tf_op jit(solution)/shard_map/ppermute | solution.py:241
  149.3 8.5 %collective-permute-start.26 = (bf16[2,3,32,1024]{3,2,1,0:T(8,128)(2,1)S(1)}, bf16[2,3,32,1024]{3,2,1,0:T(8,128)(2,1)S(1)}, u32[]{:S(2)}, u32[]{:S(2)}) collective-permute-start(bf16[2,3,32,1024]{3,2,1,0:T(8,128)(2,1)S(1)} %add_convert_fusion), channel_id=1, source_target_pairs={{0,112},{16,0},{32,16},{48,32},{64,48},{80,64},{96,80},{112,96},{1... | collective-permute-start | bytes 1179656 | tf_op jit(solution)/shard_map/ppermute | solution.py:242
  153.3 8.8 %collective-permute-start.22 = (bf16[2,3,32,1024]{3,2,1,0:T(8,128)(2,1)S(1)}, bf16[2,3,32,1024]{3,2,1,0:T(8,128)(2,1)S(1)}, u32[]{:S(2)}, u32[]{:S(2)}) collective-permute-start(bf16[2,3,32,1024]{3,2,1,0:T(8,128)(2,1)S(1)} %add_convert_fusion.3), channel_id=1, source_target_pairs={{0,16},{16,32},{32,48},{48,64},{64,80},{80,96},{96,112},{112,0},{1... | collective-permute-start | bytes 1179656 | tf_op jit(solution)/shard_map/ppermute | solution.py:241
  165.0 12.7 %collective-permute-start.27 = (bf16[3,32,1024]{2,1,0:T(8,128)(2,1)}, bf16[3,32,1024]{2,1,0:T(8,128)(2,1)S(1)}, u32[]{:S(2)}, u32[]{:S(2)}) collective-permute-start(bf16[3,32,1024]{2,1,0:T(8,128)(2,1)} %get-tuple-element.45), channel_id=1, source_target_pairs={{0,8},{8,0},{1,9},{9,1},{2,10},{10,2},{3,11},{11,3},{4,12},{12,4},... | collective-permute-start | bytes 589832 | tf_op jit(solution)/shard_map/ppermute | solution.py:395
  171.5 11.2 %collective-permute-start.29 = (bf16[3,32,1024]{2,1,0:T(8,128)(2,1)}, bf16[3,32,1024]{2,1,0:T(8,128)(2,1)S(1)}, u32[]{:S(2)}, u32[]{:S(2)}) collective-permute-start(bf16[3,32,1024]{2,1,0:T(8,128)(2,1)} %get-tuple-element.45), channel_id=1, source_target_pairs={{0,136},{8,128},{1,137},{9,129},{2,138},{10,130},{3,139},{11,131},... | collective-permute-start | bytes 589832 | tf_op jit(solution)/shard_map/ppermute | solution.py:397
  174.2 8.6 %collective-permute-start.28 = (bf16[3,32,1024]{2,1,0:T(8,128)(2,1)}, bf16[3,32,1024]{2,1,0:T(8,128)(2,1)S(1)}, u32[]{:S(2)}, u32[]{:S(2)}) collective-permute-start(bf16[3,32,1024]{2,1,0:T(8,128)(2,1)} %get-tuple-element.44.near), channel_id=1, source_target_pairs={{0,128},{1,129},{2,130},{3,131},{4,132},{5,133},{6,134},{7,135},{8... | collective-permute-start | bytes 589832 | tf_op jit(solution)/shard_map/ppermute | solution.py:396
  (23 other events, 277.1 us)

commit v7 on v6

--- a/solution.py
+++ b/solution.py
@@ -79,15 +79,19 @@
 FIRST = ((0, 0), (1, 0), (3, 0), (0, 1))
 REST = ((2, 0), (1, 1), (2, 1), (3, 1))
 GROUPS = 4
+WEIGHTS = 6
 
 
 def load_weight(place, blocks, weights, weight, sem):
     piece = weights[0].shape[1]
+    half = piece // 2
     copies = []
     for index in range(sem.shape[0]):
         for source, ref in enumerate(weights):
-            row = pl.multiple_of(index * QUARTERS * piece + place[source] * piece, piece)
-            target = weight.at[pl.ds(row, piece)]
+            part = source if source < 2 else 2 + (source - 2) // 2
+            shift = half if source in (3, 5) else 0
+            row = pl.multiple_of(index * QUARTERS * piece + place[part] * piece + shift, half)
+            target = weight.at[pl.ds(row, ref.shape[1])]
             copies.append(pltpu.make_async_copy(ref.at[blocks[index]], target, sem.at[index, source]))
     for copy in copies:
         copy.start()
@@ -118,7 +122,7 @@
 def project_first_kernel(place, blocks, *refs):
     count = len(FIRST) + 2
     features, refs = refs[:count], refs[count:]
-    weights, (out, weight, *held, feature_sem, weight_sem) = refs[:QUARTERS], refs[QUARTERS:]
+    weights, (out, weight, *held, feature_sem, weight_sem) = refs[:WEIGHTS], refs[WEIGHTS:]
     copies = load_weight(place, blocks, weights, weight, weight_sem) + load_features(features, held, feature_sem)
     for copy in copies:
         copy.wait()
@@ -136,7 +140,7 @@
 def project_rest_kernel(place, blocks, slot_layer, partial, *refs):
     count = len(REST) + 2
     features, refs = refs[:count], refs[count:]
-    weights, refs = refs[:QUARTERS], refs[QUARTERS:]
+    weights, refs = refs[:WEIGHTS], refs[WEIGHTS:]
     outs, refs = refs[: len(DISTANCES) + 1], refs[len(DISTANCES) + 1 :]
     weight, before, product, *held, feature_sem, weight_sem, before_sem = refs
     copies = load_weight(place, blocks, weights, weight, weight_sem) + load_features(features, held, feature_sem)
@@ -187,7 +191,7 @@
             pltpu.VMEM((depth, columns), jnp.bfloat16),
             *[pltpu.VMEM(feature.shape, feature.dtype) for feature in features],
             pltpu.SemaphoreType.DMA((len(features),)),
-            pltpu.SemaphoreType.DMA((len(FIRST), QUARTERS)),
+            pltpu.SemaphoreType.DMA((len(FIRST), WEIGHTS)),
         ],
         compiler_params=pltpu.CompilerParams(vmem_limit_bytes=40 * MIB),
         cost_estimate=pl.CostEstimate(
@@ -215,7 +219,7 @@
             pltpu.VMEM((layers, tokens, columns), jnp.bfloat16),
             *[pltpu.VMEM(feature.shape, feature.dtype) for feature in features],
             pltpu.SemaphoreType.DMA((len(features),)),
-            pltpu.SemaphoreType.DMA((len(REST), QUARTERS)),
+            pltpu.SemaphoreType.DMA((len(REST), WEIGHTS)),
             pltpu.SemaphoreType.DMA((GROUPS,)),
         ],
         compiler_params=pltpu.CompilerParams(vmem_limit_bytes=62 * MIB),
@@ -262,7 +266,7 @@
     )(c.reshape(1).astype(jnp.int32), own, below, above)
 
 
-def finish_kernel(state, hidden, layer_grad, near, across, teacher, teacher_across, out):
+def finish_kernel(state, hidden, layer_grad, near, teacher, across, teacher_across, out):
     core, count = state[0], state[1]
     slots, quarter, _ = near.shape
     quarters = ((C + core, near), (C + 1 - core, across), (core, teacher), (1 - core, teacher_across))
@@ -288,7 +292,7 @@
     )(jnp.stack([c, own_count]).astype(jnp.int32), hidden, layer_grad, *pieces)
 
 
-def gather_tensor(own, low, high, before):
+def gather_tensor(own, low, high):
     up = [(i, (i + 1) % X) for i in range(X)]
     down = [(i, (i - 1) % X) for i in range(X)]
     swap = [(0, 1), (1, 0)]
@@ -297,7 +301,6 @@
     g0 = lax.ppermute(own, "yl", swap)
     f3b = lax.ppermute(high, "x", up)
     f1a = lax.ppermute(low, "x", down)
-    f3a, _ = lax.optimization_barrier((f3a, before))
     f2a = lax.ppermute(f3a, "x", up)
     f2b = lax.ppermute(f1b, "x", down)
     g3 = lax.ppermute(g0, "x", up)
@@ -330,8 +333,11 @@
 
     swap = [(0, 1), (1, 0)]
     side = ("yh", "yl")
+    ring = YH * YL
+    up = [(i, (i + 1) % ring) for i in range(ring)]
+    down = [(i, (i - 1) % ring) for i in range(ring)]
+    half_rows = proj_weight.shape[1] // 2
     w_sib = lax.ppermute(proj_weight, "c", swap)
-    w_row = lax.ppermute(proj_weight, "yl", swap)
     place = jnp.stack([2 * yh + c, 2 * yh + 1 - c, 2 * (1 - yh) + c, 2 * (1 - yh) + 1 - c]).astype(jnp.int32)
 
     is_child = yh == 1
@@ -354,17 +360,16 @@
     sums = sums + lax.ppermute(sums, "x", [(i, i ^ 2) for i in range(X)])
     sums = sums + lax.ppermute(sums, "yl", swap)
     sent = lax.ppermute(arrange(teacher_slabs, 1), side, [(0, 3), (1, 2)])
-    w_row, _ = lax.optimization_barrier((w_row, sent))
-    w_far = lax.ppermute(w_row, side, [(0, 3), (3, 0), (1, 2), (2, 1)])
     arranged = jnp.where(yh == 0, arrange(teacher_slabs, 0), sent)
-    arranged, w_sib, sums = lax.optimization_barrier((arranged, w_sib, sums))
+    arranged, w_sib, sums, weight_rows = lax.optimization_barrier((arranged, w_sib, sums, proj_weight))
+    w_far_a = lax.ppermute(lax.ppermute(weight_rows[:, :half_rows], side, up), side, up)
+    w_far_b = lax.ppermute(lax.ppermute(weight_rows[:, half_rows:], side, down), side, down)
     received = lax.all_to_all(arranged, ("z", "c"), split_axis=0, concat_axis=0, tiled=True)
     received = received.reshape(Z * C * slab_count, YH, quarter, LANES)
 
-    received, w_far = lax.optimization_barrier((received, w_far))
-    w_far_sib = lax.ppermute(w_far, "c", swap)
-    weights = (proj_weight, w_sib, w_far, w_far_sib)
-    first_features, rest_features = gather_tensor(*pick(layer_map, received), w_far_sib)
+    first_features, rest_features = gather_tensor(*pick(layer_map, received))
+    w_far_a, w_far_b, _ = lax.optimization_barrier((w_far_a, w_far_b, first_features[3]))
+    weights = (proj_weight, w_sib, w_far_a, w_far_b, lax.ppermute(w_far_a, "c", swap), lax.ppermute(w_far_b, "c", swap))
     squares, inner_sum = sums[0], sums[1]
     inverse_rms = lax.rsqrt(squares / full_width + EPSILON)[:, None]
     normed = (first_hidden * inverse_rms * norm_scale).astype(jnp.bfloat16)
@@ -396,7 +401,7 @@
     teacher = lax.ppermute(kept, "yh", [(0, 1)])
     teacher_across = lax.ppermute(given, ("yh", "c"), [(0, 3), (1, 2)])
     own_count = jnp.where(is_child, layer_counts[2 * z + c], 0)
-    hidden_grad = finish(c, own_count, child_hidden, layer_grad, (kept, across, teacher, teacher_across))
+    hidden_grad = finish(c, own_count, child_hidden, layer_grad, (kept, teacher, across, teacher_across))
     key_grad = jnp.where(is_child, key_grad, jnp.zeros_like(key_grad))
     value_grad = jnp.where(is_child, value_grad, jnp.zeros_like(value_grad))
     gain_grad = jnp.where(is_child, gain_grad, 0.0)

time: 188 us -> 172 us (0.915)
  waiting for transfers between devices: 77.4 us -> 56.9 us
  starting transfers between devices: 57.4 us -> 60.2 us
    ppermute x1, waiting for transfers between devices: 16.8 us -> 0.25 us  [body(): sums = sums + lax.ppermute(sums, 'yl', swap)]
    ppermute x3 -> x6, waiting for transfers between devices: 26.1 us -> 12 us  [the longest x1 12 us: body(): lax.ppermute(weight_rows[:, :half_rows], side, up)]
    all_to_all x1, waiting for transfers between devices: 0.01 us -> 5.22 us  [body(): lax.all_to_all(arranged, ('z', 'c'), split_axis=0, concat_axis=0, tiled=T...]
    ppermute x1, waiting for transfers between devices: 5.02 us -> 0.01 us  [body(): teacher = lax.ppermute(kept, 'yh', [(0, 1)])]
    ppermute x3 -> x6, starting transfers between devices: 1.06 us -> 5.44 us  [the longest x1 2.67 us: body(): lax.ppermute(lax.ppermute(weight_rows[:, half_rows:], side, down), side,...]
    ppermute x1, waiting for transfers between devices: 6.19 us -> 1.82 us  [gather_tensor(): f1b = lax.ppermute(high, 'x', down)]
    ppermute x1, starting transfers between devices: 1.4 us -> 4.98 us  [body(): teacher = lax.ppermute(kept, 'yh', [(0, 1)])]
    ppermute x1, waiting for transfers between devices: 0.96 us -> 4.47 us  [gather_tensor(): f1a = lax.ppermute(low, 'x', down)]
  transfers between devices with their start and end apart: 31 -> 34, of which waited for: 15 -> 19; matrix products, arithmetic and copies ran while one was open for 11% -> 12% of each run, Pallas kernels for 5% -> 6%
where the time goes in v7:
time: 172 us; the launch traced here: 171 us
  starting transfers between devices  60.2 us (35%)
  waiting for transfers between devices  56.9 us (33%)
  Pallas kernels  26.7 us (16%)
  matrix products  9.32 us (5%)
  other arithmetic  8.18 us (5%)
  local copies, waits for them, and re-layouts  7.57 us (4%)
    ppermute x1, waiting for transfers between devices, body(): lax.ppermute(weight_rows[:, :half_rows], side, up)  12 us
    all_to_all x1, starting transfers between devices, body(): lax.all_to_all(arranged, ('z', 'c'), split_axis=0, concat_axis=0, tiled=T...  11.4 us
    ppermute x3, waiting for transfers between devices, reduce_z(): from_above = lax.ppermute(add(to_down, from_above), 'z', down)  10.3 us
    pallas_call x1, Pallas kernels, project_rest(): pl.pallas_call(project_rest_kernel, out_shape=[jax.ShapeDtypeStruct(shape...  8.91 us
    ppermute x3, starting transfers between devices, reduce_z(): from_above = lax.ppermute(add(to_down, from_above), 'z', down)  8.22 us
    ppermute x1, starting transfers between devices, body(): sent = lax.ppermute(arrange(teacher_slabs, 1), side, [(0, 3), (1, 2)])  6.49 us
    pallas_call x1, Pallas kernels, project_first(): pl.pallas_call(project_first_kernel, out_shape=jax.ShapeDtypeStruct(shape...  6.29 us
    ppermute x3, waiting for transfers between devices, reduce_z(): from_below = lax.ppermute(add(to_up, from_below), 'z', up)  5.53 us
  transfers between devices with their start and end apart: 34, of which 19 were waited for; matrix products, arithmetic and copies ran while one was open for 12% of the time, Pallas kernels for 6%

profile of v7, /device:TPU:1, one launch (start us, length us, event | category | flops | bytes accessed | tf_op | source)
XLA Modules:
  0.0 170.5 jit_solution(11515371440158602625)
XLA Ops:
  0.7 2.3 %arrange.3 = bf16[16,192,128]{2,1,0:T(8,128)(2,1)} custom-call(bf16[3,128,2048]{2,1,0:T(8,128)(2,1)} %slabs.3), custom_call_target="tpu_custom_call" | custom-call | bytes 1600000 | tf_op jit(solution)/shard_map/arrange/pallas_call | solution.py:36
  3.0 6.5 %collective-permute-start = (bf16[16,192,128]{2,1,0:T(8,128)(2,1)}, bf16[16,192,128]{2,1,0:T(8,128)(2,1)}, u32[]{:S(2)}, u32[]{:S(2)}) collective-permute-start(bf16[16,192,128]{2,1,0:T(8,128)(2,1)} %arrange.3), channel_id=1, source_target_pairs={{0,129},{1,128},{2,131},{3,130},{4,133},{5,132},{6,135},{7,134},{8... | collective-permute-start | bytes 2359304 | tf_op jit(solution)/shard_map/ppermute | solution.py:362
  10.4 2.4 %fusion = f32[128,1024]{1,0:T(8,128)S(1)} fusion(bf16[1,1024,1024]{2,1,0:T(8,128)(2,1)} %param.16, bf16[1,128,1024]{2,1,0:T(8,128)(2,1)S(1)} %copy-done.18), kind=kOutput, calls=%fused_computation.1 | convolution fusion | flops 268435456 | bytes 2883584 | tf_op jit(solution)/shard_map/dot_general | solution.py:350
  12.9 2.6 %fusion.11 = (f32[128]{0:T(128)S(1)}, f32[128]{0:T(128)S(1)}, f32[128,1024]{1,0:T(8,128)}) fusion(bf16[3,128,1024]{2,1,0:T(8,128)(2,1)} %hidden.1, f32[1024]{0:T(1024)S(1)} %bitcast.90, f32[128,1024]{1,0:T(8,128)S(1)} %fusion, bf16[1,1024,1024]{2,1,0:T(8,128)(2,1)S(1)} %copy-done.9, bf16[1,128,1024]{2,1,0:T(8,128)(2,1)S(1)} %copy-done), kind=kOutput, calls=%fused_computation.21 | convolution fusion | flops 269352704 | bytes 3675136 | tf_op jit(solution)/shard_map/dot_general | solution.py:347
  18.0 2.8 %collective-permute-start.3 = (f32[2,128]{1,0:T(2,128)S(1)}, f32[2,128]{1,0:T(2,128)S(1)}, u32[]{:S(2)}, u32[]{:S(2)}) collective-permute-start(f32[2,128]{1,0:T(2,128)S(1)} %fusion.30), channel_id=1, source_target_pairs={{0,4},{2,6},{4,0},{6,2},{1,5},{3,7},{5,1},{7,3},{8,12},{10,14},{12... | collective-permute-start | bytes 3080 | tf_op jit(solution)/shard_map/ppermute | solution.py:360
  22.1 2.2 %arrange.2 = bf16[16,192,128]{2,1,0:T(8,128)(2,1)} custom-call(bf16[3,128,2048]{2,1,0:T(8,128)(2,1)} %slabs.3), custom_call_target="tpu_custom_call" | custom-call | bytes 1600000 | tf_op jit(solution)/shard_map/arrange/pallas_call | solution.py:36
  25.1 2.1 %broadcast_select_fusion = bf16[16,192,128]{2,1,0:T(8,128)(2,1)} fusion(bf16[16,192,128]{2,1,0:T(8,128)(2,1)} %arrange.2, bf16[16,192,128]{2,1,0:T(8,128)(2,1)} %collective-permute-done, pred[]{:T(512)S(6)} %eq.26), kind=kLoop, calls=%fused_computation.14 | loop fusion | flops 393216 | bytes 2359297 | tf_op jit(solution)/shard_map/jit(_where)/select_n | solution.py:363
  27.2 11.4 %all-to-all-start = ((bf16[16,192,128]{2,1,0:T(8,128)(2,1)}), bf16[16,192,128]{2,1,0:T(8,128)(2,1)}, u32[]{:S(2)}, u32[]{:S(2)}) async-start(bf16[16,192,128]{2,1,0:T(8,128)(2,1)} %broadcast_select_fusion), calls=%async_computation | async-start | bytes 1572864 | tf_op jit(solution)/shard_map/all_to_all | solution.py:367
  39.1 2.3 %collective-permute-start.12 = (bf16[8,32,1024]{2,1,0:T(8,128)(2,1)S(1)}, bf16[8,32,1024]{2,1,0:T(8,128)(2,1)}, u32[]{:S(2)}, u32[]{:S(2)}) collective-permute-start(bf16[8,32,1024]{2,1,0:T(8,128)(2,1)S(1)} %get-tuple-element.50), channel_id=1, source_target_pairs={{0,129},{1,0},{128,1},{129,128},{2,131},{3,2},{130,3},{131,130},{4... | collective-permute-start | bytes 1572872 | tf_op jit(solution)/shard_map/ppermute | solution.py:366
  41.5 12.0 %collective-permute-done.10 = bf16[8,32,1024]{2,1,0:T(8,128)(2,1)} collective-permute-done((bf16[8,32,1024]{2,1,0:T(8,128)(2,1)S(1)}, bf16[8,32,1024]{2,1,0:T(8,128)(2,1)}, u32[]{:S(2)}, u32[]{:S(2)}) %collective-permute-start.10) | collective-permute-done | bytes 524320 | tf_op jit(solution)/shard_map/ppermute | solution.py:365
  53.5 2.7 %collective-permute-start.13 = (bf16[8,32,1024]{2,1,0:T(8,128)(2,1)}, bf16[8,32,1024]{2,1,0:T(8,128)(2,1)}, u32[]{:S(2)}, u32[]{:S(2)}) collective-permute-start(bf16[8,32,1024]{2,1,0:T(8,128)(2,1)} %collective-permute-done.12), channel_id=1, source_target_pairs={{0,129},{1,0},{128,1},{129,128},{2,131},{3,2},{130,3},{131,130},{4... | collective-permute-start | bytes 1572872 | tf_op jit(solution)/shard_map/ppermute | solution.py:366
  56.2 5.2 %all-to-all-done = bf16[16,192,128]{2,1,0:T(8,128)(2,1)} async-done(((bf16[16,192,128]{2,1,0:T(8,128)(2,1)}), bf16[16,192,128]{2,1,0:T(8,128)(2,1)}, u32[]{:S(2)}, u32[]{:S(2)}) %all-to-all-start) | async-done | bytes 786464 | tf_op jit(solution)/shard_map/all_to_all | solution.py:367
  61.4 2.3 %pick_layers.1 = (bf16[32,2,32,128]{3,2,1,0:T(8,128)(2,1)}, bf16[16,2,32,128]{3,2,1,0:T(8,128)(2,1)}, bf16[16,2,32,128]{3,2,1,0:T(8,128)(2,1)}) custom-call(s32[32]{0:T(128)} %layer_map.1, bf16[48,2,32,128]{3,2,1,0:T(8,128)(2,1)} %bitcast.26.received), custom_call_target="tpu_custom_call" | custom-call | bytes 1300000 | tf_op jit(solution)/shard_map/pick_layers/pallas_call | solution.py:65
  68.8 2.9 %collective-permute-done.7.refs_3_ = bf16[16,2,32,128]{3,2,1,0:T(8,128)(2,1)S(1)} collective-permute-done((bf16[16,2,32,128]{3,2,1,0:T(8,128)(2,1)}, bf16[16,2,32,128]{3,2,1,0:T(8,128)(2,1)S(1)}, u32[]{:S(2)}, u32[]{:S(2)}) %collective-permute-start.7) | collective-permute-done | bytes 262176 | tf_op jit(solution)/shard_map/ppermute | solution.py:299
  73.6 4.5 %collective-permute-done.5.refs_1_ = bf16[16,2,32,128]{3,2,1,0:T(8,128)(2,1)} collective-permute-done((bf16[16,2,32,128]{3,2,1,0:T(8,128)(2,1)}, bf16[16,2,32,128]{3,2,1,0:T(8,128)(2,1)}, u32[]{:S(2)}, u32[]{:S(2)}) %collective-permute-start.5) | collective-permute-done | bytes 262176 | tf_op jit(solution)/shard_map/ppermute | solution.py:303
  84.5 2.6 %collective-permute-done.16.refs_0_ = bf16[16,2,32,128]{3,2,1,0:T(8,128)(2,1)} collective-permute-done((bf16[16,2,32,128]{3,2,1,0:T(8,128)(2,1)S(1)}, bf16[16,2,32,128]{3,2,1,0:T(8,128)(2,1)}, u32[]{:S(2)}, u32[]{:S(2)}) %collective-permute-start.16) | collective-permute-done | bytes 262176 | tf_op jit(solution)/shard_map/ppermute | solution.py:304
  91.4 6.3 %project_first.1.partial = bf16[4,256,1024]{2,1,0:T(8,128)(2,1)S(1)} custom-call(s32[4]{0:T(128)S(1)} %get-tuple-element.53.place, s32[4]{0:T(128)S(1)} %get-tuple-element.54.blocks, bf16[32,2,32,128]{3,2,1,0:T(8,128)(2,1)S(1)} %copy-done.5, bf16[16,2,32,128]{3,2,1,0:T(8,128)(2,1)} %collective-permute-done.5.refs_1_, ...), custom_call_target="tpu_custom_call" | custom-call | flops 2147483648 | bytes 8388608 | tf_op jit(solution)/shard_map/project_first/pallas_call | solution.py:185
  99.8 1.9 %collective-permute-done.20.refs_4_ = bf16[16,2,32,128]{3,2,1,0:T(8,128)(2,1)S(1)} collective-permute-done((bf16[16,2,32,128]{3,2,1,0:T(8,128)(2,1)}, bf16[16,2,32,128]{3,2,1,0:T(8,128)(2,1)S(1)}, u32[]{:S(2)}, u32[]{:S(2)}) %collective-permute-start.20) | collective-permute-done | bytes 262176 | tf_op jit(solution)/shard_map/ppermute | solution.py:309
  102.4 8.9 %project_rest.1 = (bf16[3,32,1024]{2,1,0:T(8,128)(2,1)}, bf16[3,32,1024]{2,1,0:T(8,128)(2,1)}, bf16[2,3,32,1024]{3,2,1,0:T(8,128)(2,1)}, bf16[2,3,32,1024]{3,2,1...) custom-call(s32[4]{0:T(128)} %copy-done.6, ...), custom_call_target="tpu_custom_call" | custom-call | flops 2147483648 | bytes 11534336 | tf_op jit(solution)/shard_map/project_rest/pallas_call | solution.py:211
  112.9 4.0 %collective-permute-done.26 = bf16[3,32,1024]{2,1,0:T(8,128)(2,1)S(1)} collective-permute-done((bf16[3,32,1024]{2,1,0:T(8,128)(2,1)}, bf16[3,32,1024]{2,1,0:T(8,128)(2,1)S(1)}, u32[]{:S(2)}, u32[]{:S(2)}) %collective-permute-start.26) | collective-permute-done | bytes 196640 | tf_op jit(solution)/shard_map/ppermute | solution.py:243
  121.2 5.6 %collective-permute-done.27 = bf16[2,3,32,1024]{3,2,1,0:T(8,128)(2,1)S(1)} collective-permute-done((bf16[2,3,32,1024]{3,2,1,0:T(8,128)(2,1)S(1)}, bf16[2,3,32,1024]{3,2,1,0:T(8,128)(2,1)S(1)}, u32[]{:S(2)}, u32[]{:S(2)}) %collective-permute-start.27) | collective-permute-done | bytes 393248 | tf_op jit(solution)/shard_map/ppermute | solution.py:246
  126.9 3.1 %collective-permute-start.28 = (bf16[2,3,32,1024]{3,2,1,0:T(8,128)(2,1)S(1)}, bf16[2,3,32,1024]{3,2,1,0:T(8,128)(2,1)S(1)}, u32[]{:S(2)}, u32[]{:S(2)}) collective-permute-start(bf16[2,3,32,1024]{3,2,1,0:T(8,128)(2,1)S(1)} %add_convert_fusion.1), channel_id=1, source_target_pairs={{0,112},{16,0},{32,16},{48,32},{64,48},{80,64},{96,80},{112,96},{1... | collective-permute-start | bytes 1179656 | tf_op jit(solution)/shard_map/ppermute | solution.py:246
  132.3 3.5 %collective-permute-done.28 = bf16[2,3,32,1024]{3,2,1,0:T(8,128)(2,1)S(1)} collective-permute-done((bf16[2,3,32,1024]{3,2,1,0:T(8,128)(2,1)S(1)}, bf16[2,3,32,1024]{3,2,1,0:T(8,128)(2,1)S(1)}, u32[]{:S(2)}, u32[]{:S(2)}) %collective-permute-start.28) | collective-permute-done | bytes 393248 | tf_op jit(solution)/shard_map/ppermute | solution.py:246
  136.0 3.5 %collective-permute-start.29 = (bf16[2,3,32,1024]{3,2,1,0:T(8,128)(2,1)S(1)}, bf16[2,3,32,1024]{3,2,1,0:T(8,128)(2,1)S(1)}, u32[]{:S(2)}, u32[]{:S(2)}) collective-permute-start(bf16[2,3,32,1024]{3,2,1,0:T(8,128)(2,1)S(1)} %add_convert_fusion), channel_id=1, source_target_pairs={{0,112},{16,0},{32,16},{48,32},{64,48},{80,64},{96,80},{112,96},{1... | collective-permute-start | bytes 1179656 | tf_op jit(solution)/shard_map/ppermute | solution.py:246
  140.4 2.1 %select_bitcast_fusion = bf16[1,1024,1024]{2,1,0:T(8,128)(2,1)} fusion(pred[]{:T(512)S(6)} %eq.25, bf16[1,128,1024]{2,1,0:T(8,128)(2,1)S(1)} %copy-done.19, f32[1024]{0:T(1024)S(1)} %bitcast.92, f32[128]{0:T(128)S(1)} %get-tuple-element.47, bf16[3,128,1024]{2,1,0:T(8,128)(2,1)S(1)} %copy-done.7), kind=kOutput, calls=%fused_computation.5 | convolution fusion | flops 271056896 | bytes 2626049 | tf_op jit(solution)/shard_map/dot_general | solution.py:380
  144.2 4.0 %collective-permute-done.25.below = bf16[2,3,32,1024]{3,2,1,0:T(8,128)(2,1)S(1)} collective-permute-done((bf16[2,3,32,1024]{3,2,1,0:T(8,128)(2,1)S(1)}, bf16[2,3,32,1024]{3,2,1,0:T(8,128)(2,1)S(1)}, u32[]{:S(2)}, u32[]{:S(2)}) %collective-permute-start.25) | collective-permute-done | bytes 393248 | tf_op jit(solution)/shard_map/ppermute | solution.py:245
  148.9 2.1 %combine.1 = (bf16[3,32,1024]{2,1,0:T(8,128)(2,1)}, bf16[3,32,1024]{2,1,0:T(8,128)(2,1)}) custom-call(s32[1]{0:T(128)} %bitcast.core, bf16[2,3,32,1024]{3,2,1,0:T(8,128)(2,1)} %get-tuple-element.33.own, bf16[2,3,32,1024]{3,2,1,0:T(8,128)(2,1)} %copy-done.15, bf16[2,3,32,1024]{3,2,1,0:T(8,128)(2,1)} %copy-done.14), custom_call_target="tpu_custom_call" | custom-call | flops 589824 | bytes 1572864 | tf_op jit(solution)/shard_map/combine/pallas_call | solution.py:259
  151.0 5.0 %collective-permute-start.30 = (bf16[3,32,1024]{2,1,0:T(8,128)(2,1)}, bf16[3,32,1024]{2,1,0:T(8,128)(2,1)S(1)}, u32[]{:S(2)}, u32[]{:S(2)}) collective-permute-start(bf16[3,32,1024]{2,1,0:T(8,128)(2,1)} %get-tuple-element.42.near), channel_id=1, source_target_pairs={{0,128},{1,129},{2,130},{3,131},{4,132},{5,133},{6,134},{7,135},{8... | collective-permute-start | bytes 589832 | tf_op jit(solution)/shard_map/ppermute | solution.py:401
  156.0 4.9 %collective-permute-start.31 = (bf16[3,32,1024]{2,1,0:T(8,128)(2,1)}, bf16[3,32,1024]{2,1,0:T(8,128)(2,1)S(1)}, u32[]{:S(2)}, u32[]{:S(2)}) collective-permute-start(bf16[3,32,1024]{2,1,0:T(8,128)(2,1)} %get-tuple-element.43), channel_id=1, source_target_pairs={{0,8},{8,0},{1,9},{9,1},{2,10},{10,2},{3,11},{11,3},{4,12},{12,4},... | collective-permute-start | bytes 589832 | tf_op jit(solution)/shard_map/ppermute | solution.py:400
  162.2 2.1 %select_bitcast_fusion.1 = bf16[1,1024,1024]{2,1,0:T(8,128)(2,1)} fusion(pred[]{:T(512)S(6)} %eq.25, bf16[1,128,1024]{2,1,0:T(8,128)(2,1)S(1)} %copy-done, f32[1024]{0:T(1024)S(1)} %bitcast.93, f32[128]{0:T(128)S(1)} %get-tuple-element.47, bf16[3,128,1024]{2,1,0:T(8,128)(2,1)S(1)} %copy-done.7), kind=kOutput, calls=%fused_computation.6 | convolution fusion | flops 271056896 | bytes 2626049 | tf_op jit(solution)/shard_map/dot_general | solution.py:377
  164.3 2.9 %collective-permute-done.32.teacher_across = bf16[3,32,1024]{2,1,0:T(8,128)(2,1)S(1)} collective-permute-done((bf16[3,32,1024]{2,1,0:T(8,128)(2,1)}, bf16[3,32,1024]{2,1,0:T(8,128)(2,1)S(1)}, u32[]{:S(2)}, u32[]{:S(2)}) %collective-permute-start.32) | collective-permute-done | bytes 196640 | tf_op jit(solution)/shard_map/ppermute | solution.py:402
  167.9 2.6 %finish.1 = bf16[3,128,1024]{2,1,0:T(8,128)(2,1)} custom-call(s32[2]{0:T(128)} %pad_add_fusion.state, bf16[3,128,1024]{2,1,0:T(8,128)(2,1)} %hidden.1, f32[128,1024]{1,0:T(8,128)} %get-tuple-element.49.layer_grad, bf16[3,32,1024]{2,1,0:T(8,128)(2,1)} %get-tuple-element.42.near, bf16[3,32,1024]{2,1,0:T(8,128)(2,1)} %copy-done.20, ...), custom_call_target="tpu_custom_call" | custom-call | flops 786432 | bytes 3145728 | tf_op jit(solution)/shard_map/finish/pallas_call | solution.py:285
  (135 shorter events, 39.3 us)
Async XLA Ops:
  3.0 22.1 %collective-permute-start = (bf16[16,192,128]{2,1,0:T(8,128)(2,1)}, bf16[16,192,128]{2,1,0:T(8,128)(2,1)}, u32[]{:S(2)}, u32[]{:S(2)}) collective-permute-start(bf16[16,192,128]{2,1,0:T(8,128)(2,1)} %arrange.3), channel_id=1, source_target_pairs={{0,129},{1,128},{2,131},{3,130},{4,133},{5,132},{6,135},{7,134},{8... | collective-permute-start | bytes 2359304 | tf_op jit(solution)/shard_map/ppermute | solution.py:362
  9.4 17.7 %collective-permute-start.1 = (bf16[8,64,1024]{2,1,0:T(8,128)(2,1)S(1)}, bf16[8,64,1024]{2,1,0:T(8,128)(2,1)S(1)}, u32[]{:S(2)}, u32[]{:S(2)}) collective-permute-start(bf16[8,64,1024]{2,1,0:T(8,128)(2,1)S(1)} %copy-done.1), channel_id=1, source_target_pairs={{0,8},{8,0},{1,9},{9,1},{2,10},{10,2},{3,11},{11,3},{4,12},{12,4},... | collective-permute-start | bytes 3145736 | tf_op jit(solution)/shard_map/ppermute | solution.py:340
  18.0 4.0 %collective-permute-start.3 = (f32[2,128]{1,0:T(2,128)S(1)}, f32[2,128]{1,0:T(2,128)S(1)}, u32[]{:S(2)}, u32[]{:S(2)}) collective-permute-start(f32[2,128]{1,0:T(2,128)S(1)} %fusion.30), channel_id=1, source_target_pairs={{0,4},{2,6},{4,0},{6,2},{1,5},{3,7},{5,1},{7,3},{8,12},{10,14},{12... | collective-permute-start | bytes 3080 | tf_op jit(solution)/shard_map/ppermute | solution.py:360
  27.2 34.2 %all-to-all-start = ((bf16[16,192,128]{2,1,0:T(8,128)(2,1)}), bf16[16,192,128]{2,1,0:T(8,128)(2,1)}, u32[]{:S(2)}, u32[]{:S(2)}) async-start(bf16[16,192,128]{2,1,0:T(8,128)(2,1)} %broadcast_select_fusion), calls=%async_computation | async-start | bytes 1572864 | tf_op jit(solution)/shard_map/all_to_all | solution.py:367
  38.7 14.8 %collective-permute-start.10 = (bf16[8,32,1024]{2,1,0:T(8,128)(2,1)S(1)}, bf16[8,32,1024]{2,1,0:T(8,128)(2,1)}, u32[]{:S(2)}, u32[]{:S(2)}) collective-permute-start(bf16[8,32,1024]{2,1,0:T(8,128)(2,1)S(1)} %get-tuple-element.51), channel_id=1, source_target_pairs={{0,1},{1,128},{128,129},{129,0},{2,3},{3,130},{130,131},{131,2},{4... | collective-permute-start | bytes 1572872 | tf_op jit(solution)/shard_map/ppermute | solution.py:365
  39.1 14.4 %collective-permute-start.12 = (bf16[8,32,1024]{2,1,0:T(8,128)(2,1)S(1)}, bf16[8,32,1024]{2,1,0:T(8,128)(2,1)}, u32[]{:S(2)}, u32[]{:S(2)}) collective-permute-start(bf16[8,32,1024]{2,1,0:T(8,128)(2,1)S(1)} %get-tuple-element.50), channel_id=1, source_target_pairs={{0,129},{1,0},{128,1},{129,128},{2,131},{3,2},{130,3},{131,130},{4... | collective-permute-start | bytes 1572872 | tf_op jit(solution)/shard_map/ppermute | solution.py:366
  53.5 14.8 %collective-permute-start.11 = (bf16[8,32,1024]{2,1,0:T(8,128)(2,1)}, bf16[8,32,1024]{2,1,0:T(8,128)(2,1)S(1)}, u32[]{:S(2)}, u32[]{:S(2)}) collective-permute-start(bf16[8,32,1024]{2,1,0:T(8,128)(2,1)} %collective-permute-done.10), channel_id=1, source_target_pairs={{0,1},{1,128},{128,129},{129,0},{2,3},{3,130},{130,131},{131,2},{4... | collective-permute-start | bytes 1572872 | tf_op jit(solution)/shard_map/ppermute | solution.py:365
  53.5 15.1 %collective-permute-start.13 = (bf16[8,32,1024]{2,1,0:T(8,128)(2,1)}, bf16[8,32,1024]{2,1,0:T(8,128)(2,1)}, u32[]{:S(2)}, u32[]{:S(2)}) collective-permute-start(bf16[8,32,1024]{2,1,0:T(8,128)(2,1)} %collective-permute-done.12), channel_id=1, source_target_pairs={{0,129},{1,0},{128,1},{129,128},{2,131},{3,2},{130,3},{131,130},{4... | collective-permute-start | bytes 1572872 | tf_op jit(solution)/shard_map/ppermute | solution.py:366
  63.7 8.0 %collective-permute-start.7 = (bf16[16,2,32,128]{3,2,1,0:T(8,128)(2,1)}, bf16[16,2,32,128]{3,2,1,0:T(8,128)(2,1)S(1)}, u32[]{:S(2)}, u32[]{:S(2)}) collective-permute-start(bf16[16,2,32,128]{3,2,1,0:T(8,128)(2,1)} %get-tuple-element.27), channel_id=1, source_target_pairs={{0,2},{2,4},{4,6},{6,0},{1,3},{3,5},{5,7},{7,1},{8,10},{10,12},{12... | collective-permute-start | bytes 786440 | tf_op jit(solution)/shard_map/ppermute | solution.py:299
  64.9 8.7 %collective-permute-start.6 = (bf16[16,2,32,128]{3,2,1,0:T(8,128)(2,1)}, bf16[16,2,32,128]{3,2,1,0:T(8,128)(2,1)}, u32[]{:S(2)}, u32[]{:S(2)}) collective-permute-start(bf16[16,2,32,128]{3,2,1,0:T(8,128)(2,1)} %get-tuple-element.28), channel_id=1, source_target_pairs={{0,6},{2,0},{4,2},{6,4},{1,7},{3,1},{5,3},{7,5},{8,14},{10,8},{12,... | collective-permute-start | bytes 786440 | tf_op jit(solution)/shard_map/ppermute | solution.py:300
  66.4 11.7 %collective-permute-start.5 = (bf16[16,2,32,128]{3,2,1,0:T(8,128)(2,1)}, bf16[16,2,32,128]{3,2,1,0:T(8,128)(2,1)}, u32[]{:S(2)}, u32[]{:S(2)}) collective-permute-start(bf16[16,2,32,128]{3,2,1,0:T(8,128)(2,1)} %get-tuple-element.27), channel_id=1, source_target_pairs={{0,6},{2,0},{4,2},{6,4},{1,7},{3,1},{5,3},{7,5},{8,14},{10,8},{12,... | collective-permute-start | bytes 786440 | tf_op jit(solution)/shard_map/ppermute | solution.py:303
  68.3 11.0 %collective-permute-start.8 = (bf16[16,2,32,128]{3,2,1,0:T(8,128)(2,1)}, bf16[16,2,32,128]{3,2,1,0:T(8,128)(2,1)}, u32[]{:S(2)}, u32[]{:S(2)}) collective-permute-start(bf16[16,2,32,128]{3,2,1,0:T(8,128)(2,1)} %get-tuple-element.28), channel_id=1, source_target_pairs={{0,2},{2,4},{4,6},{6,0},{1,3},{3,5},{5,7},{7,1},{8,10},{10,12},{12... | collective-permute-start | bytes 786440 | tf_op jit(solution)/shard_map/ppermute | solution.py:302
  68.6 14.7 %collective-permute-start.9 = (bf16[32,2,32,128]{3,2,1,0:T(8,128)(2,1)}, bf16[32,2,32,128]{3,2,1,0:T(8,128)(2,1)}, u32[]{:S(2)}, u32[]{:S(2)}) collective-permute-start(bf16[32,2,32,128]{3,2,1,0:T(8,128)(2,1)} %get-tuple-element.26.refs_0_), channel_id=1, source_target_pairs={{0,1},{1,0},{2,3},{3,2},{4,5},{5,4},{6,7},{7,6},{8,9},{9,8},{10,11... | collective-permute-start | bytes 1572872 | tf_op jit(solution)/shard_map/ppermute | solution.py:301
  71.8 16.8 %collective-permute-start.14 = (bf16[8,32,1024]{2,1,0:T(8,128)(2,1)S(1)}, bf16[8,32,1024]{2,1,0:T(8,128)(2,1)}, u32[]{:S(2)}, u32[]{:S(2)}) collective-permute-start(bf16[8,32,1024]{2,1,0:T(8,128)(2,1)S(1)} %collective-permute-done.11.refs_8_), channel_id=1, source_target_pairs={{0,8},{8,0},{1,9},{9,1},{2,10},{10,2},{3,11},{11,3},{4,12},{12,4},... | collective-permute-start | bytes 1572872 | tf_op jit(solution)/shard_map/ppermute | solution.py:372
  73.6 16.8 %collective-permute-start.15 = (bf16[8,32,1024]{2,1,0:T(8,128)(2,1)}, bf16[8,32,1024]{2,1,0:T(8,128)(2,1)}, u32[]{:S(2)}, u32[]{:S(2)}) collective-permute-start(bf16[8,32,1024]{2,1,0:T(8,128)(2,1)} %collective-permute-done.13.refs_9_), channel_id=1, source_target_pairs={{0,8},{8,0},{1,9},{9,1},{2,10},{10,2},{3,11},{11,3},{4,12},{12,4},... | collective-permute-start | bytes 1572872 | tf_op jit(solution)/shard_map/ppermute | solution.py:372
  78.1 9.1 %collective-permute-start.16 = (bf16[16,2,32,128]{3,2,1,0:T(8,128)(2,1)S(1)}, bf16[16,2,32,128]{3,2,1,0:T(8,128)(2,1)}, u32[]{:S(2)}, u32[]{:S(2)}) collective-permute-start(bf16[16,2,32,128]{3,2,1,0:T(8,128)(2,1)S(1)} %collective-permute-done.7.refs_3_), channel_id=1, source_target_pairs={{0,2},{2,4},{4,6},{6,0},{1,3},{3,5},{5,7},{7,1},{8,10},{10,12},{12... | collective-permute-start | bytes 786440 | tf_op jit(solution)/shard_map/ppermute | solution.py:304
  79.3 8.9 %collective-permute-start.17 = (bf16[16,2,32,128]{3,2,1,0:T(8,128)(2,1)}, bf16[16,2,32,128]{3,2,1,0:T(8,128)(2,1)}, u32[]{:S(2)}, u32[]{:S(2)}) collective-permute-start(bf16[16,2,32,128]{3,2,1,0:T(8,128)(2,1)} %collective-permute-done.6.refs_2_), channel_id=1, source_target_pairs={{0,6},{2,0},{4,2},{6,4},{1,7},{3,1},{5,3},{7,5},{8,14},{10,8},{12,... | collective-permute-start | bytes 786440 | tf_op jit(solution)/shard_map/ppermute | solution.py:305
  83.3 19.1 %collective-permute-start.18 = (bf16[32,2,32,128]{3,2,1,0:T(8,128)(2,1)}, bf16[32,2,32,128]{3,2,1,0:T(8,128)(2,1)}, u32[]{:S(2)}, u32[]{:S(2)}) collective-permute-start(bf16[32,2,32,128]{3,2,1,0:T(8,128)(2,1)} %collective-permute-done.9.refs_5_), channel_id=1, source_target_pairs={{0,6},{2,0},{4,2},{6,4},{1,7},{3,1},{5,3},{7,5},{8,14},{10,8},{12,... | collective-permute-start | bytes 1572872 | tf_op jit(solution)/shard_map/ppermute | solution.py:307
  87.1 15.3 %collective-permute-start.21 = (bf16[32,2,32,128]{3,2,1,0:T(8,128)(2,1)}, bf16[32,2,32,128]{3,2,1,0:T(8,128)(2,1)}, u32[]{:S(2)}, u32[]{:S(2)}) collective-permute-start(bf16[32,2,32,128]{3,2,1,0:T(8,128)(2,1)} %collective-permute-done.9.refs_5_), channel_id=1, source_target_pairs={{0,2},{2,4},{4,6},{6,0},{1,3},{3,5},{5,7},{7,1},{8,10},{10,12},{12... | collective-permute-start | bytes 1572872 | tf_op jit(solution)/shard_map/ppermute | solution.py:306
  88.1 10.9 %collective-permute-start.19 = (bf16[16,2,32,128]{3,2,1,0:T(8,128)(2,1)}, bf16[16,2,32,128]{3,2,1,0:T(8,128)(2,1)S(1)}, u32[]{:S(2)}, u32[]{:S(2)}) collective-permute-start(bf16[16,2,32,128]{3,2,1,0:T(8,128)(2,1)} %collective-permute-done.16.refs_0_), channel_id=1, source_target_pairs={{0,1},{1,0},{2,3},{3,2},{4,5},{5,4},{6,7},{7,6},{8,9},{9,8},{10,11... | collective-permute-start | bytes 786440 | tf_op jit(solution)/shard_map/ppermute | solution.py:308
  88.6 13.1 %collective-permute-start.20 = (bf16[16,2,32,128]{3,2,1,0:T(8,128)(2,1)}, bf16[16,2,32,128]{3,2,1,0:T(8,128)(2,1)S(1)}, u32[]{:S(2)}, u32[]{:S(2)}) collective-permute-start(bf16[16,2,32,128]{3,2,1,0:T(8,128)(2,1)} %collective-permute-done.17.refs_1_), channel_id=1, source_target_pairs={{0,1},{1,0},{2,3},{3,2},{4,5},{5,4},{6,7},{7,6},{8,9},{9,8},{10,11... | collective-permute-start | bytes 786440 | tf_op jit(solution)/shard_map/ppermute | solution.py:309
  111.3 5.6 %collective-permute-start.26 = (bf16[3,32,1024]{2,1,0:T(8,128)(2,1)}, bf16[3,32,1024]{2,1,0:T(8,128)(2,1)S(1)}, u32[]{:S(2)}, u32[]{:S(2)}) collective-permute-start(bf16[3,32,1024]{2,1,0:T(8,128)(2,1)} %get-tuple-element.41), channel_id=1, source_target_pairs={{0,112},{16,0},{32,16},{48,32},{64,48},{80,64},{96,80},{112,96},{1... | collective-permute-start | bytes 589832 | tf_op jit(solution)/shard_map/ppermute | solution.py:243
  111.4 8.3 %collective-permute-start.22 = (bf16[3,32,1024]{2,1,0:T(8,128)(2,1)}, bf16[3,32,1024]{2,1,0:T(8,128)(2,1)S(1)}, u32[]{:S(2)}, u32[]{:S(2)}) collective-permute-start(bf16[3,32,1024]{2,1,0:T(8,128)(2,1)} %get-tuple-element.37), channel_id=1, source_target_pairs={{0,16},{16,32},{32,48},{48,64},{64,80},{80,96},{96,112},{112,0},{1... | collective-permute-start | bytes 589832 | tf_op jit(solution)/shard_map/ppermute | solution.py:242
  118.1 8.7 %collective-permute-start.27 = (bf16[2,3,32,1024]{3,2,1,0:T(8,128)(2,1)S(1)}, bf16[2,3,32,1024]{3,2,1,0:T(8,128)(2,1)S(1)}, u32[]{:S(2)}, u32[]{:S(2)}) collective-permute-start(bf16[2,3,32,1024]{3,2,1,0:T(8,128)(2,1)S(1)} %add_convert_fusion.2), channel_id=1, source_target_pairs={{0,112},{16,0},{32,16},{48,32},{64,48},{80,64},{96,80},{112,96},{1... | collective-permute-start | bytes 1179656 | tf_op jit(solution)/shard_map/ppermute | solution.py:246
  120.8 10.1 %collective-permute-start.23 = (bf16[2,3,32,1024]{3,2,1,0:T(8,128)(2,1)S(1)}, bf16[2,3,32,1024]{3,2,1,0:T(8,128)(2,1)S(1)}, u32[]{:S(2)}, u32[]{:S(2)}) collective-permute-start(bf16[2,3,32,1024]{3,2,1,0:T(8,128)(2,1)S(1)} %add_convert_fusion.5), channel_id=1, source_target_pairs={{0,16},{16,32},{32,48},{48,64},{64,80},{80,96},{96,112},{112,0},{1... | collective-permute-start | bytes 1179656 | tf_op jit(solution)/shard_map/ppermute | solution.py:245
  126.9 8.9 %collective-permute-start.28 = (bf16[2,3,32,1024]{3,2,1,0:T(8,128)(2,1)S(1)}, bf16[2,3,32,1024]{3,2,1,0:T(8,128)(2,1)S(1)}, u32[]{:S(2)}, u32[]{:S(2)}) collective-permute-start(bf16[2,3,32,1024]{3,2,1,0:T(8,128)(2,1)S(1)} %add_convert_fusion.1), channel_id=1, source_target_pairs={{0,112},{16,0},{32,16},{48,32},{64,48},{80,64},{96,80},{112,96},{1... | collective-permute-start | bytes 1179656 | tf_op jit(solution)/shard_map/ppermute | solution.py:246
  131.1 9.0 %collective-permute-start.24 = (bf16[2,3,32,1024]{3,2,1,0:T(8,128)(2,1)S(1)}, bf16[2,3,32,1024]{3,2,1,0:T(8,128)(2,1)S(1)}, u32[]{:S(2)}, u32[]{:S(2)}) collective-permute-start(bf16[2,3,32,1024]{3,2,1,0:T(8,128)(2,1)S(1)} %add_convert_fusion.4), channel_id=1, source_target_pairs={{0,16},{16,32},{32,48},{48,64},{64,80},{80,96},{96,112},{112,0},{1... | collective-permute-start | bytes 1179656 | tf_op jit(solution)/shard_map/ppermute | solution.py:245
  136.0 8.2 %collective-permute-start.29 = (bf16[2,3,32,1024]{3,2,1,0:T(8,128)(2,1)S(1)}, bf16[2,3,32,1024]{3,2,1,0:T(8,128)(2,1)S(1)}, u32[]{:S(2)}, u32[]{:S(2)}) collective-permute-start(bf16[2,3,32,1024]{3,2,1,0:T(8,128)(2,1)S(1)} %add_convert_fusion), channel_id=1, source_target_pairs={{0,112},{16,0},{32,16},{48,32},{64,48},{80,64},{96,80},{112,96},{1... | collective-permute-start | bytes 1179656 | tf_op jit(solution)/shard_map/ppermute | solution.py:246
  140.3 7.9 %collective-permute-start.25 = (bf16[2,3,32,1024]{3,2,1,0:T(8,128)(2,1)S(1)}, bf16[2,3,32,1024]{3,2,1,0:T(8,128)(2,1)S(1)}, u32[]{:S(2)}, u32[]{:S(2)}) collective-permute-start(bf16[2,3,32,1024]{3,2,1,0:T(8,128)(2,1)S(1)} %add_convert_fusion.3), channel_id=1, source_target_pairs={{0,16},{16,32},{32,48},{48,64},{64,80},{80,96},{96,112},{112,0},{1... | collective-permute-start | bytes 1179656 | tf_op jit(solution)/shard_map/ppermute | solution.py:245
  151.0 13.3 %collective-permute-start.30 = (bf16[3,32,1024]{2,1,0:T(8,128)(2,1)}, bf16[3,32,1024]{2,1,0:T(8,128)(2,1)S(1)}, u32[]{:S(2)}, u32[]{:S(2)}) collective-permute-start(bf16[3,32,1024]{2,1,0:T(8,128)(2,1)} %get-tuple-element.42.near), channel_id=1, source_target_pairs={{0,128},{1,129},{2,130},{3,131},{4,132},{5,133},{6,134},{7,135},{8... | collective-permute-start | bytes 589832 | tf_op jit(solution)/shard_map/ppermute | solution.py:401
  156.0 8.3 %collective-permute-start.31 = (bf16[3,32,1024]{2,1,0:T(8,128)(2,1)}, bf16[3,32,1024]{2,1,0:T(8,128)(2,1)S(1)}, u32[]{:S(2)}, u32[]{:S(2)}) collective-permute-start(bf16[3,32,1024]{2,1,0:T(8,128)(2,1)} %get-tuple-element.43), channel_id=1, source_target_pairs={{0,8},{8,0},{1,9},{9,1},{2,10},{10,2},{3,11},{11,3},{4,12},{12,4},... | collective-permute-start | bytes 589832 | tf_op jit(solution)/shard_map/ppermute | solution.py:400
  160.9 6.3 %collective-permute-start.32 = (bf16[3,32,1024]{2,1,0:T(8,128)(2,1)}, bf16[3,32,1024]{2,1,0:T(8,128)(2,1)S(1)}, u32[]{:S(2)}, u32[]{:S(2)}) collective-permute-start(bf16[3,32,1024]{2,1,0:T(8,128)(2,1)} %get-tuple-element.43), channel_id=1, source_target_pairs={{0,136},{8,128},{1,137},{9,129},{2,138},{10,130},{3,139},{11,131},... | collective-permute-start | bytes 589832 | tf_op jit(solution)/shard_map/ppermute | solution.py:402
  (28 other events, 369.9 us)

commit v8 on v7

--- a/solution.py
+++ b/solution.py
@@ -141,7 +141,7 @@
     count = len(REST) + 2
     features, refs = refs[:count], refs[count:]
     weights, refs = refs[:WEIGHTS], refs[WEIGHTS:]
-    outs, refs = refs[: len(DISTANCES) + 1], refs[len(DISTANCES) + 1 :]
+    outs, refs = refs[: C * len(DISTANCES)], refs[C * len(DISTANCES) :]
     weight, before, product, *held, feature_sem, weight_sem, before_sem = refs
     copies = load_weight(place, blocks, weights, weight, weight_sem) + load_features(features, held, feature_sem)
     befores = [
@@ -164,16 +164,10 @@
         befores[number].wait()
         value = (value + before[number].astype(jnp.float32)).astype(product.dtype)
         product[pl.ds(first, group)] = value.reshape(group, tokens, value.shape[1])
-    slots = outs[-1].shape[1]
+    slots = outs[0].shape[0]
     for index, out in enumerate(outs):
-        chunk = max(index - 1, 0)
-        for c in range(C):
-            for slot in range(slots):
-                value = product[slot_layer[(chunk * C + c) * slots + slot]]
-                if index > 1:
-                    out[c, slot] = value
-                elif index == c:
-                    out[slot] = value
+        for slot in range(slots):
+            out[slot] = product[slot_layer[index * slots + slot]]
 
 
 def project_first(place, blocks, features, weights):
@@ -207,7 +201,7 @@
     depth = len(REST) * halves * lanes
     slots = slot_layer.shape[0] // (len(DISTANCES) * C)
     smem, vmem = pl.BlockSpec(memory_space=pltpu.SMEM), pl.BlockSpec(memory_space=pltpu.VMEM)
-    shapes = [(slots, tokens, columns)] * C + [(C, slots, tokens, columns)] * (len(DISTANCES) - 1)
+    shapes = [(slots, tokens, columns)] * (C * len(DISTANCES))
     return pl.pallas_call(
         project_rest_kernel,
         out_shape=[jax.ShapeDtypeStruct(shape, jnp.bfloat16) for shape in shapes],
@@ -233,37 +227,24 @@
 def reduce_z(chunks):
     up = [(i, (i + 1) % Z) for i in range(Z)]
     down = [(i, (i - 1) % Z) for i in range(Z)]
-    low, high, up3, down3, up2, down2, up1, down1, own = chunks
-
-    def add(left, right):
-        return (left.astype(jnp.float32) + right.astype(jnp.float32)).astype(left.dtype)
-
-    rest = [(0, 0)] * low.ndim
-    from_below = jnp.pad(lax.ppermute(high, "z", up)[None], [(1, 0), *rest])
-    from_above = jnp.pad(lax.ppermute(low, "z", down)[None], [(0, 1), *rest])
-    for to_up, to_down in ((up3, down3), (up2, down2), (up1, down1)):
-        from_below = lax.ppermute(add(to_up, from_below), "z", up)
-        from_above = lax.ppermute(add(to_down, from_above), "z", down)
-    return own, from_below, from_above
-
-
-def combine_kernel(core, own, below, above, kept, given):
-    for out, c in ((kept, core[0]), (given, 1 - core[0])):
-        total = own[c].astype(jnp.float32) + below[c].astype(jnp.float32) + above[c].astype(jnp.float32)
-        out[...] = total.astype(out.dtype)
-
-
-def combine(c, own, below, above):
-    vmem = pl.BlockSpec(memory_space=pltpu.VMEM)
-    shape = jax.ShapeDtypeStruct(own.shape[1:], own.dtype)
-    return pl.pallas_call(
-        combine_kernel,
-        out_shape=[shape] * 2,
-        in_specs=[pl.BlockSpec(memory_space=pltpu.SMEM)] + [vmem] * 3,
-        out_specs=[vmem] * 2,
-        cost_estimate=pl.CostEstimate(flops=3 * own.size, bytes_accessed=8 * own.size, transcendentals=0),
-        name="combine",
-    )(c.reshape(1).astype(jnp.int32), own, below, above)
+    given = dict(zip(DISTANCES, chunks[0::2]))
+    kept = dict(zip(DISTANCES, chunks[1::2]))
+
+    def add(*terms):
+        return sum(term.astype(jnp.float32) for term in terms).astype(terms[0].dtype)
+
+    given_up = lax.ppermute(given[4], "z", up)
+    kept_down = lax.ppermute(kept[4], "z", down)
+    given_down = lax.ppermute(given[-3], "z", down)
+    kept_up = lax.ppermute(kept[3], "z", up)
+    for distance in (3, 2, 1):
+        given_up = lax.ppermute(add(given[distance], given_up), "z", up)
+        if distance < 3:
+            given_down = lax.ppermute(add(given[-distance], given_down), "z", down)
+        kept_down = lax.ppermute(add(kept[-distance], kept_down), "z", down)
+        if distance < 3:
+            kept_up = lax.ppermute(add(kept[distance], kept_up), "z", up)
+    return add(given[0], given_up, given_down), add(kept[0], kept_up, kept_down)
 
 
 def finish_kernel(state, hidden, layer_grad, near, teacher, across, teacher_across, out):
@@ -393,10 +374,11 @@
     prefix_end = jnp.cumsum(layer_counts)
     prefix_start = prefix_end - layer_counts
     slot_layer = jnp.clip(prefix_start[:, None] + jnp.arange(slot_count)[None, :], 0, layers - 1)
-    slot_layer = slot_layer.reshape(Z, C * slot_count)[(z + jnp.array(DISTANCES)) % Z].reshape(-1).astype(jnp.int32)
+    slot_layer = slot_layer.reshape(Z, C, slot_count)[(z + jnp.array(DISTANCES)) % Z]
+    slot_layer = jnp.where(c == 0, slot_layer[:, ::-1], slot_layer).reshape(-1).astype(jnp.int32)
     partial = project_first(place, first_blocks, first_features, weights)
     chunks = project_rest(place, rest_blocks, slot_layer, partial, rest_features, weights)
-    kept, given = combine(c, *reduce_z(chunks))
+    given, kept = reduce_z(chunks)
     across = lax.ppermute(given, "c", swap)
     teacher = lax.ppermute(kept, "yh", [(0, 1)])
     teacher_across = lax.ppermute(given, ("yh", "c"), [(0, 3), (1, 2)])

time: 172 us -> 165 us (0.959)
  waiting for transfers between devices: 56.9 us -> 37.4 us
  starting transfers between devices: 60.2 us -> 74.8 us
    ppermute x8 -> x14, waiting for transfers between devices: 19.8 us -> 6.16 us  [the longest x3 4.64 us: reduce_z(): kept_down = lax.ppermute(add(kept[-distance], kept_down), 'z', down)]
    ppermute x8 -> x14, starting transfers between devices: 10.2 us -> 22.5 us  [the longest x3 10.2 us: reduce_z(): kept_down = lax.ppermute(add(kept[-distance], kept_down), 'z', down)]
    ppermute x1, waiting for transfers between devices: 0.01 us -> 4.21 us  [body(): teacher = lax.ppermute(kept, 'yh', [(0, 1)])]
    ppermute x1, starting transfers between devices: 4.98 us -> 1.38 us  [body(): teacher = lax.ppermute(kept, 'yh', [(0, 1)])]
    all_to_all x1, waiting for transfers between devices: 5.22 us -> 2.64 us  [body(): lax.all_to_all(arranged, ('z', 'c'), split_axis=0, concat_axis=0, tiled=T...]
    ppermute x1, waiting for transfers between devices: 2.88 us -> 0.42 us  [body(): teacher_across = lax.ppermute(given, ('yh', 'c'), [(0, 3), (1, 2)])]
    ppermute x1, waiting for transfers between devices: 2.59 us -> 0.16 us  [gather_tensor(): f2a = lax.ppermute(f3a, 'x', up)]
    ppermute x1, starting transfers between devices: 4.87 us -> 7.04 us  [body(): across = lax.ppermute(given, 'c', swap)]
  transfers between devices with their start and end apart: 34 -> 40, of which waited for: 19 -> 17; matrix products, arithmetic and copies ran while one was open for 12% -> 12% of each run, Pallas kernels for 6% -> 7%
where the time goes in v8:
time: 165 us; the launch traced here: 163 us
  starting transfers between devices  74.8 us (45%)
  waiting for transfers between devices  37.4 us (23%)
  Pallas kernels  25.1 us (15%)
  matrix products  9.31 us (6%)
  local copies, waits for them, and re-layouts  7.6 us (5%)
  other arithmetic  7.12 us (4%)
  between operations  1.88 us (1%)
    ppermute x1, waiting for transfers between devices, body(): lax.ppermute(weight_rows[:, :half_rows], side, up)  11.6 us
    all_to_all x1, starting transfers between devices, body(): lax.all_to_all(arranged, ('z', 'c'), split_axis=0, concat_axis=0, tiled=T...  11.5 us
    ppermute x3, starting transfers between devices, reduce_z(): kept_down = lax.ppermute(add(kept[-distance], kept_down), 'z', down)  10.2 us
    pallas_call x1, Pallas kernels, project_rest(): pl.pallas_call(project_rest_kernel, out_shape=[jax.ShapeDtypeStruct(shape...  8.82 us
    ppermute x1, starting transfers between devices, body(): across = lax.ppermute(given, 'c', swap)  7.04 us
    pallas_call x1, Pallas kernels, project_first(): pl.pallas_call(project_first_kernel, out_shape=jax.ShapeDtypeStruct(shape...  6.88 us
    ppermute x1, starting transfers between devices, body(): sent = lax.ppermute(arrange(teacher_slabs, 1), side, [(0, 3), (1, 2)])  6.51 us
    ppermute x2, starting transfers between devices, reduce_z(): given_down = lax.ppermute(add(given[-distance], given_down), 'z', down)  6.43 us
  transfers between devices with their start and end apart: 40, of which 17 were waited for; matrix products, arithmetic and copies ran while one was open for 12% of the time, Pallas kernels for 7%

profile of v8, /device:TPU:1, one launch (start us, length us, event | category | flops | bytes accessed | tf_op | source)
XLA Modules:
  0.0 163.2 jit_solution(4621655728813912599)
XLA Ops:
  0.7 2.3 %arrange.3 = bf16[16,192,128]{2,1,0:T(8,128)(2,1)} custom-call(bf16[3,128,2048]{2,1,0:T(8,128)(2,1)} %slabs.3), custom_call_target="tpu_custom_call" | custom-call | bytes 1600000 | tf_op jit(solution)/shard_map/arrange/pallas_call | solution.py:36
  3.0 6.5 %collective-permute-start = (bf16[16,192,128]{2,1,0:T(8,128)(2,1)}, bf16[16,192,128]{2,1,0:T(8,128)(2,1)}, u32[]{:S(2)}, u32[]{:S(2)}) collective-permute-start(bf16[16,192,128]{2,1,0:T(8,128)(2,1)} %arrange.3), channel_id=1, source_target_pairs={{0,129},{1,128},{2,131},{3,130},{4,133},{5,132},{6,135},{7,134},{8... | collective-permute-start | bytes 2359304 | tf_op jit(solution)/shard_map/ppermute | solution.py:343
  10.4 2.4 %fusion = f32[128,1024]{1,0:T(8,128)S(1)} fusion(bf16[1,1024,1024]{2,1,0:T(8,128)(2,1)} %param.16, bf16[1,128,1024]{2,1,0:T(8,128)(2,1)S(1)} %copy-done.16), kind=kOutput, calls=%fused_computation.1 | convolution fusion | flops 268435456 | bytes 2883584 | tf_op jit(solution)/shard_map/dot_general | solution.py:331
  12.9 2.6 %fusion.11 = (f32[128]{0:T(128)S(1)}, f32[128]{0:T(128)S(1)}, f32[128,1024]{1,0:T(8,128)}) fusion(bf16[3,128,1024]{2,1,0:T(8,128)(2,1)} %hidden.1, f32[1024]{0:T(1024)S(1)} %bitcast.90, f32[128,1024]{1,0:T(8,128)S(1)} %fusion, bf16[1,1024,1024]{2,1,0:T(8,128)(2,1)S(1)} %copy-done.10, bf16[1,128,1024]{2,1,0:T(8,128)(2,1)S(1)} %copy-done), kind=kOutput, calls=%fused_computation.15 | convolution fusion | flops 269352704 | bytes 3675136 | tf_op jit(solution)/shard_map/dot_general | solution.py:328
  18.0 2.8 %collective-permute-start.3 = (f32[2,128]{1,0:T(2,128)S(1)}, f32[2,128]{1,0:T(2,128)S(1)}, u32[]{:S(2)}, u32[]{:S(2)}) collective-permute-start(f32[2,128]{1,0:T(2,128)S(1)} %fusion.30), channel_id=1, source_target_pairs={{0,4},{2,6},{4,0},{6,2},{1,5},{3,7},{5,1},{7,3},{8,12},{10,14},{12... | collective-permute-start | bytes 3080 | tf_op jit(solution)/shard_map/ppermute | solution.py:341
  22.2 2.2 %arrange.2 = bf16[16,192,128]{2,1,0:T(8,128)(2,1)} custom-call(bf16[3,128,2048]{2,1,0:T(8,128)(2,1)} %slabs.3), custom_call_target="tpu_custom_call" | custom-call | bytes 1600000 | tf_op jit(solution)/shard_map/arrange/pallas_call | solution.py:36
  27.2 11.5 %all-to-all-start = ((bf16[16,192,128]{2,1,0:T(8,128)(2,1)}), bf16[16,192,128]{2,1,0:T(8,128)(2,1)}, u32[]{:S(2)}, u32[]{:S(2)}) async-start(bf16[16,192,128]{2,1,0:T(8,128)(2,1)} %broadcast_select_fusion), calls=%async_computation | async-start | bytes 1572864 | tf_op jit(solution)/shard_map/all_to_all | solution.py:348
  39.9 2.3 %collective-permute-start.12 = (bf16[8,32,1024]{2,1,0:T(8,128)(2,1)}, bf16[8,32,1024]{2,1,0:T(8,128)(2,1)}, u32[]{:S(2)}, u32[]{:S(2)}) collective-permute-start(bf16[8,32,1024]{2,1,0:T(8,128)(2,1)} %get-tuple-element.60), channel_id=1, source_target_pairs={{0,129},{1,0},{128,1},{129,128},{2,131},{3,2},{130,3},{131,130},{4... | collective-permute-start | bytes 1572872 | tf_op jit(solution)/shard_map/ppermute | solution.py:347
  42.6 11.6 %collective-permute-done.10 = bf16[8,32,1024]{2,1,0:T(8,128)(2,1)} collective-permute-done((bf16[8,32,1024]{2,1,0:T(8,128)(2,1)S(1)}, bf16[8,32,1024]{2,1,0:T(8,128)(2,1)}, u32[]{:S(2)}, u32[]{:S(2)}) %collective-permute-start.10) | collective-permute-done | bytes 524320 | tf_op jit(solution)/shard_map/ppermute | solution.py:346
  54.2 2.7 %collective-permute-start.13 = (bf16[8,32,1024]{2,1,0:T(8,128)(2,1)}, bf16[8,32,1024]{2,1,0:T(8,128)(2,1)}, u32[]{:S(2)}, u32[]{:S(2)}) collective-permute-start(bf16[8,32,1024]{2,1,0:T(8,128)(2,1)} %collective-permute-done.12), channel_id=1, source_target_pairs={{0,129},{1,0},{128,1},{129,128},{2,131},{3,2},{130,3},{131,130},{4... | collective-permute-start | bytes 1572872 | tf_op jit(solution)/shard_map/ppermute | solution.py:347
  58.8 2.6 %all-to-all-done = bf16[16,192,128]{2,1,0:T(8,128)(2,1)} async-done(((bf16[16,192,128]{2,1,0:T(8,128)(2,1)}), bf16[16,192,128]{2,1,0:T(8,128)(2,1)}, u32[]{:S(2)}, u32[]{:S(2)}) %all-to-all-start) | async-done | bytes 786464 | tf_op jit(solution)/shard_map/all_to_all | solution.py:348
  61.4 2.3 %pick_layers.1 = (bf16[32,2,32,128]{3,2,1,0:T(8,128)(2,1)}, bf16[16,2,32,128]{3,2,1,0:T(8,128)(2,1)}, bf16[16,2,32,128]{3,2,1,0:T(8,128)(2,1)}) custom-call(s32[32]{0:T(128)} %layer_map.1, bf16[48,2,32,128]{3,2,1,0:T(8,128)(2,1)} %bitcast.26.received), custom_call_target="tpu_custom_call" | custom-call | bytes 1300000 | tf_op jit(solution)/shard_map/pick_layers/pallas_call | solution.py:65
  74.7 4.1 %collective-permute-done.5.refs_1_ = bf16[16,2,32,128]{3,2,1,0:T(8,128)(2,1)} collective-permute-done((bf16[16,2,32,128]{3,2,1,0:T(8,128)(2,1)}, bf16[16,2,32,128]{3,2,1,0:T(8,128)(2,1)}, u32[]{:S(2)}, u32[]{:S(2)}) %collective-permute-start.5) | collective-permute-done | bytes 262176 | tf_op jit(solution)/shard_map/ppermute | solution.py:284
  79.0 2.7 %collective-permute-start.17 = (bf16[16,2,32,128]{3,2,1,0:T(8,128)(2,1)}, bf16[16,2,32,128]{3,2,1,0:T(8,128)(2,1)S(1)}, u32[]{:S(2)}, u32[]{:S(2)}) collective-permute-start(bf16[16,2,32,128]{3,2,1,0:T(8,128)(2,1)} %collective-permute-done.6.refs_2_), channel_id=1, source_target_pairs={{0,6},{2,0},{4,2},{6,4},{1,7},{3,1},{5,3},{7,5},{8,14},{10,8},{12,... | collective-permute-start | bytes 786440 | tf_op jit(solution)/shard_map/ppermute | solution.py:286
  83.2 2.2 %fusion.19 = (f32[1024]{0:T(1024)S(1)}, f32[128,1024]{1,0:T(8,128)}) fusion(f32[128,1024]{1,0:T(8,128)} %get-tuple-element.62, f32[128]{0:T(128)S(1)} %get-tuple-element.57, bf16[3,128,1024]{2,1,0:T(8,128)(2,1)} %hidden.1, f32[128]{0:T(128)S(1)} %slice_bitcast_fusion, f32[128]{0:T(128)S(1)} %get-tuple-element.56, f32[1024]{0:T(1024)S(1)} %bitcast.91, pred[]{:T(512)S(6)} %eq.28), kind=kLoop, calls=%fused_computation.23 | loop fusion | flops 1440768 | bytes 1320449 | tf_op jit(solution)/shard_map/reduce_sum | solution.py:364
  85.4 2.1 %collective-permute-done.17.refs_1_ = bf16[16,2,32,128]{3,2,1,0:T(8,128)(2,1)S(1)} collective-permute-done((bf16[16,2,32,128]{3,2,1,0:T(8,128)(2,1)}, bf16[16,2,32,128]{3,2,1,0:T(8,128)(2,1)S(1)}, u32[]{:S(2)}, u32[]{:S(2)}) %collective-permute-start.17) | collective-permute-done | bytes 262176 | tf_op jit(solution)/shard_map/ppermute | solution.py:286
  90.8 6.9 %project_first.1.partial = bf16[4,256,1024]{2,1,0:T(8,128)(2,1)S(1)} custom-call(s32[4]{0:T(128)S(1)} %get-tuple-element.63.place, s32[4]{0:T(128)S(1)} %get-tuple-element.64.blocks, bf16[32,2,32,128]{3,2,1,0:T(8,128)(2,1)S(1)} %copy-done.7, bf16[16,2,32,128]{3,2,1,0:T(8,128)(2,1)} %collective-permute-done.5.refs_1_, ...), custom_call_target="tpu_custom_call" | custom-call | flops 2147483648 | bytes 8388608 | tf_op jit(solution)/shard_map/project_first/pallas_call | solution.py:179
  100.5 8.8 %project_rest.1 = (bf16[3,32,1024]{2,1,0:T(8,128)(2,1)}, bf16[3,32,1024]{2,1,0:T(8,128)(2,1)}, bf16[3,32,1024]{2,1,0:T(8,128)(2,1)}, bf16[3,32,1024]{2,1,0:T(8,1...) custom-call(s32[4]{0:T(128)} %copy-done.8, ...), custom_call_target="tpu_custom_call" | custom-call | flops 2147483648 | bytes 11534336 | tf_op jit(solution)/shard_map/project_rest/pallas_call | solution.py:205
  109.5 2.1 %select_bitcast_fusion = bf16[1,1024,1024]{2,1,0:T(8,128)(2,1)} fusion(pred[]{:T(512)S(6)} %eq.28, bf16[1,128,1024]{2,1,0:T(8,128)(2,1)S(1)} %copy-done.17, f32[1024]{0:T(1024)S(1)} %bitcast.92, f32[128]{0:T(128)S(1)} %get-tuple-element.57, bf16[3,128,1024]{2,1,0:T(8,128)(2,1)S(1)} %copy-done.9), kind=kOutput, calls=%fused_computation.5 | convolution fusion | flops 271056896 | bytes 2626049 | tf_op jit(solution)/shard_map/dot_general | solution.py:361
  111.7 2.7 %collective-permute-start.34 = (bf16[3,32,1024]{2,1,0:T(8,128)(2,1)S(1)}, bf16[3,32,1024]{2,1,0:T(8,128)(2,1)S(1)}, u32[]{:S(2)}, u32[]{:S(2)}) collective-permute-start(bf16[3,32,1024]{2,1,0:T(8,128)(2,1)S(1)} %copy-done.37), channel_id=1, source_target_pairs={{0,112},{16,0},{32,16},{48,32},{64,48},{80,64},{96,80},{112,96},{1... | collective-permute-start | bytes 589832 | tf_op jit(solution)/shard_map/ppermute | solution.py:238
  114.4 2.7 %collective-permute-start.25 = (bf16[3,32,1024]{2,1,0:T(8,128)(2,1)S(1)}, bf16[3,32,1024]{2,1,0:T(8,128)(2,1)S(1)}, u32[]{:S(2)}, u32[]{:S(2)}) collective-permute-start(bf16[3,32,1024]{2,1,0:T(8,128)(2,1)S(1)} %copy-done.35), channel_id=1, source_target_pairs={{0,112},{16,0},{32,16},{48,32},{64,48},{80,64},{96,80},{112,96},{1... | collective-permute-start | bytes 589832 | tf_op jit(solution)/shard_map/ppermute | solution.py:237
  117.3 2.9 %collective-permute-start.35 = (bf16[3,32,1024]{2,1,0:T(8,128)(2,1)S(1)}, bf16[3,32,1024]{2,1,0:T(8,128)(2,1)S(1)}, u32[]{:S(2)}, u32[]{:S(2)}) collective-permute-start(bf16[3,32,1024]{2,1,0:T(8,128)(2,1)S(1)} %add_convert_fusion.2), channel_id=1, source_target_pairs={{0,112},{16,0},{32,16},{48,32},{64,48},{80,64},{96,80},{112,96},{1... | collective-permute-start | bytes 589832 | tf_op jit(solution)/shard_map/ppermute | solution.py:243
  121.5 3.5 %collective-permute-start.26 = (bf16[3,32,1024]{2,1,0:T(8,128)(2,1)S(1)}, bf16[3,32,1024]{2,1,0:T(8,128)(2,1)S(1)}, u32[]{:S(2)}, u32[]{:S(2)}) collective-permute-start(bf16[3,32,1024]{2,1,0:T(8,128)(2,1)S(1)} %add_convert_fusion.9), channel_id=1, source_target_pairs={{0,112},{16,0},{32,16},{48,32},{64,48},{80,64},{96,80},{112,96},{1... | collective-permute-start | bytes 589832 | tf_op jit(solution)/shard_map/ppermute | solution.py:244
  125.7 3.5 %collective-permute-start.36 = (bf16[3,32,1024]{2,1,0:T(8,128)(2,1)S(1)}, bf16[3,32,1024]{2,1,0:T(8,128)(2,1)S(1)}, u32[]{:S(2)}, u32[]{:S(2)}) collective-permute-start(bf16[3,32,1024]{2,1,0:T(8,128)(2,1)S(1)} %add_convert_fusion.1), channel_id=1, source_target_pairs={{0,112},{16,0},{32,16},{48,32},{64,48},{80,64},{96,80},{112,96},{1... | collective-permute-start | bytes 589832 | tf_op jit(solution)/shard_map/ppermute | solution.py:243
  129.4 3.2 %collective-permute-start.27 = (bf16[3,32,1024]{2,1,0:T(8,128)(2,1)S(1)}, bf16[3,32,1024]{2,1,0:T(8,128)(2,1)S(1)}, u32[]{:S(2)}, u32[]{:S(2)}) collective-permute-start(bf16[3,32,1024]{2,1,0:T(8,128)(2,1)S(1)} %add_convert_fusion.8), channel_id=1, source_target_pairs={{0,112},{16,0},{32,16},{48,32},{64,48},{80,64},{96,80},{112,96},{1... | collective-permute-start | bytes 589832 | tf_op jit(solution)/shard_map/ppermute | solution.py:244
  132.8 4.6 %collective-permute-done.27 = bf16[3,32,1024]{2,1,0:T(8,128)(2,1)S(1)} collective-permute-done((bf16[3,32,1024]{2,1,0:T(8,128)(2,1)S(1)}, bf16[3,32,1024]{2,1,0:T(8,128)(2,1)S(1)}, u32[]{:S(2)}, u32[]{:S(2)}) %collective-permute-start.27) | collective-permute-done | bytes 196640 | tf_op jit(solution)/shard_map/ppermute | solution.py:244
  137.5 3.5 %collective-permute-start.28 = (bf16[3,32,1024]{2,1,0:T(8,128)(2,1)S(1)}, bf16[3,32,1024]{2,1,0:T(8,128)(2,1)S(1)}, u32[]{:S(2)}, u32[]{:S(2)}) collective-permute-start(bf16[3,32,1024]{2,1,0:T(8,128)(2,1)S(1)} %add_convert_fusion.7), channel_id=1, source_target_pairs={{0,112},{16,0},{32,16},{48,32},{64,48},{80,64},{96,80},{112,96},{1... | collective-permute-start | bytes 589832 | tf_op jit(solution)/shard_map/ppermute | solution.py:244
  141.1 7.0 %collective-permute-start.37 = (bf16[3,32,1024]{2,1,0:T(8,128)(2,1)S(1)}, bf16[3,32,1024]{2,1,0:T(8,128)(2,1)S(1)}, u32[]{:S(2)}, u32[]{:S(2)}) collective-permute-start(bf16[3,32,1024]{2,1,0:T(8,128)(2,1)S(1)} %add_convert_fusion), channel_id=1, source_target_pairs={{0,8},{8,0},{1,9},{9,1},{2,10},{10,2},{3,11},{11,3},{4,12},{12,4},... | collective-permute-start | bytes 589832 | tf_op jit(solution)/shard_map/ppermute | solution.py:382
  148.1 3.4 %collective-permute-start.38 = (bf16[3,32,1024]{2,1,0:T(8,128)(2,1)S(1)}, bf16[3,32,1024]{2,1,0:T(8,128)(2,1)S(1)}, u32[]{:S(2)}, u32[]{:S(2)}) collective-permute-start(bf16[3,32,1024]{2,1,0:T(8,128)(2,1)S(1)} %add_convert_fusion), channel_id=1, source_target_pairs={{0,136},{8,128},{1,137},{9,129},{2,138},{10,130},{3,139},{11,131},... | collective-permute-start | bytes 589832 | tf_op jit(solution)/shard_map/ppermute | solution.py:384
  153.1 2.1 %select_bitcast_fusion.1 = bf16[1,1024,1024]{2,1,0:T(8,128)(2,1)} fusion(pred[]{:T(512)S(6)} %eq.28, bf16[1,128,1024]{2,1,0:T(8,128)(2,1)S(1)} %copy-done, f32[1024]{0:T(1024)S(1)} %bitcast.93, f32[128]{0:T(128)S(1)} %get-tuple-element.57, bf16[3,128,1024]{2,1,0:T(8,128)(2,1)S(1)} %copy-done.9), kind=kOutput, calls=%fused_computation.6 | convolution fusion | flops 271056896 | bytes 2626049 | tf_op jit(solution)/shard_map/dot_general | solution.py:358
  155.6 4.2 %collective-permute-done.29.teacher = bf16[3,32,1024]{2,1,0:T(8,128)(2,1)S(1)} collective-permute-done((bf16[3,32,1024]{2,1,0:T(8,128)(2,1)S(1)}, bf16[3,32,1024]{2,1,0:T(8,128)(2,1)S(1)}, u32[]{:S(2)}, u32[]{:S(2)}) %collective-permute-start.29) | collective-permute-done | bytes 196640 | tf_op jit(solution)/shard_map/ppermute | solution.py:383
  160.5 2.6 %finish.1 = bf16[3,128,1024]{2,1,0:T(8,128)(2,1)} custom-call(s32[2]{0:T(128)} %pad_add_fusion.state, bf16[3,128,1024]{2,1,0:T(8,128)(2,1)} %hidden.1, f32[128,1024]{1,0:T(8,128)} %get-tuple-element.59.layer_grad, bf16[3,32,1024]{2,1,0:T(8,128)(2,1)} %copy-done.11, bf16[3,32,1024]{2,1,0:T(8,128)(2,1)} %copy-done.20, bf16[3,32,1024]{2,1,0:T(8,128)(2,1)} %copy-done.18, ...), custom_call_target="tpu_custom_call" | custom-call | flops 786432 | bytes 3145728 | tf_op jit(solution)/shard_map/finish/pallas_call | solution.py:266
  (174 shorter events, 34.4 us)
Async XLA Ops:
  3.0 22.1 %collective-permute-start = (bf16[16,192,128]{2,1,0:T(8,128)(2,1)}, bf16[16,192,128]{2,1,0:T(8,128)(2,1)}, u32[]{:S(2)}, u32[]{:S(2)}) collective-permute-start(bf16[16,192,128]{2,1,0:T(8,128)(2,1)} %arrange.3), channel_id=1, source_target_pairs={{0,129},{1,128},{2,131},{3,130},{4,133},{5,132},{6,135},{7,134},{8... | collective-permute-start | bytes 2359304 | tf_op jit(solution)/shard_map/ppermute | solution.py:343
  9.5 17.7 %collective-permute-start.1 = (bf16[8,64,1024]{2,1,0:T(8,128)(2,1)S(1)}, bf16[8,64,1024]{2,1,0:T(8,128)(2,1)S(1)}, u32[]{:S(2)}, u32[]{:S(2)}) collective-permute-start(bf16[8,64,1024]{2,1,0:T(8,128)(2,1)S(1)} %copy-done.1), channel_id=1, source_target_pairs={{0,8},{8,0},{1,9},{9,1},{2,10},{10,2},{3,11},{11,3},{4,12},{12,4},... | collective-permute-start | bytes 3145736 | tf_op jit(solution)/shard_map/ppermute | solution.py:321
  27.2 34.2 %all-to-all-start = ((bf16[16,192,128]{2,1,0:T(8,128)(2,1)}), bf16[16,192,128]{2,1,0:T(8,128)(2,1)}, u32[]{:S(2)}, u32[]{:S(2)}) async-start(bf16[16,192,128]{2,1,0:T(8,128)(2,1)} %broadcast_select_fusion), calls=%async_computation | async-start | bytes 1572864 | tf_op jit(solution)/shard_map/all_to_all | solution.py:348
  39.5 14.7 %collective-permute-start.10 = (bf16[8,32,1024]{2,1,0:T(8,128)(2,1)S(1)}, bf16[8,32,1024]{2,1,0:T(8,128)(2,1)}, u32[]{:S(2)}, u32[]{:S(2)}) collective-permute-start(bf16[8,32,1024]{2,1,0:T(8,128)(2,1)S(1)} %get-tuple-element.61), channel_id=1, source_target_pairs={{0,1},{1,128},{128,129},{129,0},{2,3},{3,130},{130,131},{131,2},{4... | collective-permute-start | bytes 1572872 | tf_op jit(solution)/shard_map/ppermute | solution.py:346
  39.9 14.4 %collective-permute-start.12 = (bf16[8,32,1024]{2,1,0:T(8,128)(2,1)}, bf16[8,32,1024]{2,1,0:T(8,128)(2,1)}, u32[]{:S(2)}, u32[]{:S(2)}) collective-permute-start(bf16[8,32,1024]{2,1,0:T(8,128)(2,1)} %get-tuple-element.60), channel_id=1, source_target_pairs={{0,129},{1,0},{128,1},{129,128},{2,131},{3,2},{130,3},{131,130},{4... | collective-permute-start | bytes 1572872 | tf_op jit(solution)/shard_map/ppermute | solution.py:347
  54.2 14.2 %collective-permute-start.11 = (bf16[8,32,1024]{2,1,0:T(8,128)(2,1)}, bf16[8,32,1024]{2,1,0:T(8,128)(2,1)S(1)}, u32[]{:S(2)}, u32[]{:S(2)}) collective-permute-start(bf16[8,32,1024]{2,1,0:T(8,128)(2,1)} %collective-permute-done.10), channel_id=1, source_target_pairs={{0,1},{1,128},{128,129},{129,0},{2,3},{3,130},{130,131},{131,2},{4... | collective-permute-start | bytes 1572872 | tf_op jit(solution)/shard_map/ppermute | solution.py:346
  54.2 15.1 %collective-permute-start.13 = (bf16[8,32,1024]{2,1,0:T(8,128)(2,1)}, bf16[8,32,1024]{2,1,0:T(8,128)(2,1)}, u32[]{:S(2)}, u32[]{:S(2)}) collective-permute-start(bf16[8,32,1024]{2,1,0:T(8,128)(2,1)} %collective-permute-done.12), channel_id=1, source_target_pairs={{0,129},{1,0},{128,1},{129,128},{2,131},{3,2},{130,3},{131,130},{4... | collective-permute-start | bytes 1572872 | tf_op jit(solution)/shard_map/ppermute | solution.py:347
  63.7 8.8 %collective-permute-start.7 = (bf16[16,2,32,128]{3,2,1,0:T(8,128)(2,1)}, bf16[16,2,32,128]{3,2,1,0:T(8,128)(2,1)S(1)}, u32[]{:S(2)}, u32[]{:S(2)}) collective-permute-start(bf16[16,2,32,128]{3,2,1,0:T(8,128)(2,1)} %get-tuple-element.32), channel_id=1, source_target_pairs={{0,2},{2,4},{4,6},{6,0},{1,3},{3,5},{5,7},{7,1},{8,10},{10,12},{12... | collective-permute-start | bytes 786440 | tf_op jit(solution)/shard_map/ppermute | solution.py:280
  64.9 8.5 %collective-permute-start.6 = (bf16[16,2,32,128]{3,2,1,0:T(8,128)(2,1)}, bf16[16,2,32,128]{3,2,1,0:T(8,128)(2,1)}, u32[]{:S(2)}, u32[]{:S(2)}) collective-permute-start(bf16[16,2,32,128]{3,2,1,0:T(8,128)(2,1)} %get-tuple-element.33), channel_id=1, source_target_pairs={{0,6},{2,0},{4,2},{6,4},{1,7},{3,1},{5,3},{7,5},{8,14},{10,8},{12,... | collective-permute-start | bytes 786440 | tf_op jit(solution)/shard_map/ppermute | solution.py:281
  67.1 11.7 %collective-permute-start.5 = (bf16[16,2,32,128]{3,2,1,0:T(8,128)(2,1)}, bf16[16,2,32,128]{3,2,1,0:T(8,128)(2,1)}, u32[]{:S(2)}, u32[]{:S(2)}) collective-permute-start(bf16[16,2,32,128]{3,2,1,0:T(8,128)(2,1)} %get-tuple-element.32), channel_id=1, source_target_pairs={{0,6},{2,0},{4,2},{6,4},{1,7},{3,1},{5,3},{7,5},{8,14},{10,8},{12,... | collective-permute-start | bytes 786440 | tf_op jit(solution)/shard_map/ppermute | solution.py:284
  68.4 10.6 %collective-permute-start.8 = (bf16[16,2,32,128]{3,2,1,0:T(8,128)(2,1)}, bf16[16,2,32,128]{3,2,1,0:T(8,128)(2,1)}, u32[]{:S(2)}, u32[]{:S(2)}) collective-permute-start(bf16[16,2,32,128]{3,2,1,0:T(8,128)(2,1)} %get-tuple-element.33), channel_id=1, source_target_pairs={{0,2},{2,4},{4,6},{6,0},{1,3},{3,5},{5,7},{7,1},{8,10},{10,12},{12... | collective-permute-start | bytes 786440 | tf_op jit(solution)/shard_map/ppermute | solution.py:283
  69.3 12.3 %collective-permute-start.9 = (bf16[32,2,32,128]{3,2,1,0:T(8,128)(2,1)}, bf16[32,2,32,128]{3,2,1,0:T(8,128)(2,1)}, u32[]{:S(2)}, u32[]{:S(2)}) collective-permute-start(bf16[32,2,32,128]{3,2,1,0:T(8,128)(2,1)} %get-tuple-element.31.refs_0_), channel_id=1, source_target_pairs={{0,1},{1,0},{2,3},{3,2},{4,5},{5,4},{6,7},{7,6},{8,9},{9,8},{10,11... | collective-permute-start | bytes 1572872 | tf_op jit(solution)/shard_map/ppermute | solution.py:282
  72.5 15.0 %collective-permute-start.14 = (bf16[8,32,1024]{2,1,0:T(8,128)(2,1)S(1)}, bf16[8,32,1024]{2,1,0:T(8,128)(2,1)S(1)}, u32[]{:S(2)}, u32[]{:S(2)}) collective-permute-start(bf16[8,32,1024]{2,1,0:T(8,128)(2,1)S(1)} %collective-permute-done.11.refs_8_), channel_id=1, source_target_pairs={{0,8},{8,0},{1,9},{9,1},{2,10},{10,2},{3,11},{11,3},{4,12},{12,4},... | collective-permute-start | bytes 1572872 | tf_op jit(solution)/shard_map/ppermute | solution.py:353
  73.5 9.6 %collective-permute-start.16 = (bf16[16,2,32,128]{3,2,1,0:T(8,128)(2,1)S(1)}, bf16[16,2,32,128]{3,2,1,0:T(8,128)(2,1)S(1)}, u32[]{:S(2)}, u32[]{:S(2)}) collective-permute-start(bf16[16,2,32,128]{3,2,1,0:T(8,128)(2,1)S(1)} %collective-permute-done.7.refs_3_), channel_id=1, source_target_pairs={{0,2},{2,4},{4,6},{6,0},{1,3},{3,5},{5,7},{7,1},{8,10},{10,12},{12... | collective-permute-start | bytes 786440 | tf_op jit(solution)/shard_map/ppermute | solution.py:285
  78.8 10.8 %collective-permute-start.15 = (bf16[8,32,1024]{2,1,0:T(8,128)(2,1)}, bf16[8,32,1024]{2,1,0:T(8,128)(2,1)S(1)}, u32[]{:S(2)}, u32[]{:S(2)}) collective-permute-start(bf16[8,32,1024]{2,1,0:T(8,128)(2,1)} %collective-permute-done.13.refs_9_), channel_id=1, source_target_pairs={{0,8},{8,0},{1,9},{9,1},{2,10},{10,2},{3,11},{11,3},{4,12},{12,4},... | collective-permute-start | bytes 1572872 | tf_op jit(solution)/shard_map/ppermute | solution.py:353
  79.0 8.6 %collective-permute-start.17 = (bf16[16,2,32,128]{3,2,1,0:T(8,128)(2,1)}, bf16[16,2,32,128]{3,2,1,0:T(8,128)(2,1)S(1)}, u32[]{:S(2)}, u32[]{:S(2)}) collective-permute-start(bf16[16,2,32,128]{3,2,1,0:T(8,128)(2,1)} %collective-permute-done.6.refs_2_), channel_id=1, source_target_pairs={{0,6},{2,0},{4,2},{6,4},{1,7},{3,1},{5,3},{7,5},{8,14},{10,8},{12,... | collective-permute-start | bytes 786440 | tf_op jit(solution)/shard_map/ppermute | solution.py:286
  81.6 18.2 %collective-permute-start.18 = (bf16[32,2,32,128]{3,2,1,0:T(8,128)(2,1)}, bf16[32,2,32,128]{3,2,1,0:T(8,128)(2,1)}, u32[]{:S(2)}, u32[]{:S(2)}) collective-permute-start(bf16[32,2,32,128]{3,2,1,0:T(8,128)(2,1)} %collective-permute-done.9.refs_5_), channel_id=1, source_target_pairs={{0,6},{2,0},{4,2},{6,4},{1,7},{3,1},{5,3},{7,5},{8,14},{10,8},{12,... | collective-permute-start | bytes 1572872 | tf_op jit(solution)/shard_map/ppermute | solution.py:288
  83.1 17.4 %collective-permute-start.21 = (bf16[32,2,32,128]{3,2,1,0:T(8,128)(2,1)}, bf16[32,2,32,128]{3,2,1,0:T(8,128)(2,1)}, u32[]{:S(2)}, u32[]{:S(2)}) collective-permute-start(bf16[32,2,32,128]{3,2,1,0:T(8,128)(2,1)} %collective-permute-done.9.refs_5_), channel_id=1, source_target_pairs={{0,2},{2,4},{4,6},{6,0},{1,3},{3,5},{5,7},{7,1},{8,10},{10,12},{12... | collective-permute-start | bytes 1572872 | tf_op jit(solution)/shard_map/ppermute | solution.py:287
  87.5 11.6 %collective-permute-start.19 = (bf16[16,2,32,128]{3,2,1,0:T(8,128)(2,1)S(1)}, bf16[16,2,32,128]{3,2,1,0:T(8,128)(2,1)S(1)}, u32[]{:S(2)}, u32[]{:S(2)}) collective-permute-start(bf16[16,2,32,128]{3,2,1,0:T(8,128)(2,1)S(1)} %collective-permute-done.16.refs_0_), channel_id=1, source_target_pairs={{0,1},{1,0},{2,3},{3,2},{4,5},{5,4},{6,7},{7,6},{8,9},{9,8},{10,11... | collective-permute-start | bytes 786440 | tf_op jit(solution)/shard_map/ppermute | solution.py:289
  87.5 11.6 %collective-permute-start.20 = (bf16[16,2,32,128]{3,2,1,0:T(8,128)(2,1)S(1)}, bf16[16,2,32,128]{3,2,1,0:T(8,128)(2,1)S(1)}, u32[]{:S(2)}, u32[]{:S(2)}) collective-permute-start(bf16[16,2,32,128]{3,2,1,0:T(8,128)(2,1)S(1)} %collective-permute-done.17.refs_1_), channel_id=1, source_target_pairs={{0,1},{1,0},{2,3},{3,2},{4,5},{5,4},{6,7},{7,6},{8,9},{9,8},{10,11... | collective-permute-start | bytes 786440 | tf_op jit(solution)/shard_map/ppermute | solution.py:290
  109.4 7.7 %collective-permute-start.30 = (bf16[3,32,1024]{2,1,0:T(8,128)(2,1)}, bf16[3,32,1024]{2,1,0:T(8,128)(2,1)S(1)}, u32[]{:S(2)}, u32[]{:S(2)}) collective-permute-start(bf16[3,32,1024]{2,1,0:T(8,128)(2,1)} %get-tuple-element.50), channel_id=1, source_target_pairs={{0,16},{16,32},{32,48},{48,64},{64,80},{80,96},{96,112},{112,0},{1... | collective-permute-start | bytes 589832 | tf_op jit(solution)/shard_map/ppermute | solution.py:236
  117.2 7.8 %collective-permute-start.31 = (bf16[3,32,1024]{2,1,0:T(8,128)(2,1)S(1)}, bf16[3,32,1024]{2,1,0:T(8,128)(2,1)S(1)}, u32[]{:S(2)}, u32[]{:S(2)}) collective-permute-start(bf16[3,32,1024]{2,1,0:T(8,128)(2,1)S(1)} %add_convert_fusion.5), channel_id=1, source_target_pairs={{0,16},{16,32},{32,48},{48,64},{64,80},{80,96},{96,112},{112,0},{1... | collective-permute-start | bytes 589832 | tf_op jit(solution)/shard_map/ppermute | solution.py:241
  117.3 8.3 %collective-permute-start.35 = (bf16[3,32,1024]{2,1,0:T(8,128)(2,1)S(1)}, bf16[3,32,1024]{2,1,0:T(8,128)(2,1)S(1)}, u32[]{:S(2)}, u32[]{:S(2)}) collective-permute-start(bf16[3,32,1024]{2,1,0:T(8,128)(2,1)S(1)} %add_convert_fusion.2), channel_id=1, source_target_pairs={{0,112},{16,0},{32,16},{48,32},{64,48},{80,64},{96,80},{112,96},{1... | collective-permute-start | bytes 589832 | tf_op jit(solution)/shard_map/ppermute | solution.py:243
  120.5 8.7 %collective-permute-start.23 = (bf16[3,32,1024]{2,1,0:T(8,128)(2,1)S(1)}, bf16[3,32,1024]{2,1,0:T(8,128)(2,1)S(1)}, u32[]{:S(2)}, u32[]{:S(2)}) collective-permute-start(bf16[3,32,1024]{2,1,0:T(8,128)(2,1)S(1)} %add_convert_fusion.11), channel_id=1, source_target_pairs={{0,16},{16,32},{32,48},{48,64},{64,80},{80,96},{96,112},{112,0},{1... | collective-permute-start | bytes 589832 | tf_op jit(solution)/shard_map/ppermute | solution.py:246
  121.5 7.9 %collective-permute-start.26 = (bf16[3,32,1024]{2,1,0:T(8,128)(2,1)S(1)}, bf16[3,32,1024]{2,1,0:T(8,128)(2,1)S(1)}, u32[]{:S(2)}, u32[]{:S(2)}) collective-permute-start(bf16[3,32,1024]{2,1,0:T(8,128)(2,1)S(1)} %add_convert_fusion.9), channel_id=1, source_target_pairs={{0,112},{16,0},{32,16},{48,32},{64,48},{80,64},{96,80},{112,96},{1... | collective-permute-start | bytes 589832 | tf_op jit(solution)/shard_map/ppermute | solution.py:244
  125.7 15.3 %collective-permute-start.36 = (bf16[3,32,1024]{2,1,0:T(8,128)(2,1)S(1)}, bf16[3,32,1024]{2,1,0:T(8,128)(2,1)S(1)}, u32[]{:S(2)}, u32[]{:S(2)}) collective-permute-start(bf16[3,32,1024]{2,1,0:T(8,128)(2,1)S(1)} %add_convert_fusion.1), channel_id=1, source_target_pairs={{0,112},{16,0},{32,16},{48,32},{64,48},{80,64},{96,80},{112,96},{1... | collective-permute-start | bytes 589832 | tf_op jit(solution)/shard_map/ppermute | solution.py:243
  129.3 22.3 %collective-permute-start.24 = (bf16[3,32,1024]{2,1,0:T(8,128)(2,1)S(1)}, bf16[3,32,1024]{2,1,0:T(8,128)(2,1)S(1)}, u32[]{:S(2)}, u32[]{:S(2)}) collective-permute-start(bf16[3,32,1024]{2,1,0:T(8,128)(2,1)S(1)} %add_convert_fusion.10), channel_id=1, source_target_pairs={{0,16},{16,32},{32,48},{48,64},{64,80},{80,96},{96,112},{112,0},{1... | collective-permute-start | bytes 589832 | tf_op jit(solution)/shard_map/ppermute | solution.py:246
  129.4 8.0 %collective-permute-start.27 = (bf16[3,32,1024]{2,1,0:T(8,128)(2,1)S(1)}, bf16[3,32,1024]{2,1,0:T(8,128)(2,1)S(1)}, u32[]{:S(2)}, u32[]{:S(2)}) collective-permute-start(bf16[3,32,1024]{2,1,0:T(8,128)(2,1)S(1)} %add_convert_fusion.8), channel_id=1, source_target_pairs={{0,112},{16,0},{32,16},{48,32},{64,48},{80,64},{96,80},{112,96},{1... | collective-permute-start | bytes 589832 | tf_op jit(solution)/shard_map/ppermute | solution.py:244
  132.7 8.3 %collective-permute-start.33 = (bf16[3,32,1024]{2,1,0:T(8,128)(2,1)S(1)}, bf16[3,32,1024]{2,1,0:T(8,128)(2,1)S(1)}, u32[]{:S(2)}, u32[]{:S(2)}) collective-permute-start(bf16[3,32,1024]{2,1,0:T(8,128)(2,1)S(1)} %add_convert_fusion.3), channel_id=1, source_target_pairs={{0,16},{16,32},{32,48},{48,64},{64,80},{80,96},{96,112},{112,0},{1... | collective-permute-start | bytes 589832 | tf_op jit(solution)/shard_map/ppermute | solution.py:241
  137.5 14.1 %collective-permute-start.28 = (bf16[3,32,1024]{2,1,0:T(8,128)(2,1)S(1)}, bf16[3,32,1024]{2,1,0:T(8,128)(2,1)S(1)}, u32[]{:S(2)}, u32[]{:S(2)}) collective-permute-start(bf16[3,32,1024]{2,1,0:T(8,128)(2,1)S(1)} %add_convert_fusion.7), channel_id=1, source_target_pairs={{0,112},{16,0},{32,16},{48,32},{64,48},{80,64},{96,80},{112,96},{1... | collective-permute-start | bytes 589832 | tf_op jit(solution)/shard_map/ppermute | solution.py:244
  141.1 14.1 %collective-permute-start.37 = (bf16[3,32,1024]{2,1,0:T(8,128)(2,1)S(1)}, bf16[3,32,1024]{2,1,0:T(8,128)(2,1)S(1)}, u32[]{:S(2)}, u32[]{:S(2)}) collective-permute-start(bf16[3,32,1024]{2,1,0:T(8,128)(2,1)S(1)} %add_convert_fusion), channel_id=1, source_target_pairs={{0,8},{8,0},{1,9},{9,1},{2,10},{10,2},{3,11},{11,3},{4,12},{12,4},... | collective-permute-start | bytes 589832 | tf_op jit(solution)/shard_map/ppermute | solution.py:382
  151.7 8.2 %collective-permute-start.29 = (bf16[3,32,1024]{2,1,0:T(8,128)(2,1)S(1)}, bf16[3,32,1024]{2,1,0:T(8,128)(2,1)S(1)}, u32[]{:S(2)}, u32[]{:S(2)}) collective-permute-start(bf16[3,32,1024]{2,1,0:T(8,128)(2,1)S(1)} %add_convert_fusion.6.near), channel_id=1, source_target_pairs={{0,128},{1,129},{2,130},{3,131},{4,132},{5,133},{6,134},{7,135},{8... | collective-permute-start | bytes 589832 | tf_op jit(solution)/shard_map/ppermute | solution.py:383
  (47 other events, 532.9 us)

commit v9 on v8

--- a/solution.py
+++ b/solution.py
@@ -280,6 +280,7 @@
     f3a = lax.ppermute(low, "x", up)
     f1b = lax.ppermute(high, "x", down)
     g0 = lax.ppermute(own, "yl", swap)
+    low, high, f3a, f1b = lax.optimization_barrier((low, high, f3a, f1b))
     f3b = lax.ppermute(high, "x", up)
     f1a = lax.ppermute(low, "x", down)
     f2a = lax.ppermute(f3a, "x", up)
@@ -348,9 +349,6 @@
     received = lax.all_to_all(arranged, ("z", "c"), split_axis=0, concat_axis=0, tiled=True)
     received = received.reshape(Z * C * slab_count, YH, quarter, LANES)
 
-    first_features, rest_features = gather_tensor(*pick(layer_map, received))
-    w_far_a, w_far_b, _ = lax.optimization_barrier((w_far_a, w_far_b, first_features[3]))
-    weights = (proj_weight, w_sib, w_far_a, w_far_b, lax.ppermute(w_far_a, "c", swap), lax.ppermute(w_far_b, "c", swap))
     squares, inner_sum = sums[0], sums[1]
     inverse_rms = lax.rsqrt(squares / full_width + EPSILON)[:, None]
     normed = (first_hidden * inverse_rms * norm_scale).astype(jnp.bfloat16)
@@ -367,6 +365,9 @@
         - first_hidden * inverse_rms**3 * inner_sum[:, None] / full_width
     )
     layer_grad = jnp.where(is_child, layer_grad, 0.0)
+    key_grad = jnp.where(is_child, key_grad, jnp.zeros_like(key_grad))
+    value_grad = jnp.where(is_child, value_grad, jnp.zeros_like(value_grad))
+    gain_grad = jnp.where(is_child, gain_grad, 0.0)
     first_blocks, rest_blocks = (
         jnp.stack([(x + step) % X * YL + (yl + yh + other) % YL for step, other in places]).astype(jnp.int32)
         for places in (FIRST, REST)
@@ -376,17 +377,20 @@
     slot_layer = jnp.clip(prefix_start[:, None] + jnp.arange(slot_count)[None, :], 0, layers - 1)
     slot_layer = slot_layer.reshape(Z, C, slot_count)[(z + jnp.array(DISTANCES)) % Z]
     slot_layer = jnp.where(c == 0, slot_layer[:, ::-1], slot_layer).reshape(-1).astype(jnp.int32)
+    own_count = jnp.where(is_child, layer_counts[2 * z + c], 0)
+    received, key_grad, value_grad, gain_grad, layer_grad, slot_layer, own_count = lax.optimization_barrier(
+        (received, key_grad, value_grad, gain_grad, layer_grad, slot_layer, own_count)
+    )
+    first_features, rest_features = gather_tensor(*pick(layer_map, received))
+    w_far_a, w_far_b, _ = lax.optimization_barrier((w_far_a, w_far_b, first_features[3]))
+    weights = (proj_weight, w_sib, w_far_a, w_far_b, lax.ppermute(w_far_a, "c", swap), lax.ppermute(w_far_b, "c", swap))
     partial = project_first(place, first_blocks, first_features, weights)
     chunks = project_rest(place, rest_blocks, slot_layer, partial, rest_features, weights)
     given, kept = reduce_z(chunks)
     across = lax.ppermute(given, "c", swap)
     teacher = lax.ppermute(kept, "yh", [(0, 1)])
     teacher_across = lax.ppermute(given, ("yh", "c"), [(0, 3), (1, 2)])
-    own_count = jnp.where(is_child, layer_counts[2 * z + c], 0)
     hidden_grad = finish(c, own_count, child_hidden, layer_grad, (kept, teacher, across, teacher_across))
-    key_grad = jnp.where(is_child, key_grad, jnp.zeros_like(key_grad))
-    value_grad = jnp.where(is_child, value_grad, jnp.zeros_like(value_grad))
-    gain_grad = jnp.where(is_child, gain_grad, 0.0)
     return (hidden_grad, key_grad[None], value_grad[None], gain_grad[None])
 
 

time: 165 us -> 178 us (1.079)
  local copies, waits for them, and re-layouts: 7.6 us -> 13 us
  starting transfers between devices: 74.8 us -> 79.1 us
  other arithmetic: 7.12 us -> 9.87 us
    ppermute x1, waiting for transfers between devices: 11.6 us -> 0.01 us  [body(): lax.ppermute(weight_rows[:, :half_rows], side, up)]
    ppermute x1, starting transfers between devices: 3.43 us -> 11 us  [body(): teacher_across = lax.ppermute(given, ('yh', 'c'), [(0, 3), (1, 2)])]
    ppermute x1, starting transfers between devices: 7.04 us -> 0.09 us  [body(): across = lax.ppermute(given, 'c', swap)]
    unnamed x78 -> x68, local copies, waits for them, and re-layouts: 4.74 us -> 10.9 us
    ppermute x1, waiting for transfers between devices: 0.48 us -> 5.33 us  [body(): sent = lax.ppermute(arrange(teacher_slabs, 1), side, [(0, 3), (1, 2)])]
    ppermute x1, waiting for transfers between devices: 0.01 us -> 4.84 us  [body(): lax.ppermute(weight_rows[:, half_rows:], side, down)]
    ppermute x1, waiting for transfers between devices: 4.21 us -> 0.01 us  [body(): teacher = lax.ppermute(kept, 'yh', [(0, 1)])]
    ppermute x1, waiting for transfers between devices: 2 us -> 5.76 us  [gather_tensor(): f3a = lax.ppermute(low, 'x', up)]
  transfers between devices with their start and end apart: 40 -> 40, of which waited for: 17 -> 14; matrix products, arithmetic and copies ran while one was open for 12% -> 10% of each run, Pallas kernels for 7% -> 7%
where the time goes in v9:
time: 178 us; the launch traced here: 177 us
  starting transfers between devices  79.1 us (44%)
  waiting for transfers between devices  39 us (22%)
  Pallas kernels  24.1 us (14%)
  local copies, waits for them, and re-layouts  13 us (7%)
  other arithmetic  9.87 us (6%)
  matrix products  9.76 us (5%)
  between operations  1.88 us (1%)
    ppermute x1, starting transfers between devices, body(): teacher_across = lax.ppermute(given, ('yh', 'c'), [(0, 3), (1, 2)])  11 us
    unnamed x68, local copies, waits for them, and re-layouts  10.9 us
    all_to_all x1, starting transfers between devices, body(): lax.all_to_all(arranged, ('z', 'c'), split_axis=0, concat_axis=0, tiled=T...  10.5 us
    pallas_call x1, Pallas kernels, project_rest(): pl.pallas_call(project_rest_kernel, out_shape=[jax.ShapeDtypeStruct(shape...  8.75 us
    ppermute x3, starting transfers between devices, reduce_z(): kept_down = lax.ppermute(add(kept[-distance], kept_down), 'z', down)  8.65 us
    pallas_call x1, Pallas kernels, project_first(): pl.pallas_call(project_first_kernel, out_shape=jax.ShapeDtypeStruct(shape...  6.07 us
    ppermute x2, starting transfers between devices, reduce_z(): given_down = lax.ppermute(add(given[-distance], given_down), 'z', down)  6.04 us
    ppermute x1, waiting for transfers between devices, gather_tensor(): f3a = lax.ppermute(low, 'x', up)  5.76 us
  transfers between devices with their start and end apart: 40, of which 14 were waited for; matrix products, arithmetic and copies ran while one was open for 10% of the time, Pallas kernels for 7%

profile of v9, /device:TPU:1, one launch (start us, length us, event | category | flops | bytes accessed | tf_op | source)
XLA Modules:
  0.0 176.7 jit_solution(5629874100359703938)
XLA Ops:
  0.7 2.6 %fusion = f32[128,1024]{1,0:T(8,128)S(1)} fusion(bf16[1,1024,1024]{2,1,0:T(8,128)(2,1)} %param.16, bf16[1,128,1024]{2,1,0:T(8,128)(2,1)} %param.18), kind=kOutput, calls=%fused_computation.1 | convolution fusion | flops 268435456 | bytes 2883584 | tf_op jit(solution)/shard_map/dot_general | solution.py:332
  9.6 5.5 %collective-permute-start = (bf16[16,192,128]{2,1,0:T(8,128)(2,1)}, bf16[16,192,128]{2,1,0:T(8,128)(2,1)}, u32[]{:S(2)}, u32[]{:S(2)}) collective-permute-start(bf16[16,192,128]{2,1,0:T(8,128)(2,1)} %arrange.3), channel_id=1, source_target_pairs={{0,129},{1,128},{2,131},{3,130},{4,133},{5,132},{6,135},{7,134},{8... | collective-permute-start | bytes 2359304 | tf_op jit(solution)/shard_map/ppermute | solution.py:344
  16.8 2.5 %collective-permute-start.3 = (f32[2,128]{1,0:T(2,128)S(1)}, f32[2,128]{1,0:T(2,128)S(1)}, u32[]{:S(2)}, u32[]{:S(2)}) collective-permute-start(f32[2,128]{1,0:T(2,128)S(1)} %fusion.30), channel_id=1, source_target_pairs={{0,4},{2,6},{4,0},{6,2},{1,5},{3,7},{5,1},{7,3},{8,12},{10,14},{12... | collective-permute-start | bytes 3080 | tf_op jit(solution)/shard_map/ppermute | solution.py:342
  25.1 5.3 %collective-permute-done = bf16[16,192,128]{2,1,0:T(8,128)(2,1)} collective-permute-done((bf16[16,192,128]{2,1,0:T(8,128)(2,1)}, bf16[16,192,128]{2,1,0:T(8,128)(2,1)}, u32[]{:S(2)}, u32[]{:S(2)}) %collective-permute-start) | collective-permute-done | bytes 786464 | tf_op jit(solution)/shard_map/ppermute | solution.py:344
  32.5 10.5 %all-to-all-start = ((bf16[16,192,128]{2,1,0:T(8,128)(2,1)}), bf16[16,192,128]{2,1,0:T(8,128)(2,1)}, u32[]{:S(2)}, u32[]{:S(2)}) async-start(bf16[16,192,128]{2,1,0:T(8,128)(2,1)} %broadcast_select_fusion), calls=%async_computation | async-start | bytes 1572864 | tf_op jit(solution)/shard_map/all_to_all | solution.py:349
  43.1 3.5 %collective-permute-start.12 = (bf16[8,32,1024]{2,1,0:T(8,128)(2,1)S(1)}, bf16[8,32,1024]{2,1,0:T(8,128)(2,1)}, u32[]{:S(2)}, u32[]{:S(2)}) collective-permute-start(bf16[8,32,1024]{2,1,0:T(8,128)(2,1)S(1)} %get-tuple-element.82), channel_id=1, source_target_pairs={{0,129},{1,0},{128,1},{129,128},{2,131},{3,2},{130,3},{131,130},{4... | collective-permute-start | bytes 1572872 | tf_op jit(solution)/shard_map/ppermute | solution.py:348
  46.6 3.1 %convert_select_fusion = bf16[1024,1024]{1,0:T(8,128)(2,1)} fusion(pred[]{:T(512)S(6)} %eq.29, bf16[1,128,1024]{2,1,0:T(8,128)(2,1)S(1)} %copy-done.19, f32[1024]{0:T(1024)S(1)} %bitcast.89, f32[128]{0:T(128)S(1)} %get-tuple-element.79, bf16[3,128,1024]{2,1,0:T(8,128)(2,1)} %hidden.1), kind=kOutput, calls=%fused_computation.5 | convolution fusion | flops 271056896 | bytes 2626049 | tf_op jit(solution)/shard_map/dot_general | solution.py:359
  52.9 4.8 %collective-permute-done.12 = bf16[8,32,1024]{2,1,0:T(8,128)(2,1)} collective-permute-done((bf16[8,32,1024]{2,1,0:T(8,128)(2,1)S(1)}, bf16[8,32,1024]{2,1,0:T(8,128)(2,1)}, u32[]{:S(2)}, u32[]{:S(2)}) %collective-permute-start.12) | collective-permute-done | bytes 524320 | tf_op jit(solution)/shard_map/ppermute | solution.py:348
  57.8 3.5 %collective-permute-start.13 = (bf16[8,32,1024]{2,1,0:T(8,128)(2,1)}, bf16[8,32,1024]{2,1,0:T(8,128)(2,1)S(1)}, u32[]{:S(2)}, u32[]{:S(2)}) collective-permute-start(bf16[8,32,1024]{2,1,0:T(8,128)(2,1)} %collective-permute-done.12), channel_id=1, source_target_pairs={{0,129},{1,0},{128,1},{129,128},{2,131},{3,2},{130,3},{131,130},{4... | collective-permute-start | bytes 1572872 | tf_op jit(solution)/shard_map/ppermute | solution.py:348
  61.9 3.9 %all-to-all-done = bf16[16,192,128]{2,1,0:T(8,128)(2,1)} async-done(((bf16[16,192,128]{2,1,0:T(8,128)(2,1)}), bf16[16,192,128]{2,1,0:T(8,128)(2,1)}, u32[]{:S(2)}, u32[]{:S(2)}) %all-to-all-start) | async-done | bytes 786464 | tf_op jit(solution)/shard_map/all_to_all | solution.py:349
  65.8 2.4 %pick_layers.1 = (bf16[32,2,32,128]{3,2,1,0:T(8,128)(2,1)}, bf16[16,2,32,128]{3,2,1,0:T(8,128)(2,1)}, bf16[16,2,32,128]{3,2,1,0:T(8,128)(2,1)}) custom-call(s32[32]{0:T(128)} %layer_map.1, bf16[48,2,32,128]{3,2,1,0:T(8,128)(2,1)} %bitcast.9.received), custom_call_target="tpu_custom_call" | custom-call | bytes 1300000 | tf_op jit(solution)/shard_map/pick_layers/pallas_call | solution.py:65
  68.4 2.4 %collective-permute-start.6 = (bf16[16,2,32,128]{3,2,1,0:T(8,128)(2,1)}, bf16[16,2,32,128]{3,2,1,0:T(8,128)(2,1)S(1)}, u32[]{:S(2)}, u32[]{:S(2)}) collective-permute-start(bf16[16,2,32,128]{3,2,1,0:T(8,128)(2,1)} %get-tuple-element.52), channel_id=1, source_target_pairs={{0,6},{2,0},{4,2},{6,4},{1,7},{3,1},{5,3},{7,5},{8,14},{10,8},{12,... | collective-permute-start | bytes 786440 | tf_op jit(solution)/shard_map/ppermute | solution.py:281
  70.8 5.8 %collective-permute-done.5.refs_3_ = bf16[16,2,32,128]{3,2,1,0:T(8,128)(2,1)S(1)} collective-permute-done((bf16[16,2,32,128]{3,2,1,0:T(8,128)(2,1)}, bf16[16,2,32,128]{3,2,1,0:T(8,128)(2,1)S(1)}, u32[]{:S(2)}, u32[]{:S(2)}) %collective-permute-start.5) | collective-permute-done | bytes 262176 | tf_op jit(solution)/shard_map/ppermute | solution.py:280
  76.6 2.6 %collective-permute-start.7 = (bf16[16,2,32,128]{3,2,1,0:T(8,128)(2,1)}, bf16[16,2,32,128]{3,2,1,0:T(8,128)(2,1)S(1)}, u32[]{:S(2)}, u32[]{:S(2)}) collective-permute-start(bf16[16,2,32,128]{3,2,1,0:T(8,128)(2,1)} %get-tuple-element.49), channel_id=1, source_target_pairs={{0,6},{2,0},{4,2},{6,4},{1,7},{3,1},{5,3},{7,5},{8,14},{10,8},{12,... | collective-permute-start | bytes 786440 | tf_op jit(solution)/shard_map/ppermute | solution.py:285
  79.2 2.7 %collective-permute-start.17 = (bf16[16,2,32,128]{3,2,1,0:T(8,128)(2,1)S(1)}, bf16[16,2,32,128]{3,2,1,0:T(8,128)(2,1)S(1)}, u32[]{:S(2)}, u32[]{:S(2)}) collective-permute-start(bf16[16,2,32,128]{3,2,1,0:T(8,128)(2,1)S(1)} %collective-permute-done.6.refs_2_), channel_id=1, source_target_pairs={{0,6},{2,0},{4,2},{6,4},{1,7},{3,1},{5,3},{7,5},{8,14},{10,8},{12,... | collective-permute-start | bytes 786440 | tf_op jit(solution)/shard_map/ppermute | solution.py:287
  82.7 2.9 %collective-permute-done.7.refs_1_ = bf16[16,2,32,128]{3,2,1,0:T(8,128)(2,1)S(1)} collective-permute-done((bf16[16,2,32,128]{3,2,1,0:T(8,128)(2,1)}, bf16[16,2,32,128]{3,2,1,0:T(8,128)(2,1)S(1)}, u32[]{:S(2)}, u32[]{:S(2)}) %collective-permute-start.7) | collective-permute-done | bytes 262176 | tf_op jit(solution)/shard_map/ppermute | solution.py:285
  91.8 3.4 %collective-permute-start.18 = (bf16[32,2,32,128]{3,2,1,0:T(8,128)(2,1)}, bf16[32,2,32,128]{3,2,1,0:T(8,128)(2,1)}, u32[]{:S(2)}, u32[]{:S(2)}) collective-permute-start(bf16[32,2,32,128]{3,2,1,0:T(8,128)(2,1)} %collective-permute-done.9.refs_5_), channel_id=1, source_target_pairs={{0,6},{2,0},{4,2},{6,4},{1,7},{3,1},{5,3},{7,5},{8,14},{10,8},{12,... | collective-permute-start | bytes 1572872 | tf_op jit(solution)/shard_map/ppermute | solution.py:289
  95.3 2.5 %collective-permute-done.16.refs_0_ = bf16[16,2,32,128]{3,2,1,0:T(8,128)(2,1)} collective-permute-done((bf16[16,2,32,128]{3,2,1,0:T(8,128)(2,1)S(1)}, bf16[16,2,32,128]{3,2,1,0:T(8,128)(2,1)}, u32[]{:S(2)}, u32[]{:S(2)}) %collective-permute-start.16) | collective-permute-done | bytes 262176 | tf_op jit(solution)/shard_map/ppermute | solution.py:286
  103.8 6.1 %project_first.1.partial = bf16[4,256,1024]{2,1,0:T(8,128)(2,1)S(1)} custom-call(s32[4]{0:T(128)S(1)} %get-tuple-element.85.place, s32[4]{0:T(128)S(1)} %get-tuple-element.86.blocks, bf16[32,2,32,128]{3,2,1,0:T(8,128)(2,1)S(1)} %copy-done.5, bf16[16,2,32,128]{3,2,1,0:T(8,128)(2,1)S(1)} %copy-done.9, bf16[16,2,32,128]{3,2,1,0:T(8,128)(2,1)S(1)} %copy-done.7, ...), custom_call_target="tpu_custom_call" | custom-call | flops 2147483648 | bytes 8388608 | tf_op jit(solution)/shard_map/project_first/pallas_call | solution.py:179
  112.7 8.7 %project_rest.1 = (bf16[3,32,1024]{2,1,0:T(8,128)(2,1)}, bf16[3,32,1024]{2,1,0:T(8,128)(2,1)}, bf16[3,32,1024]{2,1,0:T(8,128)(2,1)}, bf16[3,32,1024]{2,1,0:T(8,1...) custom-call(s32[4]{0:T(128)} %copy-done.12, ...), custom_call_target="tpu_custom_call" | custom-call | flops 2147483648 | bytes 11534336 | tf_op jit(solution)/shard_map/project_rest/pallas_call | solution.py:205
  121.6 2.7 %collective-permute-start.25 = (bf16[3,32,1024]{2,1,0:T(8,128)(2,1)}, bf16[3,32,1024]{2,1,0:T(8,128)(2,1)S(1)}, u32[]{:S(2)}, u32[]{:S(2)}) collective-permute-start(bf16[3,32,1024]{2,1,0:T(8,128)(2,1)} %get-tuple-element.64), channel_id=1, source_target_pairs={{0,112},{16,0},{32,16},{48,32},{64,48},{80,64},{96,80},{112,96},{1... | collective-permute-start | bytes 589832 | tf_op jit(solution)/shard_map/ppermute | solution.py:237
  124.2 2.7 %collective-permute-start.34 = (bf16[3,32,1024]{2,1,0:T(8,128)(2,1)}, bf16[3,32,1024]{2,1,0:T(8,128)(2,1)S(1)}, u32[]{:S(2)}, u32[]{:S(2)}) collective-permute-start(bf16[3,32,1024]{2,1,0:T(8,128)(2,1)} %get-tuple-element.72), channel_id=1, source_target_pairs={{0,112},{16,0},{32,16},{48,32},{64,48},{80,64},{96,80},{112,96},{1... | collective-permute-start | bytes 589832 | tf_op jit(solution)/shard_map/ppermute | solution.py:238
  129.6 2.7 %collective-permute-start.26 = (bf16[3,32,1024]{2,1,0:T(8,128)(2,1)S(1)}, bf16[3,32,1024]{2,1,0:T(8,128)(2,1)S(1)}, u32[]{:S(2)}, u32[]{:S(2)}) collective-permute-start(bf16[3,32,1024]{2,1,0:T(8,128)(2,1)S(1)} %add_convert_fusion.9), channel_id=1, source_target_pairs={{0,112},{16,0},{32,16},{48,32},{64,48},{80,64},{96,80},{112,96},{1... | collective-permute-start | bytes 589832 | tf_op jit(solution)/shard_map/ppermute | solution.py:244
  134.4 2.7 %collective-permute-start.35 = (bf16[3,32,1024]{2,1,0:T(8,128)(2,1)S(1)}, bf16[3,32,1024]{2,1,0:T(8,128)(2,1)S(1)}, u32[]{:S(2)}, u32[]{:S(2)}) collective-permute-start(bf16[3,32,1024]{2,1,0:T(8,128)(2,1)S(1)} %add_convert_fusion.2), channel_id=1, source_target_pairs={{0,112},{16,0},{32,16},{48,32},{64,48},{80,64},{96,80},{112,96},{1... | collective-permute-start | bytes 589832 | tf_op jit(solution)/shard_map/ppermute | solution.py:243
  137.4 2.7 %collective-permute-start.27 = (bf16[3,32,1024]{2,1,0:T(8,128)(2,1)S(1)}, bf16[3,32,1024]{2,1,0:T(8,128)(2,1)S(1)}, u32[]{:S(2)}, u32[]{:S(2)}) collective-permute-start(bf16[3,32,1024]{2,1,0:T(8,128)(2,1)S(1)} %add_convert_fusion.8), channel_id=1, source_target_pairs={{0,112},{16,0},{32,16},{48,32},{64,48},{80,64},{96,80},{112,96},{1... | collective-permute-start | bytes 589832 | tf_op jit(solution)/shard_map/ppermute | solution.py:244
  140.6 3.3 %collective-permute-start.36 = (bf16[3,32,1024]{2,1,0:T(8,128)(2,1)S(1)}, bf16[3,32,1024]{2,1,0:T(8,128)(2,1)S(1)}, u32[]{:S(2)}, u32[]{:S(2)}) collective-permute-start(bf16[3,32,1024]{2,1,0:T(8,128)(2,1)S(1)} %add_convert_fusion.1), channel_id=1, source_target_pairs={{0,112},{16,0},{32,16},{48,32},{64,48},{80,64},{96,80},{112,96},{1... | collective-permute-start | bytes 589832 | tf_op jit(solution)/shard_map/ppermute | solution.py:243
  144.0 3.2 %collective-permute-start.28 = (bf16[3,32,1024]{2,1,0:T(8,128)(2,1)S(1)}, bf16[3,32,1024]{2,1,0:T(8,128)(2,1)S(1)}, u32[]{:S(2)}, u32[]{:S(2)}) collective-permute-start(bf16[3,32,1024]{2,1,0:T(8,128)(2,1)S(1)} %add_convert_fusion.7), channel_id=1, source_target_pairs={{0,112},{16,0},{32,16},{48,32},{64,48},{80,64},{96,80},{112,96},{1... | collective-permute-start | bytes 589832 | tf_op jit(solution)/shard_map/ppermute | solution.py:244
  147.9 4.9 %collective-permute-done.28 = bf16[3,32,1024]{2,1,0:T(8,128)(2,1)S(1)} collective-permute-done((bf16[3,32,1024]{2,1,0:T(8,128)(2,1)S(1)}, bf16[3,32,1024]{2,1,0:T(8,128)(2,1)S(1)}, u32[]{:S(2)}, u32[]{:S(2)}) %collective-permute-start.28) | collective-permute-done | bytes 196640 | tf_op jit(solution)/shard_map/ppermute | solution.py:244
  152.9 5.1 %collective-permute-start.29 = (bf16[3,32,1024]{2,1,0:T(8,128)(2,1)S(1)}, bf16[3,32,1024]{2,1,0:T(8,128)(2,1)S(1)}, u32[]{:S(2)}, u32[]{:S(2)}) collective-permute-start(bf16[3,32,1024]{2,1,0:T(8,128)(2,1)S(1)} %add_convert_fusion.6.near), channel_id=1, source_target_pairs={{0,128},{1,129},{2,130},{3,131},{4,132},{5,133},{6,134},{7,135},{8... | collective-permute-start | bytes 589832 | tf_op jit(solution)/shard_map/ppermute | solution.py:391
  158.1 11.0 %collective-permute-start.38 = (bf16[3,32,1024]{2,1,0:T(8,128)(2,1)S(1)}, bf16[3,32,1024]{2,1,0:T(8,128)(2,1)S(1)}, u32[]{:S(2)}, u32[]{:S(2)}) collective-permute-start(bf16[3,32,1024]{2,1,0:T(8,128)(2,1)S(1)} %add_convert_fusion), channel_id=1, source_target_pairs={{0,136},{8,128},{1,137},{9,129},{2,138},{10,130},{3,139},{11,131},... | collective-permute-start | bytes 589832 | tf_op jit(solution)/shard_map/ppermute | solution.py:392
  169.9 2.8 %collective-permute-done.38.teacher_across = bf16[3,32,1024]{2,1,0:T(8,128)(2,1)S(1)} collective-permute-done((bf16[3,32,1024]{2,1,0:T(8,128)(2,1)S(1)}, bf16[3,32,1024]{2,1,0:T(8,128)(2,1)S(1)}, u32[]{:S(2)}, u32[]{:S(2)}) %collective-permute-start.38) | collective-permute-done | bytes 196640 | tf_op jit(solution)/shard_map/ppermute | solution.py:392
  174.1 2.6 %finish.1 = bf16[3,128,1024]{2,1,0:T(8,128)(2,1)} custom-call(s32[2]{0:T(128)} %pad_add_fusion.state, bf16[3,128,1024]{2,1,0:T(8,128)(2,1)} %hidden.1, f32[128,1024]{1,0:T(8,128)} %get-tuple-element.43.layer_grad, bf16[3,32,1024]{2,1,0:T(8,128)(2,1)} %copy-done.15, bf16[3,32,1024]{2,1,0:T(8,128)(2,1)} %copy-done.20, bf16[3,32,1024]{2,1,0:T(8,128)(2,1)} %copy-done.22, ...), custom_call_target="tpu_custom_call" | custom-call | flops 786432 | bytes 3145728 | tf_op jit(solution)/shard_map/finish/pallas_call | solution.py:266
  (164 shorter events, 43.6 us)
Async XLA Ops:
  5.3 11.5 %collective-permute-start.2 = (f32[2,128]{1,0:T(2,128)S(1)}, f32[2,128]{1,0:T(2,128)S(1)}, u32[]{:S(2)}, u32[]{:S(2)}) collective-permute-start(f32[2,128]{1,0:T(2,128)S(1)} %pad_maximum_fusion), channel_id=1, source_target_pairs={{0,2},{2,0},{4,6},{6,4},{1,3},{3,1},{5,7},{7,5},{8,10},{10,8},{12,... | collective-permute-start | bytes 3080 | tf_op jit(solution)/shard_map/ppermute | solution.py:341
  9.6 20.8 %collective-permute-start = (bf16[16,192,128]{2,1,0:T(8,128)(2,1)}, bf16[16,192,128]{2,1,0:T(8,128)(2,1)}, u32[]{:S(2)}, u32[]{:S(2)}) collective-permute-start(bf16[16,192,128]{2,1,0:T(8,128)(2,1)} %arrange.3), channel_id=1, source_target_pairs={{0,129},{1,128},{2,131},{3,130},{4,133},{5,132},{6,135},{7,134},{8... | collective-permute-start | bytes 2359304 | tf_op jit(solution)/shard_map/ppermute | solution.py:344
  15.1 17.4 %collective-permute-start.1 = (bf16[8,64,1024]{2,1,0:T(8,128)(2,1)S(1)}, bf16[8,64,1024]{2,1,0:T(8,128)(2,1)S(1)}, u32[]{:S(2)}, u32[]{:S(2)}) collective-permute-start(bf16[8,64,1024]{2,1,0:T(8,128)(2,1)S(1)} %copy-done.1), channel_id=1, source_target_pairs={{0,8},{8,0},{1,9},{9,1},{2,10},{10,2},{3,11},{11,3},{4,12},{12,4},... | collective-permute-start | bytes 3145736 | tf_op jit(solution)/shard_map/ppermute | solution.py:322
  32.5 33.3 %all-to-all-start = ((bf16[16,192,128]{2,1,0:T(8,128)(2,1)}), bf16[16,192,128]{2,1,0:T(8,128)(2,1)}, u32[]{:S(2)}, u32[]{:S(2)}) async-start(bf16[16,192,128]{2,1,0:T(8,128)(2,1)} %broadcast_select_fusion), calls=%async_computation | async-start | bytes 1572864 | tf_op jit(solution)/shard_map/all_to_all | solution.py:349
  43.1 14.7 %collective-permute-start.12 = (bf16[8,32,1024]{2,1,0:T(8,128)(2,1)S(1)}, bf16[8,32,1024]{2,1,0:T(8,128)(2,1)}, u32[]{:S(2)}, u32[]{:S(2)}) collective-permute-start(bf16[8,32,1024]{2,1,0:T(8,128)(2,1)S(1)} %get-tuple-element.82), channel_id=1, source_target_pairs={{0,129},{1,0},{128,1},{129,128},{2,131},{3,2},{130,3},{131,130},{4... | collective-permute-start | bytes 1572872 | tf_op jit(solution)/shard_map/ppermute | solution.py:348
  46.6 14.7 %collective-permute-start.10 = (bf16[8,32,1024]{2,1,0:T(8,128)(2,1)S(1)}, bf16[8,32,1024]{2,1,0:T(8,128)(2,1)}, u32[]{:S(2)}, u32[]{:S(2)}) collective-permute-start(bf16[8,32,1024]{2,1,0:T(8,128)(2,1)S(1)} %get-tuple-element.83), channel_id=1, source_target_pairs={{0,1},{1,128},{128,129},{129,0},{2,3},{3,130},{130,131},{131,2},{4... | collective-permute-start | bytes 1572872 | tf_op jit(solution)/shard_map/ppermute | solution.py:347
  57.8 21.4 %collective-permute-start.13 = (bf16[8,32,1024]{2,1,0:T(8,128)(2,1)}, bf16[8,32,1024]{2,1,0:T(8,128)(2,1)S(1)}, u32[]{:S(2)}, u32[]{:S(2)}) collective-permute-start(bf16[8,32,1024]{2,1,0:T(8,128)(2,1)} %collective-permute-done.12), channel_id=1, source_target_pairs={{0,129},{1,0},{128,1},{129,128},{2,131},{3,2},{130,3},{131,130},{4... | collective-permute-start | bytes 1572872 | tf_op jit(solution)/shard_map/ppermute | solution.py:348
  61.3 17.8 %collective-permute-start.11 = (bf16[8,32,1024]{2,1,0:T(8,128)(2,1)}, bf16[8,32,1024]{2,1,0:T(8,128)(2,1)}, u32[]{:S(2)}, u32[]{:S(2)}) collective-permute-start(bf16[8,32,1024]{2,1,0:T(8,128)(2,1)} %collective-permute-done.10), channel_id=1, source_target_pairs={{0,1},{1,128},{128,129},{129,0},{2,3},{3,130},{130,131},{131,2},{4... | collective-permute-start | bytes 1572872 | tf_op jit(solution)/shard_map/ppermute | solution.py:347
  68.1 8.4 %collective-permute-start.5 = (bf16[16,2,32,128]{3,2,1,0:T(8,128)(2,1)}, bf16[16,2,32,128]{3,2,1,0:T(8,128)(2,1)S(1)}, u32[]{:S(2)}, u32[]{:S(2)}) collective-permute-start(bf16[16,2,32,128]{3,2,1,0:T(8,128)(2,1)} %get-tuple-element.49), channel_id=1, source_target_pairs={{0,2},{2,4},{4,6},{6,0},{1,3},{3,5},{5,7},{7,1},{8,10},{10,12},{12... | collective-permute-start | bytes 786440 | tf_op jit(solution)/shard_map/ppermute | solution.py:280
  68.4 8.2 %collective-permute-start.6 = (bf16[16,2,32,128]{3,2,1,0:T(8,128)(2,1)}, bf16[16,2,32,128]{3,2,1,0:T(8,128)(2,1)S(1)}, u32[]{:S(2)}, u32[]{:S(2)}) collective-permute-start(bf16[16,2,32,128]{3,2,1,0:T(8,128)(2,1)} %get-tuple-element.52), channel_id=1, source_target_pairs={{0,6},{2,0},{4,2},{6,4},{1,7},{3,1},{5,3},{7,5},{8,14},{10,8},{12,... | collective-permute-start | bytes 786440 | tf_op jit(solution)/shard_map/ppermute | solution.py:281
  70.8 18.5 %collective-permute-start.9 = (bf16[32,2,32,128]{3,2,1,0:T(8,128)(2,1)}, bf16[32,2,32,128]{3,2,1,0:T(8,128)(2,1)}, u32[]{:S(2)}, u32[]{:S(2)}) collective-permute-start(bf16[32,2,32,128]{3,2,1,0:T(8,128)(2,1)} %get-tuple-element.46.refs_0_), channel_id=1, source_target_pairs={{0,1},{1,0},{2,3},{3,2},{4,5},{5,4},{6,7},{7,6},{8,9},{9,8},{10,11... | collective-permute-start | bytes 1572872 | tf_op jit(solution)/shard_map/ppermute | solution.py:282
  76.6 9.0 %collective-permute-start.7 = (bf16[16,2,32,128]{3,2,1,0:T(8,128)(2,1)}, bf16[16,2,32,128]{3,2,1,0:T(8,128)(2,1)S(1)}, u32[]{:S(2)}, u32[]{:S(2)}) collective-permute-start(bf16[16,2,32,128]{3,2,1,0:T(8,128)(2,1)} %get-tuple-element.49), channel_id=1, source_target_pairs={{0,6},{2,0},{4,2},{6,4},{1,7},{3,1},{5,3},{7,5},{8,14},{10,8},{12,... | collective-permute-start | bytes 786440 | tf_op jit(solution)/shard_map/ppermute | solution.py:285
  79.1 9.5 %collective-permute-start.8 = (bf16[16,2,32,128]{3,2,1,0:T(8,128)(2,1)}, bf16[16,2,32,128]{3,2,1,0:T(8,128)(2,1)S(1)}, u32[]{:S(2)}, u32[]{:S(2)}) collective-permute-start(bf16[16,2,32,128]{3,2,1,0:T(8,128)(2,1)} %get-tuple-element.52), channel_id=1, source_target_pairs={{0,2},{2,4},{4,6},{6,0},{1,3},{3,5},{5,7},{7,1},{8,10},{10,12},{12... | collective-permute-start | bytes 786440 | tf_op jit(solution)/shard_map/ppermute | solution.py:284
  79.1 18.6 %collective-permute-start.14 = (bf16[8,32,1024]{2,1,0:T(8,128)(2,1)}, bf16[8,32,1024]{2,1,0:T(8,128)(2,1)}, u32[]{:S(2)}, u32[]{:S(2)}) collective-permute-start(bf16[8,32,1024]{2,1,0:T(8,128)(2,1)} %collective-permute-done.11.refs_8_), channel_id=1, source_target_pairs={{0,8},{8,0},{1,9},{9,1},{2,10},{10,2},{3,11},{11,3},{4,12},{12,4},... | collective-permute-start | bytes 1572872 | tf_op jit(solution)/shard_map/ppermute | solution.py:386
  79.2 11.8 %collective-permute-start.17 = (bf16[16,2,32,128]{3,2,1,0:T(8,128)(2,1)S(1)}, bf16[16,2,32,128]{3,2,1,0:T(8,128)(2,1)S(1)}, u32[]{:S(2)}, u32[]{:S(2)}) collective-permute-start(bf16[16,2,32,128]{3,2,1,0:T(8,128)(2,1)S(1)} %collective-permute-done.6.refs_2_), channel_id=1, source_target_pairs={{0,6},{2,0},{4,2},{6,4},{1,7},{3,1},{5,3},{7,5},{8,14},{10,8},{12,... | collective-permute-start | bytes 786440 | tf_op jit(solution)/shard_map/ppermute | solution.py:287
  86.3 13.6 %collective-permute-start.15 = (bf16[8,32,1024]{2,1,0:T(8,128)(2,1)S(1)}, bf16[8,32,1024]{2,1,0:T(8,128)(2,1)}, u32[]{:S(2)}, u32[]{:S(2)}) collective-permute-start(bf16[8,32,1024]{2,1,0:T(8,128)(2,1)S(1)} %collective-permute-done.13.refs_9_), channel_id=1, source_target_pairs={{0,8},{8,0},{1,9},{9,1},{2,10},{10,2},{3,11},{11,3},{4,12},{12,4},... | collective-permute-start | bytes 1572872 | tf_op jit(solution)/shard_map/ppermute | solution.py:386
  89.3 8.5 %collective-permute-start.16 = (bf16[16,2,32,128]{3,2,1,0:T(8,128)(2,1)S(1)}, bf16[16,2,32,128]{3,2,1,0:T(8,128)(2,1)}, u32[]{:S(2)}, u32[]{:S(2)}) collective-permute-start(bf16[16,2,32,128]{3,2,1,0:T(8,128)(2,1)S(1)} %collective-permute-done.5.refs_3_), channel_id=1, source_target_pairs={{0,2},{2,4},{4,6},{6,0},{1,3},{3,5},{5,7},{7,1},{8,10},{10,12},{12... | collective-permute-start | bytes 786440 | tf_op jit(solution)/shard_map/ppermute | solution.py:286
  89.3 23.4 %collective-permute-start.21 = (bf16[32,2,32,128]{3,2,1,0:T(8,128)(2,1)}, bf16[32,2,32,128]{3,2,1,0:T(8,128)(2,1)}, u32[]{:S(2)}, u32[]{:S(2)}) collective-permute-start(bf16[32,2,32,128]{3,2,1,0:T(8,128)(2,1)} %collective-permute-done.9.refs_5_), channel_id=1, source_target_pairs={{0,2},{2,4},{4,6},{6,0},{1,3},{3,5},{5,7},{7,1},{8,10},{10,12},{12... | collective-permute-start | bytes 1572872 | tf_op jit(solution)/shard_map/ppermute | solution.py:288
  91.8 20.9 %collective-permute-start.18 = (bf16[32,2,32,128]{3,2,1,0:T(8,128)(2,1)}, bf16[32,2,32,128]{3,2,1,0:T(8,128)(2,1)}, u32[]{:S(2)}, u32[]{:S(2)}) collective-permute-start(bf16[32,2,32,128]{3,2,1,0:T(8,128)(2,1)} %collective-permute-done.9.refs_5_), channel_id=1, source_target_pairs={{0,6},{2,0},{4,2},{6,4},{1,7},{3,1},{5,3},{7,5},{8,14},{10,8},{12,... | collective-permute-start | bytes 1572872 | tf_op jit(solution)/shard_map/ppermute | solution.py:289
  97.8 13.5 %collective-permute-start.20 = (bf16[16,2,32,128]{3,2,1,0:T(8,128)(2,1)}, bf16[16,2,32,128]{3,2,1,0:T(8,128)(2,1)S(1)}, u32[]{:S(2)}, u32[]{:S(2)}) collective-permute-start(bf16[16,2,32,128]{3,2,1,0:T(8,128)(2,1)} %copy-done.16), channel_id=1, source_target_pairs={{0,1},{1,0},{2,3},{3,2},{4,5},{5,4},{6,7},{7,6},{8,9},{9,8},{10,11... | collective-permute-start | bytes 786440 | tf_op jit(solution)/shard_map/ppermute | solution.py:291
  97.8 14.2 %collective-permute-start.19 = (bf16[16,2,32,128]{3,2,1,0:T(8,128)(2,1)}, bf16[16,2,32,128]{3,2,1,0:T(8,128)(2,1)S(1)}, u32[]{:S(2)}, u32[]{:S(2)}) collective-permute-start(bf16[16,2,32,128]{3,2,1,0:T(8,128)(2,1)} %collective-permute-done.16.refs_0_), channel_id=1, source_target_pairs={{0,1},{1,0},{2,3},{3,2},{4,5},{5,4},{6,7},{7,6},{8,9},{9,8},{10,11... | collective-permute-start | bytes 786440 | tf_op jit(solution)/shard_map/ppermute | solution.py:290
  124.2 8.1 %collective-permute-start.30 = (bf16[3,32,1024]{2,1,0:T(8,128)(2,1)}, bf16[3,32,1024]{2,1,0:T(8,128)(2,1)S(1)}, u32[]{:S(2)}, u32[]{:S(2)}) collective-permute-start(bf16[3,32,1024]{2,1,0:T(8,128)(2,1)} %get-tuple-element.69), channel_id=1, source_target_pairs={{0,16},{16,32},{32,48},{48,64},{64,80},{80,96},{96,112},{112,0},{1... | collective-permute-start | bytes 589832 | tf_op jit(solution)/shard_map/ppermute | solution.py:236
  124.2 9.2 %collective-permute-start.34 = (bf16[3,32,1024]{2,1,0:T(8,128)(2,1)}, bf16[3,32,1024]{2,1,0:T(8,128)(2,1)S(1)}, u32[]{:S(2)}, u32[]{:S(2)}) collective-permute-start(bf16[3,32,1024]{2,1,0:T(8,128)(2,1)} %get-tuple-element.72), channel_id=1, source_target_pairs={{0,112},{16,0},{32,16},{48,32},{64,48},{80,64},{96,80},{112,96},{1... | collective-permute-start | bytes 589832 | tf_op jit(solution)/shard_map/ppermute | solution.py:238
  128.5 8.6 %collective-permute-start.23 = (bf16[3,32,1024]{2,1,0:T(8,128)(2,1)S(1)}, bf16[3,32,1024]{2,1,0:T(8,128)(2,1)S(1)}, u32[]{:S(2)}, u32[]{:S(2)}) collective-permute-start(bf16[3,32,1024]{2,1,0:T(8,128)(2,1)S(1)} %add_convert_fusion.11), channel_id=1, source_target_pairs={{0,16},{16,32},{32,48},{48,64},{64,80},{80,96},{96,112},{112,0},{1... | collective-permute-start | bytes 589832 | tf_op jit(solution)/shard_map/ppermute | solution.py:246
  129.6 7.7 %collective-permute-start.26 = (bf16[3,32,1024]{2,1,0:T(8,128)(2,1)S(1)}, bf16[3,32,1024]{2,1,0:T(8,128)(2,1)S(1)}, u32[]{:S(2)}, u32[]{:S(2)}) collective-permute-start(bf16[3,32,1024]{2,1,0:T(8,128)(2,1)S(1)} %add_convert_fusion.9), channel_id=1, source_target_pairs={{0,112},{16,0},{32,16},{48,32},{64,48},{80,64},{96,80},{112,96},{1... | collective-permute-start | bytes 589832 | tf_op jit(solution)/shard_map/ppermute | solution.py:244
  137.2 10.7 %collective-permute-start.24 = (bf16[3,32,1024]{2,1,0:T(8,128)(2,1)S(1)}, bf16[3,32,1024]{2,1,0:T(8,128)(2,1)S(1)}, u32[]{:S(2)}, u32[]{:S(2)}) collective-permute-start(bf16[3,32,1024]{2,1,0:T(8,128)(2,1)S(1)} %add_convert_fusion.10), channel_id=1, source_target_pairs={{0,16},{16,32},{32,48},{48,64},{64,80},{80,96},{96,112},{112,0},{1... | collective-permute-start | bytes 589832 | tf_op jit(solution)/shard_map/ppermute | solution.py:246
  140.4 7.3 %collective-permute-start.32 = (bf16[3,32,1024]{2,1,0:T(8,128)(2,1)S(1)}, bf16[3,32,1024]{2,1,0:T(8,128)(2,1)S(1)}, u32[]{:S(2)}, u32[]{:S(2)}) collective-permute-start(bf16[3,32,1024]{2,1,0:T(8,128)(2,1)S(1)} %add_convert_fusion.4), channel_id=1, source_target_pairs={{0,16},{16,32},{32,48},{48,64},{64,80},{80,96},{96,112},{112,0},{1... | collective-permute-start | bytes 589832 | tf_op jit(solution)/shard_map/ppermute | solution.py:241
  140.6 17.4 %collective-permute-start.36 = (bf16[3,32,1024]{2,1,0:T(8,128)(2,1)S(1)}, bf16[3,32,1024]{2,1,0:T(8,128)(2,1)S(1)}, u32[]{:S(2)}, u32[]{:S(2)}) collective-permute-start(bf16[3,32,1024]{2,1,0:T(8,128)(2,1)S(1)} %add_convert_fusion.1), channel_id=1, source_target_pairs={{0,112},{16,0},{32,16},{48,32},{64,48},{80,64},{96,80},{112,96},{1... | collective-permute-start | bytes 589832 | tf_op jit(solution)/shard_map/ppermute | solution.py:243
  144.0 8.8 %collective-permute-start.28 = (bf16[3,32,1024]{2,1,0:T(8,128)(2,1)S(1)}, bf16[3,32,1024]{2,1,0:T(8,128)(2,1)S(1)}, u32[]{:S(2)}, u32[]{:S(2)}) collective-permute-start(bf16[3,32,1024]{2,1,0:T(8,128)(2,1)S(1)} %add_convert_fusion.7), channel_id=1, source_target_pairs={{0,112},{16,0},{32,16},{48,32},{64,48},{80,64},{96,80},{112,96},{1... | collective-permute-start | bytes 589832 | tf_op jit(solution)/shard_map/ppermute | solution.py:244
  147.8 10.2 %collective-permute-start.33 = (bf16[3,32,1024]{2,1,0:T(8,128)(2,1)S(1)}, bf16[3,32,1024]{2,1,0:T(8,128)(2,1)S(1)}, u32[]{:S(2)}, u32[]{:S(2)}) collective-permute-start(bf16[3,32,1024]{2,1,0:T(8,128)(2,1)S(1)} %add_convert_fusion.3), channel_id=1, source_target_pairs={{0,16},{16,32},{32,48},{48,64},{64,80},{80,96},{96,112},{112,0},{1... | collective-permute-start | bytes 589832 | tf_op jit(solution)/shard_map/ppermute | solution.py:241
  152.9 17.0 %collective-permute-start.29 = (bf16[3,32,1024]{2,1,0:T(8,128)(2,1)S(1)}, bf16[3,32,1024]{2,1,0:T(8,128)(2,1)S(1)}, u32[]{:S(2)}, u32[]{:S(2)}) collective-permute-start(bf16[3,32,1024]{2,1,0:T(8,128)(2,1)S(1)} %add_convert_fusion.6.near), channel_id=1, source_target_pairs={{0,128},{1,129},{2,130},{3,131},{4,132},{5,133},{6,134},{7,135},{8... | collective-permute-start | bytes 589832 | tf_op jit(solution)/shard_map/ppermute | solution.py:391
  158.1 14.6 %collective-permute-start.38 = (bf16[3,32,1024]{2,1,0:T(8,128)(2,1)S(1)}, bf16[3,32,1024]{2,1,0:T(8,128)(2,1)S(1)}, u32[]{:S(2)}, u32[]{:S(2)}) collective-permute-start(bf16[3,32,1024]{2,1,0:T(8,128)(2,1)S(1)} %add_convert_fusion), channel_id=1, source_target_pairs={{0,136},{8,128},{1,137},{9,129},{2,138},{10,130},{3,139},{11,131},... | collective-permute-start | bytes 589832 | tf_op jit(solution)/shard_map/ppermute | solution.py:392
  (42 other events, 395.7 us)

commit v10 on v9

--- a/solution.py
+++ b/solution.py
@@ -16,29 +16,26 @@
 
 
 def arrange_kernel(slabs, out):
-    slab_count, width, _ = slabs.shape
+    _, width, _ = slabs.shape
     tokens = width // C
     for c in range(C):
         for z in range(Z):
-            for slab in range(slab_count):
-                for h in range(YH):
-                    lane = (h * Z + z) * LANES
-                    row = (slab * YH + h) * tokens
-                    out[z * C + c, row : row + tokens, :] = slabs[
-                        slab, c * tokens : (c + 1) * tokens, lane : lane + LANES
-                    ]
+            for h in range(YH):
+                lane = (h * Z + z) * LANES
+                out[z * C + c, h * tokens : (h + 1) * tokens, :] = slabs[
+                    0, c * tokens : (c + 1) * tokens, lane : lane + LANES
+                ]
 
 
 def arrange(teacher_slabs, section):
     slab_count, tokens, width = teacher_slabs.shape
-    rows = slab_count * YH * (tokens // QUARTERS)
-    shape = jax.ShapeDtypeStruct((Z * C, rows, LANES), teacher_slabs.dtype)
+    rows = YH * (tokens // QUARTERS)
     return pl.pallas_call(
         arrange_kernel,
-        grid=(1,),
-        out_shape=shape,
-        in_specs=[pl.BlockSpec((slab_count, tokens // YH, width), lambda i: (0, section, 0))],
-        out_specs=pl.BlockSpec(shape.shape, lambda i: (0, 0, 0)),
+        grid=(slab_count,),
+        out_shape=jax.ShapeDtypeStruct((Z * C, slab_count * rows, LANES), teacher_slabs.dtype),
+        in_specs=[pl.BlockSpec((1, tokens // YH, width), lambda i: (i, section, 0))],
+        out_specs=pl.BlockSpec((Z * C, rows, LANES), lambda i: (0, i, 0)),
         cost_estimate=pl.CostEstimate(flops=0, bytes_accessed=1600000, transcendentals=0),
         name="arrange",
     )(teacher_slabs)
@@ -244,30 +241,38 @@
         kept_down = lax.ppermute(add(kept[-distance], kept_down), "z", down)
         if distance < 3:
             kept_up = lax.ppermute(add(kept[distance], kept_up), "z", up)
-    return add(given[0], given_up, given_down), add(kept[0], kept_up, kept_down)
-
-
-def finish_kernel(state, hidden, layer_grad, near, teacher, across, teacher_across, out):
+    given_sum = add(given[0], given_up, given_down)
+    return given_sum, add(kept[0], kept_up, kept_down)
+
+
+def finish_kernel(state, hidden, layer_grad, teacher_across, across, teacher, near, out):
     core, count = state[0], state[1]
-    slots, quarter, _ = near.shape
+    slot = pl.program_id(0)
+    quarter = near.shape[1]
     quarters = ((C + core, near), (C + 1 - core, across), (core, teacher), (1 - core, teacher_across))
     for index, ref in quarters:
         rows = pl.ds(pl.multiple_of(index * quarter, quarter), quarter)
-        for slot in range(slots):
-            value = hidden[slot, rows, :].astype(jnp.float32) - ref[slot].astype(jnp.float32)
-            value = jnp.where(slot < count, value, 0.0)
-            if slot == 0:
-                value = value + layer_grad[rows, :]
-            out[slot, rows, :] = value.astype(out.dtype)
+        value = hidden[0, rows, :].astype(jnp.float32) - ref[0].astype(jnp.float32)
+        value = jnp.where(slot < count, value, 0.0)
+        value = value + jnp.where(slot == 0, layer_grad[rows, :], 0.0)
+        out[0, rows, :] = value.astype(out.dtype)
 
 
 def finish(c, own_count, hidden, layer_grad, pieces):
-    vmem = pl.BlockSpec(memory_space=pltpu.VMEM)
+    slots, tokens, columns = hidden.shape
+    whole = pl.BlockSpec((1, tokens, columns), lambda i: (i, 0, 0))
+    piece = pl.BlockSpec((1, tokens // QUARTERS, columns), lambda i: (i, 0, 0))
     return pl.pallas_call(
         finish_kernel,
+        grid=(slots,),
         out_shape=jax.ShapeDtypeStruct(hidden.shape, hidden.dtype),
-        in_specs=[pl.BlockSpec(memory_space=pltpu.SMEM)] + [vmem] * 6,
-        out_specs=vmem,
+        in_specs=[
+            pl.BlockSpec(memory_space=pltpu.SMEM),
+            whole,
+            pl.BlockSpec((tokens, columns), lambda i: (0, 0)),
+        ]
+        + [piece] * len(pieces),
+        out_specs=whole,
         cost_estimate=pl.CostEstimate(flops=2 * hidden.size, bytes_accessed=8 * hidden.size, transcendentals=0),
         name="finish",
     )(jnp.stack([c, own_count]).astype(jnp.int32), hidden, layer_grad, *pieces)
@@ -280,7 +285,6 @@
     f3a = lax.ppermute(low, "x", up)
     f1b = lax.ppermute(high, "x", down)
     g0 = lax.ppermute(own, "yl", swap)
-    low, high, f3a, f1b = lax.optimization_barrier((low, high, f3a, f1b))
     f3b = lax.ppermute(high, "x", up)
     f1a = lax.ppermute(low, "x", down)
     f2a = lax.ppermute(f3a, "x", up)
@@ -323,6 +327,7 @@
     place = jnp.stack([2 * yh + c, 2 * yh + 1 - c, 2 * (1 - yh) + c, 2 * (1 - yh) + 1 - c]).astype(jnp.int32)
 
     is_child = yh == 1
+    leaving, key_weight, value_weight = lax.optimization_barrier((arrange(teacher_slabs, 1), key_weight, value_weight))
     first_hidden = child_hidden[0].astype(jnp.float32)
     norm_scale = norm_gain[0]
     contract_last = (((1,), (1,)), ((), ()))
@@ -341,7 +346,7 @@
     sums = sums + lax.ppermute(sums, "x", [(i, i ^ 1) for i in range(X)])
     sums = sums + lax.ppermute(sums, "x", [(i, i ^ 2) for i in range(X)])
     sums = sums + lax.ppermute(sums, "yl", swap)
-    sent = lax.ppermute(arrange(teacher_slabs, 1), side, [(0, 3), (1, 2)])
+    sent = lax.ppermute(leaving, side, [(0, 3), (1, 2)])
     arranged = jnp.where(yh == 0, arrange(teacher_slabs, 0), sent)
     arranged, w_sib, sums, weight_rows = lax.optimization_barrier((arranged, w_sib, sums, proj_weight))
     w_far_a = lax.ppermute(lax.ppermute(weight_rows[:, :half_rows], side, up), side, up)
@@ -368,6 +373,10 @@
     key_grad = jnp.where(is_child, key_grad, jnp.zeros_like(key_grad))
     value_grad = jnp.where(is_child, value_grad, jnp.zeros_like(value_grad))
     gain_grad = jnp.where(is_child, gain_grad, 0.0)
+    received, key_grad, gain_grad, layer_grad = lax.optimization_barrier((received, key_grad, gain_grad, layer_grad))
+    first_features, rest_features = gather_tensor(*pick(layer_map, received))
+    w_far_a, w_far_b, _ = lax.optimization_barrier((w_far_a, w_far_b, first_features[3]))
+    weights = (proj_weight, w_sib, w_far_a, w_far_b, lax.ppermute(w_far_a, "c", swap), lax.ppermute(w_far_b, "c", swap))
     first_blocks, rest_blocks = (
         jnp.stack([(x + step) % X * YL + (yl + yh + other) % YL for step, other in places]).astype(jnp.int32)
         for places in (FIRST, REST)
@@ -377,20 +386,14 @@
     slot_layer = jnp.clip(prefix_start[:, None] + jnp.arange(slot_count)[None, :], 0, layers - 1)
     slot_layer = slot_layer.reshape(Z, C, slot_count)[(z + jnp.array(DISTANCES)) % Z]
     slot_layer = jnp.where(c == 0, slot_layer[:, ::-1], slot_layer).reshape(-1).astype(jnp.int32)
-    own_count = jnp.where(is_child, layer_counts[2 * z + c], 0)
-    received, key_grad, value_grad, gain_grad, layer_grad, slot_layer, own_count = lax.optimization_barrier(
-        (received, key_grad, value_grad, gain_grad, layer_grad, slot_layer, own_count)
-    )
-    first_features, rest_features = gather_tensor(*pick(layer_map, received))
-    w_far_a, w_far_b, _ = lax.optimization_barrier((w_far_a, w_far_b, first_features[3]))
-    weights = (proj_weight, w_sib, w_far_a, w_far_b, lax.ppermute(w_far_a, "c", swap), lax.ppermute(w_far_b, "c", swap))
     partial = project_first(place, first_blocks, first_features, weights)
     chunks = project_rest(place, rest_blocks, slot_layer, partial, rest_features, weights)
     given, kept = reduce_z(chunks)
     across = lax.ppermute(given, "c", swap)
     teacher = lax.ppermute(kept, "yh", [(0, 1)])
     teacher_across = lax.ppermute(given, ("yh", "c"), [(0, 3), (1, 2)])
-    hidden_grad = finish(c, own_count, child_hidden, layer_grad, (kept, teacher, across, teacher_across))
+    own_count = jnp.where(is_child, layer_counts[2 * z + c], 0)
+    hidden_grad = finish(c, own_count, child_hidden, layer_grad, (teacher_across, across, teacher, kept))
     return (hidden_grad, key_grad[None], value_grad[None], gain_grad[None])
 
 

time: 178 us -> 167 us (0.938)
  starting transfers between devices: 79.1 us -> 68.4 us
  local copies, waits for them, and re-layouts: 13 us -> 6.61 us
  Pallas kernels: 24.1 us -> 26.8 us
  waiting for transfers between devices: 39 us -> 41 us
    ppermute x1, waiting for transfers between devices: 0.01 us -> 9.93 us  [body(): lax.ppermute(weight_rows[:, :half_rows], side, up)]
    ppermute x3, waiting for transfers between devices: 0.82 us -> 8.67 us  [reduce_z(): given_up = lax.ppermute(add(given[distance], given_up), 'z', up)]
    unnamed x68 -> x54, local copies, waits for them, and re-layouts: 10.9 us -> 4.53 us
    ppermute x1, waiting for transfers between devices: 4.84 us -> 0.01 us  [body(): lax.ppermute(weight_rows[:, half_rows:], side, down)]
    ppermute x3, waiting for transfers between devices: 4.97 us -> 0.15 us  [reduce_z(): kept_down = lax.ppermute(add(kept[-distance], kept_down), 'z', down)]
    ppermute x1, waiting for transfers between devices: 5.33 us -> 0.74 us  [body(): sent = lax.ppermute(leaving, side, [(0, 3), (1, 2)])]
    ppermute x1, waiting for transfers between devices: 0.01 us -> 4.09 us  [gather_tensor(): f1b = lax.ppermute(high, 'x', down)]
    ppermute x1, starting transfers between devices: 5.07 us -> 1.37 us  [body(): teacher = lax.ppermute(kept, 'yh', [(0, 1)])]
  transfers between devices with their start and end apart: 40 -> 40, of which waited for: 14 -> 15; matrix products, arithmetic and copies ran while one was open for 10% -> 14% of each run, Pallas kernels for 7% -> 7%
where the time goes in v10:
time: 167 us; the launch traced here: 166 us
  starting transfers between devices  68.4 us (41%)
  waiting for transfers between devices  41 us (25%)
  Pallas kernels  26.8 us (16%)
  other arithmetic  10.8 us (6%)
  matrix products  10.5 us (6%)
  local copies, waits for them, and re-layouts  6.61 us (4%)
  between operations  1.8 us (1%)
    all_to_all x1, starting transfers between devices, body(): lax.all_to_all(arranged, ('z', 'c'), split_axis=0, concat_axis=0, tiled=T...  10.7 us
    ppermute x1, waiting for transfers between devices, body(): lax.ppermute(weight_rows[:, :half_rows], side, up)  9.93 us
    pallas_call x1, Pallas kernels, project_rest(): pl.pallas_call(project_rest_kernel, out_shape=[jax.ShapeDtypeStruct(shape...  8.77 us
    ppermute x1, starting transfers between devices, body(): teacher_across = lax.ppermute(given, ('yh', 'c'), [(0, 3), (1, 2)])  8.76 us
    ppermute x3, waiting for transfers between devices, reduce_z(): given_up = lax.ppermute(add(given[distance], given_up), 'z', up)  8.67 us
    ppermute x3, starting transfers between devices, reduce_z(): kept_down = lax.ppermute(add(kept[-distance], kept_down), 'z', down)  8.49 us
    ppermute x1, starting transfers between devices, body(): sent = lax.ppermute(leaving, side, [(0, 3), (1, 2)])  6.5 us
    pallas_call x1, Pallas kernels, project_first(): pl.pallas_call(project_first_kernel, out_shape=jax.ShapeDtypeStruct(shape...  6.29 us
  transfers between devices with their start and end apart: 40, of which 15 were waited for; matrix products, arithmetic and copies ran while one was open for 14% of the time, Pallas kernels for 7%

profile of v10, /device:TPU:1, one launch (start us, length us, event | category | flops | bytes accessed | tf_op | source)
XLA Modules:
  0.0 165.8 jit_solution(9529652416070515302)
XLA Ops:
  0.7 3.0 %arrange.3 = bf16[16,192,128]{2,1,0:T(8,128)(2,1)} custom-call(bf16[3,128,2048]{2,1,0:T(8,128)(2,1)} %slabs.3), custom_call_target="tpu_custom_call" | custom-call | bytes 1600000 | tf_op jit(solution)/shard_map/arrange/pallas_call | solution.py:33
  3.7 6.5 %collective-permute-start = (bf16[16,192,128]{2,1,0:T(8,128)(2,1)}, bf16[16,192,128]{2,1,0:T(8,128)(2,1)}, u32[]{:S(2)}, u32[]{:S(2)}) collective-permute-start(bf16[16,192,128]{2,1,0:T(8,128)(2,1)} %arrange.3), channel_id=1, source_target_pairs={{0,129},{1,128},{2,131},{3,130},{4,133},{5,132},{6,135},{7,134},{8... | collective-permute-start | bytes 2359304 | tf_op jit(solution)/shard_map/ppermute | solution.py:349
  11.2 2.4 %fusion = f32[1024,128]{0,1:T(8,128)S(1)} fusion(bf16[1,1024,1024]{2,1,0:T(8,128)(2,1)} %param.16, bf16[1,128,1024]{2,1,0:T(8,128)(2,1)S(1)} %copy-done.11), kind=kOutput, calls=%fused_computation.1 | convolution fusion | flops 268435456 | bytes 2883584 | tf_op jit(solution)/shard_map/dot_general | solution.py:337
  13.6 1.9 %fusion.14 = (f32[128]{0:T(128)S(1)}, f32[128]{0:T(128)S(1)}, f32[128,1024]{1,0:T(8,128)S(1)}) fusion(bf16[3,128,1024]{2,1,0:T(8,128)(2,1)} %hidden.1, f32[1024]{0:T(1024)S(1)} %bitcast.93, f32[1024,128]{0,1:T(8,128)S(1)} %fusion, bf16[1,128,1024]{2,1,0:T(8,128)(2,1)S(1)} %copy-done, bf16[1,1024,1024]{2,1,0:T(8,128)(2,1)S(1)} %copy-done.7), kind=kOutput, calls=%fused_computation.16 | convolution fusion | flops 269352704 | bytes 3675136 | tf_op jit(solution)/shard_map/dot_general | solution.py:334
  18.0 2.8 %collective-permute-start.3 = (f32[2,128]{1,0:T(2,128)S(1)}, f32[2,128]{1,0:T(2,128)S(1)}, u32[]{:S(2)}, u32[]{:S(2)}) collective-permute-start(f32[2,128]{1,0:T(2,128)S(1)} %fusion.33), channel_id=1, source_target_pairs={{0,4},{2,6},{4,0},{6,2},{1,5},{3,7},{5,1},{7,3},{8,12},{10,14},{12... | collective-permute-start | bytes 3080 | tf_op jit(solution)/shard_map/ppermute | solution.py:347
  22.2 2.9 %arrange.2 = bf16[16,192,128]{2,1,0:T(8,128)(2,1)} custom-call(bf16[3,128,2048]{2,1,0:T(8,128)(2,1)} %slabs.3), custom_call_target="tpu_custom_call" | custom-call | bytes 1600000 | tf_op jit(solution)/shard_map/arrange/pallas_call | solution.py:33
  25.8 2.1 %broadcast_select_fusion = bf16[16,192,128]{2,1,0:T(8,128)(2,1)} fusion(bf16[16,192,128]{2,1,0:T(8,128)(2,1)} %arrange.2, bf16[16,192,128]{2,1,0:T(8,128)(2,1)} %collective-permute-done, pred[]{:T(512)S(6)} %eq.29), kind=kLoop, calls=%fused_computation.9 | loop fusion | flops 393216 | bytes 2359297 | tf_op jit(solution)/shard_map/jit(_where)/select_n | solution.py:350
  27.9 10.7 %all-to-all-start = ((bf16[16,192,128]{2,1,0:T(8,128)(2,1)}), bf16[16,192,128]{2,1,0:T(8,128)(2,1)}, u32[]{:S(2)}, u32[]{:S(2)}) async-start(bf16[16,192,128]{2,1,0:T(8,128)(2,1)} %broadcast_select_fusion), calls=%async_computation | async-start | bytes 1572864 | tf_op jit(solution)/shard_map/all_to_all | solution.py:354
  39.9 1.8 %collective-permute-start.12 = (bf16[8,32,1024]{2,1,0:T(8,128)(2,1)S(1)}, bf16[8,32,1024]{2,1,0:T(8,128)(2,1)}, u32[]{:S(2)}, u32[]{:S(2)}) collective-permute-start(bf16[8,32,1024]{2,1,0:T(8,128)(2,1)S(1)} %get-tuple-element.74), channel_id=1, source_target_pairs={{0,129},{1,0},{128,1},{129,128},{2,131},{3,2},{130,3},{131,130},{4... | collective-permute-start | bytes 1572872 | tf_op jit(solution)/shard_map/ppermute | solution.py:353
  41.6 2.1 %fusion.22 = (f32[128,1024]{1,0:T(8,128)}, f32[1024]{0:T(1024)S(1)}) fusion(f32[128,1024]{1,0:T(8,128)S(1)} %get-tuple-element.76, f32[128]{0:T(128)S(1)} %slice_bitcast_fusion, f32[128]{0:T(128)S(1)} %get-tuple-element.70, f32[128]{0:T(128)S(1)} %get-tuple-element.71, f32[1024]{0:T(1024)S(1)} %bitcast.94, pred[]{:T(512)S(6)} %eq.28, ...), kind=kLoop, calls=%fused_computation.24 | loop fusion | flops 1440768 | bytes 1320449 | tf_op jit(solution)/shard_map/jit(_where)/select_n | solution.py:372
  43.7 9.9 %collective-permute-done.10 = bf16[8,32,1024]{2,1,0:T(8,128)(2,1)} collective-permute-done((bf16[8,32,1024]{2,1,0:T(8,128)(2,1)S(1)}, bf16[8,32,1024]{2,1,0:T(8,128)(2,1)}, u32[]{:S(2)}, u32[]{:S(2)}) %collective-permute-start.10) | collective-permute-done | bytes 524320 | tf_op jit(solution)/shard_map/ppermute | solution.py:352
  54.2 2.7 %collective-permute-start.13 = (bf16[8,32,1024]{2,1,0:T(8,128)(2,1)}, bf16[8,32,1024]{2,1,0:T(8,128)(2,1)}, u32[]{:S(2)}, u32[]{:S(2)}) collective-permute-start(bf16[8,32,1024]{2,1,0:T(8,128)(2,1)} %collective-permute-done.12), channel_id=1, source_target_pairs={{0,129},{1,0},{128,1},{129,128},{2,131},{3,2},{130,3},{131,130},{4... | collective-permute-start | bytes 1572872 | tf_op jit(solution)/shard_map/ppermute | solution.py:353
  56.9 3.1 %convert_select_fusion = bf16[1024,1024]{1,0:T(8,128)(2,1)} fusion(pred[]{:T(512)S(6)} %eq.28, bf16[1,128,1024]{2,1,0:T(8,128)(2,1)S(1)} %copy-done, f32[1024]{0:T(1024)S(1)} %bitcast.95, f32[128]{0:T(128)S(1)} %get-tuple-element.71, bf16[3,128,1024]{2,1,0:T(8,128)(2,1)} %hidden.1), kind=kOutput, calls=%fused_computation.6 | convolution fusion | flops 271056896 | bytes 2626049 | tf_op jit(solution)/shard_map/dot_general | solution.py:361
  61.4 2.3 %pick_layers.1 = (bf16[32,2,32,128]{3,2,1,0:T(8,128)(2,1)}, bf16[16,2,32,128]{3,2,1,0:T(8,128)(2,1)}, bf16[16,2,32,128]{3,2,1,0:T(8,128)(2,1)}) custom-call(s32[32]{0:T(128)} %layer_map.1, bf16[48,2,32,128]{3,2,1,0:T(8,128)(2,1)} %bitcast.12.received), custom_call_target="tpu_custom_call" | custom-call | bytes 1300000 | tf_op jit(solution)/shard_map/pick_layers/pallas_call | solution.py:62
  69.5 3.5 %collective-permute-done.7.refs_3_ = bf16[16,2,32,128]{3,2,1,0:T(8,128)(2,1)S(1)} collective-permute-done((bf16[16,2,32,128]{3,2,1,0:T(8,128)(2,1)}, bf16[16,2,32,128]{3,2,1,0:T(8,128)(2,1)S(1)}, u32[]{:S(2)}, u32[]{:S(2)}) %collective-permute-start.7) | collective-permute-done | bytes 262176 | tf_op jit(solution)/shard_map/ppermute | solution.py:285
  74.3 4.1 %collective-permute-done.6.refs_2_ = bf16[16,2,32,128]{3,2,1,0:T(8,128)(2,1)} collective-permute-done((bf16[16,2,32,128]{3,2,1,0:T(8,128)(2,1)}, bf16[16,2,32,128]{3,2,1,0:T(8,128)(2,1)}, u32[]{:S(2)}, u32[]{:S(2)}) %collective-permute-start.6) | collective-permute-done | bytes 262176 | tf_op jit(solution)/shard_map/ppermute | solution.py:286
  80.2 2.8 %collective-permute-start.17 = (bf16[16,2,32,128]{3,2,1,0:T(8,128)(2,1)}, bf16[16,2,32,128]{3,2,1,0:T(8,128)(2,1)}, u32[]{:S(2)}, u32[]{:S(2)}) collective-permute-start(bf16[16,2,32,128]{3,2,1,0:T(8,128)(2,1)} %collective-permute-done.6.refs_2_), channel_id=1, source_target_pairs={{0,6},{2,0},{4,2},{6,4},{1,7},{3,1},{5,3},{7,5},{8,14},{10,8},{12,... | collective-permute-start | bytes 786440 | tf_op jit(solution)/shard_map/ppermute | solution.py:291
  85.1 3.9 %collective-permute-done.17.refs_1_ = bf16[16,2,32,128]{3,2,1,0:T(8,128)(2,1)} collective-permute-done((bf16[16,2,32,128]{3,2,1,0:T(8,128)(2,1)}, bf16[16,2,32,128]{3,2,1,0:T(8,128)(2,1)}, u32[]{:S(2)}, u32[]{:S(2)}) %collective-permute-start.17) | collective-permute-done | bytes 262176 | tf_op jit(solution)/shard_map/ppermute | solution.py:291
  92.2 6.3 %project_first.1.partial = bf16[4,256,1024]{2,1,0:T(8,128)(2,1)S(1)} custom-call(s32[4]{0:T(128)S(1)} %get-tuple-element.77.place, s32[4]{0:T(128)S(1)} %get-tuple-element.78.blocks, bf16[32,2,32,128]{3,2,1,0:T(8,128)(2,1)S(1)} %copy-done.5, bf16[16,2,32,128]{3,2,1,0:T(8,128)(2,1)} %collective-permute-done.5.refs_1_, ...), custom_call_target="tpu_custom_call" | custom-call | flops 2147483648 | bytes 8388608 | tf_op jit(solution)/shard_map/project_first/pallas_call | solution.py:176
  102.2 8.8 %project_rest.1 = (bf16[3,32,1024]{2,1,0:T(8,128)(2,1)}, bf16[3,32,1024]{2,1,0:T(8,128)(2,1)}, bf16[3,32,1024]{2,1,0:T(8,128)(2,1)}, bf16[3,32,1024]{2,1,0:T(8,1...) custom-call(s32[4]{0:T(128)} %copy-done.6, ...), custom_call_target="tpu_custom_call" | custom-call | flops 2147483648 | bytes 11534336 | tf_op jit(solution)/shard_map/project_rest/pallas_call | solution.py:202
  114.3 1.8 %collective-permute-start.34 = (bf16[3,32,1024]{2,1,0:T(8,128)(2,1)}, bf16[3,32,1024]{2,1,0:T(8,128)(2,1)S(1)}, u32[]{:S(2)}, u32[]{:S(2)}) collective-permute-start(bf16[3,32,1024]{2,1,0:T(8,128)(2,1)} %get-tuple-element.65), channel_id=1, source_target_pairs={{0,112},{16,0},{32,16},{48,32},{64,48},{80,64},{96,80},{112,96},{1... | collective-permute-start | bytes 589832 | tf_op jit(solution)/shard_map/ppermute | solution.py:234
  117.2 2.7 %collective-permute-start.27 = (bf16[3,32,1024]{2,1,0:T(8,128)(2,1)S(1)}, bf16[3,32,1024]{2,1,0:T(8,128)(2,1)S(1)}, u32[]{:S(2)}, u32[]{:S(2)}) collective-permute-start(bf16[3,32,1024]{2,1,0:T(8,128)(2,1)S(1)} %add_convert_fusion.8), channel_id=1, source_target_pairs={{0,112},{16,0},{32,16},{48,32},{64,48},{80,64},{96,80},{112,96},{1... | collective-permute-start | bytes 589832 | tf_op jit(solution)/shard_map/ppermute | solution.py:240
  122.0 2.7 %collective-permute-start.35 = (bf16[3,32,1024]{2,1,0:T(8,128)(2,1)S(1)}, bf16[3,32,1024]{2,1,0:T(8,128)(2,1)S(1)}, u32[]{:S(2)}, u32[]{:S(2)}) collective-permute-start(bf16[3,32,1024]{2,1,0:T(8,128)(2,1)S(1)} %add_convert_fusion.3), channel_id=1, source_target_pairs={{0,112},{16,0},{32,16},{48,32},{64,48},{80,64},{96,80},{112,96},{1... | collective-permute-start | bytes 589832 | tf_op jit(solution)/shard_map/ppermute | solution.py:241
  125.9 2.7 %collective-permute-start.28 = (bf16[3,32,1024]{2,1,0:T(8,128)(2,1)S(1)}, bf16[3,32,1024]{2,1,0:T(8,128)(2,1)S(1)}, u32[]{:S(2)}, u32[]{:S(2)}) collective-permute-start(bf16[3,32,1024]{2,1,0:T(8,128)(2,1)S(1)} %add_convert_fusion.7), channel_id=1, source_target_pairs={{0,112},{16,0},{32,16},{48,32},{64,48},{80,64},{96,80},{112,96},{1... | collective-permute-start | bytes 589832 | tf_op jit(solution)/shard_map/ppermute | solution.py:240
  129.0 3.0 %collective-permute-start.36 = (bf16[3,32,1024]{2,1,0:T(8,128)(2,1)S(1)}, bf16[3,32,1024]{2,1,0:T(8,128)(2,1)S(1)}, u32[]{:S(2)}, u32[]{:S(2)}) collective-permute-start(bf16[3,32,1024]{2,1,0:T(8,128)(2,1)S(1)} %add_convert_fusion.2), channel_id=1, source_target_pairs={{0,112},{16,0},{32,16},{48,32},{64,48},{80,64},{96,80},{112,96},{1... | collective-permute-start | bytes 589832 | tf_op jit(solution)/shard_map/ppermute | solution.py:241
  133.5 2.8 %collective-permute-done.24 = bf16[3,32,1024]{2,1,0:T(8,128)(2,1)S(1)} collective-permute-done((bf16[3,32,1024]{2,1,0:T(8,128)(2,1)S(1)}, bf16[3,32,1024]{2,1,0:T(8,128)(2,1)S(1)}, u32[]{:S(2)}, u32[]{:S(2)}) %collective-permute-start.24) | collective-permute-done | bytes 196640 | tf_op jit(solution)/shard_map/ppermute | solution.py:238
  136.5 2.7 %collective-permute-start.37 = (bf16[3,32,1024]{2,1,0:T(8,128)(2,1)S(1)}, bf16[3,32,1024]{2,1,0:T(8,128)(2,1)S(1)}, u32[]{:S(2)}, u32[]{:S(2)}) collective-permute-start(bf16[3,32,1024]{2,1,0:T(8,128)(2,1)S(1)} %add_convert_fusion.1), channel_id=1, source_target_pairs={{0,112},{16,0},{32,16},{48,32},{64,48},{80,64},{96,80},{112,96},{1... | collective-permute-start | bytes 589832 | tf_op jit(solution)/shard_map/ppermute | solution.py:241
  139.3 5.9 %collective-permute-done.25 = bf16[3,32,1024]{2,1,0:T(8,128)(2,1)S(1)} collective-permute-done((bf16[3,32,1024]{2,1,0:T(8,128)(2,1)S(1)}, bf16[3,32,1024]{2,1,0:T(8,128)(2,1)S(1)}, u32[]{:S(2)}, u32[]{:S(2)}) %collective-permute-start.25) | collective-permute-done | bytes 196640 | tf_op jit(solution)/shard_map/ppermute | solution.py:238
  145.2 8.8 %collective-permute-start.29 = (bf16[3,32,1024]{2,1,0:T(8,128)(2,1)S(1)}, bf16[3,32,1024]{2,1,0:T(8,128)(2,1)S(1)}, u32[]{:S(2)}, u32[]{:S(2)}) collective-permute-start(bf16[3,32,1024]{2,1,0:T(8,128)(2,1)S(1)} %add_convert_fusion.6), channel_id=1, source_target_pairs={{0,136},{8,128},{1,137},{9,129},{2,138},{10,130},{3,139},{11,131},... | collective-permute-start | bytes 589832 | tf_op jit(solution)/shard_map/ppermute | solution.py:394
  155.6 3.1 %select_bitcast_fusion = bf16[1,1024,1024]{2,1,0:T(8,128)(2,1)} fusion(pred[]{:T(512)S(6)} %eq.28, bf16[1,128,1024]{2,1,0:T(8,128)(2,1)S(1)} %copy-done.12, f32[1024]{0:T(1024)S(1)} %bitcast.96, f32[128]{0:T(128)S(1)} %get-tuple-element.71, bf16[3,128,1024]{2,1,0:T(8,128)(2,1)} %hidden.1), kind=kOutput, calls=%fused_computation.5 | convolution fusion | flops 271056896 | bytes 2626049 | tf_op jit(solution)/shard_map/dot_general | solution.py:364
  158.7 2.9 %collective-permute-done.38.teacher = bf16[3,32,1024]{2,1,0:T(8,128)(2,1)S(1)} collective-permute-done((bf16[3,32,1024]{2,1,0:T(8,128)(2,1)S(1)}, bf16[3,32,1024]{2,1,0:T(8,128)(2,1)S(1)}, u32[]{:S(2)}, u32[]{:S(2)}) %collective-permute-start.38) | collective-permute-done | bytes 196640 | tf_op jit(solution)/shard_map/ppermute | solution.py:393
  162.3 3.5 %finish.1 = bf16[3,128,1024]{2,1,0:T(8,128)(2,1)} custom-call(s32[2]{0:T(128)} %pad_add_fusion.state, bf16[3,128,1024]{2,1,0:T(8,128)(2,1)} %hidden.1, f32[128,1024]{1,0:T(8,128)} %get-tuple-element.41.layer_grad, bf16[3,32,1024]{2,1,0:T(8,128)(2,1)} %copy-done.13, bf16[3,32,1024]{2,1,0:T(8,128)(2,1)} %copy-done.14, bf16[3,32,1024]{2,1,0:T(8,128)(2,1)} %copy-done.15, ...), custom_call_target="tpu_custom_call" | custom-call | flops 786432 | bytes 3145728 | tf_op jit(solution)/shard_map/finish/pallas_call | solution.py:265
  (150 shorter events, 37.9 us)
Async XLA Ops:
  3.7 22.1 %collective-permute-start = (bf16[16,192,128]{2,1,0:T(8,128)(2,1)}, bf16[16,192,128]{2,1,0:T(8,128)(2,1)}, u32[]{:S(2)}, u32[]{:S(2)}) collective-permute-start(bf16[16,192,128]{2,1,0:T(8,128)(2,1)} %arrange.3), channel_id=1, source_target_pairs={{0,129},{1,128},{2,131},{3,130},{4,133},{5,132},{6,135},{7,134},{8... | collective-permute-start | bytes 2359304 | tf_op jit(solution)/shard_map/ppermute | solution.py:349
  10.2 17.7 %collective-permute-start.1 = (bf16[8,64,1024]{2,1,0:T(8,128)(2,1)S(1)}, bf16[8,64,1024]{2,1,0:T(8,128)(2,1)S(1)}, u32[]{:S(2)}, u32[]{:S(2)}) collective-permute-start(bf16[8,64,1024]{2,1,0:T(8,128)(2,1)S(1)} %copy-done.1), channel_id=1, source_target_pairs={{0,8},{8,0},{1,9},{9,1},{2,10},{10,2},{3,11},{11,3},{4,12},{12,4},... | collective-permute-start | bytes 3145736 | tf_op jit(solution)/shard_map/ppermute | solution.py:326
  27.9 33.5 %all-to-all-start = ((bf16[16,192,128]{2,1,0:T(8,128)(2,1)}), bf16[16,192,128]{2,1,0:T(8,128)(2,1)}, u32[]{:S(2)}, u32[]{:S(2)}) async-start(bf16[16,192,128]{2,1,0:T(8,128)(2,1)} %broadcast_select_fusion), calls=%async_computation | async-start | bytes 1572864 | tf_op jit(solution)/shard_map/all_to_all | solution.py:354
  38.7 14.9 %collective-permute-start.10 = (bf16[8,32,1024]{2,1,0:T(8,128)(2,1)S(1)}, bf16[8,32,1024]{2,1,0:T(8,128)(2,1)}, u32[]{:S(2)}, u32[]{:S(2)}) collective-permute-start(bf16[8,32,1024]{2,1,0:T(8,128)(2,1)S(1)} %get-tuple-element.75), channel_id=1, source_target_pairs={{0,1},{1,128},{128,129},{129,0},{2,3},{3,130},{130,131},{131,2},{4... | collective-permute-start | bytes 1572872 | tf_op jit(solution)/shard_map/ppermute | solution.py:352
  39.9 14.4 %collective-permute-start.12 = (bf16[8,32,1024]{2,1,0:T(8,128)(2,1)S(1)}, bf16[8,32,1024]{2,1,0:T(8,128)(2,1)}, u32[]{:S(2)}, u32[]{:S(2)}) collective-permute-start(bf16[8,32,1024]{2,1,0:T(8,128)(2,1)S(1)} %get-tuple-element.74), channel_id=1, source_target_pairs={{0,129},{1,0},{128,1},{129,128},{2,131},{3,2},{130,3},{131,130},{4... | collective-permute-start | bytes 1572872 | tf_op jit(solution)/shard_map/ppermute | solution.py:353
  53.6 14.4 %collective-permute-start.11 = (bf16[8,32,1024]{2,1,0:T(8,128)(2,1)}, bf16[8,32,1024]{2,1,0:T(8,128)(2,1)S(1)}, u32[]{:S(2)}, u32[]{:S(2)}) collective-permute-start(bf16[8,32,1024]{2,1,0:T(8,128)(2,1)} %collective-permute-done.10), channel_id=1, source_target_pairs={{0,1},{1,128},{128,129},{129,0},{2,3},{3,130},{130,131},{131,2},{4... | collective-permute-start | bytes 1572872 | tf_op jit(solution)/shard_map/ppermute | solution.py:352
  54.2 15.0 %collective-permute-start.13 = (bf16[8,32,1024]{2,1,0:T(8,128)(2,1)}, bf16[8,32,1024]{2,1,0:T(8,128)(2,1)}, u32[]{:S(2)}, u32[]{:S(2)}) collective-permute-start(bf16[8,32,1024]{2,1,0:T(8,128)(2,1)} %collective-permute-done.12), channel_id=1, source_target_pairs={{0,129},{1,0},{128,1},{129,128},{2,131},{3,2},{130,3},{131,130},{4... | collective-permute-start | bytes 1572872 | tf_op jit(solution)/shard_map/ppermute | solution.py:353
  63.7 9.3 %collective-permute-start.7 = (bf16[16,2,32,128]{3,2,1,0:T(8,128)(2,1)}, bf16[16,2,32,128]{3,2,1,0:T(8,128)(2,1)S(1)}, u32[]{:S(2)}, u32[]{:S(2)}) collective-permute-start(bf16[16,2,32,128]{3,2,1,0:T(8,128)(2,1)} %get-tuple-element.44), channel_id=1, source_target_pairs={{0,2},{2,4},{4,6},{6,0},{1,3},{3,5},{5,7},{7,1},{8,10},{10,12},{12... | collective-permute-start | bytes 786440 | tf_op jit(solution)/shard_map/ppermute | solution.py:285
  64.9 8.9 %collective-permute-start.5 = (bf16[16,2,32,128]{3,2,1,0:T(8,128)(2,1)}, bf16[16,2,32,128]{3,2,1,0:T(8,128)(2,1)}, u32[]{:S(2)}, u32[]{:S(2)}) collective-permute-start(bf16[16,2,32,128]{3,2,1,0:T(8,128)(2,1)} %get-tuple-element.44), channel_id=1, source_target_pairs={{0,6},{2,0},{4,2},{6,4},{1,7},{3,1},{5,3},{7,5},{8,14},{10,8},{12,... | collective-permute-start | bytes 786440 | tf_op jit(solution)/shard_map/ppermute | solution.py:289
  66.7 11.7 %collective-permute-start.6 = (bf16[16,2,32,128]{3,2,1,0:T(8,128)(2,1)}, bf16[16,2,32,128]{3,2,1,0:T(8,128)(2,1)}, u32[]{:S(2)}, u32[]{:S(2)}) collective-permute-start(bf16[16,2,32,128]{3,2,1,0:T(8,128)(2,1)} %get-tuple-element.45), channel_id=1, source_target_pairs={{0,6},{2,0},{4,2},{6,4},{1,7},{3,1},{5,3},{7,5},{8,14},{10,8},{12,... | collective-permute-start | bytes 786440 | tf_op jit(solution)/shard_map/ppermute | solution.py:286
  68.0 15.0 %collective-permute-start.9 = (bf16[32,2,32,128]{3,2,1,0:T(8,128)(2,1)}, bf16[32,2,32,128]{3,2,1,0:T(8,128)(2,1)}, u32[]{:S(2)}, u32[]{:S(2)}) collective-permute-start(bf16[32,2,32,128]{3,2,1,0:T(8,128)(2,1)} %get-tuple-element.43.refs_0_), channel_id=1, source_target_pairs={{0,1},{1,0},{2,3},{3,2},{4,5},{5,4},{6,7},{7,6},{8,9},{9,8},{10,11... | collective-permute-start | bytes 1572872 | tf_op jit(solution)/shard_map/ppermute | solution.py:287
  69.2 11.0 %collective-permute-start.8 = (bf16[16,2,32,128]{3,2,1,0:T(8,128)(2,1)}, bf16[16,2,32,128]{3,2,1,0:T(8,128)(2,1)}, u32[]{:S(2)}, u32[]{:S(2)}) collective-permute-start(bf16[16,2,32,128]{3,2,1,0:T(8,128)(2,1)} %get-tuple-element.45), channel_id=1, source_target_pairs={{0,2},{2,4},{4,6},{6,0},{1,3},{3,5},{5,7},{7,1},{8,10},{10,12},{12... | collective-permute-start | bytes 786440 | tf_op jit(solution)/shard_map/ppermute | solution.py:288
  73.0 16.0 %collective-permute-start.14 = (bf16[8,32,1024]{2,1,0:T(8,128)(2,1)S(1)}, bf16[8,32,1024]{2,1,0:T(8,128)(2,1)}, u32[]{:S(2)}, u32[]{:S(2)}) collective-permute-start(bf16[8,32,1024]{2,1,0:T(8,128)(2,1)S(1)} %collective-permute-done.11.refs_8_), channel_id=1, source_target_pairs={{0,8},{8,0},{1,9},{9,1},{2,10},{10,2},{3,11},{11,3},{4,12},{12,4},... | collective-permute-start | bytes 1572872 | tf_op jit(solution)/shard_map/ppermute | solution.py:379
  73.9 10.3 %collective-permute-start.16 = (bf16[16,2,32,128]{3,2,1,0:T(8,128)(2,1)S(1)}, bf16[16,2,32,128]{3,2,1,0:T(8,128)(2,1)}, u32[]{:S(2)}, u32[]{:S(2)}) collective-permute-start(bf16[16,2,32,128]{3,2,1,0:T(8,128)(2,1)S(1)} %collective-permute-done.7.refs_3_), channel_id=1, source_target_pairs={{0,2},{2,4},{4,6},{6,0},{1,3},{3,5},{5,7},{7,1},{8,10},{10,12},{12... | collective-permute-start | bytes 786440 | tf_op jit(solution)/shard_map/ppermute | solution.py:290
  78.4 12.7 %collective-permute-start.15 = (bf16[8,32,1024]{2,1,0:T(8,128)(2,1)}, bf16[8,32,1024]{2,1,0:T(8,128)(2,1)}, u32[]{:S(2)}, u32[]{:S(2)}) collective-permute-start(bf16[8,32,1024]{2,1,0:T(8,128)(2,1)} %collective-permute-done.13.refs_9_), channel_id=1, source_target_pairs={{0,8},{8,0},{1,9},{9,1},{2,10},{10,2},{3,11},{11,3},{4,12},{12,4},... | collective-permute-start | bytes 1572872 | tf_op jit(solution)/shard_map/ppermute | solution.py:379
  80.2 8.8 %collective-permute-start.17 = (bf16[16,2,32,128]{3,2,1,0:T(8,128)(2,1)}, bf16[16,2,32,128]{3,2,1,0:T(8,128)(2,1)}, u32[]{:S(2)}, u32[]{:S(2)}) collective-permute-start(bf16[16,2,32,128]{3,2,1,0:T(8,128)(2,1)} %collective-permute-done.6.refs_2_), channel_id=1, source_target_pairs={{0,6},{2,0},{4,2},{6,4},{1,7},{3,1},{5,3},{7,5},{8,14},{10,8},{12,... | collective-permute-start | bytes 786440 | tf_op jit(solution)/shard_map/ppermute | solution.py:291
  83.0 19.2 %collective-permute-start.18 = (bf16[32,2,32,128]{3,2,1,0:T(8,128)(2,1)}, bf16[32,2,32,128]{3,2,1,0:T(8,128)(2,1)}, u32[]{:S(2)}, u32[]{:S(2)}) collective-permute-start(bf16[32,2,32,128]{3,2,1,0:T(8,128)(2,1)} %collective-permute-done.9.refs_5_), channel_id=1, source_target_pairs={{0,6},{2,0},{4,2},{6,4},{1,7},{3,1},{5,3},{7,5},{8,14},{10,8},{12,... | collective-permute-start | bytes 1572872 | tf_op jit(solution)/shard_map/ppermute | solution.py:293
  84.1 18.0 %collective-permute-start.21 = (bf16[32,2,32,128]{3,2,1,0:T(8,128)(2,1)}, bf16[32,2,32,128]{3,2,1,0:T(8,128)(2,1)}, u32[]{:S(2)}, u32[]{:S(2)}) collective-permute-start(bf16[32,2,32,128]{3,2,1,0:T(8,128)(2,1)} %collective-permute-done.9.refs_5_), channel_id=1, source_target_pairs={{0,2},{2,4},{4,6},{6,0},{1,3},{3,5},{5,7},{7,1},{8,10},{10,12},{12... | collective-permute-start | bytes 1572872 | tf_op jit(solution)/shard_map/ppermute | solution.py:292
  89.0 10.8 %collective-permute-start.19 = (bf16[16,2,32,128]{3,2,1,0:T(8,128)(2,1)}, bf16[16,2,32,128]{3,2,1,0:T(8,128)(2,1)S(1)}, u32[]{:S(2)}, u32[]{:S(2)}) collective-permute-start(bf16[16,2,32,128]{3,2,1,0:T(8,128)(2,1)} %collective-permute-done.16.refs_0_), channel_id=1, source_target_pairs={{0,1},{1,0},{2,3},{3,2},{4,5},{5,4},{6,7},{7,6},{8,9},{9,8},{10,11... | collective-permute-start | bytes 786440 | tf_op jit(solution)/shard_map/ppermute | solution.py:294
  89.0 12.4 %collective-permute-start.20 = (bf16[16,2,32,128]{3,2,1,0:T(8,128)(2,1)}, bf16[16,2,32,128]{3,2,1,0:T(8,128)(2,1)S(1)}, u32[]{:S(2)}, u32[]{:S(2)}) collective-permute-start(bf16[16,2,32,128]{3,2,1,0:T(8,128)(2,1)} %collective-permute-done.17.refs_1_), channel_id=1, source_target_pairs={{0,1},{1,0},{2,3},{3,2},{4,5},{5,4},{6,7},{7,6},{8,9},{9,8},{10,11... | collective-permute-start | bytes 786440 | tf_op jit(solution)/shard_map/ppermute | solution.py:295
  116.2 8.6 %collective-permute-start.31 = (bf16[3,32,1024]{2,1,0:T(8,128)(2,1)}, bf16[3,32,1024]{2,1,0:T(8,128)(2,1)S(1)}, u32[]{:S(2)}, u32[]{:S(2)}) collective-permute-start(bf16[3,32,1024]{2,1,0:T(8,128)(2,1)} %get-tuple-element.61), channel_id=1, source_target_pairs={{0,16},{16,32},{32,48},{48,64},{64,80},{80,96},{96,112},{112,0},{1... | collective-permute-start | bytes 589832 | tf_op jit(solution)/shard_map/ppermute | solution.py:236
  117.2 8.6 %collective-permute-start.27 = (bf16[3,32,1024]{2,1,0:T(8,128)(2,1)S(1)}, bf16[3,32,1024]{2,1,0:T(8,128)(2,1)S(1)}, u32[]{:S(2)}, u32[]{:S(2)}) collective-permute-start(bf16[3,32,1024]{2,1,0:T(8,128)(2,1)S(1)} %add_convert_fusion.8), channel_id=1, source_target_pairs={{0,112},{16,0},{32,16},{48,32},{64,48},{80,64},{96,80},{112,96},{1... | collective-permute-start | bytes 589832 | tf_op jit(solution)/shard_map/ppermute | solution.py:240
  120.9 7.7 %collective-permute-start.23 = (bf16[3,32,1024]{2,1,0:T(8,128)(2,1)S(1)}, bf16[3,32,1024]{2,1,0:T(8,128)(2,1)S(1)}, u32[]{:S(2)}, u32[]{:S(2)}) collective-permute-start(bf16[3,32,1024]{2,1,0:T(8,128)(2,1)S(1)} %add_convert_fusion.11), channel_id=1, source_target_pairs={{0,16},{16,32},{32,48},{48,64},{64,80},{80,96},{96,112},{112,0},{1... | collective-permute-start | bytes 589832 | tf_op jit(solution)/shard_map/ppermute | solution.py:238
  125.7 7.6 %collective-permute-start.32 = (bf16[3,32,1024]{2,1,0:T(8,128)(2,1)S(1)}, bf16[3,32,1024]{2,1,0:T(8,128)(2,1)S(1)}, u32[]{:S(2)}, u32[]{:S(2)}) collective-permute-start(bf16[3,32,1024]{2,1,0:T(8,128)(2,1)S(1)} %add_convert_fusion.5), channel_id=1, source_target_pairs={{0,16},{16,32},{32,48},{48,64},{64,80},{80,96},{96,112},{112,0},{1... | collective-permute-start | bytes 589832 | tf_op jit(solution)/shard_map/ppermute | solution.py:243
  125.9 13.3 %collective-permute-start.28 = (bf16[3,32,1024]{2,1,0:T(8,128)(2,1)S(1)}, bf16[3,32,1024]{2,1,0:T(8,128)(2,1)S(1)}, u32[]{:S(2)}, u32[]{:S(2)}) collective-permute-start(bf16[3,32,1024]{2,1,0:T(8,128)(2,1)S(1)} %add_convert_fusion.7), channel_id=1, source_target_pairs={{0,112},{16,0},{32,16},{48,32},{64,48},{80,64},{96,80},{112,96},{1... | collective-permute-start | bytes 589832 | tf_op jit(solution)/shard_map/ppermute | solution.py:240
  128.7 7.6 %collective-permute-start.24 = (bf16[3,32,1024]{2,1,0:T(8,128)(2,1)S(1)}, bf16[3,32,1024]{2,1,0:T(8,128)(2,1)S(1)}, u32[]{:S(2)}, u32[]{:S(2)}) collective-permute-start(bf16[3,32,1024]{2,1,0:T(8,128)(2,1)S(1)} %add_convert_fusion.10), channel_id=1, source_target_pairs={{0,16},{16,32},{32,48},{48,64},{64,80},{80,96},{96,112},{112,0},{1... | collective-permute-start | bytes 589832 | tf_op jit(solution)/shard_map/ppermute | solution.py:238
  129.0 7.4 %collective-permute-start.36 = (bf16[3,32,1024]{2,1,0:T(8,128)(2,1)S(1)}, bf16[3,32,1024]{2,1,0:T(8,128)(2,1)S(1)}, u32[]{:S(2)}, u32[]{:S(2)}) collective-permute-start(bf16[3,32,1024]{2,1,0:T(8,128)(2,1)S(1)} %add_convert_fusion.2), channel_id=1, source_target_pairs={{0,112},{16,0},{32,16},{48,32},{64,48},{80,64},{96,80},{112,96},{1... | collective-permute-start | bytes 589832 | tf_op jit(solution)/shard_map/ppermute | solution.py:241
  133.4 20.7 %collective-permute-start.33 = (bf16[3,32,1024]{2,1,0:T(8,128)(2,1)S(1)}, bf16[3,32,1024]{2,1,0:T(8,128)(2,1)S(1)}, u32[]{:S(2)}, u32[]{:S(2)}) collective-permute-start(bf16[3,32,1024]{2,1,0:T(8,128)(2,1)S(1)} %add_convert_fusion.4), channel_id=1, source_target_pairs={{0,16},{16,32},{32,48},{48,64},{64,80},{80,96},{96,112},{112,0},{1... | collective-permute-start | bytes 589832 | tf_op jit(solution)/shard_map/ppermute | solution.py:243
  136.4 8.8 %collective-permute-start.25 = (bf16[3,32,1024]{2,1,0:T(8,128)(2,1)S(1)}, bf16[3,32,1024]{2,1,0:T(8,128)(2,1)S(1)}, u32[]{:S(2)}, u32[]{:S(2)}) collective-permute-start(bf16[3,32,1024]{2,1,0:T(8,128)(2,1)S(1)} %add_convert_fusion.9), channel_id=1, source_target_pairs={{0,16},{16,32},{32,48},{48,64},{64,80},{80,96},{96,112},{112,0},{1... | collective-permute-start | bytes 589832 | tf_op jit(solution)/shard_map/ppermute | solution.py:238
  136.5 17.6 %collective-permute-start.37 = (bf16[3,32,1024]{2,1,0:T(8,128)(2,1)S(1)}, bf16[3,32,1024]{2,1,0:T(8,128)(2,1)S(1)}, u32[]{:S(2)}, u32[]{:S(2)}) collective-permute-start(bf16[3,32,1024]{2,1,0:T(8,128)(2,1)S(1)} %add_convert_fusion.1), channel_id=1, source_target_pairs={{0,112},{16,0},{32,16},{48,32},{64,48},{80,64},{96,80},{112,96},{1... | collective-permute-start | bytes 589832 | tf_op jit(solution)/shard_map/ppermute | solution.py:241
  145.2 13.5 %collective-permute-start.29 = (bf16[3,32,1024]{2,1,0:T(8,128)(2,1)S(1)}, bf16[3,32,1024]{2,1,0:T(8,128)(2,1)S(1)}, u32[]{:S(2)}, u32[]{:S(2)}) collective-permute-start(bf16[3,32,1024]{2,1,0:T(8,128)(2,1)S(1)} %add_convert_fusion.6), channel_id=1, source_target_pairs={{0,136},{8,128},{1,137},{9,129},{2,138},{10,130},{3,139},{11,131},... | collective-permute-start | bytes 589832 | tf_op jit(solution)/shard_map/ppermute | solution.py:394
  154.2 7.4 %collective-permute-start.38 = (bf16[3,32,1024]{2,1,0:T(8,128)(2,1)S(1)}, bf16[3,32,1024]{2,1,0:T(8,128)(2,1)S(1)}, u32[]{:S(2)}, u32[]{:S(2)}) collective-permute-start(bf16[3,32,1024]{2,1,0:T(8,128)(2,1)S(1)} %add_convert_fusion.near), channel_id=1, source_target_pairs={{0,128},{1,129},{2,130},{3,131},{4,132},{5,133},{6,134},{7,135},{8... | collective-permute-start | bytes 589832 | tf_op jit(solution)/shard_map/ppermute | solution.py:393
  (35 other events, 459.5 us)

commit v11 on v8

--- a/solution.py
+++ b/solution.py
@@ -273,13 +273,14 @@
     )(jnp.stack([c, own_count]).astype(jnp.int32), hidden, layer_grad, *pieces)
 
 
-def gather_tensor(own, low, high):
+def gather_tensor(own, low, high, far):
     up = [(i, (i + 1) % X) for i in range(X)]
     down = [(i, (i - 1) % X) for i in range(X)]
     swap = [(0, 1), (1, 0)]
     f3a = lax.ppermute(low, "x", up)
     f1b = lax.ppermute(high, "x", down)
     g0 = lax.ppermute(own, "yl", swap)
+    low, high, *far = lax.optimization_barrier((low, high, *far))
     f3b = lax.ppermute(high, "x", up)
     f1a = lax.ppermute(low, "x", down)
     f2a = lax.ppermute(f3a, "x", up)
@@ -288,7 +289,8 @@
     g1 = lax.ppermute(g0, "x", down)
     g2a = lax.ppermute(f2a, "yl", swap)
     g2b = lax.ppermute(f2b, "yl", swap)
-    return (own, f1a, f1b, f3a, f3b, g0), (f2a, f2b, g1, g2a, g2b, g3)
+    *far, _ = lax.optimization_barrier((*far, f3a))
+    return (own, f1a, f1b, f3a, f3b, g0), (f2a, f2b, g1, g2a, g2b, g3), far
 
 
 def body(
@@ -343,13 +345,14 @@
     sent = lax.ppermute(arrange(teacher_slabs, 1), side, [(0, 3), (1, 2)])
     arranged = jnp.where(yh == 0, arrange(teacher_slabs, 0), sent)
     arranged, w_sib, sums, weight_rows = lax.optimization_barrier((arranged, w_sib, sums, proj_weight))
-    w_far_a = lax.ppermute(lax.ppermute(weight_rows[:, :half_rows], side, up), side, up)
-    w_far_b = lax.ppermute(lax.ppermute(weight_rows[:, half_rows:], side, down), side, down)
+    w_mid_a = lax.ppermute(weight_rows[:, :half_rows], side, up)
+    w_mid_b = lax.ppermute(weight_rows[:, half_rows:], side, down)
     received = lax.all_to_all(arranged, ("z", "c"), split_axis=0, concat_axis=0, tiled=True)
     received = received.reshape(Z * C * slab_count, YH, quarter, LANES)
-
-    first_features, rest_features = gather_tensor(*pick(layer_map, received))
-    w_far_a, w_far_b, _ = lax.optimization_barrier((w_far_a, w_far_b, first_features[3]))
+    w_far_a, w_far_b = lax.ppermute(w_mid_a, side, up), lax.ppermute(w_mid_b, side, down)
+    received, _, _ = lax.optimization_barrier((received, w_mid_a, w_mid_b))
+
+    first_features, rest_features, (w_far_a, w_far_b) = gather_tensor(*pick(layer_map, received), (w_far_a, w_far_b))
     weights = (proj_weight, w_sib, w_far_a, w_far_b, lax.ppermute(w_far_a, "c", swap), lax.ppermute(w_far_b, "c", swap))
     squares, inner_sum = sums[0], sums[1]
     inverse_rms = lax.rsqrt(squares / full_width + EPSILON)[:, None]

time: 165 us -> 171 us (1.036)
  starting transfers between devices: 74.8 us -> 78.1 us
  waiting for transfers between devices: 37.4 us -> 39.8 us
    ppermute x4, waiting for transfers between devices: 11.6 us -> 14.8 us  [the longest x1 11.7 us: body(): w_mid_a = lax.ppermute(weight_rows[:, :half_rows], side, up)]
    ppermute x1, starting transfers between devices: 0.12 us -> 3.08 us  [body(): lax.ppermute(w_far_b, 'c', swap)]
    ppermute x1, starting transfers between devices: 0.16 us -> 2.72 us  [body(): lax.ppermute(w_far_a, 'c', swap)]
    ppermute x1, waiting for transfers between devices: 2 us -> 0.01 us  [gather_tensor(): f3a = lax.ppermute(low, 'x', up)]
  transfers between devices with their start and end apart: 40 -> 40, of which waited for: 17 -> 17; matrix products, arithmetic and copies ran while one was open for 12% -> 11% of each run, Pallas kernels for 7% -> 7%
where the time goes in v11:
time: 171 us; the launch traced here: 168 us
  starting transfers between devices  78.1 us (46%)
  waiting for transfers between devices  39.8 us (23%)
  Pallas kernels  25.1 us (15%)
  matrix products  9.31 us (5%)
  other arithmetic  7.14 us (4%)
  local copies, waits for them, and re-layouts  6.95 us (4%)
  between operations  1.84 us (1%)
    ppermute x1, waiting for transfers between devices, body(): w_mid_a = lax.ppermute(weight_rows[:, :half_rows], side, up)  11.7 us
    all_to_all x1, starting transfers between devices, body(): lax.all_to_all(arranged, ('z', 'c'), split_axis=0, concat_axis=0, tiled=T...  11.5 us
    ppermute x3, starting transfers between devices, reduce_z(): kept_down = lax.ppermute(add(kept[-distance], kept_down), 'z', down)  10.1 us
    pallas_call x1, Pallas kernels, project_rest(): pl.pallas_call(project_rest_kernel, out_shape=[jax.ShapeDtypeStruct(shape...  8.82 us
    pallas_call x1, Pallas kernels, project_first(): pl.pallas_call(project_first_kernel, out_shape=jax.ShapeDtypeStruct(shape...  6.88 us
    ppermute x1, starting transfers between devices, body(): sent = lax.ppermute(arrange(teacher_slabs, 1), side, [(0, 3), (1, 2)])  6.51 us
    ppermute x2, starting transfers between devices, reduce_z(): given_down = lax.ppermute(add(given[-distance], given_down), 'z', down)  6.24 us
    ppermute x1, starting transfers between devices, body(): across = lax.ppermute(given, 'c', swap)  5.77 us
  transfers between devices with their start and end apart: 40, of which 17 were waited for; matrix products, arithmetic and copies ran while one was open for 11% of the time, Pallas kernels for 7%

profile of v11, /device:TPU:1, one launch (start us, length us, event | category | flops | bytes accessed | tf_op | source)
XLA Modules:
  0.0 168.2 jit_solution(322178235108686367)
XLA Ops:
  0.7 2.3 %arrange.3 = bf16[16,192,128]{2,1,0:T(8,128)(2,1)} custom-call(bf16[3,128,2048]{2,1,0:T(8,128)(2,1)} %slabs.3), custom_call_target="tpu_custom_call" | custom-call | bytes 1600000 | tf_op jit(solution)/shard_map/arrange/pallas_call | solution.py:36
  3.0 6.5 %collective-permute-start = (bf16[16,192,128]{2,1,0:T(8,128)(2,1)}, bf16[16,192,128]{2,1,0:T(8,128)(2,1)}, u32[]{:S(2)}, u32[]{:S(2)}) collective-permute-start(bf16[16,192,128]{2,1,0:T(8,128)(2,1)} %arrange.3), channel_id=1, source_target_pairs={{0,129},{1,128},{2,131},{3,130},{4,133},{5,132},{6,135},{7,134},{8... | collective-permute-start | bytes 2359304 | tf_op jit(solution)/shard_map/ppermute | solution.py:345
  10.4 2.4 %fusion = f32[128,1024]{1,0:T(8,128)S(1)} fusion(bf16[1,1024,1024]{2,1,0:T(8,128)(2,1)} %param.16, bf16[1,128,1024]{2,1,0:T(8,128)(2,1)S(1)} %copy-done.16), kind=kOutput, calls=%fused_computation.1 | convolution fusion | flops 268435456 | bytes 2883584 | tf_op jit(solution)/shard_map/dot_general | solution.py:333
  12.9 2.6 %fusion.11 = (f32[128]{0:T(128)S(1)}, f32[128]{0:T(128)S(1)}, f32[128,1024]{1,0:T(8,128)}) fusion(bf16[3,128,1024]{2,1,0:T(8,128)(2,1)} %hidden.1, f32[1024]{0:T(1024)S(1)} %bitcast.90, f32[128,1024]{1,0:T(8,128)S(1)} %fusion, bf16[1,1024,1024]{2,1,0:T(8,128)(2,1)S(1)} %copy-done.10, bf16[1,128,1024]{2,1,0:T(8,128)(2,1)S(1)} %copy-done), kind=kOutput, calls=%fused_computation.15 | convolution fusion | flops 269352704 | bytes 3675136 | tf_op jit(solution)/shard_map/dot_general | solution.py:330
  18.0 2.8 %collective-permute-start.3 = (f32[2,128]{1,0:T(2,128)S(1)}, f32[2,128]{1,0:T(2,128)S(1)}, u32[]{:S(2)}, u32[]{:S(2)}) collective-permute-start(f32[2,128]{1,0:T(2,128)S(1)} %fusion.30), channel_id=1, source_target_pairs={{0,4},{2,6},{4,0},{6,2},{1,5},{3,7},{5,1},{7,3},{8,12},{10,14},{12... | collective-permute-start | bytes 3080 | tf_op jit(solution)/shard_map/ppermute | solution.py:343
  22.2 2.2 %arrange.2 = bf16[16,192,128]{2,1,0:T(8,128)(2,1)} custom-call(bf16[3,128,2048]{2,1,0:T(8,128)(2,1)} %slabs.3), custom_call_target="tpu_custom_call" | custom-call | bytes 1600000 | tf_op jit(solution)/shard_map/arrange/pallas_call | solution.py:36
  27.2 11.5 %all-to-all-start = ((bf16[16,192,128]{2,1,0:T(8,128)(2,1)}), bf16[16,192,128]{2,1,0:T(8,128)(2,1)}, u32[]{:S(2)}, u32[]{:S(2)}) async-start(bf16[16,192,128]{2,1,0:T(8,128)(2,1)} %broadcast_select_fusion), calls=%async_computation | async-start | bytes 1572864 | tf_op jit(solution)/shard_map/all_to_all | solution.py:350
  39.9 2.3 %collective-permute-start.6 = (bf16[8,32,1024]{2,1,0:T(8,128)(2,1)}, bf16[8,32,1024]{2,1,0:T(8,128)(2,1)}, u32[]{:S(2)}, u32[]{:S(2)}) collective-permute-start(bf16[8,32,1024]{2,1,0:T(8,128)(2,1)} %get-tuple-element.70), channel_id=1, source_target_pairs={{0,129},{1,0},{128,1},{129,128},{2,131},{3,2},{130,3},{131,130},{4... | collective-permute-start | bytes 1572872 | tf_op jit(solution)/shard_map/ppermute | solution.py:349
  42.5 11.7 %collective-permute-done.5 = bf16[8,32,1024]{2,1,0:T(8,128)(2,1)} collective-permute-done((bf16[8,32,1024]{2,1,0:T(8,128)(2,1)S(1)}, bf16[8,32,1024]{2,1,0:T(8,128)(2,1)}, u32[]{:S(2)}, u32[]{:S(2)}) %collective-permute-start.5) | collective-permute-done | bytes 524320 | tf_op jit(solution)/shard_map/ppermute | solution.py:348
  54.2 2.7 %collective-permute-start.8 = (bf16[8,32,1024]{2,1,0:T(8,128)(2,1)}, bf16[8,32,1024]{2,1,0:T(8,128)(2,1)}, u32[]{:S(2)}, u32[]{:S(2)}) collective-permute-start(bf16[8,32,1024]{2,1,0:T(8,128)(2,1)} %collective-permute-done.6), channel_id=1, source_target_pairs={{0,129},{1,0},{128,1},{129,128},{2,131},{3,2},{130,3},{131,130},{4... | collective-permute-start | bytes 1572872 | tf_op jit(solution)/shard_map/ppermute | solution.py:352
  58.8 2.6 %all-to-all-done = bf16[16,192,128]{2,1,0:T(8,128)(2,1)} async-done(((bf16[16,192,128]{2,1,0:T(8,128)(2,1)}), bf16[16,192,128]{2,1,0:T(8,128)(2,1)}, u32[]{:S(2)}, u32[]{:S(2)}) %all-to-all-start) | async-done | bytes 786464 | tf_op jit(solution)/shard_map/all_to_all | solution.py:350
  61.4 2.3 %pick_layers.1 = (bf16[32,2,32,128]{3,2,1,0:T(8,128)(2,1)}, bf16[16,2,32,128]{3,2,1,0:T(8,128)(2,1)}, bf16[16,2,32,128]{3,2,1,0:T(8,128)(2,1)}) custom-call(s32[32]{0:T(128)} %layer_map.1, bf16[48,2,32,128]{3,2,1,0:T(8,128)(2,1)} %bitcast.26.received), custom_call_target="tpu_custom_call" | custom-call | bytes 1300000 | tf_op jit(solution)/shard_map/pick_layers/pallas_call | solution.py:65
  64.9 3.2 %collective-permute-done.7.refs_8_ = bf16[8,32,1024]{2,1,0:T(8,128)(2,1)S(1)} collective-permute-done((bf16[8,32,1024]{2,1,0:T(8,128)(2,1)}, bf16[8,32,1024]{2,1,0:T(8,128)(2,1)S(1)}, u32[]{:S(2)}, u32[]{:S(2)}) %collective-permute-start.7) | collective-permute-done | bytes 524320 | tf_op jit(solution)/shard_map/ppermute | solution.py:352
  74.0 2.7 %collective-permute-start.14 = (bf16[8,32,1024]{2,1,0:T(8,128)(2,1)S(1)}, bf16[8,32,1024]{2,1,0:T(8,128)(2,1)S(1)}, u32[]{:S(2)}, u32[]{:S(2)}) collective-permute-start(bf16[8,32,1024]{2,1,0:T(8,128)(2,1)S(1)} %collective-permute-done.7.refs_8_), channel_id=1, source_target_pairs={{0,8},{8,0},{1,9},{9,1},{2,10},{10,2},{3,11},{11,3},{4,12},{12,4},... | collective-permute-start | bytes 1572872 | tf_op jit(solution)/shard_map/ppermute | solution.py:356
  76.9 4.7 %collective-permute-done.9.refs_1_ = bf16[16,2,32,128]{3,2,1,0:T(8,128)(2,1)} collective-permute-done((bf16[16,2,32,128]{3,2,1,0:T(8,128)(2,1)}, bf16[16,2,32,128]{3,2,1,0:T(8,128)(2,1)}, u32[]{:S(2)}, u32[]{:S(2)}) %collective-permute-start.9) | collective-permute-done | bytes 262176 | tf_op jit(solution)/shard_map/ppermute | solution.py:285
  81.6 3.1 %collective-permute-start.15 = (bf16[8,32,1024]{2,1,0:T(8,128)(2,1)}, bf16[8,32,1024]{2,1,0:T(8,128)(2,1)S(1)}, u32[]{:S(2)}, u32[]{:S(2)}) collective-permute-start(bf16[8,32,1024]{2,1,0:T(8,128)(2,1)} %collective-permute-done.8.refs_9_), channel_id=1, source_target_pairs={{0,8},{8,0},{1,9},{9,1},{2,10},{10,2},{3,11},{11,3},{4,12},{12,4},... | collective-permute-start | bytes 1572872 | tf_op jit(solution)/shard_map/ppermute | solution.py:356
  84.7 2.7 %collective-permute-start.17 = (bf16[16,2,32,128]{3,2,1,0:T(8,128)(2,1)}, bf16[16,2,32,128]{3,2,1,0:T(8,128)(2,1)S(1)}, u32[]{:S(2)}, u32[]{:S(2)}) collective-permute-start(bf16[16,2,32,128]{3,2,1,0:T(8,128)(2,1)} %collective-permute-done.10.refs_2_), channel_id=1, source_target_pairs={{0,6},{2,0},{4,2},{6,4},{1,7},{3,1},{5,3},{7,5},{8,14},{10,8},{12,... | collective-permute-start | bytes 786440 | tf_op jit(solution)/shard_map/ppermute | solution.py:287
  88.8 2.2 %fusion.19 = (f32[1024]{0:T(1024)S(1)}, f32[128,1024]{1,0:T(8,128)}) fusion(f32[128,1024]{1,0:T(8,128)} %get-tuple-element.72, f32[128]{0:T(128)S(1)} %get-tuple-element.67, bf16[3,128,1024]{2,1,0:T(8,128)(2,1)} %hidden.1, f32[128]{0:T(128)S(1)} %slice_bitcast_fusion, f32[128]{0:T(128)S(1)} %get-tuple-element.66, f32[1024]{0:T(1024)S(1)} %bitcast.91, pred[]{:T(512)S(6)} %eq.28), kind=kLoop, calls=%fused_computation.23 | loop fusion | flops 1440768 | bytes 1320449 | tf_op jit(solution)/shard_map/reduce_sum | solution.py:367
  91.0 2.4 %collective-permute-done.17.refs_1_ = bf16[16,2,32,128]{3,2,1,0:T(8,128)(2,1)S(1)} collective-permute-done((bf16[16,2,32,128]{3,2,1,0:T(8,128)(2,1)}, bf16[16,2,32,128]{3,2,1,0:T(8,128)(2,1)S(1)}, u32[]{:S(2)}, u32[]{:S(2)}) %collective-permute-start.17) | collective-permute-done | bytes 262176 | tf_op jit(solution)/shard_map/ppermute | solution.py:287
  96.7 6.9 %project_first.1.partial = bf16[4,256,1024]{2,1,0:T(8,128)(2,1)S(1)} custom-call(s32[4]{0:T(128)S(1)} %get-tuple-element.73.place, s32[4]{0:T(128)S(1)} %get-tuple-element.74.blocks, bf16[32,2,32,128]{3,2,1,0:T(8,128)(2,1)S(1)} %copy-done.7, bf16[16,2,32,128]{3,2,1,0:T(8,128)(2,1)} %collective-permute-done.9.refs_1_, ...), custom_call_target="tpu_custom_call" | custom-call | flops 2147483648 | bytes 8388608 | tf_op jit(solution)/shard_map/project_first/pallas_call | solution.py:179
  106.4 8.8 %project_rest.1 = (bf16[3,32,1024]{2,1,0:T(8,128)(2,1)}, bf16[3,32,1024]{2,1,0:T(8,128)(2,1)}, bf16[3,32,1024]{2,1,0:T(8,128)(2,1)}, bf16[3,32,1024]{2,1,0:T(8,1...) custom-call(s32[4]{0:T(128)} %copy-done.8, ...), custom_call_target="tpu_custom_call" | custom-call | flops 2147483648 | bytes 11534336 | tf_op jit(solution)/shard_map/project_rest/pallas_call | solution.py:205
  120.3 2.7 %collective-permute-start.25 = (bf16[3,32,1024]{2,1,0:T(8,128)(2,1)S(1)}, bf16[3,32,1024]{2,1,0:T(8,128)(2,1)S(1)}, u32[]{:S(2)}, u32[]{:S(2)}) collective-permute-start(bf16[3,32,1024]{2,1,0:T(8,128)(2,1)S(1)} %copy-done.35), channel_id=1, source_target_pairs={{0,112},{16,0},{32,16},{48,32},{64,48},{80,64},{96,80},{112,96},{1... | collective-permute-start | bytes 589832 | tf_op jit(solution)/shard_map/ppermute | solution.py:237
  123.4 2.7 %collective-permute-start.35 = (bf16[3,32,1024]{2,1,0:T(8,128)(2,1)S(1)}, bf16[3,32,1024]{2,1,0:T(8,128)(2,1)S(1)}, u32[]{:S(2)}, u32[]{:S(2)}) collective-permute-start(bf16[3,32,1024]{2,1,0:T(8,128)(2,1)S(1)} %add_convert_fusion.2), channel_id=1, source_target_pairs={{0,112},{16,0},{32,16},{48,32},{64,48},{80,64},{96,80},{112,96},{1... | collective-permute-start | bytes 589832 | tf_op jit(solution)/shard_map/ppermute | solution.py:243
  127.6 3.5 %collective-permute-start.26 = (bf16[3,32,1024]{2,1,0:T(8,128)(2,1)S(1)}, bf16[3,32,1024]{2,1,0:T(8,128)(2,1)S(1)}, u32[]{:S(2)}, u32[]{:S(2)}) collective-permute-start(bf16[3,32,1024]{2,1,0:T(8,128)(2,1)S(1)} %add_convert_fusion.9), channel_id=1, source_target_pairs={{0,112},{16,0},{32,16},{48,32},{64,48},{80,64},{96,80},{112,96},{1... | collective-permute-start | bytes 589832 | tf_op jit(solution)/shard_map/ppermute | solution.py:244
  131.9 3.5 %collective-permute-start.36 = (bf16[3,32,1024]{2,1,0:T(8,128)(2,1)S(1)}, bf16[3,32,1024]{2,1,0:T(8,128)(2,1)S(1)}, u32[]{:S(2)}, u32[]{:S(2)}) collective-permute-start(bf16[3,32,1024]{2,1,0:T(8,128)(2,1)S(1)} %add_convert_fusion.1), channel_id=1, source_target_pairs={{0,112},{16,0},{32,16},{48,32},{64,48},{80,64},{96,80},{112,96},{1... | collective-permute-start | bytes 589832 | tf_op jit(solution)/shard_map/ppermute | solution.py:243
  135.6 3.2 %collective-permute-start.27 = (bf16[3,32,1024]{2,1,0:T(8,128)(2,1)S(1)}, bf16[3,32,1024]{2,1,0:T(8,128)(2,1)S(1)}, u32[]{:S(2)}, u32[]{:S(2)}) collective-permute-start(bf16[3,32,1024]{2,1,0:T(8,128)(2,1)S(1)} %add_convert_fusion.8), channel_id=1, source_target_pairs={{0,112},{16,0},{32,16},{48,32},{64,48},{80,64},{96,80},{112,96},{1... | collective-permute-start | bytes 589832 | tf_op jit(solution)/shard_map/ppermute | solution.py:244
  138.9 4.7 %collective-permute-done.27 = bf16[3,32,1024]{2,1,0:T(8,128)(2,1)S(1)} collective-permute-done((bf16[3,32,1024]{2,1,0:T(8,128)(2,1)S(1)}, bf16[3,32,1024]{2,1,0:T(8,128)(2,1)S(1)}, u32[]{:S(2)}, u32[]{:S(2)}) %collective-permute-start.27) | collective-permute-done | bytes 196640 | tf_op jit(solution)/shard_map/ppermute | solution.py:244
  143.7 3.4 %collective-permute-start.28 = (bf16[3,32,1024]{2,1,0:T(8,128)(2,1)S(1)}, bf16[3,32,1024]{2,1,0:T(8,128)(2,1)S(1)}, u32[]{:S(2)}, u32[]{:S(2)}) collective-permute-start(bf16[3,32,1024]{2,1,0:T(8,128)(2,1)S(1)} %add_convert_fusion.7), channel_id=1, source_target_pairs={{0,112},{16,0},{32,16},{48,32},{64,48},{80,64},{96,80},{112,96},{1... | collective-permute-start | bytes 589832 | tf_op jit(solution)/shard_map/ppermute | solution.py:244
  147.2 5.8 %collective-permute-start.37 = (bf16[3,32,1024]{2,1,0:T(8,128)(2,1)S(1)}, bf16[3,32,1024]{2,1,0:T(8,128)(2,1)S(1)}, u32[]{:S(2)}, u32[]{:S(2)}) collective-permute-start(bf16[3,32,1024]{2,1,0:T(8,128)(2,1)S(1)} %add_convert_fusion), channel_id=1, source_target_pairs={{0,8},{8,0},{1,9},{9,1},{2,10},{10,2},{3,11},{11,3},{4,12},{12,4},... | collective-permute-start | bytes 589832 | tf_op jit(solution)/shard_map/ppermute | solution.py:385
  153.0 3.6 %collective-permute-start.38 = (bf16[3,32,1024]{2,1,0:T(8,128)(2,1)S(1)}, bf16[3,32,1024]{2,1,0:T(8,128)(2,1)S(1)}, u32[]{:S(2)}, u32[]{:S(2)}) collective-permute-start(bf16[3,32,1024]{2,1,0:T(8,128)(2,1)S(1)} %add_convert_fusion), channel_id=1, source_target_pairs={{0,136},{8,128},{1,137},{9,129},{2,138},{10,130},{3,139},{11,131},... | collective-permute-start | bytes 589832 | tf_op jit(solution)/shard_map/ppermute | solution.py:387
  160.7 4.2 %collective-permute-done.29.teacher = bf16[3,32,1024]{2,1,0:T(8,128)(2,1)S(1)} collective-permute-done((bf16[3,32,1024]{2,1,0:T(8,128)(2,1)S(1)}, bf16[3,32,1024]{2,1,0:T(8,128)(2,1)S(1)}, u32[]{:S(2)}, u32[]{:S(2)}) %collective-permute-start.29) | collective-permute-done | bytes 196640 | tf_op jit(solution)/shard_map/ppermute | solution.py:386
  165.6 2.7 %finish.1 = bf16[3,128,1024]{2,1,0:T(8,128)(2,1)} custom-call(s32[2]{0:T(128)} %pad_add_fusion.state, bf16[3,128,1024]{2,1,0:T(8,128)(2,1)} %hidden.1, f32[128,1024]{1,0:T(8,128)} %get-tuple-element.69.layer_grad, bf16[3,32,1024]{2,1,0:T(8,128)(2,1)} %copy-done.11, bf16[3,32,1024]{2,1,0:T(8,128)(2,1)} %copy-done.20, bf16[3,32,1024]{2,1,0:T(8,128)(2,1)} %copy-done.18, ...), custom_call_target="tpu_custom_call" | custom-call | flops 786432 | bytes 3145728 | tf_op jit(solution)/shard_map/finish/pallas_call | solution.py:266
  (174 shorter events, 38.0 us)
Async XLA Ops:
  3.0 22.1 %collective-permute-start = (bf16[16,192,128]{2,1,0:T(8,128)(2,1)}, bf16[16,192,128]{2,1,0:T(8,128)(2,1)}, u32[]{:S(2)}, u32[]{:S(2)}) collective-permute-start(bf16[16,192,128]{2,1,0:T(8,128)(2,1)} %arrange.3), channel_id=1, source_target_pairs={{0,129},{1,128},{2,131},{3,130},{4,133},{5,132},{6,135},{7,134},{8... | collective-permute-start | bytes 2359304 | tf_op jit(solution)/shard_map/ppermute | solution.py:345
  9.5 17.7 %collective-permute-start.1 = (bf16[8,64,1024]{2,1,0:T(8,128)(2,1)S(1)}, bf16[8,64,1024]{2,1,0:T(8,128)(2,1)S(1)}, u32[]{:S(2)}, u32[]{:S(2)}) collective-permute-start(bf16[8,64,1024]{2,1,0:T(8,128)(2,1)S(1)} %copy-done.1), channel_id=1, source_target_pairs={{0,8},{8,0},{1,9},{9,1},{2,10},{10,2},{3,11},{11,3},{4,12},{12,4},... | collective-permute-start | bytes 3145736 | tf_op jit(solution)/shard_map/ppermute | solution.py:323
  27.2 34.2 %all-to-all-start = ((bf16[16,192,128]{2,1,0:T(8,128)(2,1)}), bf16[16,192,128]{2,1,0:T(8,128)(2,1)}, u32[]{:S(2)}, u32[]{:S(2)}) async-start(bf16[16,192,128]{2,1,0:T(8,128)(2,1)} %broadcast_select_fusion), calls=%async_computation | async-start | bytes 1572864 | tf_op jit(solution)/shard_map/all_to_all | solution.py:350
  39.5 14.7 %collective-permute-start.5 = (bf16[8,32,1024]{2,1,0:T(8,128)(2,1)S(1)}, bf16[8,32,1024]{2,1,0:T(8,128)(2,1)}, u32[]{:S(2)}, u32[]{:S(2)}) collective-permute-start(bf16[8,32,1024]{2,1,0:T(8,128)(2,1)S(1)} %get-tuple-element.71), channel_id=1, source_target_pairs={{0,1},{1,128},{128,129},{129,0},{2,3},{3,130},{130,131},{131,2},{4... | collective-permute-start | bytes 1572872 | tf_op jit(solution)/shard_map/ppermute | solution.py:348
  39.9 14.4 %collective-permute-start.6 = (bf16[8,32,1024]{2,1,0:T(8,128)(2,1)}, bf16[8,32,1024]{2,1,0:T(8,128)(2,1)}, u32[]{:S(2)}, u32[]{:S(2)}) collective-permute-start(bf16[8,32,1024]{2,1,0:T(8,128)(2,1)} %get-tuple-element.70), channel_id=1, source_target_pairs={{0,129},{1,0},{128,1},{129,128},{2,131},{3,2},{130,3},{131,130},{4... | collective-permute-start | bytes 1572872 | tf_op jit(solution)/shard_map/ppermute | solution.py:349
  54.2 13.9 %collective-permute-start.7 = (bf16[8,32,1024]{2,1,0:T(8,128)(2,1)}, bf16[8,32,1024]{2,1,0:T(8,128)(2,1)S(1)}, u32[]{:S(2)}, u32[]{:S(2)}) collective-permute-start(bf16[8,32,1024]{2,1,0:T(8,128)(2,1)} %collective-permute-done.5), channel_id=1, source_target_pairs={{0,1},{1,128},{128,129},{129,0},{2,3},{3,130},{130,131},{131,2},{4... | collective-permute-start | bytes 1572872 | tf_op jit(solution)/shard_map/ppermute | solution.py:352
  54.2 13.9 %collective-permute-start.8 = (bf16[8,32,1024]{2,1,0:T(8,128)(2,1)}, bf16[8,32,1024]{2,1,0:T(8,128)(2,1)}, u32[]{:S(2)}, u32[]{:S(2)}) collective-permute-start(bf16[8,32,1024]{2,1,0:T(8,128)(2,1)} %collective-permute-done.6), channel_id=1, source_target_pairs={{0,129},{1,0},{128,1},{129,128},{2,131},{3,2},{130,3},{131,130},{4... | collective-permute-start | bytes 1572872 | tf_op jit(solution)/shard_map/ppermute | solution.py:352
  63.7 10.3 %collective-permute-start.11 = (bf16[16,2,32,128]{3,2,1,0:T(8,128)(2,1)}, bf16[16,2,32,128]{3,2,1,0:T(8,128)(2,1)S(1)}, u32[]{:S(2)}, u32[]{:S(2)}) collective-permute-start(bf16[16,2,32,128]{3,2,1,0:T(8,128)(2,1)} %get-tuple-element.41), channel_id=1, source_target_pairs={{0,2},{2,4},{4,6},{6,0},{1,3},{3,5},{5,7},{7,1},{8,10},{10,12},{12... | collective-permute-start | bytes 786440 | tf_op jit(solution)/shard_map/ppermute | solution.py:280
  68.1 8.8 %collective-permute-start.12 = (bf16[16,2,32,128]{3,2,1,0:T(8,128)(2,1)}, bf16[16,2,32,128]{3,2,1,0:T(8,128)(2,1)}, u32[]{:S(2)}, u32[]{:S(2)}) collective-permute-start(bf16[16,2,32,128]{3,2,1,0:T(8,128)(2,1)} %get-tuple-element.42), channel_id=1, source_target_pairs={{0,2},{2,4},{4,6},{6,0},{1,3},{3,5},{5,7},{7,1},{8,10},{10,12},{12... | collective-permute-start | bytes 786440 | tf_op jit(solution)/shard_map/ppermute | solution.py:284
  70.0 14.7 %collective-permute-start.10 = (bf16[16,2,32,128]{3,2,1,0:T(8,128)(2,1)}, bf16[16,2,32,128]{3,2,1,0:T(8,128)(2,1)}, u32[]{:S(2)}, u32[]{:S(2)}) collective-permute-start(bf16[16,2,32,128]{3,2,1,0:T(8,128)(2,1)} %get-tuple-element.42), channel_id=1, source_target_pairs={{0,6},{2,0},{4,2},{6,4},{1,7},{3,1},{5,3},{7,5},{8,14},{10,8},{12,... | collective-permute-start | bytes 786440 | tf_op jit(solution)/shard_map/ppermute | solution.py:281
  71.5 10.1 %collective-permute-start.9 = (bf16[16,2,32,128]{3,2,1,0:T(8,128)(2,1)}, bf16[16,2,32,128]{3,2,1,0:T(8,128)(2,1)}, u32[]{:S(2)}, u32[]{:S(2)}) collective-permute-start(bf16[16,2,32,128]{3,2,1,0:T(8,128)(2,1)} %get-tuple-element.41), channel_id=1, source_target_pairs={{0,6},{2,0},{4,2},{6,4},{1,7},{3,1},{5,3},{7,5},{8,14},{10,8},{12,... | collective-permute-start | bytes 786440 | tf_op jit(solution)/shard_map/ppermute | solution.py:285
  72.8 14.6 %collective-permute-start.13 = (bf16[32,2,32,128]{3,2,1,0:T(8,128)(2,1)}, bf16[32,2,32,128]{3,2,1,0:T(8,128)(2,1)}, u32[]{:S(2)}, u32[]{:S(2)}) collective-permute-start(bf16[32,2,32,128]{3,2,1,0:T(8,128)(2,1)} %get-tuple-element.38.refs_0_), channel_id=1, source_target_pairs={{0,1},{1,0},{2,3},{3,2},{4,5},{5,4},{6,7},{7,6},{8,9},{9,8},{10,11... | collective-permute-start | bytes 1572872 | tf_op jit(solution)/shard_map/ppermute | solution.py:282
  74.0 19.4 %collective-permute-start.14 = (bf16[8,32,1024]{2,1,0:T(8,128)(2,1)S(1)}, bf16[8,32,1024]{2,1,0:T(8,128)(2,1)S(1)}, u32[]{:S(2)}, u32[]{:S(2)}) collective-permute-start(bf16[8,32,1024]{2,1,0:T(8,128)(2,1)S(1)} %collective-permute-done.7.refs_8_), channel_id=1, source_target_pairs={{0,8},{8,0},{1,9},{9,1},{2,10},{10,2},{3,11},{11,3},{4,12},{12,4},... | collective-permute-start | bytes 1572872 | tf_op jit(solution)/shard_map/ppermute | solution.py:356
  76.9 10.6 %collective-permute-start.16 = (bf16[16,2,32,128]{3,2,1,0:T(8,128)(2,1)S(1)}, bf16[16,2,32,128]{3,2,1,0:T(8,128)(2,1)S(1)}, u32[]{:S(2)}, u32[]{:S(2)}) collective-permute-start(bf16[16,2,32,128]{3,2,1,0:T(8,128)(2,1)S(1)} %collective-permute-done.11.refs_3_), channel_id=1, source_target_pairs={{0,2},{2,4},{4,6},{6,0},{1,3},{3,5},{5,7},{7,1},{8,10},{10,12},{12... | collective-permute-start | bytes 786440 | tf_op jit(solution)/shard_map/ppermute | solution.py:286
  81.6 13.9 %collective-permute-start.15 = (bf16[8,32,1024]{2,1,0:T(8,128)(2,1)}, bf16[8,32,1024]{2,1,0:T(8,128)(2,1)S(1)}, u32[]{:S(2)}, u32[]{:S(2)}) collective-permute-start(bf16[8,32,1024]{2,1,0:T(8,128)(2,1)} %collective-permute-done.8.refs_9_), channel_id=1, source_target_pairs={{0,8},{8,0},{1,9},{9,1},{2,10},{10,2},{3,11},{11,3},{4,12},{12,4},... | collective-permute-start | bytes 1572872 | tf_op jit(solution)/shard_map/ppermute | solution.py:356
  84.7 8.7 %collective-permute-start.17 = (bf16[16,2,32,128]{3,2,1,0:T(8,128)(2,1)}, bf16[16,2,32,128]{3,2,1,0:T(8,128)(2,1)S(1)}, u32[]{:S(2)}, u32[]{:S(2)}) collective-permute-start(bf16[16,2,32,128]{3,2,1,0:T(8,128)(2,1)} %collective-permute-done.10.refs_2_), channel_id=1, source_target_pairs={{0,6},{2,0},{4,2},{6,4},{1,7},{3,1},{5,3},{7,5},{8,14},{10,8},{12,... | collective-permute-start | bytes 786440 | tf_op jit(solution)/shard_map/ppermute | solution.py:287
  87.4 18.3 %collective-permute-start.18 = (bf16[32,2,32,128]{3,2,1,0:T(8,128)(2,1)}, bf16[32,2,32,128]{3,2,1,0:T(8,128)(2,1)}, u32[]{:S(2)}, u32[]{:S(2)}) collective-permute-start(bf16[32,2,32,128]{3,2,1,0:T(8,128)(2,1)} %collective-permute-done.13.refs_5_), channel_id=1, source_target_pairs={{0,6},{2,0},{4,2},{6,4},{1,7},{3,1},{5,3},{7,5},{8,14},{10,8},{12,... | collective-permute-start | bytes 1572872 | tf_op jit(solution)/shard_map/ppermute | solution.py:289
  87.5 18.9 %collective-permute-start.21 = (bf16[32,2,32,128]{3,2,1,0:T(8,128)(2,1)}, bf16[32,2,32,128]{3,2,1,0:T(8,128)(2,1)}, u32[]{:S(2)}, u32[]{:S(2)}) collective-permute-start(bf16[32,2,32,128]{3,2,1,0:T(8,128)(2,1)} %collective-permute-done.13.refs_5_), channel_id=1, source_target_pairs={{0,2},{2,4},{4,6},{6,0},{1,3},{3,5},{5,7},{7,1},{8,10},{10,12},{12... | collective-permute-start | bytes 1572872 | tf_op jit(solution)/shard_map/ppermute | solution.py:288
  93.4 11.6 %collective-permute-start.19 = (bf16[16,2,32,128]{3,2,1,0:T(8,128)(2,1)S(1)}, bf16[16,2,32,128]{3,2,1,0:T(8,128)(2,1)S(1)}, u32[]{:S(2)}, u32[]{:S(2)}) collective-permute-start(bf16[16,2,32,128]{3,2,1,0:T(8,128)(2,1)S(1)} %collective-permute-done.16.refs_0_), channel_id=1, source_target_pairs={{0,1},{1,0},{2,3},{3,2},{4,5},{5,4},{6,7},{7,6},{8,9},{9,8},{10,11... | collective-permute-start | bytes 786440 | tf_op jit(solution)/shard_map/ppermute | solution.py:290
  93.4 12.2 %collective-permute-start.20 = (bf16[16,2,32,128]{3,2,1,0:T(8,128)(2,1)S(1)}, bf16[16,2,32,128]{3,2,1,0:T(8,128)(2,1)S(1)}, u32[]{:S(2)}, u32[]{:S(2)}) collective-permute-start(bf16[16,2,32,128]{3,2,1,0:T(8,128)(2,1)S(1)} %collective-permute-done.17.refs_1_), channel_id=1, source_target_pairs={{0,1},{1,0},{2,3},{3,2},{4,5},{5,4},{6,7},{7,6},{8,9},{9,8},{10,11... | collective-permute-start | bytes 786440 | tf_op jit(solution)/shard_map/ppermute | solution.py:291
  123.0 8.1 %collective-permute-start.31 = (bf16[3,32,1024]{2,1,0:T(8,128)(2,1)S(1)}, bf16[3,32,1024]{2,1,0:T(8,128)(2,1)S(1)}, u32[]{:S(2)}, u32[]{:S(2)}) collective-permute-start(bf16[3,32,1024]{2,1,0:T(8,128)(2,1)S(1)} %add_convert_fusion.5), channel_id=1, source_target_pairs={{0,16},{16,32},{32,48},{48,64},{64,80},{80,96},{96,112},{112,0},{1... | collective-permute-start | bytes 589832 | tf_op jit(solution)/shard_map/ppermute | solution.py:241
  123.4 8.4 %collective-permute-start.35 = (bf16[3,32,1024]{2,1,0:T(8,128)(2,1)S(1)}, bf16[3,32,1024]{2,1,0:T(8,128)(2,1)S(1)}, u32[]{:S(2)}, u32[]{:S(2)}) collective-permute-start(bf16[3,32,1024]{2,1,0:T(8,128)(2,1)S(1)} %add_convert_fusion.2), channel_id=1, source_target_pairs={{0,112},{16,0},{32,16},{48,32},{64,48},{80,64},{96,80},{112,96},{1... | collective-permute-start | bytes 589832 | tf_op jit(solution)/shard_map/ppermute | solution.py:243
  126.2 9.1 %collective-permute-start.23 = (bf16[3,32,1024]{2,1,0:T(8,128)(2,1)S(1)}, bf16[3,32,1024]{2,1,0:T(8,128)(2,1)S(1)}, u32[]{:S(2)}, u32[]{:S(2)}) collective-permute-start(bf16[3,32,1024]{2,1,0:T(8,128)(2,1)S(1)} %add_convert_fusion.11), channel_id=1, source_target_pairs={{0,16},{16,32},{32,48},{48,64},{64,80},{80,96},{96,112},{112,0},{1... | collective-permute-start | bytes 589832 | tf_op jit(solution)/shard_map/ppermute | solution.py:246
  127.6 7.9 %collective-permute-start.26 = (bf16[3,32,1024]{2,1,0:T(8,128)(2,1)S(1)}, bf16[3,32,1024]{2,1,0:T(8,128)(2,1)S(1)}, u32[]{:S(2)}, u32[]{:S(2)}) collective-permute-start(bf16[3,32,1024]{2,1,0:T(8,128)(2,1)S(1)} %add_convert_fusion.9), channel_id=1, source_target_pairs={{0,112},{16,0},{32,16},{48,32},{64,48},{80,64},{96,80},{112,96},{1... | collective-permute-start | bytes 589832 | tf_op jit(solution)/shard_map/ppermute | solution.py:244
  131.9 15.3 %collective-permute-start.36 = (bf16[3,32,1024]{2,1,0:T(8,128)(2,1)S(1)}, bf16[3,32,1024]{2,1,0:T(8,128)(2,1)S(1)}, u32[]{:S(2)}, u32[]{:S(2)}) collective-permute-start(bf16[3,32,1024]{2,1,0:T(8,128)(2,1)S(1)} %add_convert_fusion.1), channel_id=1, source_target_pairs={{0,112},{16,0},{32,16},{48,32},{64,48},{80,64},{96,80},{112,96},{1... | collective-permute-start | bytes 589832 | tf_op jit(solution)/shard_map/ppermute | solution.py:243
  135.4 21.2 %collective-permute-start.24 = (bf16[3,32,1024]{2,1,0:T(8,128)(2,1)S(1)}, bf16[3,32,1024]{2,1,0:T(8,128)(2,1)S(1)}, u32[]{:S(2)}, u32[]{:S(2)}) collective-permute-start(bf16[3,32,1024]{2,1,0:T(8,128)(2,1)S(1)} %add_convert_fusion.10), channel_id=1, source_target_pairs={{0,16},{16,32},{32,48},{48,64},{64,80},{80,96},{96,112},{112,0},{1... | collective-permute-start | bytes 589832 | tf_op jit(solution)/shard_map/ppermute | solution.py:246
  135.6 8.1 %collective-permute-start.27 = (bf16[3,32,1024]{2,1,0:T(8,128)(2,1)S(1)}, bf16[3,32,1024]{2,1,0:T(8,128)(2,1)S(1)}, u32[]{:S(2)}, u32[]{:S(2)}) collective-permute-start(bf16[3,32,1024]{2,1,0:T(8,128)(2,1)S(1)} %add_convert_fusion.8), channel_id=1, source_target_pairs={{0,112},{16,0},{32,16},{48,32},{64,48},{80,64},{96,80},{112,96},{1... | collective-permute-start | bytes 589832 | tf_op jit(solution)/shard_map/ppermute | solution.py:244
  138.9 8.3 %collective-permute-start.33 = (bf16[3,32,1024]{2,1,0:T(8,128)(2,1)S(1)}, bf16[3,32,1024]{2,1,0:T(8,128)(2,1)S(1)}, u32[]{:S(2)}, u32[]{:S(2)}) collective-permute-start(bf16[3,32,1024]{2,1,0:T(8,128)(2,1)S(1)} %add_convert_fusion.3), channel_id=1, source_target_pairs={{0,16},{16,32},{32,48},{48,64},{64,80},{80,96},{96,112},{112,0},{1... | collective-permute-start | bytes 589832 | tf_op jit(solution)/shard_map/ppermute | solution.py:241
  143.7 12.9 %collective-permute-start.28 = (bf16[3,32,1024]{2,1,0:T(8,128)(2,1)S(1)}, bf16[3,32,1024]{2,1,0:T(8,128)(2,1)S(1)}, u32[]{:S(2)}, u32[]{:S(2)}) collective-permute-start(bf16[3,32,1024]{2,1,0:T(8,128)(2,1)S(1)} %add_convert_fusion.7), channel_id=1, source_target_pairs={{0,112},{16,0},{32,16},{48,32},{64,48},{80,64},{96,80},{112,96},{1... | collective-permute-start | bytes 589832 | tf_op jit(solution)/shard_map/ppermute | solution.py:244
  147.2 13.0 %collective-permute-start.37 = (bf16[3,32,1024]{2,1,0:T(8,128)(2,1)S(1)}, bf16[3,32,1024]{2,1,0:T(8,128)(2,1)S(1)}, u32[]{:S(2)}, u32[]{:S(2)}) collective-permute-start(bf16[3,32,1024]{2,1,0:T(8,128)(2,1)S(1)} %add_convert_fusion), channel_id=1, source_target_pairs={{0,8},{8,0},{1,9},{9,1},{2,10},{10,2},{3,11},{11,3},{4,12},{12,4},... | collective-permute-start | bytes 589832 | tf_op jit(solution)/shard_map/ppermute | solution.py:385
  153.0 7.7 %collective-permute-start.38 = (bf16[3,32,1024]{2,1,0:T(8,128)(2,1)S(1)}, bf16[3,32,1024]{2,1,0:T(8,128)(2,1)S(1)}, u32[]{:S(2)}, u32[]{:S(2)}) collective-permute-start(bf16[3,32,1024]{2,1,0:T(8,128)(2,1)S(1)} %add_convert_fusion), channel_id=1, source_target_pairs={{0,136},{8,128},{1,137},{9,129},{2,138},{10,130},{3,139},{11,131},... | collective-permute-start | bytes 589832 | tf_op jit(solution)/shard_map/ppermute | solution.py:387
  156.7 8.2 %collective-permute-start.29 = (bf16[3,32,1024]{2,1,0:T(8,128)(2,1)S(1)}, bf16[3,32,1024]{2,1,0:T(8,128)(2,1)S(1)}, u32[]{:S(2)}, u32[]{:S(2)}) collective-permute-start(bf16[3,32,1024]{2,1,0:T(8,128)(2,1)S(1)} %add_convert_fusion.6.near), channel_id=1, source_target_pairs={{0,128},{1,129},{2,130},{3,131},{4,132},{5,133},{6,134},{7,135},{8... | collective-permute-start | bytes 589832 | tf_op jit(solution)/shard_map/ppermute | solution.py:386
  (47 other events, 550.1 us)

commit v12 on v8

--- a/solution.py
+++ b/solution.py
@@ -76,8 +76,8 @@
 
 
 DISTANCES = (4, 3, -3, 2, -2, 1, -1, 0)
-FIRST = ((0, 0), (1, 0), (3, 0), (0, 1))
-REST = ((2, 0), (1, 1), (2, 1), (3, 1))
+FIRST = ((0, 0), (1, 0), (3, 0), (0, 1), (2, 0))
+REST = ((1, 1), (2, 1), (3, 1))
 GROUPS = 4
 WEIGHTS = 6
 
@@ -120,25 +120,25 @@
 
 
 def project_first_kernel(place, blocks, *refs):
-    count = len(FIRST) + 2
+    count = len(FIRST) + 3
     features, refs = refs[:count], refs[count:]
     weights, (out, weight, *held, feature_sem, weight_sem) = refs[:WEIGHTS], refs[WEIGHTS:]
     copies = load_weight(place, blocks, weights, weight, weight_sem) + load_features(features, held, feature_sem)
     for copy in copies:
         copy.wait()
-    own, up_a, up_b, down_a, down_b, row = held
+    own, up_a, up_b, down_a, down_b, row, two_a, two_b = held
     group = own.shape[0] // GROUPS
     for number in range(GROUPS):
         first = number * group
         side = number // (GROUPS // 2)
         offset = (number - side * (GROUPS // 2)) * group
-        refs = (own, (up_a, up_b)[side], (down_a, down_b)[side], row)
-        left = left_rows(refs, (first, offset, offset, first), group)
+        refs = (own, (up_a, up_b)[side], (down_a, down_b)[side], row, (two_a, two_b)[side])
+        left = left_rows(refs, (first, offset, offset, first, offset), group)
         out[number] = jnp.dot(left, weight[...], preferred_element_type=jnp.float32).astype(out.dtype)
 
 
 def project_rest_kernel(place, blocks, slot_layer, partial, *refs):
-    count = len(REST) + 2
+    count = len(REST) + 1
     features, refs = refs[:count], refs[count:]
     weights, refs = refs[:WEIGHTS], refs[WEIGHTS:]
     outs, refs = refs[: C * len(DISTANCES)], refs[C * len(DISTANCES) :]
@@ -151,15 +151,15 @@
         copy.start()
     for copy in copies:
         copy.wait()
-    layers, halves, tokens, lanes = features[2].shape
+    layers, halves, tokens, lanes = features[0].shape
     group = layers // GROUPS
-    near_a, near_b, row_1, row_2a, row_2b, row_3 = held
+    row_1, row_2a, row_2b, row_3 = held
     for number in range(GROUPS):
         first = number * group
         side = number // (GROUPS // 2)
         offset = (number - side * (GROUPS // 2)) * group
-        refs = ((near_a, near_b)[side], row_1, (row_2a, row_2b)[side], row_3)
-        left = left_rows(refs, (offset, first, offset, first), group)
+        refs = (row_1, (row_2a, row_2b)[side], row_3)
+        left = left_rows(refs, (first, offset, first), group)
         value = jnp.dot(left, weight[...], preferred_element_type=jnp.float32)
         befores[number].wait()
         value = (value + before[number].astype(jnp.float32)).astype(product.dtype)
@@ -196,7 +196,7 @@
 
 
 def project_rest(place, blocks, slot_layer, partial, features, weights):
-    layers, halves, tokens, lanes = features[2].shape
+    layers, halves, tokens, lanes = features[0].shape
     columns = weights[0].shape[2]
     depth = len(REST) * halves * lanes
     slots = slot_layer.shape[0] // (len(DISTANCES) * C)
@@ -288,7 +288,7 @@
     g1 = lax.ppermute(g0, "x", down)
     g2a = lax.ppermute(f2a, "yl", swap)
     g2b = lax.ppermute(f2b, "yl", swap)
-    return (own, f1a, f1b, f3a, f3b, g0), (f2a, f2b, g1, g2a, g2b, g3)
+    return (own, f1a, f1b, f3a, f3b, g0, f2a, f2b), (g1, g2a, g2b, g3)
 
 
 def body(

time: 165 us -> 165 us (level)
    ppermute x1, starting transfers between devices: 3.43 us -> 1.29 us  [body(): teacher_across = lax.ppermute(given, ('yh', 'c'), [(0, 3), (1, 2)])]
    ppermute x1, starting transfers between devices: 7.04 us -> 9.03 us  [body(): across = lax.ppermute(given, 'c', swap)]
    unnamed x78 -> x74, local copies, waits for them, and re-layouts: 4.74 us -> 4.58 us
  transfers between devices with their start and end apart: 40 -> 40, of which waited for: 17 -> 16; matrix products, arithmetic and copies ran while one was open for 12% -> 12% of each run, Pallas kernels for 7% -> 8%
where the time goes in v12:
time: 165 us; the launch traced here: 162 us
  starting transfers between devices  74.1 us (45%)
  waiting for transfers between devices  37.2 us (23%)
  Pallas kernels  25.2 us (15%)
  matrix products  9.32 us (6%)
  local copies, waits for them, and re-layouts  7.49 us (5%)
  other arithmetic  7.23 us (4%)
  between operations  1.86 us (1%)
    ppermute x1, waiting for transfers between devices, body(): lax.ppermute(weight_rows[:, :half_rows], side, up)  11.6 us
    all_to_all x1, starting transfers between devices, body(): lax.all_to_all(arranged, ('z', 'c'), split_axis=0, concat_axis=0, tiled=T...  11.5 us
    ppermute x3, starting transfers between devices, reduce_z(): kept_down = lax.ppermute(add(kept[-distance], kept_down), 'z', down)  9.12 us
    ppermute x1, starting transfers between devices, body(): across = lax.ppermute(given, 'c', swap)  9.03 us
    pallas_call x1, Pallas kernels, project_first(): pl.pallas_call(project_first_kernel, out_shape=jax.ShapeDtypeStruct(shape...  8.09 us
    pallas_call x1, Pallas kernels, project_rest(): pl.pallas_call(project_rest_kernel, out_shape=[jax.ShapeDtypeStruct(shape...  7.7 us
    ppermute x1, starting transfers between devices, body(): sent = lax.ppermute(arrange(teacher_slabs, 1), side, [(0, 3), (1, 2)])  6.51 us
    ppermute x2, starting transfers between devices, reduce_z(): given_down = lax.ppermute(add(given[-distance], given_down), 'z', down)  6.43 us
  transfers between devices with their start and end apart: 40, of which 16 were waited for; matrix products, arithmetic and copies ran while one was open for 12% of the time, Pallas kernels for 8%

profile of v12, /device:TPU:1, one launch (start us, length us, event | category | flops | bytes accessed | tf_op | source)
XLA Modules:
  0.0 162.4 jit_solution(4901170313911255971)
XLA Ops:
  0.7 2.3 %arrange.3 = bf16[16,192,128]{2,1,0:T(8,128)(2,1)} custom-call(bf16[3,128,2048]{2,1,0:T(8,128)(2,1)} %slabs.3), custom_call_target="tpu_custom_call" | custom-call | bytes 1600000 | tf_op jit(solution)/shard_map/arrange/pallas_call | solution.py:36
  3.0 6.5 %collective-permute-start = (bf16[16,192,128]{2,1,0:T(8,128)(2,1)}, bf16[16,192,128]{2,1,0:T(8,128)(2,1)}, u32[]{:S(2)}, u32[]{:S(2)}) collective-permute-start(bf16[16,192,128]{2,1,0:T(8,128)(2,1)} %arrange.3), channel_id=1, source_target_pairs={{0,129},{1,128},{2,131},{3,130},{4,133},{5,132},{6,135},{7,134},{8... | collective-permute-start | bytes 2359304 | tf_op jit(solution)/shard_map/ppermute | solution.py:343
  10.4 2.4 %fusion = f32[128,1024]{1,0:T(8,128)S(1)} fusion(bf16[1,1024,1024]{2,1,0:T(8,128)(2,1)} %param.16, bf16[1,128,1024]{2,1,0:T(8,128)(2,1)S(1)} %copy-done.14), kind=kOutput, calls=%fused_computation.1 | convolution fusion | flops 268435456 | bytes 2883584 | tf_op jit(solution)/shard_map/dot_general | solution.py:331
  12.9 2.6 %fusion.11 = (f32[128]{0:T(128)S(1)}, f32[128]{0:T(128)S(1)}, f32[128,1024]{1,0:T(8,128)}) fusion(bf16[3,128,1024]{2,1,0:T(8,128)(2,1)} %hidden.1, f32[1024]{0:T(1024)S(1)} %bitcast.90, f32[128,1024]{1,0:T(8,128)S(1)} %fusion, bf16[1,1024,1024]{2,1,0:T(8,128)(2,1)S(1)} %copy-done.10, bf16[1,128,1024]{2,1,0:T(8,128)(2,1)S(1)} %copy-done), kind=kOutput, calls=%fused_computation.15 | convolution fusion | flops 269352704 | bytes 3675136 | tf_op jit(solution)/shard_map/dot_general | solution.py:328
  18.0 2.8 %collective-permute-start.3 = (f32[2,128]{1,0:T(2,128)S(1)}, f32[2,128]{1,0:T(2,128)S(1)}, u32[]{:S(2)}, u32[]{:S(2)}) collective-permute-start(f32[2,128]{1,0:T(2,128)S(1)} %fusion.30), channel_id=1, source_target_pairs={{0,4},{2,6},{4,0},{6,2},{1,5},{3,7},{5,1},{7,3},{8,12},{10,14},{12... | collective-permute-start | bytes 3080 | tf_op jit(solution)/shard_map/ppermute | solution.py:341
  22.2 2.2 %arrange.2 = bf16[16,192,128]{2,1,0:T(8,128)(2,1)} custom-call(bf16[3,128,2048]{2,1,0:T(8,128)(2,1)} %slabs.3), custom_call_target="tpu_custom_call" | custom-call | bytes 1600000 | tf_op jit(solution)/shard_map/arrange/pallas_call | solution.py:36
  27.2 11.5 %all-to-all-start = ((bf16[16,192,128]{2,1,0:T(8,128)(2,1)}), bf16[16,192,128]{2,1,0:T(8,128)(2,1)}, u32[]{:S(2)}, u32[]{:S(2)}) async-start(bf16[16,192,128]{2,1,0:T(8,128)(2,1)} %broadcast_select_fusion), calls=%async_computation | async-start | bytes 1572864 | tf_op jit(solution)/shard_map/all_to_all | solution.py:348
  39.9 2.3 %collective-permute-start.14 = (bf16[8,32,1024]{2,1,0:T(8,128)(2,1)}, bf16[8,32,1024]{2,1,0:T(8,128)(2,1)}, u32[]{:S(2)}, u32[]{:S(2)}) collective-permute-start(bf16[8,32,1024]{2,1,0:T(8,128)(2,1)} %get-tuple-element.60), channel_id=1, source_target_pairs={{0,129},{1,0},{128,1},{129,128},{2,131},{3,2},{130,3},{131,130},{4... | collective-permute-start | bytes 1572872 | tf_op jit(solution)/shard_map/ppermute | solution.py:347
  42.6 11.6 %collective-permute-done.12 = bf16[8,32,1024]{2,1,0:T(8,128)(2,1)} collective-permute-done((bf16[8,32,1024]{2,1,0:T(8,128)(2,1)S(1)}, bf16[8,32,1024]{2,1,0:T(8,128)(2,1)}, u32[]{:S(2)}, u32[]{:S(2)}) %collective-permute-start.12) | collective-permute-done | bytes 524320 | tf_op jit(solution)/shard_map/ppermute | solution.py:346
  54.2 2.7 %collective-permute-start.15 = (bf16[8,32,1024]{2,1,0:T(8,128)(2,1)}, bf16[8,32,1024]{2,1,0:T(8,128)(2,1)}, u32[]{:S(2)}, u32[]{:S(2)}) collective-permute-start(bf16[8,32,1024]{2,1,0:T(8,128)(2,1)} %collective-permute-done.14), channel_id=1, source_target_pairs={{0,129},{1,0},{128,1},{129,128},{2,131},{3,2},{130,3},{131,130},{4... | collective-permute-start | bytes 1572872 | tf_op jit(solution)/shard_map/ppermute | solution.py:347
  58.8 2.6 %all-to-all-done = bf16[16,192,128]{2,1,0:T(8,128)(2,1)} async-done(((bf16[16,192,128]{2,1,0:T(8,128)(2,1)}), bf16[16,192,128]{2,1,0:T(8,128)(2,1)}, u32[]{:S(2)}, u32[]{:S(2)}) %all-to-all-start) | async-done | bytes 786464 | tf_op jit(solution)/shard_map/all_to_all | solution.py:348
  61.4 2.3 %pick_layers.1 = (bf16[32,2,32,128]{3,2,1,0:T(8,128)(2,1)}, bf16[16,2,32,128]{3,2,1,0:T(8,128)(2,1)}, bf16[16,2,32,128]{3,2,1,0:T(8,128)(2,1)}) custom-call(s32[32]{0:T(128)} %layer_map.1, bf16[48,2,32,128]{3,2,1,0:T(8,128)(2,1)} %bitcast.26.received), custom_call_target="tpu_custom_call" | custom-call | bytes 1300000 | tf_op jit(solution)/shard_map/pick_layers/pallas_call | solution.py:65
  70.3 2.3 %collective-permute-done.7.refs_3_ = bf16[16,2,32,128]{3,2,1,0:T(8,128)(2,1)S(1)} collective-permute-done((bf16[16,2,32,128]{3,2,1,0:T(8,128)(2,1)}, bf16[16,2,32,128]{3,2,1,0:T(8,128)(2,1)S(1)}, u32[]{:S(2)}, u32[]{:S(2)}) %collective-permute-start.7) | collective-permute-done | bytes 262176 | tf_op jit(solution)/shard_map/ppermute | solution.py:280
  74.7 4.1 %collective-permute-done.5.refs_1_ = bf16[16,2,32,128]{3,2,1,0:T(8,128)(2,1)} collective-permute-done((bf16[16,2,32,128]{3,2,1,0:T(8,128)(2,1)}, bf16[16,2,32,128]{3,2,1,0:T(8,128)(2,1)}, u32[]{:S(2)}, u32[]{:S(2)}) %collective-permute-start.5) | collective-permute-done | bytes 262176 | tf_op jit(solution)/shard_map/ppermute | solution.py:284
  79.0 2.7 %collective-permute-start.11 = (bf16[16,2,32,128]{3,2,1,0:T(8,128)(2,1)}, bf16[16,2,32,128]{3,2,1,0:T(8,128)(2,1)S(1)}, u32[]{:S(2)}, u32[]{:S(2)}) collective-permute-start(bf16[16,2,32,128]{3,2,1,0:T(8,128)(2,1)} %collective-permute-done.6.refs_2_), channel_id=1, source_target_pairs={{0,6},{2,0},{4,2},{6,4},{1,7},{3,1},{5,3},{7,5},{8,14},{10,8},{12,... | collective-permute-start | bytes 786440 | tf_op jit(solution)/shard_map/ppermute | solution.py:286
  81.6 2.5 %collective-permute-start.18 = (bf16[32,2,32,128]{3,2,1,0:T(8,128)(2,1)}, bf16[32,2,32,128]{3,2,1,0:T(8,128)(2,1)}, u32[]{:S(2)}, u32[]{:S(2)}) collective-permute-start(bf16[32,2,32,128]{3,2,1,0:T(8,128)(2,1)} %collective-permute-done.9.refs_5_), channel_id=1, source_target_pairs={{0,6},{2,0},{4,2},{6,4},{1,7},{3,1},{5,3},{7,5},{8,14},{10,8},{12,... | collective-permute-start | bytes 1572872 | tf_op jit(solution)/shard_map/ppermute | solution.py:288
  84.1 2.2 %fusion.19 = (f32[1024]{0:T(1024)S(1)}, f32[128,1024]{1,0:T(8,128)}) fusion(f32[128,1024]{1,0:T(8,128)} %get-tuple-element.62, f32[128]{0:T(128)S(1)} %get-tuple-element.57, bf16[3,128,1024]{2,1,0:T(8,128)(2,1)} %hidden.1, f32[128]{0:T(128)S(1)} %slice_bitcast_fusion, f32[128]{0:T(128)S(1)} %get-tuple-element.56, f32[1024]{0:T(1024)S(1)} %bitcast.91, pred[]{:T(512)S(6)} %eq.28), kind=kLoop, calls=%fused_computation.23 | loop fusion | flops 1440768 | bytes 1320449 | tf_op jit(solution)/shard_map/reduce_sum | solution.py:364
  90.6 8.1 %project_first.1.partial = bf16[4,256,1024]{2,1,0:T(8,128)(2,1)S(1)} custom-call(s32[4]{0:T(128)S(1)} %pad_add_fusion.1.place, s32[5]{0:T(128)S(1)} %stack.83.blocks, bf16[32,2,32,128]{3,2,1,0:T(8,128)(2,1)S(1)} %copy-done.8, bf16[16,2,32,128]{3,2,1,0:T(8,128)(2,1)} %collective-permute-done.5.refs_1_, ...), custom_call_target="tpu_custom_call" | custom-call | flops 2684354560 | bytes 8388608 | tf_op jit(solution)/shard_map/project_first/pallas_call | solution.py:179
  101.5 7.7 %project_rest.1 = (bf16[3,32,1024]{2,1,0:T(8,128)(2,1)}, bf16[3,32,1024]{2,1,0:T(8,128)(2,1)}, bf16[3,32,1024]{2,1,0:T(8,128)(2,1)}, bf16[3,32,1024]{2,1,0:T(8,1...) custom-call(s32[4]{0:T(128)} %copy-done.7, ...), custom_call_target="tpu_custom_call" | custom-call | flops 1610612736 | bytes 11534336 | tf_op jit(solution)/shard_map/project_rest/pallas_call | solution.py:205
  109.5 2.1 %select_bitcast_fusion = bf16[1,1024,1024]{2,1,0:T(8,128)(2,1)} fusion(pred[]{:T(512)S(6)} %eq.28, bf16[1,128,1024]{2,1,0:T(8,128)(2,1)S(1)} %copy-done.15, f32[1024]{0:T(1024)S(1)} %bitcast.92, f32[128]{0:T(128)S(1)} %get-tuple-element.57, bf16[3,128,1024]{2,1,0:T(8,128)(2,1)S(1)} %copy-done.9), kind=kOutput, calls=%fused_computation.5 | convolution fusion | flops 271056896 | bytes 2626049 | tf_op jit(solution)/shard_map/dot_general | solution.py:361
  111.6 2.7 %collective-permute-start.34 = (bf16[3,32,1024]{2,1,0:T(8,128)(2,1)S(1)}, bf16[3,32,1024]{2,1,0:T(8,128)(2,1)S(1)}, u32[]{:S(2)}, u32[]{:S(2)}) collective-permute-start(bf16[3,32,1024]{2,1,0:T(8,128)(2,1)S(1)} %copy-done.35), channel_id=1, source_target_pairs={{0,112},{16,0},{32,16},{48,32},{64,48},{80,64},{96,80},{112,96},{1... | collective-permute-start | bytes 589832 | tf_op jit(solution)/shard_map/ppermute | solution.py:238
  114.3 2.7 %collective-permute-start.25 = (bf16[3,32,1024]{2,1,0:T(8,128)(2,1)S(1)}, bf16[3,32,1024]{2,1,0:T(8,128)(2,1)S(1)}, u32[]{:S(2)}, u32[]{:S(2)}) collective-permute-start(bf16[3,32,1024]{2,1,0:T(8,128)(2,1)S(1)} %copy-done.33), channel_id=1, source_target_pairs={{0,112},{16,0},{32,16},{48,32},{64,48},{80,64},{96,80},{112,96},{1... | collective-permute-start | bytes 589832 | tf_op jit(solution)/shard_map/ppermute | solution.py:237
  117.3 2.9 %collective-permute-start.35 = (bf16[3,32,1024]{2,1,0:T(8,128)(2,1)S(1)}, bf16[3,32,1024]{2,1,0:T(8,128)(2,1)S(1)}, u32[]{:S(2)}, u32[]{:S(2)}) collective-permute-start(bf16[3,32,1024]{2,1,0:T(8,128)(2,1)S(1)} %add_convert_fusion.2), channel_id=1, source_target_pairs={{0,112},{16,0},{32,16},{48,32},{64,48},{80,64},{96,80},{112,96},{1... | collective-permute-start | bytes 589832 | tf_op jit(solution)/shard_map/ppermute | solution.py:243
  121.1 3.1 %collective-permute-start.26 = (bf16[3,32,1024]{2,1,0:T(8,128)(2,1)S(1)}, bf16[3,32,1024]{2,1,0:T(8,128)(2,1)S(1)}, u32[]{:S(2)}, u32[]{:S(2)}) collective-permute-start(bf16[3,32,1024]{2,1,0:T(8,128)(2,1)S(1)} %add_convert_fusion.9), channel_id=1, source_target_pairs={{0,112},{16,0},{32,16},{48,32},{64,48},{80,64},{96,80},{112,96},{1... | collective-permute-start | bytes 589832 | tf_op jit(solution)/shard_map/ppermute | solution.py:244
  125.0 3.5 %collective-permute-start.36 = (bf16[3,32,1024]{2,1,0:T(8,128)(2,1)S(1)}, bf16[3,32,1024]{2,1,0:T(8,128)(2,1)S(1)}, u32[]{:S(2)}, u32[]{:S(2)}) collective-permute-start(bf16[3,32,1024]{2,1,0:T(8,128)(2,1)S(1)} %add_convert_fusion.1), channel_id=1, source_target_pairs={{0,112},{16,0},{32,16},{48,32},{64,48},{80,64},{96,80},{112,96},{1... | collective-permute-start | bytes 589832 | tf_op jit(solution)/shard_map/ppermute | solution.py:243
  129.5 2.7 %collective-permute-start.27 = (bf16[3,32,1024]{2,1,0:T(8,128)(2,1)S(1)}, bf16[3,32,1024]{2,1,0:T(8,128)(2,1)S(1)}, u32[]{:S(2)}, u32[]{:S(2)}) collective-permute-start(bf16[3,32,1024]{2,1,0:T(8,128)(2,1)S(1)} %add_convert_fusion.8), channel_id=1, source_target_pairs={{0,112},{16,0},{32,16},{48,32},{64,48},{80,64},{96,80},{112,96},{1... | collective-permute-start | bytes 589832 | tf_op jit(solution)/shard_map/ppermute | solution.py:244
  132.3 4.6 %collective-permute-done.27 = bf16[3,32,1024]{2,1,0:T(8,128)(2,1)S(1)} collective-permute-done((bf16[3,32,1024]{2,1,0:T(8,128)(2,1)S(1)}, bf16[3,32,1024]{2,1,0:T(8,128)(2,1)S(1)}, u32[]{:S(2)}, u32[]{:S(2)}) %collective-permute-start.27) | collective-permute-done | bytes 196640 | tf_op jit(solution)/shard_map/ppermute | solution.py:244
  137.0 3.3 %collective-permute-start.28 = (bf16[3,32,1024]{2,1,0:T(8,128)(2,1)S(1)}, bf16[3,32,1024]{2,1,0:T(8,128)(2,1)S(1)}, u32[]{:S(2)}, u32[]{:S(2)}) collective-permute-start(bf16[3,32,1024]{2,1,0:T(8,128)(2,1)S(1)} %add_convert_fusion.7), channel_id=1, source_target_pairs={{0,112},{16,0},{32,16},{48,32},{64,48},{80,64},{96,80},{112,96},{1... | collective-permute-start | bytes 589832 | tf_op jit(solution)/shard_map/ppermute | solution.py:244
  140.4 9.0 %collective-permute-start.37 = (bf16[3,32,1024]{2,1,0:T(8,128)(2,1)S(1)}, bf16[3,32,1024]{2,1,0:T(8,128)(2,1)S(1)}, u32[]{:S(2)}, u32[]{:S(2)}) collective-permute-start(bf16[3,32,1024]{2,1,0:T(8,128)(2,1)S(1)} %add_convert_fusion), channel_id=1, source_target_pairs={{0,8},{8,0},{1,9},{9,1},{2,10},{10,2},{3,11},{11,3},{4,12},{12,4},... | collective-permute-start | bytes 589832 | tf_op jit(solution)/shard_map/ppermute | solution.py:382
  152.2 2.1 %select_bitcast_fusion.1 = bf16[1,1024,1024]{2,1,0:T(8,128)(2,1)} fusion(pred[]{:T(512)S(6)} %eq.28, bf16[1,128,1024]{2,1,0:T(8,128)(2,1)S(1)} %copy-done, f32[1024]{0:T(1024)S(1)} %bitcast.93, f32[128]{0:T(128)S(1)} %get-tuple-element.57, bf16[3,128,1024]{2,1,0:T(8,128)(2,1)S(1)} %copy-done.9), kind=kOutput, calls=%fused_computation.6 | convolution fusion | flops 271056896 | bytes 2626049 | tf_op jit(solution)/shard_map/dot_general | solution.py:358
  154.9 4.2 %collective-permute-done.29.teacher = bf16[3,32,1024]{2,1,0:T(8,128)(2,1)S(1)} collective-permute-done((bf16[3,32,1024]{2,1,0:T(8,128)(2,1)S(1)}, bf16[3,32,1024]{2,1,0:T(8,128)(2,1)S(1)}, u32[]{:S(2)}, u32[]{:S(2)}) %collective-permute-start.29) | collective-permute-done | bytes 196640 | tf_op jit(solution)/shard_map/ppermute | solution.py:383
  159.8 2.6 %finish.1 = bf16[3,128,1024]{2,1,0:T(8,128)(2,1)} custom-call(s32[2]{0:T(128)} %pad_add_fusion.state, bf16[3,128,1024]{2,1,0:T(8,128)(2,1)} %hidden.1, f32[128,1024]{1,0:T(8,128)} %get-tuple-element.59.layer_grad, bf16[3,32,1024]{2,1,0:T(8,128)(2,1)} %copy-done.11, bf16[3,32,1024]{2,1,0:T(8,128)(2,1)} %copy-done.18, bf16[3,32,1024]{2,1,0:T(8,128)(2,1)} %copy-done.16, ...), custom_call_target="tpu_custom_call" | custom-call | flops 786432 | bytes 3145728 | tf_op jit(solution)/shard_map/finish/pallas_call | solution.py:266
  (171 shorter events, 33.5 us)
Async XLA Ops:
  3.0 22.1 %collective-permute-start = (bf16[16,192,128]{2,1,0:T(8,128)(2,1)}, bf16[16,192,128]{2,1,0:T(8,128)(2,1)}, u32[]{:S(2)}, u32[]{:S(2)}) collective-permute-start(bf16[16,192,128]{2,1,0:T(8,128)(2,1)} %arrange.3), channel_id=1, source_target_pairs={{0,129},{1,128},{2,131},{3,130},{4,133},{5,132},{6,135},{7,134},{8... | collective-permute-start | bytes 2359304 | tf_op jit(solution)/shard_map/ppermute | solution.py:343
  9.5 17.7 %collective-permute-start.1 = (bf16[8,64,1024]{2,1,0:T(8,128)(2,1)S(1)}, bf16[8,64,1024]{2,1,0:T(8,128)(2,1)S(1)}, u32[]{:S(2)}, u32[]{:S(2)}) collective-permute-start(bf16[8,64,1024]{2,1,0:T(8,128)(2,1)S(1)} %copy-done.1), channel_id=1, source_target_pairs={{0,8},{8,0},{1,9},{9,1},{2,10},{10,2},{3,11},{11,3},{4,12},{12,4},... | collective-permute-start | bytes 3145736 | tf_op jit(solution)/shard_map/ppermute | solution.py:321
  27.2 34.2 %all-to-all-start = ((bf16[16,192,128]{2,1,0:T(8,128)(2,1)}), bf16[16,192,128]{2,1,0:T(8,128)(2,1)}, u32[]{:S(2)}, u32[]{:S(2)}) async-start(bf16[16,192,128]{2,1,0:T(8,128)(2,1)} %broadcast_select_fusion), calls=%async_computation | async-start | bytes 1572864 | tf_op jit(solution)/shard_map/all_to_all | solution.py:348
  39.5 14.7 %collective-permute-start.12 = (bf16[8,32,1024]{2,1,0:T(8,128)(2,1)S(1)}, bf16[8,32,1024]{2,1,0:T(8,128)(2,1)}, u32[]{:S(2)}, u32[]{:S(2)}) collective-permute-start(bf16[8,32,1024]{2,1,0:T(8,128)(2,1)S(1)} %get-tuple-element.61), channel_id=1, source_target_pairs={{0,1},{1,128},{128,129},{129,0},{2,3},{3,130},{130,131},{131,2},{4... | collective-permute-start | bytes 1572872 | tf_op jit(solution)/shard_map/ppermute | solution.py:346
  39.9 14.4 %collective-permute-start.14 = (bf16[8,32,1024]{2,1,0:T(8,128)(2,1)}, bf16[8,32,1024]{2,1,0:T(8,128)(2,1)}, u32[]{:S(2)}, u32[]{:S(2)}) collective-permute-start(bf16[8,32,1024]{2,1,0:T(8,128)(2,1)} %get-tuple-element.60), channel_id=1, source_target_pairs={{0,129},{1,0},{128,1},{129,128},{2,131},{3,2},{130,3},{131,130},{4... | collective-permute-start | bytes 1572872 | tf_op jit(solution)/shard_map/ppermute | solution.py:347
  54.2 14.8 %collective-permute-start.13 = (bf16[8,32,1024]{2,1,0:T(8,128)(2,1)}, bf16[8,32,1024]{2,1,0:T(8,128)(2,1)S(1)}, u32[]{:S(2)}, u32[]{:S(2)}) collective-permute-start(bf16[8,32,1024]{2,1,0:T(8,128)(2,1)} %collective-permute-done.12), channel_id=1, source_target_pairs={{0,1},{1,128},{128,129},{129,0},{2,3},{3,130},{130,131},{131,2},{4... | collective-permute-start | bytes 1572872 | tf_op jit(solution)/shard_map/ppermute | solution.py:346
  54.2 15.1 %collective-permute-start.15 = (bf16[8,32,1024]{2,1,0:T(8,128)(2,1)}, bf16[8,32,1024]{2,1,0:T(8,128)(2,1)}, u32[]{:S(2)}, u32[]{:S(2)}) collective-permute-start(bf16[8,32,1024]{2,1,0:T(8,128)(2,1)} %collective-permute-done.14), channel_id=1, source_target_pairs={{0,129},{1,0},{128,1},{129,128},{2,131},{3,2},{130,3},{131,130},{4... | collective-permute-start | bytes 1572872 | tf_op jit(solution)/shard_map/ppermute | solution.py:347
  63.7 8.8 %collective-permute-start.7 = (bf16[16,2,32,128]{3,2,1,0:T(8,128)(2,1)}, bf16[16,2,32,128]{3,2,1,0:T(8,128)(2,1)S(1)}, u32[]{:S(2)}, u32[]{:S(2)}) collective-permute-start(bf16[16,2,32,128]{3,2,1,0:T(8,128)(2,1)} %get-tuple-element.32), channel_id=1, source_target_pairs={{0,2},{2,4},{4,6},{6,0},{1,3},{3,5},{5,7},{7,1},{8,10},{10,12},{12... | collective-permute-start | bytes 786440 | tf_op jit(solution)/shard_map/ppermute | solution.py:280
  64.9 8.5 %collective-permute-start.6 = (bf16[16,2,32,128]{3,2,1,0:T(8,128)(2,1)}, bf16[16,2,32,128]{3,2,1,0:T(8,128)(2,1)}, u32[]{:S(2)}, u32[]{:S(2)}) collective-permute-start(bf16[16,2,32,128]{3,2,1,0:T(8,128)(2,1)} %get-tuple-element.33), channel_id=1, source_target_pairs={{0,6},{2,0},{4,2},{6,4},{1,7},{3,1},{5,3},{7,5},{8,14},{10,8},{12,... | collective-permute-start | bytes 786440 | tf_op jit(solution)/shard_map/ppermute | solution.py:281
  67.7 11.1 %collective-permute-start.5 = (bf16[16,2,32,128]{3,2,1,0:T(8,128)(2,1)}, bf16[16,2,32,128]{3,2,1,0:T(8,128)(2,1)}, u32[]{:S(2)}, u32[]{:S(2)}) collective-permute-start(bf16[16,2,32,128]{3,2,1,0:T(8,128)(2,1)} %get-tuple-element.32), channel_id=1, source_target_pairs={{0,6},{2,0},{4,2},{6,4},{1,7},{3,1},{5,3},{7,5},{8,14},{10,8},{12,... | collective-permute-start | bytes 786440 | tf_op jit(solution)/shard_map/ppermute | solution.py:284
  69.0 10.0 %collective-permute-start.8 = (bf16[16,2,32,128]{3,2,1,0:T(8,128)(2,1)}, bf16[16,2,32,128]{3,2,1,0:T(8,128)(2,1)}, u32[]{:S(2)}, u32[]{:S(2)}) collective-permute-start(bf16[16,2,32,128]{3,2,1,0:T(8,128)(2,1)} %get-tuple-element.33), channel_id=1, source_target_pairs={{0,2},{2,4},{4,6},{6,0},{1,3},{3,5},{5,7},{7,1},{8,10},{10,12},{12... | collective-permute-start | bytes 786440 | tf_op jit(solution)/shard_map/ppermute | solution.py:283
  69.3 12.3 %collective-permute-start.9 = (bf16[32,2,32,128]{3,2,1,0:T(8,128)(2,1)}, bf16[32,2,32,128]{3,2,1,0:T(8,128)(2,1)}, u32[]{:S(2)}, u32[]{:S(2)}) collective-permute-start(bf16[32,2,32,128]{3,2,1,0:T(8,128)(2,1)} %get-tuple-element.31.refs_0_), channel_id=1, source_target_pairs={{0,1},{1,0},{2,3},{3,2},{4,5},{5,4},{6,7},{7,6},{8,9},{9,8},{10,11... | collective-permute-start | bytes 1572872 | tf_op jit(solution)/shard_map/ppermute | solution.py:282
  72.5 15.0 %collective-permute-start.16 = (bf16[8,32,1024]{2,1,0:T(8,128)(2,1)S(1)}, bf16[8,32,1024]{2,1,0:T(8,128)(2,1)S(1)}, u32[]{:S(2)}, u32[]{:S(2)}) collective-permute-start(bf16[8,32,1024]{2,1,0:T(8,128)(2,1)S(1)} %collective-permute-done.13.refs_10_.refs_6_), channel_id=1, source_target_pairs={{0,8},{8,0},{1,9},{9,1},{2,10},{10,2},{3,11},{11,3},{4,12},{12,4},... | collective-permute-start | bytes 1572872 | tf_op jit(solution)/shard_map/ppermute | solution.py:353
  73.5 10.6 %collective-permute-start.10 = (bf16[16,2,32,128]{3,2,1,0:T(8,128)(2,1)S(1)}, bf16[16,2,32,128]{3,2,1,0:T(8,128)(2,1)S(1)}, u32[]{:S(2)}, u32[]{:S(2)}) collective-permute-start(bf16[16,2,32,128]{3,2,1,0:T(8,128)(2,1)S(1)} %collective-permute-done.7.refs_3_), channel_id=1, source_target_pairs={{0,2},{2,4},{4,6},{6,0},{1,3},{3,5},{5,7},{7,1},{8,10},{10,12},{12... | collective-permute-start | bytes 786440 | tf_op jit(solution)/shard_map/ppermute | solution.py:285
  78.8 10.8 %collective-permute-start.17 = (bf16[8,32,1024]{2,1,0:T(8,128)(2,1)}, bf16[8,32,1024]{2,1,0:T(8,128)(2,1)S(1)}, u32[]{:S(2)}, u32[]{:S(2)}) collective-permute-start(bf16[8,32,1024]{2,1,0:T(8,128)(2,1)} %collective-permute-done.15.refs_11_.refs_7_), channel_id=1, source_target_pairs={{0,8},{8,0},{1,9},{9,1},{2,10},{10,2},{3,11},{11,3},{4,12},{12,4},... | collective-permute-start | bytes 1572872 | tf_op jit(solution)/shard_map/ppermute | solution.py:353
  79.0 8.6 %collective-permute-start.11 = (bf16[16,2,32,128]{3,2,1,0:T(8,128)(2,1)}, bf16[16,2,32,128]{3,2,1,0:T(8,128)(2,1)S(1)}, u32[]{:S(2)}, u32[]{:S(2)}) collective-permute-start(bf16[16,2,32,128]{3,2,1,0:T(8,128)(2,1)} %collective-permute-done.6.refs_2_), channel_id=1, source_target_pairs={{0,6},{2,0},{4,2},{6,4},{1,7},{3,1},{5,3},{7,5},{8,14},{10,8},{12,... | collective-permute-start | bytes 786440 | tf_op jit(solution)/shard_map/ppermute | solution.py:286
  81.6 19.2 %collective-permute-start.18 = (bf16[32,2,32,128]{3,2,1,0:T(8,128)(2,1)}, bf16[32,2,32,128]{3,2,1,0:T(8,128)(2,1)}, u32[]{:S(2)}, u32[]{:S(2)}) collective-permute-start(bf16[32,2,32,128]{3,2,1,0:T(8,128)(2,1)} %collective-permute-done.9.refs_5_), channel_id=1, source_target_pairs={{0,6},{2,0},{4,2},{6,4},{1,7},{3,1},{5,3},{7,5},{8,14},{10,8},{12,... | collective-permute-start | bytes 1572872 | tf_op jit(solution)/shard_map/ppermute | solution.py:288
  84.1 17.4 %collective-permute-start.21 = (bf16[32,2,32,128]{3,2,1,0:T(8,128)(2,1)}, bf16[32,2,32,128]{3,2,1,0:T(8,128)(2,1)}, u32[]{:S(2)}, u32[]{:S(2)}) collective-permute-start(bf16[32,2,32,128]{3,2,1,0:T(8,128)(2,1)} %collective-permute-done.9.refs_5_), channel_id=1, source_target_pairs={{0,2},{2,4},{4,6},{6,0},{1,3},{3,5},{5,7},{7,1},{8,10},{10,12},{12... | collective-permute-start | bytes 1572872 | tf_op jit(solution)/shard_map/ppermute | solution.py:287
  87.5 12.6 %collective-permute-start.19 = (bf16[16,2,32,128]{3,2,1,0:T(8,128)(2,1)S(1)}, bf16[16,2,32,128]{3,2,1,0:T(8,128)(2,1)S(1)}, u32[]{:S(2)}, u32[]{:S(2)}) collective-permute-start(bf16[16,2,32,128]{3,2,1,0:T(8,128)(2,1)S(1)} %collective-permute-done.10.refs_6_), channel_id=1, source_target_pairs={{0,1},{1,0},{2,3},{3,2},{4,5},{5,4},{6,7},{7,6},{8,9},{9,8},{10,11... | collective-permute-start | bytes 786440 | tf_op jit(solution)/shard_map/ppermute | solution.py:289
  87.5 12.6 %collective-permute-start.20 = (bf16[16,2,32,128]{3,2,1,0:T(8,128)(2,1)S(1)}, bf16[16,2,32,128]{3,2,1,0:T(8,128)(2,1)S(1)}, u32[]{:S(2)}, u32[]{:S(2)}) collective-permute-start(bf16[16,2,32,128]{3,2,1,0:T(8,128)(2,1)S(1)} %collective-permute-done.11.refs_7_), channel_id=1, source_target_pairs={{0,1},{1,0},{2,3},{3,2},{4,5},{5,4},{6,7},{7,6},{8,9},{9,8},{10,11... | collective-permute-start | bytes 786440 | tf_op jit(solution)/shard_map/ppermute | solution.py:290
  109.3 7.7 %collective-permute-start.30 = (bf16[3,32,1024]{2,1,0:T(8,128)(2,1)}, bf16[3,32,1024]{2,1,0:T(8,128)(2,1)S(1)}, u32[]{:S(2)}, u32[]{:S(2)}) collective-permute-start(bf16[3,32,1024]{2,1,0:T(8,128)(2,1)} %get-tuple-element.50), channel_id=1, source_target_pairs={{0,16},{16,32},{32,48},{48,64},{64,80},{80,96},{96,112},{112,0},{1... | collective-permute-start | bytes 589832 | tf_op jit(solution)/shard_map/ppermute | solution.py:236
  117.3 7.7 %collective-permute-start.35 = (bf16[3,32,1024]{2,1,0:T(8,128)(2,1)S(1)}, bf16[3,32,1024]{2,1,0:T(8,128)(2,1)S(1)}, u32[]{:S(2)}, u32[]{:S(2)}) collective-permute-start(bf16[3,32,1024]{2,1,0:T(8,128)(2,1)S(1)} %add_convert_fusion.2), channel_id=1, source_target_pairs={{0,112},{16,0},{32,16},{48,32},{64,48},{80,64},{96,80},{112,96},{1... | collective-permute-start | bytes 589832 | tf_op jit(solution)/shard_map/ppermute | solution.py:243
  121.0 8.3 %collective-permute-start.23 = (bf16[3,32,1024]{2,1,0:T(8,128)(2,1)S(1)}, bf16[3,32,1024]{2,1,0:T(8,128)(2,1)S(1)}, u32[]{:S(2)}, u32[]{:S(2)}) collective-permute-start(bf16[3,32,1024]{2,1,0:T(8,128)(2,1)S(1)} %add_convert_fusion.11), channel_id=1, source_target_pairs={{0,16},{16,32},{32,48},{48,64},{64,80},{80,96},{96,112},{112,0},{1... | collective-permute-start | bytes 589832 | tf_op jit(solution)/shard_map/ppermute | solution.py:246
  121.1 8.3 %collective-permute-start.26 = (bf16[3,32,1024]{2,1,0:T(8,128)(2,1)S(1)}, bf16[3,32,1024]{2,1,0:T(8,128)(2,1)S(1)}, u32[]{:S(2)}, u32[]{:S(2)}) collective-permute-start(bf16[3,32,1024]{2,1,0:T(8,128)(2,1)S(1)} %add_convert_fusion.9), channel_id=1, source_target_pairs={{0,112},{16,0},{32,16},{48,32},{64,48},{80,64},{96,80},{112,96},{1... | collective-permute-start | bytes 589832 | tf_op jit(solution)/shard_map/ppermute | solution.py:244
  124.4 7.8 %collective-permute-start.32 = (bf16[3,32,1024]{2,1,0:T(8,128)(2,1)S(1)}, bf16[3,32,1024]{2,1,0:T(8,128)(2,1)S(1)}, u32[]{:S(2)}, u32[]{:S(2)}) collective-permute-start(bf16[3,32,1024]{2,1,0:T(8,128)(2,1)S(1)} %add_convert_fusion.4), channel_id=1, source_target_pairs={{0,16},{16,32},{32,48},{48,64},{64,80},{80,96},{96,112},{112,0},{1... | collective-permute-start | bytes 589832 | tf_op jit(solution)/shard_map/ppermute | solution.py:241
  125.0 15.3 %collective-permute-start.36 = (bf16[3,32,1024]{2,1,0:T(8,128)(2,1)S(1)}, bf16[3,32,1024]{2,1,0:T(8,128)(2,1)S(1)}, u32[]{:S(2)}, u32[]{:S(2)}) collective-permute-start(bf16[3,32,1024]{2,1,0:T(8,128)(2,1)S(1)} %add_convert_fusion.1), channel_id=1, source_target_pairs={{0,112},{16,0},{32,16},{48,32},{64,48},{80,64},{96,80},{112,96},{1... | collective-permute-start | bytes 589832 | tf_op jit(solution)/shard_map/ppermute | solution.py:243
  129.3 21.4 %collective-permute-start.24 = (bf16[3,32,1024]{2,1,0:T(8,128)(2,1)S(1)}, bf16[3,32,1024]{2,1,0:T(8,128)(2,1)S(1)}, u32[]{:S(2)}, u32[]{:S(2)}) collective-permute-start(bf16[3,32,1024]{2,1,0:T(8,128)(2,1)S(1)} %add_convert_fusion.10), channel_id=1, source_target_pairs={{0,16},{16,32},{32,48},{48,64},{64,80},{80,96},{96,112},{112,0},{1... | collective-permute-start | bytes 589832 | tf_op jit(solution)/shard_map/ppermute | solution.py:246
  129.5 7.5 %collective-permute-start.27 = (bf16[3,32,1024]{2,1,0:T(8,128)(2,1)S(1)}, bf16[3,32,1024]{2,1,0:T(8,128)(2,1)S(1)}, u32[]{:S(2)}, u32[]{:S(2)}) collective-permute-start(bf16[3,32,1024]{2,1,0:T(8,128)(2,1)S(1)} %add_convert_fusion.8), channel_id=1, source_target_pairs={{0,112},{16,0},{32,16},{48,32},{64,48},{80,64},{96,80},{112,96},{1... | collective-permute-start | bytes 589832 | tf_op jit(solution)/shard_map/ppermute | solution.py:244
  132.3 8.1 %collective-permute-start.33 = (bf16[3,32,1024]{2,1,0:T(8,128)(2,1)S(1)}, bf16[3,32,1024]{2,1,0:T(8,128)(2,1)S(1)}, u32[]{:S(2)}, u32[]{:S(2)}) collective-permute-start(bf16[3,32,1024]{2,1,0:T(8,128)(2,1)S(1)} %add_convert_fusion.3), channel_id=1, source_target_pairs={{0,16},{16,32},{32,48},{48,64},{64,80},{80,96},{96,112},{112,0},{1... | collective-permute-start | bytes 589832 | tf_op jit(solution)/shard_map/ppermute | solution.py:241
  137.0 13.7 %collective-permute-start.28 = (bf16[3,32,1024]{2,1,0:T(8,128)(2,1)S(1)}, bf16[3,32,1024]{2,1,0:T(8,128)(2,1)S(1)}, u32[]{:S(2)}, u32[]{:S(2)}) collective-permute-start(bf16[3,32,1024]{2,1,0:T(8,128)(2,1)S(1)} %add_convert_fusion.7), channel_id=1, source_target_pairs={{0,112},{16,0},{32,16},{48,32},{64,48},{80,64},{96,80},{112,96},{1... | collective-permute-start | bytes 589832 | tf_op jit(solution)/shard_map/ppermute | solution.py:244
  140.4 13.9 %collective-permute-start.37 = (bf16[3,32,1024]{2,1,0:T(8,128)(2,1)S(1)}, bf16[3,32,1024]{2,1,0:T(8,128)(2,1)S(1)}, u32[]{:S(2)}, u32[]{:S(2)}) collective-permute-start(bf16[3,32,1024]{2,1,0:T(8,128)(2,1)S(1)} %add_convert_fusion), channel_id=1, source_target_pairs={{0,8},{8,0},{1,9},{9,1},{2,10},{10,2},{3,11},{11,3},{4,12},{12,4},... | collective-permute-start | bytes 589832 | tf_op jit(solution)/shard_map/ppermute | solution.py:382
  150.9 8.2 %collective-permute-start.29 = (bf16[3,32,1024]{2,1,0:T(8,128)(2,1)S(1)}, bf16[3,32,1024]{2,1,0:T(8,128)(2,1)S(1)}, u32[]{:S(2)}, u32[]{:S(2)}) collective-permute-start(bf16[3,32,1024]{2,1,0:T(8,128)(2,1)S(1)} %add_convert_fusion.6.near), channel_id=1, source_target_pairs={{0,128},{1,129},{2,130},{3,131},{4,132},{5,133},{6,134},{7,135},{8... | collective-permute-start | bytes 589832 | tf_op jit(solution)/shard_map/ppermute | solution.py:383
  (45 other events, 500.9 us)
